TPU v7x, 32 devices: a whole 2x2x4 slice. The times are simulated.
32 devices in a mesh: groups: 2 (over y), ctx: 4 (over z), head: 4 (over x, core).
Axes of the slice: x: 2, y: 2, z: 4, core: 2. Of those that a mesh axis runs over, the one named last changes fastest.
Arguments:
- queries: bfloat16 [1024, 6144], P(('groups', 'ctx'), 'head'), parts along dimension 0, may hold values from -128 to 128
- latent: bfloat16 [1024, 576], P(('groups', 'ctx')), parts along dimension 0, may hold values from -8 to 8
- w_keys: bfloat16 [512, 4096], P(None, 'head'), may hold values from -0.25 to 0.25
- w_values: bfloat16 [512, 4096], P(None, 'head'), may hold values from -0.25 to 0.25
- w_out: bfloat16 [4096, 3584], P('head'), may hold values from -0.375 to 0.375
- block_order: int32 [16], P('groups'), parts along dimension 0, may hold values from 0 to 7, as said below
- valid_lengths: int32 [16], P('groups'), parts along dimension 0, may hold values from 1 to 64, as said below
Outputs:
- mixed: bfloat16 [1024, 3584], P(('groups', 'ctx'), 'head'), parts along dimension 0
There are 2 independent parts, one for each index of `groups`. A program takes and returns all parts, laid end to end along the dimension named above; an argument that names none is the same for every part. Nothing has to cross between parts.
Inputs may be any that keep to these rules, and one draw needn't show every extreme that they name: `block_order`: a permutation of 0 to 7. `valid_lengths`: the half-block at place 0 of the prompt is always whole.
All inputs are finite; a program needn't handle non-finite values.
Results may differ from a plain program's by a relative error of at most 0.012.
Values may be sent and summed in bfloat16 or wider, within the bound.
No kernel may reach another device: no remote copies, remote signals or barrier semaphores. Data moves between devices by JAX's collectives and lax.ppermute only.
A program may use at most 64 MiB of HBM per device.

v0:
```python
import jax
import jax.numpy as jnp
from jax import lax
from jax.sharding import PartitionSpec as P

LATENT = 512
ROPE = 64
HEAD_DIM = 128


def from_behind(value, axis, steps):
    count = lax.axis_size(axis)
    pairs = [(source, (source + steps) % count) for source in range(count)]
    return lax.ppermute(value, axis, pairs)


def shards(queries, latent, w_keys, w_values, w_out, block_order, valid_lengths):
    ctx_count = lax.axis_size("ctx")
    ctx_place = lax.axis_index("ctx")
    tok_rows = queries.shape[0]
    half_rows = tok_rows // 2
    heads_here = w_keys.shape[1] // HEAD_DIM
    score_scale = (HEAD_DIM + ROPE) ** (-0.5)
    shaped = queries.reshape(tok_rows, heads_here, HEAD_DIM + ROPE)
    query_nope = shaped[:, :, :HEAD_DIM]
    query_rope = shaped[:, :, HEAD_DIM:]
    row_index = jnp.arange(tok_rows, dtype=jnp.int32)
    own_slots = 2 * ctx_place + row_index // half_rows
    query_pos = block_order[own_slots] * half_rows + row_index % half_rows
    key_offsets = jnp.arange(half_rows, dtype=jnp.int32)

    def expand(piece):
        rows_here = piece.shape[0]
        compressed = piece[:, :LATENT]
        key_rope = piece[:, LATENT:]
        key_flat = jnp.dot(compressed, w_keys, preferred_element_type=jnp.float32).astype(
            jnp.bfloat16
        )
        value_flat = jnp.dot(compressed, w_values, preferred_element_type=jnp.float32).astype(
            jnp.bfloat16
        )
        key_nope = key_flat.reshape(rows_here, heads_here, HEAD_DIM)
        value_heads = value_flat.reshape(rows_here, heads_here, HEAD_DIM)
        return (key_nope, value_heads, key_rope)

    def absorb(state, piece, slot):
        peak_old, total_old, sums_old = state
        key_nope, value_heads, key_rope = expand(piece)
        scores = jnp.einsum(
            "qhd,khd->hqk", query_nope, key_nope, preferred_element_type=jnp.float32
        )
        scores = scores + jnp.einsum(
            "qhd,kd->hqk", query_rope, key_rope, preferred_element_type=jnp.float32
        )
        key_pos = block_order[slot] * half_rows + key_offsets
        visible = (key_pos[None, :] <= query_pos[:, None]) & (key_offsets < valid_lengths[slot])[
            None, :
        ]
        masked = jnp.where(visible[None], scores * score_scale, jnp.float32(-1e30))
        peak_new = jnp.maximum(peak_old, jnp.max(masked, axis=2))
        weights = jnp.where(visible[None], jnp.exp(masked - peak_new[:, :, None]), jnp.float32(0.0))
        factor = jnp.exp(peak_old - peak_new)
        total_new = total_old * factor + jnp.sum(weights, axis=2)
        added = jnp.einsum(
            "hqk,khd->hqd",
            weights.astype(jnp.bfloat16),
            value_heads,
            preferred_element_type=jnp.float32,
        )
        sums_new = sums_old * factor[:, :, None] + added
        return (peak_new, total_new, sums_new)

    def take_block(state, block, source):
        for which_half in range(2):
            slot = 2 * source + which_half
            piece = block[which_half * half_rows : (which_half + 1) * half_rows]
            state = absorb(state, piece, slot)
        return state

    state = (
        jnp.full((heads_here, tok_rows), -1e30, jnp.float32),
        jnp.zeros((heads_here, tok_rows), jnp.float32),
        jnp.zeros((heads_here, tok_rows, HEAD_DIM), jnp.float32),
    )
    state = take_block(state, latent, ctx_place)

    def turn_one(step, carry):
        moving, inner_state = carry
        moving = from_behind(moving, "ctx", 1)
        inner_state = take_block(inner_state, moving, (ctx_place - step) % ctx_count)
        return (moving, inner_state)

    moving, state = lax.fori_loop(1, ctx_count, turn_one, (latent, state))
    peak_all, total_all, sums_all = state
    attended = (sums_all / total_all[:, :, None]).transpose(1, 0, 2)
    attended = attended.reshape(tok_rows, heads_here * HEAD_DIM).astype(jnp.bfloat16)
    share = lax.psum_scatter(
        lax.dot_general(
            w_out, attended, (((0,), (1,)), ((), ())), preferred_element_type=jnp.float32
        ).astype(jnp.bfloat16),
        "head",
        scatter_dimension=0,
        tiled=True,
    ).astype(jnp.float32)
    return share.T.astype(jnp.bfloat16)


def solution(mesh):
    in_specs = (
        P(("groups", "ctx"), "head"),
        P(("groups", "ctx"), None),
        P(None, "head"),
        P(None, "head"),
        P("head", None),
        P("groups"),
        P("groups"),
    )
    out_specs = P(("groups", "ctx"), "head")
    return jax.shard_map(shards, mesh=mesh, in_specs=in_specs, out_specs=out_specs, check_vma=False)
```

profile of v0, /device:TPU:0, one launch (start us, length us, event | category | flops | bytes accessed | tf_op | source)
XLA Modules:
  0.0 115.2 jit_solution(18014148416753274203)
XLA Ops:
  6.6 1.4 %copy.40 = bf16[128,1536]{0,1:T(8,128)(2,1)S(1)} copy(bf16[128,1536]{1,0:T(8,128)(2,1)} %param.9) | data formatting | bytes 786432 | tf_op args[0]
  8.0 1.1 copy.48
  9.4 2.4 %fusion.54 = bf16[8,8,8,128]{3,2,1,0:T(8,128)(2,1)} fusion(bf16[512,1024]{1,0:T(8,128)(2,1)} %param.11, bf16[128,576]{0,1:T(8,128)(2,1)} %param.10), kind=kOutput, calls=%fused_computation.97 | convolution fusion | flops 67174400 | bytes 1310720 | tf_op jit(solution)/shard_map/dot_general | solution.py:36
  11.7 2.3 %fusion.53 = bf16[8,8,8,128]{3,2,1,0:T(8,128)(2,1)} fusion(bf16[512,1024]{1,0:T(8,128)(2,1)} %param.11, bf16[128,576]{0,1:T(8,128)(2,1)} %param.10), kind=kOutput, calls=%fused_computation.96 | convolution fusion | flops 67174400 | bytes 1310720 | tf_op jit(solution)/shard_map/dot_general | solution.py:36
  14.0 1.6 %fusion.55 = bf16[8,8,8,128]{3,2,1,0:T(8,128)(2,1)S(1)} fusion(bf16[512,1024]{1,0:T(8,128)(2,1)} %param.12, bf16[128,576]{0,1:T(8,128)(2,1)} %param.10), kind=kOutput, calls=%fused_computation.98 | convolution fusion | flops 67174400 | bytes 1310720 | tf_op jit(solution)/shard_map/dot_general | solution.py:39
  15.6 2.4 %fusion.56 = bf16[8,8,8,128]{3,2,1,0:T(8,128)(2,1)} fusion(bf16[512,1024]{1,0:T(8,128)(2,1)} %param.12, bf16[128,576]{0,1:T(8,128)(2,1)} %param.10), kind=kOutput, calls=%fused_computation.99 | convolution fusion | flops 67174400 | bytes 1310720 | tf_op jit(solution)/shard_map/dot_general | solution.py:39
  18.0 0.7 slice.101
  18.8 0.7 fusion.97
  20.6 0.6 iota_add_fusion.3
  21.2 1.1 iota_compare_fusion.2
  22.4 1.2 %iota_compare_fusion.3 = pred[64]{0:T(512)(128)(4,1)} fusion(s32[]{:T(128)} %bitcast.11), kind=kLoop, calls=%fused_computation.152 | loop fusion | flops 64 | bytes 68 | tf_op jit(solution)/shard_map/lt | solution.py:56
  23.5 1.1 copy.52
  24.6 4.9 %fusion.81 = s32[128]{0:T(128)S(1)} fusion(s32[]{:T(128)} %bitcast.3, s32[]{:T(128)} %bitcast.4, s32[]{:T(128)} %bitcast.5, s32[]{:T(128)} %bitcast.6, s32[]{:T(128)} %bitcast.7, s32[]{:T(128)} %bitcast.9, s32[]{:T(128)} %bitcast.8, s32[]{:T(128)} %bitcast.2, s32[]{:T(128)} %mul.176), kind=kLoop, calls=%fused_computation.146 | loop fusion | flops 4352 | bytes 548 | tf_op jit(solution)/shard_map/add | solution.py:29
  29.5 0.8 compare_and_fusion.3
  30.3 1.1 fusion.100
  31.4 1.1 fusion.99
  32.7 0.4 fusion.46
  33.2 1.2 %convolution_add_fusion.2 = f32[8,128,128]{2,1,0:T(8,128)S(1)} fusion(f32[8,128,128]{2,1,0:T(8,128)S(1)} %fusion.46, f32[8,128,64]{1,2,0:T(8,128)S(1)} %get-tuple-element.581, bf16[8,8,8,128]{3,2,1,0:T(8,128)(2,1)} %fusion.56, f32[8,128]{1,0:T(8,128)S(1)} %get-tuple-element.751, pred[128,64]{0,1:T(8,128)(4,1)S(1)} %get-tuple-element.565), kind=kOutput, calls=%fused_computation.79 | convolution fusion | flops 17104896 | bytes 1454080 | tf_op jit(solution)/shard_map/hqk,khd->hqd/dot_general | solution.py:64
  34.4 42.3 %while.23 = (s32[]{:T(128)}, bf16[128,576]{1,0:T(8,128)(2,1)}, f32[8,128]{1,0:T(8,128)S(1)}, f32[8,128]{1,0:T(8,128)S(1)}, f32[8,128,128]{2,1,0:T(8,128)S(1)}, /...) while((s32[]{:T(128)}, bf16[128,576]{1,0:T(8,128)(2,1)}, ...), condition=%wide.region_9.10_spmd.clone.clone, body=%wide.region_4.9_spmd.clone.clone.sunk | while | flops 354460160 | bytes 12102510 | solution.py:93
  34.4 3.1 %collective-permute-start = (bf16[128,576]{1,0:T(8,128)(2,1)}, bf16[128,576]{1,0:T(8,128)(2,1)S(1)}, u32[]{:S(2)}, u32[]{:S(2)}) collective-permute-start(bf16[128,576]{1,0:T(8,128)(2,1)} %get-tuple-element.779), channel_id=1, source_target_pairs={{0,4},{4,8},{8,12},{12,0},{1,5},{5,9},{9,13},{13,1},{2,6},{6,10},{... | collective-permute-start | bytes 442376 | tf_op jit(solution)/shard_map/while/body/eval_jaxpr/ppermute | solution.py:14
  37.5 0.7 fusion.165
  39.4 0.7 iota_compare_fusion.6
  40.1 0.6 iota_compare_fusion.7
  40.7 4.9 %fusion.164 = s32[128]{0:T(128)S(1)} fusion(s32[]{:T(128)} %get-tuple-element.820, s32[]{:T(128)} %get-tuple-element.821, s32[]{:T(128)} %get-tuple-element.822, s32[]{:T(128)} %get-tuple-element.823, s32[]{:T(128)} %get-tuple-element.824, s32[]{:T(128)} %get-tuple-element.825, s32[]{:T(128)} %get-tuple-element.826, s32[]{:T(128)} %get-tuple-element.827, ...), kind=kLoop, calls=%fused_computation.71.clone.1 | loop fusion | flops 4352 | bytes 548 | tf_op jit(solution)/shard_map/add | solution.py:29
  45.7 0.3 fusion.167
  46.3 0.3 fusion.163
  47.8 0.5 fusion.173
  48.8 0.7 copy.116
  49.5 1.6 %collective-permute-start = (bf16[128,576]{1,0:T(8,128)(2,1)}, bf16[128,576]{1,0:T(8,128)(2,1)S(1)}, u32[]{:S(2)}, u32[]{:S(2)}) collective-permute-start(bf16[128,576]{1,0:T(8,128)(2,1)} %get-tuple-element.779), channel_id=1, source_target_pairs={{0,4},{4,8},{8,12},{12,0},{1,5},{5,9},{9,13},{13,1},{2,6},{6,10},{... | collective-permute-start | bytes 442376 | tf_op jit(solution)/shard_map/while/body/eval_jaxpr/ppermute | solution.py:14
  51.1 0.7 fusion.165
  53.1 0.7 iota_compare_fusion.6
  53.8 0.6 iota_compare_fusion.7
  54.3 4.9 %fusion.164 = s32[128]{0:T(128)S(1)} fusion(s32[]{:T(128)} %get-tuple-element.820, s32[]{:T(128)} %get-tuple-element.821, s32[]{:T(128)} %get-tuple-element.822, s32[]{:T(128)} %get-tuple-element.823, s32[]{:T(128)} %get-tuple-element.824, s32[]{:T(128)} %get-tuple-element.825, s32[]{:T(128)} %get-tuple-element.826, s32[]{:T(128)} %get-tuple-element.827, ...), kind=kLoop, calls=%fused_computation.71.clone.1 | loop fusion | flops 4352 | bytes 548 | tf_op jit(solution)/shard_map/add | solution.py:29
  59.9 0.3 fusion.163
  61.4 0.5 fusion.173
  62.4 0.7 copy.116
  63.1 1.6 %collective-permute-start = (bf16[128,576]{1,0:T(8,128)(2,1)}, bf16[128,576]{1,0:T(8,128)(2,1)S(1)}, u32[]{:S(2)}, u32[]{:S(2)}) collective-permute-start(bf16[128,576]{1,0:T(8,128)(2,1)} %get-tuple-element.779), channel_id=1, source_target_pairs={{0,4},{4,8},{8,12},{12,0},{1,5},{5,9},{9,13},{13,1},{2,6},{6,10},{... | collective-permute-start | bytes 442376 | tf_op jit(solution)/shard_map/while/body/eval_jaxpr/ppermute | solution.py:14
  64.7 0.7 fusion.165
  66.7 0.7 iota_compare_fusion.6
  67.4 0.6 iota_compare_fusion.7
  67.9 4.9 %fusion.164 = s32[128]{0:T(128)S(1)} fusion(s32[]{:T(128)} %get-tuple-element.820, s32[]{:T(128)} %get-tuple-element.821, s32[]{:T(128)} %get-tuple-element.822, s32[]{:T(128)} %get-tuple-element.823, s32[]{:T(128)} %get-tuple-element.824, s32[]{:T(128)} %get-tuple-element.825, s32[]{:T(128)} %get-tuple-element.826, s32[]{:T(128)} %get-tuple-element.827, ...), kind=kLoop, calls=%fused_computation.71.clone.1 | loop fusion | flops 4352 | bytes 548 | tf_op jit(solution)/shard_map/add | solution.py:29
  73.5 0.3 fusion.163
  75.0 0.5 fusion.173
  76.0 0.7 copy.116
  77.0 4.2 %fusion.45 = bf16[3584,128]{0,1:T(8,128)(2,1)S(1)} fusion(bf16[128,1024]{0,1:T(8,128)(2,1)S(1)} %bitcast.224, bf16[1024,3584]{1,0:T(8,128)(2,1)} %param.13), kind=kOutput, calls=%fused_computation.78 | convolution fusion | flops 939982848 | bytes 8519680 | tf_op jit(solution)/shard_map/dot_general | solution.py:98
  81.2 1.3 %copy.50 = bf16[3584,128]{1,0:T(8,128)(2,1)} copy(bf16[3584,128]{0,1:T(8,128)(2,1)S(1)} %fusion.45) | data formatting | bytes 1835008
  82.5 24.1 %reduce-scatter.4.cloned.1.call-done = bf16[896,128]{1,0:T(8,128)(2,1)} async-done(((bf16[3584,128]{1,0:T(8,128)(2,1)}), bf16[896,128]{1,0:T(8,128)(2,1)}) %reduce-scatter.4.cloned.1.call-update) | async-done | bytes 229392
  106.6 1.8 %copy.51 = bf16[896,128]{0,1:T(8,128)(2,1)} copy(bf16[896,128]{1,0:T(8,128)(2,1)} %reduce-scatter.4.cloned.1.call-done) | data formatting | bytes 458752
  (72 shorter events, 7.6 us)
Async XLA Ops:
  6.5 27.8 %copy-start = (bf16[512,1024]{1,0:T(8,128)(2,1)S(1)}, bf16[512,1024]{1,0:T(8,128)(2,1)}, u32[]{:S(2)}) copy-start(bf16[512,1024]{1,0:T(8,128)(2,1)} %param.11) | copy-start | bytes 3145732
  6.5 27.8 %copy-start.1 = (bf16[512,1024]{1,0:T(8,128)(2,1)S(1)}, bf16[512,1024]{1,0:T(8,128)(2,1)}, u32[]{:S(2)}) copy-start(bf16[512,1024]{1,0:T(8,128)(2,1)} %param.12) | copy-start | bytes 3145732
  6.5 12.2 %copy-start.3 = (s32[8]{0:T(128)S(1)}, s32[8]{0:T(128)}, u32[]{:S(2)}) copy-start(s32[8]{0:T(128)} %param.14) | copy-start | bytes 100
  6.5 12.2 %copy-start.4 = (s32[8]{0:T(128)S(1)}, s32[8]{0:T(128)}, u32[]{:S(2)}) copy-start(s32[8]{0:T(128)} %param.15) | copy-start | bytes 100
  6.5 100.1 %reduce-scatter.4.cloned.1.call-start = ((), (), s32[]{:S(2)}) async-start(), calls=%async_computation.1 | async-start | bytes 1146880
  9.0 13.3 %copy-start.2 = (bf16[128,576]{1,0:T(8,128)(2,1)}, bf16[128,576]{1,0:T(8,128)(2,1)S(1)}, u32[]{:S(2)}) copy-start(bf16[128,576]{1,0:T(8,128)(2,1)S(1)} %copy.48) | copy-start | bytes 442372
  34.4 11.3 %collective-permute-start = (bf16[128,576]{1,0:T(8,128)(2,1)}, bf16[128,576]{1,0:T(8,128)(2,1)S(1)}, u32[]{:S(2)}, u32[]{:S(2)}) collective-permute-start(bf16[128,576]{1,0:T(8,128)(2,1)} %get-tuple-element.779), channel_id=1, source_target_pairs={{0,4},{4,8},{8,12},{12,0},{1,5},{5,9},{9,13},{13,1},{2,6},{6,10},{... | collective-permute-start | bytes 442376 | tf_op jit(solution)/shard_map/while/body/eval_jaxpr/ppermute | solution.py:14
  49.5 9.8 %collective-permute-start = (bf16[128,576]{1,0:T(8,128)(2,1)}, bf16[128,576]{1,0:T(8,128)(2,1)S(1)}, u32[]{:S(2)}, u32[]{:S(2)}) collective-permute-start(bf16[128,576]{1,0:T(8,128)(2,1)} %get-tuple-element.779), channel_id=1, source_target_pairs={{0,4},{4,8},{8,12},{12,0},{1,5},{5,9},{9,13},{13,1},{2,6},{6,10},{... | collective-permute-start | bytes 442376 | tf_op jit(solution)/shard_map/while/body/eval_jaxpr/ppermute | solution.py:14
  63.1 9.8 %collective-permute-start = (bf16[128,576]{1,0:T(8,128)(2,1)}, bf16[128,576]{1,0:T(8,128)(2,1)S(1)}, u32[]{:S(2)}, u32[]{:S(2)}) collective-permute-start(bf16[128,576]{1,0:T(8,128)(2,1)} %get-tuple-element.779), channel_id=1, source_target_pairs={{0,4},{4,8},{8,12},{12,0},{1,5},{5,9},{9,13},{13,1},{2,6},{6,10},{... | collective-permute-start | bytes 442376 | tf_op jit(solution)/shard_map/while/body/eval_jaxpr/ppermute | solution.py:14
Sparse Core Ops, SparseCore 0:
  82.6 23.9 reduce-scatter.3
where the time goes:
time: 116 us; the launch traced here: 115 us
  other arithmetic  27.8 us (24%)
  matrix products  25.7 us (22%)
  waiting for transfers between devices  24.1 us (21%)
  between operations  14.8 us (13%)
  local copies, waits for them, and re-layouts  12.3 us (11%)
  starting transfers between devices  6.26 us (5%)
  loops' own time  4.27 us (4%)
    unnamed x2, waiting for transfers between devices  24.1 us
    add x4, other arithmetic, shards(): query_pos = block_order[own_slots] * half_rows + row_index % half_rows  19.5 us
    unnamed x16, local copies, waits for them, and re-layouts  7.33 us
    dot_general x8, matrix products, expand(): jnp.dot(compressed, w_keys, preferred_element_type=jnp.float32)  6.51 us
    ppermute x3, starting transfers between devices, from_behind(): return lax.ppermute(value, axis, pairs)  6.23 us
    lt x8, other arithmetic, absorb(): key_offsets < valid_lengths[slot]  6.07 us
    dot_general x8, matrix products, expand(): jnp.dot(compressed, w_values, preferred_element_type=jnp.float32)  5.81 us
    another operation x1, loops' own time, shards(): moving, state = lax.fori_loop(1, ctx_count, turn_one, (latent, state))  4.27 us
  transfers between devices with their start and end apart: 4, of which 1 were waited for; matrix products, arithmetic and copies ran while one was open for 18% of the time, Pallas kernels for 0%

commit v1 on v0

v1 whole, which is shorter than its diff:
```python
import functools

import jax
import jax.numpy as jnp
from jax import lax
from jax.experimental import pallas as pl
from jax.experimental.pallas import tpu as pltpu
from jax.sharding import PartitionSpec as P

LATENT = 512
ROPE = 64
HEAD_DIM = 128
QUERY = HEAD_DIM + ROPE
PARTS = 4
ROWS_AT_ONCE = 256
NT = (((1,), (1,)), ((), ()))
VMEM_BYTES = 48 * 1024 * 1024


def shifted(value, axis, steps):
    count = lax.axis_size(axis)
    return lax.ppermute(value, axis, [(i, (i + steps) % count) for i in range(count)])


def crossed(value, axis, bit):
    count = lax.axis_size(axis)
    return lax.ppermute(value, axis, [(i, i ^ bit) for i in range(count)])


def fold_keys_kernel(queries_ref, w_keys_ref, folded_ref):
    rows = queries_ref.shape[0]
    for head in range(w_keys_ref.shape[1] // HEAD_DIM):
        nope = queries_ref[:, head * QUERY : head * QUERY + HEAD_DIM]
        rope = queries_ref[:, head * QUERY + HEAD_DIM : (head + 1) * QUERY]
        weight = w_keys_ref[:, head * HEAD_DIM : (head + 1) * HEAD_DIM]
        here = slice(head * rows, (head + 1) * rows)
        product = lax.dot_general(nope, weight, NT, preferred_element_type=jnp.float32)
        folded_ref[here, :LATENT] = product.astype(jnp.bfloat16)
        folded_ref[here, LATENT:] = rope


def fold_keys(queries, w_keys):
    rows = queries.shape[0]
    heads = w_keys.shape[1] // HEAD_DIM
    return pl.pallas_call(
        fold_keys_kernel,
        out_shape=jax.ShapeDtypeStruct((heads * rows, LATENT + ROPE), jnp.bfloat16),
        in_specs=[pl.BlockSpec(memory_space=pltpu.VMEM)] * 2,
        out_specs=pl.BlockSpec(memory_space=pltpu.VMEM),
        compiler_params=pltpu.CompilerParams(vmem_limit_bytes=VMEM_BYTES),
        cost_estimate=pl.CostEstimate(
            flops=2 * rows * heads * HEAD_DIM * LATENT,
            bytes_accessed=2 * (queries.size + w_keys.size + heads * rows * (LATENT + ROPE)),
            transcendentals=0,
        ),
        name="fold_keys",
    )(queries, w_keys)


def attend_kernel(count, rows, order_ref, lens_ref, place_ref, folded_ref, w_values_ref, w_out_ref, *rest):
    blocks, rest = rest[:count], rest[count:]
    outs, rest = rest[:PARTS], rest[PARTS:]
    keys_ref, w_part_ref, attended_ref, block_sems, part_sems = rest
    half = rows // 2
    width = w_out_ref.shape[1] // PARTS
    heads = w_values_ref.shape[1] // HEAD_DIM
    exponent = (HEAD_DIM + ROPE) ** -0.5 * 1.4426950408889634
    ctx = place_ref[0]

    block_copies = []
    for step in range(count):
        copy = pltpu.make_async_copy(
            blocks[step], keys_ref.at[pl.ds(step * rows, rows)], block_sems.at[step]
        )
        copy.start()
        block_copies.append(copy)
    part_copies = []
    for part in range(PARTS):
        start = pl.multiple_of(place_ref[1 + part] * width, 128)
        copy = pltpu.make_async_copy(
            w_out_ref.at[:, pl.ds(start, width)], w_part_ref.at[part], part_sems.at[part]
        )
        copy.start()
        part_copies.append(copy)

    row = lax.broadcasted_iota(jnp.int32, (rows, rows), 0)
    lane = lax.broadcasted_iota(jnp.int32, (rows, rows), 1)
    query_pos = jnp.where(row < half, order_ref[2 * ctx], order_ref[2 * ctx + 1]) * half + row % half
    seen = []
    for step in range(count):
        source = lax.rem(ctx + (count - step), count)
        first, second = 2 * source, 2 * source + 1
        offset = lane % half
        key_pos = jnp.where(lane < half, order_ref[first], order_ref[second]) * half + offset
        length = jnp.where(lane < half, lens_ref[first], lens_ref[second])
        seen.append((key_pos <= query_pos) & (offset < length))
    visible = jnp.concatenate(seen, axis=1)
    stacked = ROWS_AT_ONCE // rows
    visible = jnp.concatenate([visible] * stacked, axis=0)

    for copy in block_copies:
        copy.wait()
    for group in range(heads // stacked):
        lines = slice(group * ROWS_AT_ONCE, (group + 1) * ROWS_AT_ONCE)
        scores = lax.dot_general(
            folded_ref[lines, :], keys_ref[...], NT, preferred_element_type=jnp.float32
        )
        scores = jnp.where(visible, scores, jnp.float32(-1e30))
        peak = jnp.max(scores, axis=1, keepdims=True)
        weights = jnp.exp2((scores - peak) * jnp.float32(exponent))
        total = jnp.sum(weights, axis=1, keepdims=True)
        mixed = jnp.dot(
            weights.astype(jnp.bfloat16), keys_ref[:, :LATENT], preferred_element_type=jnp.float32
        )
        mixed = (mixed / total).astype(jnp.bfloat16)
        for inner in range(stacked):
            head = group * stacked + inner
            columns = slice(head * HEAD_DIM, (head + 1) * HEAD_DIM)
            value = jnp.dot(
                mixed[inner * rows : (inner + 1) * rows, :],
                w_values_ref[:, columns],
                preferred_element_type=jnp.float32,
            )
            attended_ref[:, columns] = value.astype(jnp.bfloat16)

    for part in range(PARTS):
        part_copies[part].wait()
        outs[part][...] = jnp.dot(
            attended_ref[...], w_part_ref[part], preferred_element_type=jnp.float32
        ).astype(outs[part].dtype)


def attend(folded, blocks, w_values, w_out, block_order, valid_lengths, place, out_types):
    count = len(blocks)
    rows = blocks[0].shape[0]
    width = w_out.shape[1] // PARTS
    heads = w_values.shape[1] // HEAD_DIM
    keys = count * rows
    flops = 2 * heads * rows * (keys * (2 * LATENT + ROPE) + LATENT * HEAD_DIM)
    flops += 2 * rows * w_out.size
    smem = pl.BlockSpec(memory_space=pltpu.SMEM)
    vmem = pl.BlockSpec(memory_space=pltpu.VMEM)
    hbm = pl.BlockSpec(memory_space=pl.ANY)
    return pl.pallas_call(
        functools.partial(attend_kernel, count, rows),
        out_shape=[jax.ShapeDtypeStruct((rows, width), kind) for kind in out_types],
        in_specs=[smem, smem, smem, vmem, vmem, hbm] + [hbm] * count,
        out_specs=[vmem] * PARTS,
        scratch_shapes=[
            pltpu.VMEM((keys, LATENT + ROPE), jnp.bfloat16),
            pltpu.VMEM((PARTS, w_out.shape[0], width), jnp.bfloat16),
            pltpu.VMEM((rows, heads * HEAD_DIM), jnp.bfloat16),
            pltpu.SemaphoreType.DMA((count,)),
            pltpu.SemaphoreType.DMA((PARTS,)),
        ],
        compiler_params=pltpu.CompilerParams(vmem_limit_bytes=VMEM_BYTES),
        cost_estimate=pl.CostEstimate(
            flops=flops,
            bytes_accessed=2 * (folded.size + w_values.size + w_out.size + keys * (LATENT + ROPE)),
            transcendentals=heads * rows * keys,
        ),
        name="attend",
    )(block_order, valid_lengths, place, folded, w_values, w_out, *blocks)


def shards(queries, latent, w_keys, w_values, w_out, block_order, valid_lengths):
    ctx_count = lax.axis_size("ctx")
    head_count = lax.axis_size("head")
    ctx_place = lax.axis_index("ctx")
    head_place = lax.axis_index("head")
    blocks = [latent] + [shifted(latent, "ctx", step) for step in range(1, ctx_count)]
    folded = fold_keys(queries, w_keys)
    pairwise = head_count == 4
    if pairwise:
        parts = [head_place ^ 3, head_place ^ 1, head_place ^ 2, head_place]
        out_types = [jnp.bfloat16, jnp.bfloat16, jnp.float32, jnp.float32]
    else:
        parts = list(range(PARTS))
        out_types = [jnp.bfloat16] * PARTS
    place = jnp.stack([jnp.int32(item) for item in [ctx_place] + parts])
    across, beside, far, own = attend(
        folded, blocks, w_values, w_out, block_order, valid_lengths, place, out_types
    )
    if not pairwise:
        whole = jnp.concatenate([across, beside, far, own], axis=1)
        return lax.psum_scatter(whole, "head", scatter_dimension=1, tiled=True)
    far = far + crossed(across, "head", 1).astype(jnp.float32)
    near = crossed(beside, "head", 1).astype(jnp.float32)
    far = crossed(far.astype(jnp.bfloat16), "head", 2).astype(jnp.float32)
    return (own + near + far).astype(jnp.bfloat16)


def solution(mesh):
    in_specs = (
        P(("groups", "ctx"), "head"),
        P(("groups", "ctx"), None),
        P(None, "head"),
        P(None, "head"),
        P("head", None),
        P("groups"),
        P("groups"),
    )
    out_specs = P(("groups", "ctx"), "head")
    return jax.shard_map(shards, mesh=mesh, in_specs=in_specs, out_specs=out_specs, check_vma=False)
```

time: 116 us -> 39.3 us (0.34)
  other arithmetic: 27.8 us -> 0.82 us
  matrix products: 25.7 us -> 0 us
  between operations: 14.8 us -> 0.04 us
  waiting for transfers between devices: 24.1 us -> 17.2 us
  Pallas kernels: 0 us -> 6.79 us
  local copies, waits for them, and re-layouts: 12.3 us -> 5.9 us
  loops' own time: 4.27 us -> 0 us
  starting transfers between devices: 6.26 us -> 8.25 us
    dot_general x41 -> x0, matrix products: 25.7 us -> none  [the longest x8 6.51 us: expand(): jnp.dot(compressed, w_keys, preferred_element_type=jnp.float32)]
    unnamed x2 -> x0, waiting for transfers between devices: 24.1 us -> none
    add x16 -> x0, other arithmetic: 20.1 us -> none  [the longest x4 19.5 us: shards(): query_pos = block_order[own_slots] * half_rows + row_index % half_rows]
    ppermute x3 -> x6, waiting for transfers between devices: 0.01 us -> 17.2 us  [the longest x3 10.1 us: shifted(): lax.ppermute(value, axis, [(i, (i + steps) % count) for i in range(count)])]
    pallas_call x0 -> x2, Pallas kernels: none -> 6.79 us  [the longest x1 6.35 us: attend(): pl.pallas_call(functools.partial(attend_kernel, count, rows), out_shape=[...]
    lt x8 -> x0, other arithmetic: 6.07 us -> none  [absorb(): key_offsets < valid_lengths[slot]]
    another operation x1 -> x0, loops' own time: 4.27 us -> none  [shards(): moving, state = lax.fori_loop(1, ctx_count, turn_one, (latent, state))]
    dynamic_slice x4 -> x0, local copies, waits for them, and re-layouts: 2.72 us -> none  [absorb(): valid_lengths[slot]]
  transfers between devices with their start and end apart: 4 -> 6, of which waited for: 1 -> 4; matrix products, arithmetic and copies ran while one was open for 18% -> 0% of each run, Pallas kernels for 0% -> 1%
where the time goes in v1:
time: 39.3 us; the launch traced here: 39 us
  waiting for transfers between devices  17.2 us (44%)
  starting transfers between devices  8.25 us (21%)
  Pallas kernels  6.79 us (17%)
  local copies, waits for them, and re-layouts  5.9 us (15%)
  other arithmetic  0.82 us (2%)
    ppermute x3, waiting for transfers between devices, shifted(): lax.ppermute(value, axis, [(i, (i + steps) % count) for i in range(count)])  10.1 us
    ppermute x3, waiting for transfers between devices, crossed(): return lax.ppermute(value, axis, [(i, i ^ bit) for i in range(count)])  7.12 us
    pallas_call x1, Pallas kernels, attend(): pl.pallas_call(functools.partial(attend_kernel, count, rows), out_shape=[...  6.35 us
    ppermute x3, starting transfers between devices, shifted(): lax.ppermute(value, axis, [(i, (i + steps) % count) for i in range(count)])  6.11 us
    unnamed x11, local copies, waits for them, and re-layouts  5.81 us
    ppermute x3, starting transfers between devices, crossed(): return lax.ppermute(value, axis, [(i, i ^ bit) for i in range(count)])  2.13 us
  transfers between devices with their start and end apart: 6, of which 4 were waited for; matrix products, arithmetic and copies ran while one was open for 0% of the time, Pallas kernels for 1%

profile of v1, /device:TPU:0, one launch (start us, length us, event | category | flops | bytes accessed | tf_op | source)
XLA Modules:
  0.0 39.0 jit_solution(12964055902834949232)
XLA Ops:
  0.0 1.1 %copy.11.rest_0_ = bf16[128,576]{1,0:T(8,128)(2,1)S(1)} copy(bf16[128,576]{0,1:T(8,128)(2,1)} %param.8) | data formatting | bytes 294912 | tf_op args[1]
  1.1 5.1 %collective-permute-start.2 = (bf16[128,576]{1,0:T(8,128)(2,1)S(1)}, bf16[128,576]{1,0:T(8,128)(2,1)S(1)}, u32[]{:S(2)}, u32[]{:S(2)}) collective-permute-start(bf16[128,576]{1,0:T(8,128)(2,1)S(1)} %copy.11.rest_0_), channel_id=1, source_target_pairs={{0,12},{4,0},{8,4},{12,8},{1,13},{5,1},{9,5},{13,9},{2,14},{6,2},{... | collective-permute-start | bytes 442376 | tf_op jit(solution)/shard_map/ppermute | solution.py:22
  6.2 0.0 collective-permute-start.1
  6.2 1.0 %collective-permute-start = (bf16[128,576]{1,0:T(8,128)(2,1)S(1)}, bf16[128,576]{1,0:T(8,128)(2,1)S(1)}, u32[]{:S(2)}, u32[]{:S(2)}) collective-permute-start(bf16[128,576]{1,0:T(8,128)(2,1)S(1)} %copy.11.rest_0_), channel_id=1, source_target_pairs={{0,4},{4,8},{8,12},{12,0},{1,5},{5,9},{9,13},{13,1},{2,6},{6,10},{... | collective-permute-start | bytes 442376 | tf_op jit(solution)/shard_map/ppermute | solution.py:22
  7.2 0.1 stack.23.place_ref
  7.3 0.0 copy-start
  7.3 1.2 %copy-done = bf16[512,1024]{1,0:T(8,128)(2,1)S(1)} copy-done((bf16[512,1024]{1,0:T(8,128)(2,1)S(1)}, bf16[512,1024]{1,0:T(8,128)(2,1)}, u32[]{:S(2)}) %copy-start) | copy-done | bytes 1048600
  8.5 0.0 copy-start.2
  8.5 1.0 %copy-done.2 = bf16[128,1536]{1,0:T(8,128)(2,1)S(1)} copy-done((bf16[128,1536]{1,0:T(8,128)(2,1)S(1)}, bf16[128,1536]{1,0:T(8,128)(2,1)}, u32[]{:S(2)}) %copy-start.2) | copy-done | bytes 393240
  9.5 0.4 %fold_keys.1.folded_ref = bf16[1024,576]{1,0:T(8,128)(2,1)S(1)} custom-call(bf16[128,1536]{1,0:T(8,128)(2,1)S(1)} %copy-done.2, bf16[512,1024]{1,0:T(8,128)(2,1)S(1)} %copy-done), custom_call_target="tpu_custom_call" | custom-call | flops 134217728 | bytes 2621440 | tf_op jit(solution)/shard_map/fold_keys/pallas_call | solution.py:45
  9.9 0.9 %collective-permute-done.2.rest_3_ = bf16[128,576]{1,0:T(8,128)(2,1)S(1)} collective-permute-done((bf16[128,576]{1,0:T(8,128)(2,1)S(1)}, bf16[128,576]{1,0:T(8,128)(2,1)S(1)}, u32[]{:S(2)}, u32[]{:S(2)}) %collective-permute-start.2) | collective-permute-done | bytes 147488 | tf_op jit(solution)/shard_map/ppermute | solution.py:22
  10.8 9.2 %collective-permute-done.1.rest_2_ = bf16[128,576]{1,0:T(8,128)(2,1)S(1)} collective-permute-done((bf16[128,576]{1,0:T(8,128)(2,1)S(1)}, bf16[128,576]{1,0:T(8,128)(2,1)S(1)}, u32[]{:S(2)}, u32[]{:S(2)}) %collective-permute-start.1) | collective-permute-done | bytes 147488 | tf_op jit(solution)/shard_map/ppermute | solution.py:22
  20.0 0.0 collective-permute-done.rest_1_
  20.0 0.0 copy-start.1
  20.1 1.2 %copy-done.1 = bf16[512,1024]{1,0:T(8,128)(2,1)S(1)} copy-done((bf16[512,1024]{1,0:T(8,128)(2,1)S(1)}, bf16[512,1024]{1,0:T(8,128)(2,1)}, u32[]{:S(2)}) %copy-start.1) | copy-done | bytes 1048600
  21.3 0.0 copy-start.3
  21.3 0.7 %copy-done.3 = s32[8]{0:T(128)S(1)} copy-done((s32[8]{0:T(128)S(1)}, s32[8]{0:T(128)}, u32[]{:S(2)}) %copy-start.3) | copy-done | bytes 56
  21.9 0.0 copy-start.4
  21.9 0.7 %copy-done.4 = s32[8]{0:T(128)S(1)} copy-done((s32[8]{0:T(128)S(1)}, s32[8]{0:T(128)}, u32[]{:S(2)}) %copy-start.4) | copy-done | bytes 56
  22.6 6.3 %attend.1 = (bf16[128,896]{1,0:T(8,128)(2,1)S(1)}, bf16[128,896]{1,0:T(8,128)(2,1)S(1)}, f32[128,896]{1,0:T(8,128)S(1)}, f32[128,896]{1,0:T(8,128)S(1)}) custom-call(s32[8]{0:T(128)S(1)} %copy-done.3, s32[8]{0:T(128)S(1)} %copy-done.4, s32[5]{0:T(128)S(1)} %stack.23.place_ref, bf16[1024,576]{1,0:T(8,128)(2,1)S(1)} %fold_keys.1.folded_ref, ...), custom_call_target="tpu_custom_call" | custom-call | flops 2214592512 | bytes 10158080 | tf_op jit(solution)/shard_map/attend/pallas_call | solution.py:144
  28.9 0.1 collective-permute-start.4
  29.0 0.5 %collective-permute-start.3 = (bf16[128,896]{1,0:T(8,128)(2,1)S(1)}, bf16[128,896]{1,0:T(8,128)(2,1)S(1)}, u32[]{:S(2)}, u32[]{:S(2)}) collective-permute-start(bf16[128,896]{1,0:T(8,128)(2,1)S(1)} %get-tuple-element.10), channel_id=1, source_target_pairs={{0,1},{1,0},{2,3},{3,2},{4,5},{5,4},{6,7},{7,6},{8,9},{9,8},{10,11... | collective-permute-start | bytes 688136 | tf_op jit(solution)/shard_map/ppermute | solution.py:27
  29.5 1.0 %collective-permute-done.4 = bf16[128,896]{1,0:T(8,128)(2,1)S(1)} collective-permute-done((bf16[128,896]{1,0:T(8,128)(2,1)S(1)}, bf16[128,896]{1,0:T(8,128)(2,1)S(1)}, u32[]{:S(2)}, u32[]{:S(2)}) %collective-permute-start.4) | collective-permute-done | bytes 229408 | tf_op jit(solution)/shard_map/ppermute | solution.py:27
  30.5 0.1 add_convert_fusion.1
  30.6 1.6 %collective-permute-start.5 = (bf16[128,896]{1,0:T(8,128)(2,1)S(1)}, bf16[128,896]{1,0:T(8,128)(2,1)S(1)}, u32[]{:S(2)}, u32[]{:S(2)}) collective-permute-start(bf16[128,896]{1,0:T(8,128)(2,1)S(1)} %add_convert_fusion.1), channel_id=1, source_target_pairs={{0,2},{1,3},{2,0},{3,1},{4,6},{5,7},{6,4},{7,5},{8,10},{9,11},{10,... | collective-permute-start | bytes 688136 | tf_op jit(solution)/shard_map/ppermute | solution.py:27
  32.1 0.0 collective-permute-done.3
  32.1 6.1 %collective-permute-done.5 = bf16[128,896]{1,0:T(8,128)(2,1)S(1)} collective-permute-done((bf16[128,896]{1,0:T(8,128)(2,1)S(1)}, bf16[128,896]{1,0:T(8,128)(2,1)S(1)}, u32[]{:S(2)}, u32[]{:S(2)}) %collective-permute-start.5) | collective-permute-done | bytes 229408 | tf_op jit(solution)/shard_map/ppermute | solution.py:27
  38.3 0.8 %add_convert_fusion = bf16[128,896]{1,0:T(8,128)(2,1)} fusion(bf16[128,896]{1,0:T(8,128)(2,1)S(1)} %collective-permute-done.5, f32[128,896]{1,0:T(8,128)S(1)} %get-tuple-element.9, bf16[128,896]{1,0:T(8,128)(2,1)S(1)} %collective-permute-done.3), kind=kLoop, calls=%fused_computation | loop fusion | flops 573440 | bytes 1146880 | tf_op jit(solution)/shard_map/convert_element_type | solution.py:190
Async XLA Ops:
  1.1 9.7 %collective-permute-start.2 = (bf16[128,576]{1,0:T(8,128)(2,1)S(1)}, bf16[128,576]{1,0:T(8,128)(2,1)S(1)}, u32[]{:S(2)}, u32[]{:S(2)}) collective-permute-start(bf16[128,576]{1,0:T(8,128)(2,1)S(1)} %copy.11.rest_0_), channel_id=1, source_target_pairs={{0,12},{4,0},{8,4},{12,8},{1,13},{5,1},{9,5},{13,9},{2,14},{6,2},{... | collective-permute-start | bytes 442376 | tf_op jit(solution)/shard_map/ppermute | solution.py:22
  6.2 13.9 %collective-permute-start.1 = (bf16[128,576]{1,0:T(8,128)(2,1)S(1)}, bf16[128,576]{1,0:T(8,128)(2,1)S(1)}, u32[]{:S(2)}, u32[]{:S(2)}) collective-permute-start(bf16[128,576]{1,0:T(8,128)(2,1)S(1)} %copy.11.rest_0_), channel_id=1, source_target_pairs={{0,8},{4,12},{8,0},{12,4},{1,9},{5,13},{9,1},{13,5},{2,10},{6,14},... | collective-permute-start | bytes 442376 | tf_op jit(solution)/shard_map/ppermute | solution.py:22
  6.2 13.9 %collective-permute-start = (bf16[128,576]{1,0:T(8,128)(2,1)S(1)}, bf16[128,576]{1,0:T(8,128)(2,1)S(1)}, u32[]{:S(2)}, u32[]{:S(2)}) collective-permute-start(bf16[128,576]{1,0:T(8,128)(2,1)S(1)} %copy.11.rest_0_), channel_id=1, source_target_pairs={{0,4},{4,8},{8,12},{12,0},{1,5},{5,9},{9,13},{13,1},{2,6},{6,10},{... | collective-permute-start | bytes 442376 | tf_op jit(solution)/shard_map/ppermute | solution.py:22
  7.3 1.2 %copy-start = (bf16[512,1024]{1,0:T(8,128)(2,1)S(1)}, bf16[512,1024]{1,0:T(8,128)(2,1)}, u32[]{:S(2)}) copy-start(bf16[512,1024]{1,0:T(8,128)(2,1)} %w_keys_ref.1) | copy-start | bytes 3145732
  8.5 1.0 %copy-start.2 = (bf16[128,1536]{1,0:T(8,128)(2,1)S(1)}, bf16[128,1536]{1,0:T(8,128)(2,1)}, u32[]{:S(2)}) copy-start(bf16[128,1536]{1,0:T(8,128)(2,1)} %queries_ref.1) | copy-start | bytes 1179652
  20.0 1.2 %copy-start.1 = (bf16[512,1024]{1,0:T(8,128)(2,1)S(1)}, bf16[512,1024]{1,0:T(8,128)(2,1)}, u32[]{:S(2)}) copy-start(bf16[512,1024]{1,0:T(8,128)(2,1)} %w_values_ref.1) | copy-start | bytes 3145732
  21.3 0.7 %copy-start.3 = (s32[8]{0:T(128)S(1)}, s32[8]{0:T(128)}, u32[]{:S(2)}) copy-start(s32[8]{0:T(128)} %order_ref.1) | copy-start | bytes 100
  21.9 0.7 %copy-start.4 = (s32[8]{0:T(128)S(1)}, s32[8]{0:T(128)}, u32[]{:S(2)}) copy-start(s32[8]{0:T(128)} %lens_ref.1) | copy-start | bytes 100
  28.9 1.6 %collective-permute-start.4 = (bf16[128,896]{1,0:T(8,128)(2,1)S(1)}, bf16[128,896]{1,0:T(8,128)(2,1)S(1)}, u32[]{:S(2)}, u32[]{:S(2)}) collective-permute-start(bf16[128,896]{1,0:T(8,128)(2,1)S(1)} %get-tuple-element.12), channel_id=1, source_target_pairs={{0,1},{1,0},{2,3},{3,2},{4,5},{5,4},{6,7},{7,6},{8,9},{9,8},{10,11... | collective-permute-start | bytes 688136 | tf_op jit(solution)/shard_map/ppermute | solution.py:27
  29.0 3.1 %collective-permute-start.3 = (bf16[128,896]{1,0:T(8,128)(2,1)S(1)}, bf16[128,896]{1,0:T(8,128)(2,1)S(1)}, u32[]{:S(2)}, u32[]{:S(2)}) collective-permute-start(bf16[128,896]{1,0:T(8,128)(2,1)S(1)} %get-tuple-element.10), channel_id=1, source_target_pairs={{0,1},{1,0},{2,3},{3,2},{4,5},{5,4},{6,7},{7,6},{8,9},{9,8},{10,11... | collective-permute-start | bytes 688136 | tf_op jit(solution)/shard_map/ppermute | solution.py:27
  30.6 7.7 %collective-permute-start.5 = (bf16[128,896]{1,0:T(8,128)(2,1)S(1)}, bf16[128,896]{1,0:T(8,128)(2,1)S(1)}, u32[]{:S(2)}, u32[]{:S(2)}) collective-permute-start(bf16[128,896]{1,0:T(8,128)(2,1)S(1)} %add_convert_fusion.1), channel_id=1, source_target_pairs={{0,2},{1,3},{2,0},{3,1},{4,6},{5,7},{6,4},{7,5},{8,10},{9,11},{10,... | collective-permute-start | bytes 688136 | tf_op jit(solution)/shard_map/ppermute | solution.py:27

commit v2 on v1

v2 whole, which is shorter than its diff:
```python
import functools

import jax
import jax.numpy as jnp
from jax import lax
from jax.experimental import pallas as pl
from jax.experimental.pallas import tpu as pltpu
from jax.sharding import PartitionSpec as P

LATENT = 512
ROPE = 64
HEAD_DIM = 128
QUERY = HEAD_DIM + ROPE
PARTS = 4
ROWS_AT_ONCE = 256
NT = (((1,), (1,)), ((), ()))
VMEM_BYTES = 32 * 1024 * 1024
HIDDEN = -1e30


def routed(value, route):
    ctx_count = lax.axis_size("ctx")
    head_count = lax.axis_size("head")
    pairs = []
    for ctx in range(ctx_count):
        for head in range(head_count):
            target = route(ctx, head)
            if target is not None:
                pairs.append((ctx * head_count + head, target[0] * head_count + target[1]))
    return lax.ppermute(value, ("ctx", "head"), pairs)


def is_paired():
    return lax.axis_size("ctx") == 4 and lax.axis_size("head") == 4


def key_sources():
    count = lax.axis_size("ctx")
    ctx = lax.axis_index("ctx")
    if is_paired():
        step = 1 + 2 * (lax.axis_index("head") & 1)
        return [ctx, (ctx - step) & 3, (ctx + step) & 3, ctx ^ 2]
    return [ctx] + [lax.rem(ctx + (count - step), count) for step in range(1, count)]


def part_order():
    if is_paired():
        head = lax.axis_index("head")
        return [head ^ 3, head ^ 1, head ^ 2, head]
    return list(range(PARTS))


def prepare_kernel(
    rows,
    order_hbm,
    lens_hbm,
    queries_ref,
    w_keys_ref,
    w_values_ref,
    w_out_ref,
    folded_ref,
    bias_ref,
    values_ref,
    parts_ref,
    order_ref,
    lens_ref,
    query_buffer,
    key_buffer,
    sems,
    part_sems,
):
    half = rows // 2
    width = w_out_ref.shape[1] // PARTS
    scalars = [
        pltpu.make_async_copy(order_hbm, order_ref, sems.at[3]),
        pltpu.make_async_copy(lens_hbm, lens_ref, sems.at[4]),
    ]
    first = [
        pltpu.make_async_copy(queries_ref, query_buffer, sems.at[0]),
        pltpu.make_async_copy(w_keys_ref, key_buffer, sems.at[1]),
    ]
    later = [pltpu.make_async_copy(w_values_ref, values_ref, sems.at[2])]
    for slot, part in enumerate(part_order()):
        start = pl.multiple_of(part * width, 128)
        later.append(
            pltpu.make_async_copy(
                w_out_ref.at[:, pl.ds(start, width)], parts_ref.at[slot], part_sems.at[slot]
            )
        )
    for copy in scalars + first + later:
        copy.start()

    for copy in scalars:
        copy.wait()
    ctx = lax.axis_index("ctx")
    row = lax.broadcasted_iota(jnp.int32, (rows, rows), 0)
    lane = lax.broadcasted_iota(jnp.int32, (rows, rows), 1)
    query_pos = jnp.where(row < half, order_ref[2 * ctx], order_ref[2 * ctx + 1]) * half + row % half
    offset = lane % half
    for step, source in enumerate(key_sources()):
        key_place = jnp.where(lane < half, order_ref[2 * source], order_ref[2 * source + 1])
        length = jnp.where(lane < half, lens_ref[2 * source], lens_ref[2 * source + 1])
        visible = (key_place * half + offset <= query_pos) & (offset < length)
        bias_ref[:, step * rows : (step + 1) * rows] = jnp.where(visible, 0.0, HIDDEN)

    for copy in first:
        copy.wait()
    for head in range(w_keys_ref.shape[1] // HEAD_DIM):
        nope = query_buffer[:, head * QUERY : head * QUERY + HEAD_DIM]
        rope = query_buffer[:, head * QUERY + HEAD_DIM : (head + 1) * QUERY]
        weight = key_buffer[:, head * HEAD_DIM : (head + 1) * HEAD_DIM]
        here = slice(head * rows, (head + 1) * rows)
        product = lax.dot_general(nope, weight, NT, preferred_element_type=jnp.float32)
        folded_ref[here, :LATENT] = product.astype(jnp.bfloat16)
        folded_ref[here, LATENT:] = rope
    for copy in later:
        copy.wait()


def prepare(*operands):
    order, lens, queries, w_keys, w_values, w_out = operands
    rows = queries.shape[0]
    count = lax.axis_size("ctx")
    heads = w_keys.shape[1] // HEAD_DIM
    vmem = pl.BlockSpec(memory_space=pltpu.VMEM)
    hbm = pl.BlockSpec(memory_space=pltpu.HBM)
    return pl.pallas_call(
        functools.partial(prepare_kernel, rows),
        out_shape=[
            jax.ShapeDtypeStruct((heads * rows, LATENT + ROPE), jnp.bfloat16),
            jax.ShapeDtypeStruct((rows, count * rows), jnp.float32),
            jax.ShapeDtypeStruct(w_values.shape, jnp.bfloat16),
            jax.ShapeDtypeStruct((PARTS, w_out.shape[0], w_out.shape[1] // PARTS), jnp.bfloat16),
        ],
        in_specs=[hbm] * 6,
        out_specs=[vmem] * 4,
        scratch_shapes=[
            pltpu.SMEM(order.shape, jnp.int32),
            pltpu.SMEM(lens.shape, jnp.int32),
            pltpu.VMEM(queries.shape, jnp.bfloat16),
            pltpu.VMEM(w_keys.shape, jnp.bfloat16),
            pltpu.SemaphoreType.DMA((5,)),
            pltpu.SemaphoreType.DMA((PARTS,)),
        ],
        compiler_params=pltpu.CompilerParams(vmem_limit_bytes=VMEM_BYTES),
        cost_estimate=pl.CostEstimate(
            flops=2 * rows * heads * HEAD_DIM * LATENT,
            bytes_accessed=2 * (queries.size + w_keys.size + w_values.size + w_out.size),
            transcendentals=0,
        ),
        name="prepare",
    )(*[pltpu.with_memory_space_constraint(item, pltpu.HBM) for item in operands])


def attend_kernel(count, folded_ref, bias_ref, values_ref, parts_ref, *rest):
    blocks, rest = rest[: count + 1], rest[count + 1 :]
    outs, rest = rest[:PARTS], rest[PARTS:]
    keys_ref, attended_ref = rest
    rows = bias_ref.shape[0]
    heads = values_ref.shape[1] // HEAD_DIM
    exponent = QUERY**-0.5 * 1.4426950408889634

    for step in range(count - 1):
        keys_ref[:, step * rows : (step + 1) * rows] = blocks[step][...]
    last = slice((count - 1) * rows, count * rows)

    direct = (lax.axis_index("ctx") ^ lax.axis_index("head")) & 1 == 0

    @pl.when(direct)
    def _():
        keys_ref[:, last] = blocks[count - 1][...]

    @pl.when(jnp.logical_not(direct))
    def _():
        keys_ref[:, last] = blocks[count][...]

    stacked = ROWS_AT_ONCE // rows
    bias = jnp.concatenate([bias_ref[...]] * stacked, axis=0)
    for group in range(heads // stacked):
        lines = slice(group * ROWS_AT_ONCE, (group + 1) * ROWS_AT_ONCE)
        scores = jnp.dot(folded_ref[lines, :], keys_ref[...], preferred_element_type=jnp.float32)
        scores = scores + bias
        peak = jnp.max(scores, axis=1, keepdims=True)
        weights = jnp.exp2((scores - peak) * jnp.float32(exponent))
        total = jnp.sum(weights, axis=1, keepdims=True)
        mixed = lax.dot_general(
            weights.astype(jnp.bfloat16), keys_ref[:LATENT, :], NT, preferred_element_type=jnp.float32
        )
        mixed = (mixed / total).astype(jnp.bfloat16)
        for inner in range(stacked):
            head = group * stacked + inner
            columns = slice(head * HEAD_DIM, (head + 1) * HEAD_DIM)
            value = jnp.dot(
                mixed[inner * rows : (inner + 1) * rows, :],
                values_ref[:, columns],
                preferred_element_type=jnp.float32,
            )
            attended_ref[:, columns] = value.astype(jnp.bfloat16)

    for part in range(PARTS):
        outs[part][...] = jnp.dot(
            attended_ref[...], parts_ref[part], preferred_element_type=jnp.float32
        ).astype(outs[part].dtype)


def attend(prepared, blocks, out_types):
    folded, bias, values, parts = prepared
    rows, keys = bias.shape
    heads = values.shape[1] // HEAD_DIM
    width = parts.shape[2]
    flops = 2 * heads * rows * (keys * (2 * LATENT + ROPE) + LATENT * HEAD_DIM)
    flops += 2 * rows * parts.size
    vmem = pl.BlockSpec(memory_space=pltpu.VMEM)
    return pl.pallas_call(
        functools.partial(attend_kernel, keys // rows),
        out_shape=[jax.ShapeDtypeStruct((rows, width), kind) for kind in out_types],
        in_specs=[vmem] * (4 + len(blocks)),
        out_specs=[vmem] * PARTS,
        scratch_shapes=[
            pltpu.VMEM((LATENT + ROPE, keys), jnp.bfloat16),
            pltpu.VMEM((rows, heads * HEAD_DIM), jnp.bfloat16),
        ],
        compiler_params=pltpu.CompilerParams(vmem_limit_bytes=VMEM_BYTES),
        cost_estimate=pl.CostEstimate(
            flops=flops,
            bytes_accessed=2 * (folded.size + values.size + parts.size + keys * (LATENT + ROPE)),
            transcendentals=heads * rows * keys,
        ),
        name="attend",
    )(folded, bias, values, parts, *blocks)


def shards(queries, latent, w_keys, w_values, w_out, block_order, valid_lengths):
    ctx_count = lax.axis_size("ctx")
    block = latent.T
    prepared = prepare(block_order, valid_lengths, queries, w_keys, w_values, w_out)

    if not is_paired():
        blocks = [block]
        for step in range(1, ctx_count):
            blocks.append(routed(block, lambda ctx, head: ((ctx + step) % ctx_count, head)))
        blocks.append(blocks[-1])
        shares = attend(prepared, blocks, [jnp.bfloat16] * PARTS)
        whole = jnp.concatenate(shares, axis=1)
        return lax.psum_scatter(whole, "head", scatter_dimension=1, tiled=True)

    def next_to(ctx, head):
        return (ctx + 1 + 2 * (head & 1)) & 3, head

    def two_away(ctx, head):
        return (ctx ^ 2, head) if (ctx ^ head) & 1 == 0 else None

    def other_core(ctx, head):
        return ctx, head ^ 1

    def other_core_two_away(ctx, head):
        return (ctx, head ^ 1) if (ctx ^ head) & 1 == 0 else None

    near = routed(block, next_to)
    far = routed(block, two_away)
    near, far, prepared = lax.optimization_barrier((near, far, prepared))
    near_swapped = routed(near, other_core)
    far_swapped = routed(far, other_core_two_away)
    across, beside, far, own = attend(
        prepared,
        [block, near, near_swapped, far, far_swapped],
        [jnp.bfloat16, jnp.bfloat16, jnp.float32, jnp.float32],
    )
    far = far + routed(across, other_core).astype(jnp.float32)
    near = routed(beside, other_core).astype(jnp.float32)
    far = routed(far.astype(jnp.bfloat16), lambda ctx, head: (ctx, head ^ 2)).astype(jnp.float32)
    return (own + near + far).astype(jnp.bfloat16)


def solution(mesh):
    in_specs = (
        P(("groups", "ctx"), "head"),
        P(("groups", "ctx"), None),
        P(None, "head"),
        P(None, "head"),
        P("head", None),
        P("groups"),
        P("groups"),
    )
    out_specs = P(("groups", "ctx"), "head")
    return jax.shard_map(shards, mesh=mesh, in_specs=in_specs, out_specs=out_specs, check_vma=False)
```

time: 39.3 us -> 32 us (0.81)
  local copies, waits for them, and re-layouts: 5.9 us -> 0.01 us
  waiting for transfers between devices: 17.2 us -> 11.8 us
  starting transfers between devices: 8.25 us -> 11.1 us
  Pallas kernels: 6.79 us -> 8.04 us
    unnamed x11 -> x2, local copies, waits for them, and re-layouts: 5.81 us -> 0.01 us
    ppermute x6 -> x7, waiting for transfers between devices: 17.2 us -> 11.8 us  [routed(): return lax.ppermute(value, ('ctx', 'head'), pairs)]
    ppermute x6 -> x7, starting transfers between devices: 8.25 us -> 11.1 us  [routed(): return lax.ppermute(value, ('ctx', 'head'), pairs)]
    pallas_call x2, Pallas kernels: 6.79 us -> 8.04 us  [the longest x1 4.05 us: attend(): pl.pallas_call(functools.partial(attend_kernel, keys // rows), out_shape=...]
  transfers between devices with their start and end apart: 6 -> 7, of which waited for: 4 -> 4; matrix products, arithmetic and copies ran while one was open for 0% -> 0% of each run, Pallas kernels for 1% -> 13%
where the time goes in v2:
time: 32 us; the launch traced here: 31.8 us
  waiting for transfers between devices  11.8 us (37%)
  starting transfers between devices  11.1 us (35%)
  Pallas kernels  8.04 us (25%)
  other arithmetic  0.83 us (3%)
    ppermute x7, waiting for transfers between devices, routed(): return lax.ppermute(value, ('ctx', 'head'), pairs)  11.8 us
    ppermute x7, starting transfers between devices, routed(): return lax.ppermute(value, ('ctx', 'head'), pairs)  11.1 us
    pallas_call x1, Pallas kernels, attend(): pl.pallas_call(functools.partial(attend_kernel, keys // rows), out_shape=...  4.05 us
    pallas_call x1, Pallas kernels, prepare(): pl.pallas_call(functools.partial(prepare_kernel, rows), out_shape=[jax.Sh...  3.99 us
    convert_element_type x1, other arithmetic, shards(): return (own + near + far).astype(jnp.bfloat16)  0.77 us
  transfers between devices with their start and end apart: 7, of which 4 were waited for; matrix products, arithmetic and copies ran while one was open for 0% of the time, Pallas kernels for 13%

profile of v2, /device:TPU:0, one launch (start us, length us, event | category | flops | bytes accessed | tf_op | source)
XLA Modules:
  0.0 31.8 jit_solution(177150446911494235)
XLA Ops:
  0.0 0.0 copy-start
  0.0 6.1 %collective-permute-start.1 = (bf16[576,128]{1,0:T(8,128)(2,1)}, bf16[576,128]{1,0:T(8,128)(2,1)S(1)}, u32[]{:S(2)}, u32[]{:S(2)}) collective-permute-start(bf16[576,128]{1,0:T(8,128)(2,1)} %bitcast.1), channel_id=1, source_target_pairs={{0,8},{2,10},{5,13},{7,15},{8,0},{10,2},{13,5},{15,7},{16,24},{18,... | collective-permute-start | bytes 442376 | tf_op jit(solution)/shard_map/ppermute | solution.py:30
  6.1 0.1 collective-permute-start
  6.1 4.0 %prepare.1 = (bf16[1024,576]{1,0:T(8,128)(2,1)S(1)}, f32[128,512]{1,0:T(8,128)S(1)}, bf16[512,1024]{1,0:T(8,128)(2,1)S(1)}, bf16[4,1024,896]{2,1,0:T(8,128)(2,1)S(1)}) custom-call(s32[8]{0:T(128)} %order_hbm.1, s32[8]{0:T(128)} %lens_hbm.1, bf16[128,1536]{1,0:T(8,128)(2,1)} %queries_ref.1, bf16[512,1024]{1,0:T(8,128)(2,1)} %w_keys_ref.1, ...), custom_call_target="tpu_custom_call" | custom-call | flops 134217728 | bytes 9830400 | tf_op jit(solution)/shard_map/prepare/pallas_call | solution.py:127
  10.1 3.7 %collective-permute-done.1.rest_3_ = bf16[576,128]{1,0:T(8,128)(2,1)S(1)} collective-permute-done((bf16[576,128]{1,0:T(8,128)(2,1)}, bf16[576,128]{1,0:T(8,128)(2,1)S(1)}, u32[]{:S(2)}, u32[]{:S(2)}) %collective-permute-start.1) | collective-permute-done | bytes 147488 | tf_op jit(solution)/shard_map/ppermute | solution.py:30
  13.8 0.0 collective-permute-done.rest_1_
  13.8 0.0 collective-permute-start.2
  13.8 2.4 %collective-permute-start.3 = (bf16[576,128]{1,0:T(8,128)(2,1)S(1)}, bf16[576,128]{1,0:T(8,128)(2,1)S(1)}, u32[]{:S(2)}, u32[]{:S(2)}) collective-permute-start(bf16[576,128]{1,0:T(8,128)(2,1)S(1)} %collective-permute-done.1.rest_3_), channel_id=1, source_target_pairs={{0,1},{2,3},{5,4},{7,6},{8,9},{10,11},{13,12},{15,14},{16,17},{18,... | collective-permute-start | bytes 442376 | tf_op jit(solution)/shard_map/ppermute | solution.py:30
  16.3 0.0 collective-permute-done.2.rest_2_
  16.3 1.0 %collective-permute-done.3.rest_4_ = bf16[576,128]{1,0:T(8,128)(2,1)S(1)} collective-permute-done((bf16[576,128]{1,0:T(8,128)(2,1)S(1)}, bf16[576,128]{1,0:T(8,128)(2,1)S(1)}, u32[]{:S(2)}, u32[]{:S(2)}) %collective-permute-start.3) | collective-permute-done | bytes 147488 | tf_op jit(solution)/shard_map/ppermute | solution.py:30
  17.2 0.0 copy-done
  17.2 4.0 %attend.1 = (bf16[128,896]{1,0:T(8,128)(2,1)S(1)}, bf16[128,896]{1,0:T(8,128)(2,1)S(1)}, f32[128,896]{1,0:T(8,128)S(1)}, f32[128,896]{1,0:T(8,128)S(1)}) custom-call(bf16[1024,576]{1,0:T(8,128)(2,1)S(1)} %get-tuple-element.23.folded_ref, f32[128,512]{1,0:T(8,128)S(1)} %get-tuple-element.24.bias_ref, bf16[512,1024]{1,0:T(8,128)(2,1)S(1)} %get-tuple-element.25.values_ref, ...), custom_call_target="tpu_custom_call" | custom-call | flops 2214592512 | bytes 10158080 | tf_op jit(solution)/shard_map/attend/pallas_call | solution.py:214
  21.3 0.4 %collective-permute-start.5 = (bf16[128,896]{1,0:T(8,128)(2,1)S(1)}, bf16[128,896]{1,0:T(8,128)(2,1)S(1)}, u32[]{:S(2)}, u32[]{:S(2)}) collective-permute-start(bf16[128,896]{1,0:T(8,128)(2,1)S(1)} %get-tuple-element.32), channel_id=1, source_target_pairs={{0,1},{1,0},{2,3},{3,2},{4,5},{5,4},{6,7},{7,6},{8,9},{9,8},{10,11... | collective-permute-start | bytes 688136 | tf_op jit(solution)/shard_map/ppermute | solution.py:30
  21.7 0.2 collective-permute-start.4
  21.9 1.0 %collective-permute-done.5 = bf16[128,896]{1,0:T(8,128)(2,1)S(1)} collective-permute-done((bf16[128,896]{1,0:T(8,128)(2,1)S(1)}, bf16[128,896]{1,0:T(8,128)(2,1)S(1)}, u32[]{:S(2)}, u32[]{:S(2)}) %collective-permute-start.5) | collective-permute-done | bytes 229408 | tf_op jit(solution)/shard_map/ppermute | solution.py:30
  22.8 0.1 add_convert_fusion.1
  22.9 2.0 %collective-permute-start.6 = (bf16[128,896]{1,0:T(8,128)(2,1)S(1)}, bf16[128,896]{1,0:T(8,128)(2,1)S(1)}, u32[]{:S(2)}, u32[]{:S(2)}) collective-permute-start(bf16[128,896]{1,0:T(8,128)(2,1)S(1)} %add_convert_fusion.1), channel_id=1, source_target_pairs={{0,2},{1,3},{2,0},{3,1},{4,6},{5,7},{6,4},{7,5},{8,10},{9,11},{10,... | collective-permute-start | bytes 688136 | tf_op jit(solution)/shard_map/ppermute | solution.py:30
  24.9 0.0 collective-permute-done.4
  24.9 6.1 %collective-permute-done.6 = bf16[128,896]{1,0:T(8,128)(2,1)S(1)} collective-permute-done((bf16[128,896]{1,0:T(8,128)(2,1)S(1)}, bf16[128,896]{1,0:T(8,128)(2,1)S(1)}, u32[]{:S(2)}, u32[]{:S(2)}) %collective-permute-start.6) | collective-permute-done | bytes 229408 | tf_op jit(solution)/shard_map/ppermute | solution.py:30
  31.0 0.8 %add_convert_fusion = bf16[128,896]{1,0:T(8,128)(2,1)} fusion(bf16[128,896]{1,0:T(8,128)(2,1)S(1)} %collective-permute-done.6, f32[128,896]{1,0:T(8,128)S(1)} %get-tuple-element.29, bf16[128,896]{1,0:T(8,128)(2,1)S(1)} %collective-permute-done.4), kind=kLoop, calls=%fused_computation | loop fusion | flops 573440 | bytes 1146880 | tf_op jit(solution)/shard_map/convert_element_type | solution.py:272
Async XLA Ops:
  0.0 17.2 %copy-start = (bf16[128,576]{0,1:T(8,128)(2,1)S(1)}, bf16[128,576]{0,1:T(8,128)(2,1)}, u32[]{:S(2)}) copy-start(bf16[128,576]{0,1:T(8,128)(2,1)} %param.8) | copy-start | bytes 442372
  0.0 13.8 %collective-permute-start.1 = (bf16[576,128]{1,0:T(8,128)(2,1)}, bf16[576,128]{1,0:T(8,128)(2,1)S(1)}, u32[]{:S(2)}, u32[]{:S(2)}) collective-permute-start(bf16[576,128]{1,0:T(8,128)(2,1)} %bitcast.1), channel_id=1, source_target_pairs={{0,8},{2,10},{5,13},{7,15},{8,0},{10,2},{13,5},{15,7},{16,24},{18,... | collective-permute-start | bytes 442376 | tf_op jit(solution)/shard_map/ppermute | solution.py:30
  6.1 7.8 %collective-permute-start = (bf16[576,128]{1,0:T(8,128)(2,1)}, bf16[576,128]{1,0:T(8,128)(2,1)S(1)}, u32[]{:S(2)}, u32[]{:S(2)}) collective-permute-start(bf16[576,128]{1,0:T(8,128)(2,1)} %bitcast.2), channel_id=1, source_target_pairs={{0,4},{1,13},{2,6},{3,15},{4,8},{5,1},{6,10},{7,3},{8,12},{9,5},{1... | collective-permute-start | bytes 442376 | tf_op jit(solution)/shard_map/ppermute | solution.py:30
  13.8 2.4 %collective-permute-start.2 = (bf16[576,128]{1,0:T(8,128)(2,1)S(1)}, bf16[576,128]{1,0:T(8,128)(2,1)S(1)}, u32[]{:S(2)}, u32[]{:S(2)}) collective-permute-start(bf16[576,128]{1,0:T(8,128)(2,1)S(1)} %collective-permute-done.rest_1_), channel_id=1, source_target_pairs={{0,1},{1,0},{2,3},{3,2},{4,5},{5,4},{6,7},{7,6},{8,9},{9,8},{10,11... | collective-permute-start | bytes 442376 | tf_op jit(solution)/shard_map/ppermute | solution.py:30
  13.8 3.4 %collective-permute-start.3 = (bf16[576,128]{1,0:T(8,128)(2,1)S(1)}, bf16[576,128]{1,0:T(8,128)(2,1)S(1)}, u32[]{:S(2)}, u32[]{:S(2)}) collective-permute-start(bf16[576,128]{1,0:T(8,128)(2,1)S(1)} %collective-permute-done.1.rest_3_), channel_id=1, source_target_pairs={{0,1},{2,3},{5,4},{7,6},{8,9},{10,11},{13,12},{15,14},{16,17},{18,... | collective-permute-start | bytes 442376 | tf_op jit(solution)/shard_map/ppermute | solution.py:30
  21.3 1.6 %collective-permute-start.5 = (bf16[128,896]{1,0:T(8,128)(2,1)S(1)}, bf16[128,896]{1,0:T(8,128)(2,1)S(1)}, u32[]{:S(2)}, u32[]{:S(2)}) collective-permute-start(bf16[128,896]{1,0:T(8,128)(2,1)S(1)} %get-tuple-element.32), channel_id=1, source_target_pairs={{0,1},{1,0},{2,3},{3,2},{4,5},{5,4},{6,7},{7,6},{8,9},{9,8},{10,11... | collective-permute-start | bytes 688136 | tf_op jit(solution)/shard_map/ppermute | solution.py:30
  21.7 3.2 %collective-permute-start.4 = (bf16[128,896]{1,0:T(8,128)(2,1)S(1)}, bf16[128,896]{1,0:T(8,128)(2,1)S(1)}, u32[]{:S(2)}, u32[]{:S(2)}) collective-permute-start(bf16[128,896]{1,0:T(8,128)(2,1)S(1)} %get-tuple-element.30), channel_id=1, source_target_pairs={{0,1},{1,0},{2,3},{3,2},{4,5},{5,4},{6,7},{7,6},{8,9},{9,8},{10,11... | collective-permute-start | bytes 688136 | tf_op jit(solution)/shard_map/ppermute | solution.py:30
  22.9 8.1 %collective-permute-start.6 = (bf16[128,896]{1,0:T(8,128)(2,1)S(1)}, bf16[128,896]{1,0:T(8,128)(2,1)S(1)}, u32[]{:S(2)}, u32[]{:S(2)}) collective-permute-start(bf16[128,896]{1,0:T(8,128)(2,1)S(1)} %add_convert_fusion.1), channel_id=1, source_target_pairs={{0,2},{1,3},{2,0},{3,1},{4,6},{5,7},{6,4},{7,5},{8,10},{9,11},{10,... | collective-permute-start | bytes 688136 | tf_op jit(solution)/shard_map/ppermute | solution.py:30

commit v3 on v2

--- a/solution.py
+++ b/solution.py
@@ -248,28 +248,30 @@
         return (ctx + 1 + 2 * (head & 1)) & 3, head
 
     def two_away(ctx, head):
-        return (ctx ^ 2, head) if (ctx ^ head) & 1 == 0 else None
+        return (ctx ^ 2 if (ctx ^ head) & 1 == 0 else ctx), head
 
     def other_core(ctx, head):
         return ctx, head ^ 1
 
-    def other_core_two_away(ctx, head):
-        return (ctx, head ^ 1) if (ctx ^ head) & 1 == 0 else None
+    def other_chip(ctx, head):
+        return ctx, head ^ 2
 
     near = routed(block, next_to)
     far = routed(block, two_away)
-    near, far, prepared = lax.optimization_barrier((near, far, prepared))
+    near, prepared = lax.optimization_barrier((near, prepared))
     near_swapped = routed(near, other_core)
-    far_swapped = routed(far, other_core_two_away)
-    across, beside, far, own = attend(
+    far, _ = lax.optimization_barrier((far, near))
+    far_swapped = routed(far, other_core)
+    across, beside, far_part, own = attend(
         prepared,
         [block, near, near_swapped, far, far_swapped],
         [jnp.bfloat16, jnp.bfloat16, jnp.float32, jnp.float32],
     )
-    far = far + routed(across, other_core).astype(jnp.float32)
-    near = routed(beside, other_core).astype(jnp.float32)
-    far = routed(far.astype(jnp.bfloat16), lambda ctx, head: (ctx, head ^ 2)).astype(jnp.float32)
-    return (own + near + far).astype(jnp.bfloat16)
+    far_part = (far_part + routed(across, other_core).astype(jnp.float32)).astype(jnp.bfloat16)
+    far_part, beside = lax.optimization_barrier((far_part, beside))
+    far_part = routed(far_part, other_chip).astype(jnp.float32)
+    beside = routed(beside, other_core).astype(jnp.float32)
+    return (own + beside + far_part).astype(jnp.bfloat16)
 
 
 def solution(mesh):

time: 32 us -> 28.7 us (0.90)
  waiting for transfers between devices: 11.8 us -> 9.4 us
  starting transfers between devices: 11.1 us -> 10.2 us
    ppermute x7, waiting for transfers between devices: 11.8 us -> 9.4 us  [routed(): return lax.ppermute(value, ('ctx', 'head'), pairs)]
    ppermute x7, starting transfers between devices: 11.1 us -> 10.2 us  [routed(): return lax.ppermute(value, ('ctx', 'head'), pairs)]
  transfers between devices with their start and end apart: 7 -> 7, of which waited for: 4 -> 5; matrix products, arithmetic and copies ran while one was open for 0% -> 0% of each run, Pallas kernels for 13% -> 14%
where the time goes in v3:
time: 28.7 us; the launch traced here: 28.5 us
  starting transfers between devices  10.2 us (36%)
  waiting for transfers between devices  9.4 us (33%)
  Pallas kernels  8.04 us (28%)
  other arithmetic  0.81 us (3%)
    ppermute x7, starting transfers between devices, routed(): return lax.ppermute(value, ('ctx', 'head'), pairs)  10.2 us
    ppermute x7, waiting for transfers between devices, routed(): return lax.ppermute(value, ('ctx', 'head'), pairs)  9.4 us
    pallas_call x1, Pallas kernels, attend(): pl.pallas_call(functools.partial(attend_kernel, keys // rows), out_shape=...  4.05 us
    pallas_call x1, Pallas kernels, prepare(): pl.pallas_call(functools.partial(prepare_kernel, rows), out_shape=[jax.Sh...  3.99 us
    convert_element_type x1, other arithmetic, shards(): return (own + beside + far_part).astype(jnp.bfloat16)  0.76 us
  transfers between devices with their start and end apart: 7, of which 5 were waited for; matrix products, arithmetic and copies ran while one was open for 0% of the time, Pallas kernels for 14%

profile of v3, /device:TPU:0, one launch (start us, length us, event | category | flops | bytes accessed | tf_op | source)
XLA Modules:
  0.0 28.5 jit_solution(6614560353587133885)
XLA Ops:
  0.0 0.0 copy-start
  0.0 3.0 %collective-permute-start = (bf16[576,128]{1,0:T(8,128)(2,1)}, bf16[576,128]{1,0:T(8,128)(2,1)S(1)}, u32[]{:S(2)}, u32[]{:S(2)}) collective-permute-start(bf16[576,128]{1,0:T(8,128)(2,1)} %bitcast.1), channel_id=1, source_target_pairs={{0,4},{1,13},{2,6},{3,15},{4,8},{5,1},{6,10},{7,3},{8,12},{9,5},{1... | collective-permute-start | bytes 442376 | tf_op jit(solution)/shard_map/ppermute | solution.py:30
  3.0 4.5 %collective-permute-start.2 = (bf16[576,128]{1,0:T(8,128)(2,1)}, bf16[576,128]{1,0:T(8,128)(2,1)S(1)}, u32[]{:S(2)}, u32[]{:S(2)}) collective-permute-start(bf16[576,128]{1,0:T(8,128)(2,1)} %bitcast.2), channel_id=1, source_target_pairs={{0,8},{1,1},{2,10},{3,3},{4,4},{5,13},{6,6},{7,15},{8,0},{9,9},{10... | collective-permute-start | bytes 442376 | tf_op jit(solution)/shard_map/ppermute | solution.py:30
  7.5 4.0 %prepare.1 = (bf16[1024,576]{1,0:T(8,128)(2,1)S(1)}, f32[128,512]{1,0:T(8,128)S(1)}, bf16[512,1024]{1,0:T(8,128)(2,1)S(1)}, bf16[4,1024,896]{2,1,0:T(8,128)(2,1)S(1)}) custom-call(s32[8]{0:T(128)} %order_hbm.1, s32[8]{0:T(128)} %lens_hbm.1, bf16[128,1536]{1,0:T(8,128)(2,1)} %queries_ref.1, bf16[512,1024]{1,0:T(8,128)(2,1)} %w_keys_ref.1, ...), custom_call_target="tpu_custom_call" | custom-call | flops 134217728 | bytes 9830400 | tf_op jit(solution)/shard_map/prepare/pallas_call | solution.py:127
  11.5 0.0 collective-permute-done.rest_1_
  11.5 0.9 %collective-permute-done.2.rest_3_ = bf16[576,128]{1,0:T(8,128)(2,1)S(1)} collective-permute-done((bf16[576,128]{1,0:T(8,128)(2,1)}, bf16[576,128]{1,0:T(8,128)(2,1)S(1)}, u32[]{:S(2)}, u32[]{:S(2)}) %collective-permute-start.2) | collective-permute-done | bytes 147488 | tf_op jit(solution)/shard_map/ppermute | solution.py:30
  12.4 0.0 collective-permute-start.3
  12.4 0.5 %collective-permute-start.1 = (bf16[576,128]{1,0:T(8,128)(2,1)S(1)}, bf16[576,128]{1,0:T(8,128)(2,1)S(1)}, u32[]{:S(2)}, u32[]{:S(2)}) collective-permute-start(bf16[576,128]{1,0:T(8,128)(2,1)S(1)} %collective-permute-done.rest_1_), channel_id=1, source_target_pairs={{0,1},{1,0},{2,3},{3,2},{4,5},{5,4},{6,7},{7,6},{8,9},{9,8},{10,11... | collective-permute-start | bytes 442376 | tf_op jit(solution)/shard_map/ppermute | solution.py:30
  12.9 0.9 %collective-permute-done.3.rest_4_ = bf16[576,128]{1,0:T(8,128)(2,1)S(1)} collective-permute-done((bf16[576,128]{1,0:T(8,128)(2,1)S(1)}, bf16[576,128]{1,0:T(8,128)(2,1)S(1)}, u32[]{:S(2)}, u32[]{:S(2)}) %collective-permute-start.3) | collective-permute-done | bytes 147488 | tf_op jit(solution)/shard_map/ppermute | solution.py:30
  13.8 0.2 collective-permute-done.1.rest_2_
  14.0 0.0 copy-done
  14.0 4.0 %attend.1 = (bf16[128,896]{1,0:T(8,128)(2,1)S(1)}, bf16[128,896]{1,0:T(8,128)(2,1)S(1)}, f32[128,896]{1,0:T(8,128)S(1)}, f32[128,896]{1,0:T(8,128)S(1)}) custom-call(bf16[1024,576]{1,0:T(8,128)(2,1)S(1)} %get-tuple-element.25.folded_ref, f32[128,512]{1,0:T(8,128)S(1)} %get-tuple-element.26.bias_ref, bf16[512,1024]{1,0:T(8,128)(2,1)S(1)} %get-tuple-element.27.values_ref, ...), custom_call_target="tpu_custom_call" | custom-call | flops 2214592512 | bytes 10158080 | tf_op jit(solution)/shard_map/attend/pallas_call | solution.py:214
  18.1 0.4 %collective-permute-start.4 = (bf16[128,896]{1,0:T(8,128)(2,1)S(1)}, bf16[128,896]{1,0:T(8,128)(2,1)S(1)}, u32[]{:S(2)}, u32[]{:S(2)}) collective-permute-start(bf16[128,896]{1,0:T(8,128)(2,1)S(1)} %get-tuple-element.33), channel_id=1, source_target_pairs={{0,1},{1,0},{2,3},{3,2},{4,5},{5,4},{6,7},{7,6},{8,9},{9,8},{10,11... | collective-permute-start | bytes 688136 | tf_op jit(solution)/shard_map/ppermute | solution.py:30
  18.4 1.2 %collective-permute-done.4 = bf16[128,896]{1,0:T(8,128)(2,1)S(1)} collective-permute-done((bf16[128,896]{1,0:T(8,128)(2,1)S(1)}, bf16[128,896]{1,0:T(8,128)(2,1)S(1)}, u32[]{:S(2)}, u32[]{:S(2)}) %collective-permute-start.4) | collective-permute-done | bytes 229408 | tf_op jit(solution)/shard_map/ppermute | solution.py:30
  19.6 0.1 add_convert_fusion.1
  19.7 0.4 %collective-permute-start.5 = (bf16[128,896]{1,0:T(8,128)(2,1)S(1)}, bf16[128,896]{1,0:T(8,128)(2,1)S(1)}, u32[]{:S(2)}, u32[]{:S(2)}) collective-permute-start(bf16[128,896]{1,0:T(8,128)(2,1)S(1)} %get-tuple-element.35), channel_id=1, source_target_pairs={{0,1},{1,0},{2,3},{3,2},{4,5},{5,4},{6,7},{7,6},{8,9},{9,8},{10,11... | collective-permute-start | bytes 688136 | tf_op jit(solution)/shard_map/ppermute | solution.py:30
  20.1 1.5 %collective-permute-start.6 = (bf16[128,896]{1,0:T(8,128)(2,1)S(1)}, bf16[128,896]{1,0:T(8,128)(2,1)S(1)}, u32[]{:S(2)}, u32[]{:S(2)}) collective-permute-start(bf16[128,896]{1,0:T(8,128)(2,1)S(1)} %add_convert_fusion.1), channel_id=1, source_target_pairs={{0,2},{1,3},{2,0},{3,1},{4,6},{5,7},{6,4},{7,5},{8,10},{9,11},{10,... | collective-permute-start | bytes 688136 | tf_op jit(solution)/shard_map/ppermute | solution.py:30
  21.5 0.0 collective-permute-done.5
  21.5 6.2 %collective-permute-done.6 = bf16[128,896]{1,0:T(8,128)(2,1)S(1)} collective-permute-done((bf16[128,896]{1,0:T(8,128)(2,1)S(1)}, bf16[128,896]{1,0:T(8,128)(2,1)S(1)}, u32[]{:S(2)}, u32[]{:S(2)}) %collective-permute-start.6) | collective-permute-done | bytes 229408 | tf_op jit(solution)/shard_map/ppermute | solution.py:30
  27.8 0.8 %add_convert_fusion = bf16[128,896]{1,0:T(8,128)(2,1)} fusion(bf16[128,896]{1,0:T(8,128)(2,1)S(1)} %collective-permute-done.6, f32[128,896]{1,0:T(8,128)S(1)} %get-tuple-element.31, bf16[128,896]{1,0:T(8,128)(2,1)S(1)} %collective-permute-done.5), kind=kLoop, calls=%fused_computation | loop fusion | flops 573440 | bytes 1146880 | tf_op jit(solution)/shard_map/convert_element_type | solution.py:274
Async XLA Ops:
  0.0 14.0 %copy-start = (bf16[128,576]{0,1:T(8,128)(2,1)S(1)}, bf16[128,576]{0,1:T(8,128)(2,1)}, u32[]{:S(2)}) copy-start(bf16[128,576]{0,1:T(8,128)(2,1)} %param.8) | copy-start | bytes 442372
  0.0 11.5 %collective-permute-start = (bf16[576,128]{1,0:T(8,128)(2,1)}, bf16[576,128]{1,0:T(8,128)(2,1)S(1)}, u32[]{:S(2)}, u32[]{:S(2)}) collective-permute-start(bf16[576,128]{1,0:T(8,128)(2,1)} %bitcast.1), channel_id=1, source_target_pairs={{0,4},{1,13},{2,6},{3,15},{4,8},{5,1},{6,10},{7,3},{8,12},{9,5},{1... | collective-permute-start | bytes 442376 | tf_op jit(solution)/shard_map/ppermute | solution.py:30
  3.0 9.4 %collective-permute-start.2 = (bf16[576,128]{1,0:T(8,128)(2,1)}, bf16[576,128]{1,0:T(8,128)(2,1)S(1)}, u32[]{:S(2)}, u32[]{:S(2)}) collective-permute-start(bf16[576,128]{1,0:T(8,128)(2,1)} %bitcast.2), channel_id=1, source_target_pairs={{0,8},{1,1},{2,10},{3,3},{4,4},{5,13},{6,6},{7,15},{8,0},{9,9},{10... | collective-permute-start | bytes 442376 | tf_op jit(solution)/shard_map/ppermute | solution.py:30
  12.4 1.4 %collective-permute-start.3 = (bf16[576,128]{1,0:T(8,128)(2,1)S(1)}, bf16[576,128]{1,0:T(8,128)(2,1)S(1)}, u32[]{:S(2)}, u32[]{:S(2)}) collective-permute-start(bf16[576,128]{1,0:T(8,128)(2,1)S(1)} %collective-permute-done.2.rest_3_), channel_id=1, source_target_pairs={{0,1},{1,0},{2,3},{3,2},{4,5},{5,4},{6,7},{7,6},{8,9},{9,8},{10,11... | collective-permute-start | bytes 442376 | tf_op jit(solution)/shard_map/ppermute | solution.py:30
  12.4 1.6 %collective-permute-start.1 = (bf16[576,128]{1,0:T(8,128)(2,1)S(1)}, bf16[576,128]{1,0:T(8,128)(2,1)S(1)}, u32[]{:S(2)}, u32[]{:S(2)}) collective-permute-start(bf16[576,128]{1,0:T(8,128)(2,1)S(1)} %collective-permute-done.rest_1_), channel_id=1, source_target_pairs={{0,1},{1,0},{2,3},{3,2},{4,5},{5,4},{6,7},{7,6},{8,9},{9,8},{10,11... | collective-permute-start | bytes 442376 | tf_op jit(solution)/shard_map/ppermute | solution.py:30
  18.1 1.6 %collective-permute-start.4 = (bf16[128,896]{1,0:T(8,128)(2,1)S(1)}, bf16[128,896]{1,0:T(8,128)(2,1)S(1)}, u32[]{:S(2)}, u32[]{:S(2)}) collective-permute-start(bf16[128,896]{1,0:T(8,128)(2,1)S(1)} %get-tuple-element.33), channel_id=1, source_target_pairs={{0,1},{1,0},{2,3},{3,2},{4,5},{5,4},{6,7},{7,6},{8,9},{9,8},{10,11... | collective-permute-start | bytes 688136 | tf_op jit(solution)/shard_map/ppermute | solution.py:30
  19.7 1.9 %collective-permute-start.5 = (bf16[128,896]{1,0:T(8,128)(2,1)S(1)}, bf16[128,896]{1,0:T(8,128)(2,1)S(1)}, u32[]{:S(2)}, u32[]{:S(2)}) collective-permute-start(bf16[128,896]{1,0:T(8,128)(2,1)S(1)} %get-tuple-element.35), channel_id=1, source_target_pairs={{0,1},{1,0},{2,3},{3,2},{4,5},{5,4},{6,7},{7,6},{8,9},{9,8},{10,11... | collective-permute-start | bytes 688136 | tf_op jit(solution)/shard_map/ppermute | solution.py:30
  20.1 7.7 %collective-permute-start.6 = (bf16[128,896]{1,0:T(8,128)(2,1)S(1)}, bf16[128,896]{1,0:T(8,128)(2,1)S(1)}, u32[]{:S(2)}, u32[]{:S(2)}) collective-permute-start(bf16[128,896]{1,0:T(8,128)(2,1)S(1)} %add_convert_fusion.1), channel_id=1, source_target_pairs={{0,2},{1,3},{2,0},{3,1},{4,6},{5,7},{6,4},{7,5},{8,10},{9,11},{10,... | collective-permute-start | bytes 688136 | tf_op jit(solution)/shard_map/ppermute | solution.py:30

commit v4 on v3

v4 whole, which is shorter than its diff:
```python
import functools

import jax
import jax.numpy as jnp
from jax import lax
from jax.experimental import pallas as pl
from jax.experimental.pallas import tpu as pltpu
from jax.sharding import PartitionSpec as P

LATENT = 512
ROPE = 64
HEAD_DIM = 128
QUERY = HEAD_DIM + ROPE
PARTS = 4
ROWS_AT_ONCE = 256
NT = (((1,), (1,)), ((), ()))
VMEM_BYTES = 32 * 1024 * 1024
HIDDEN = -1e30


def routed(value, route):
    ctx_count = lax.axis_size("ctx")
    head_count = lax.axis_size("head")
    pairs = []
    for ctx in range(ctx_count):
        for head in range(head_count):
            target = route(ctx, head)
            if target is not None:
                pairs.append((ctx * head_count + head, target[0] * head_count + target[1]))
    return lax.ppermute(value, ("ctx", "head"), pairs)


def is_paired():
    return lax.axis_size("ctx") == 4 and lax.axis_size("head") == 4


def key_sources():
    count = lax.axis_size("ctx")
    ctx = lax.axis_index("ctx")
    if is_paired():
        step = jnp.where(ctx < 2, 1, 3)
        return [ctx, (ctx + step) & 3, ctx ^ 2, (ctx - step) & 3]
    return [ctx] + [lax.rem(ctx + (count - step), count) for step in range(1, count)]


def part_order():
    if is_paired():
        head = lax.axis_index("head")
        return [head ^ 3, head ^ 1, head ^ 2, head]
    return list(range(PARTS))


def part_copy(w_out_ref, slot, target, sem):
    width = target.shape[1]
    start = pl.multiple_of(part_order()[slot] * width, 128)
    return pltpu.make_async_copy(w_out_ref.at[:, pl.ds(start, width)], target, sem)


def prepare_kernel(
    rows,
    order_hbm,
    lens_hbm,
    queries_ref,
    w_keys_ref,
    w_values_ref,
    w_out_ref,
    folded_ref,
    bias_ref,
    values_ref,
    part_ref,
    order_ref,
    lens_ref,
    query_buffer,
    key_buffer,
    sems,
):
    half = rows // 2
    scalars = [
        pltpu.make_async_copy(order_hbm, order_ref, sems.at[3]),
        pltpu.make_async_copy(lens_hbm, lens_ref, sems.at[4]),
    ]
    first = [
        pltpu.make_async_copy(queries_ref, query_buffer, sems.at[0]),
        pltpu.make_async_copy(w_keys_ref, key_buffer, sems.at[1]),
    ]
    later = [
        pltpu.make_async_copy(w_values_ref, values_ref, sems.at[2]),
        part_copy(w_out_ref, 0, part_ref, sems.at[5]),
    ]
    for copy in scalars + first + later:
        copy.start()

    for copy in scalars:
        copy.wait()
    ctx = lax.axis_index("ctx")
    row = lax.broadcasted_iota(jnp.int32, (rows, rows), 0)
    lane = lax.broadcasted_iota(jnp.int32, (rows, rows), 1)
    query_pos = jnp.where(row < half, order_ref[2 * ctx], order_ref[2 * ctx + 1]) * half + row % half
    offset = lane % half
    for step, source in enumerate(key_sources()):
        key_place = jnp.where(lane < half, order_ref[2 * source], order_ref[2 * source + 1])
        length = jnp.where(lane < half, lens_ref[2 * source], lens_ref[2 * source + 1])
        visible = (key_place * half + offset <= query_pos) & (offset < length)
        bias_ref[:, step * rows : (step + 1) * rows] = jnp.where(visible, 0.0, HIDDEN)

    for copy in first:
        copy.wait()
    for head in range(w_keys_ref.shape[1] // HEAD_DIM):
        nope = query_buffer[:, head * QUERY : head * QUERY + HEAD_DIM]
        rope = query_buffer[:, head * QUERY + HEAD_DIM : (head + 1) * QUERY]
        weight = key_buffer[:, head * HEAD_DIM : (head + 1) * HEAD_DIM]
        here = slice(head * rows, (head + 1) * rows)
        product = lax.dot_general(nope, weight, NT, preferred_element_type=jnp.float32)
        folded_ref[here, :LATENT] = product.astype(jnp.bfloat16)
        folded_ref[here, LATENT:] = rope
    for copy in later:
        copy.wait()


VMEM = pl.BlockSpec(memory_space=pltpu.VMEM)
HBM = pl.BlockSpec(memory_space=pltpu.HBM)


def in_hbm(value):
    return pltpu.with_memory_space_constraint(value, pltpu.HBM)


def prepare(*operands):
    order, lens, queries, w_keys, w_values, w_out = operands
    rows = queries.shape[0]
    count = lax.axis_size("ctx")
    heads = w_keys.shape[1] // HEAD_DIM
    return pl.pallas_call(
        functools.partial(prepare_kernel, rows),
        out_shape=[
            jax.ShapeDtypeStruct((heads * rows, LATENT + ROPE), jnp.bfloat16),
            jax.ShapeDtypeStruct((rows, count * rows), jnp.float32),
            jax.ShapeDtypeStruct(w_values.shape, jnp.bfloat16),
            jax.ShapeDtypeStruct((w_out.shape[0], w_out.shape[1] // PARTS), jnp.bfloat16),
        ],
        in_specs=[HBM] * 6,
        out_specs=[VMEM] * 4,
        scratch_shapes=[
            pltpu.SMEM(order.shape, jnp.int32),
            pltpu.SMEM(lens.shape, jnp.int32),
            pltpu.VMEM(queries.shape, jnp.bfloat16),
            pltpu.VMEM(w_keys.shape, jnp.bfloat16),
            pltpu.SemaphoreType.DMA((6,)),
        ],
        compiler_params=pltpu.CompilerParams(vmem_limit_bytes=VMEM_BYTES),
        cost_estimate=pl.CostEstimate(
            flops=2 * rows * heads * HEAD_DIM * LATENT,
            bytes_accessed=2 * (queries.size + w_keys.size + w_values.size + w_out.size // PARTS),
            transcendentals=0,
        ),
        name="prepare",
    )(*[in_hbm(item) for item in operands])


def on_long_side():
    return (lax.axis_index("ctx") < 2) == (lax.axis_index("head") & 1 == 1)


def at_an_end():
    ctx = lax.axis_index("ctx")
    return (ctx == 0) | (ctx == 3)


def place_if(keys_ref, slot, block_ref, condition):
    rows = block_ref.shape[1]

    @pl.when(condition)
    def _():
        keys_ref[:, slot * rows : (slot + 1) * rows] = block_ref[...]


EXPONENT = QUERY**-0.5 * 1.4426950408889634


def begin_kernel(paired, folded_ref, bias_ref, w_out_ref, *rest):
    blocks = rest[: 3 if paired else 1]
    peak_ref, total_ref, sums_ref, part_a, part_b, keys_ref, sems = rest[len(blocks) :]
    copies = [
        part_copy(w_out_ref, 1, part_a, sems.at[0]),
        part_copy(w_out_ref, 2, part_b, sems.at[1]),
    ]
    for copy in copies:
        copy.start()
    rows, keys = bias_ref.shape[0], keys_ref.shape[1]
    keys_ref[:, :rows] = blocks[0][...]
    if paired:
        long_side = on_long_side()
        place_if(keys_ref, 1, blocks[1], long_side)
        place_if(keys_ref, 1, blocks[2], jnp.logical_not(long_side))
    stacked = ROWS_AT_ONCE // rows
    bias = jnp.concatenate([bias_ref[:, :keys]] * stacked, axis=0)
    for group in range(folded_ref.shape[0] // ROWS_AT_ONCE):
        lines = slice(group * ROWS_AT_ONCE, (group + 1) * ROWS_AT_ONCE)
        scores = jnp.dot(folded_ref[lines, :], keys_ref[...], preferred_element_type=jnp.float32)
        scores = scores + bias
        peak = jnp.max(scores, axis=1, keepdims=True)
        weights = jnp.exp2((scores - peak) * jnp.float32(EXPONENT))
        total = jnp.sum(weights, axis=1, keepdims=True)
        peak_ref[lines, :] = jnp.broadcast_to(peak, (ROWS_AT_ONCE, 128))
        total_ref[lines, :] = jnp.broadcast_to(total, (ROWS_AT_ONCE, 128))
        sums_ref[lines, :] = lax.dot_general(
            weights.astype(jnp.bfloat16), keys_ref[:LATENT, :], NT, preferred_element_type=jnp.float32
        )
    for copy in copies:
        copy.wait()


def begin(folded, bias, w_out, blocks):
    lines = folded.shape[0]
    rows = bias.shape[0]
    keys = rows * (2 if is_paired() else 1)
    part = jax.ShapeDtypeStruct((w_out.shape[0], w_out.shape[1] // PARTS), jnp.bfloat16)
    return pl.pallas_call(
        functools.partial(begin_kernel, is_paired()),
        out_shape=[
            jax.ShapeDtypeStruct((lines, 128), jnp.float32),
            jax.ShapeDtypeStruct((lines, 128), jnp.float32),
            jax.ShapeDtypeStruct((lines, LATENT), jnp.float32),
            part,
            part,
        ],
        in_specs=[VMEM, VMEM, HBM] + [VMEM] * len(blocks),
        out_specs=[VMEM] * 5,
        scratch_shapes=[
            pltpu.VMEM((LATENT + ROPE, keys), jnp.bfloat16),
            pltpu.SemaphoreType.DMA((2,)),
        ],
        compiler_params=pltpu.CompilerParams(vmem_limit_bytes=VMEM_BYTES),
        cost_estimate=pl.CostEstimate(
            flops=2 * lines * keys * (2 * LATENT + ROPE),
            bytes_accessed=w_out.size,
            transcendentals=lines * keys,
        ),
        name="begin",
    )(folded, bias, in_hbm(w_out), *blocks)


def finish_kernel(paired, count, *refs):
    folded_ref, bias_ref, values_ref, peak_ref, total_ref, sums_ref = refs[:6]
    part_refs, w_out_ref, refs = refs[6:9], refs[9], refs[10:]
    blocks, refs = refs[:count], refs[count:]
    outs, (keys_ref, attended_ref, last_part, sem) = refs[:PARTS], refs[PARTS:]
    last_copy = part_copy(w_out_ref, 3, last_part, sem.at[0])
    last_copy.start()
    rows, keys = bias_ref.shape[0], keys_ref.shape[1]
    if paired:
        near, near_swapped, far, far_swapped, last, last_swapped = blocks
        long_side, end = on_long_side(), at_an_end()
        short_side, middle = jnp.logical_not(long_side), jnp.logical_not(end)
        place_if(keys_ref, 0, far, long_side)
        place_if(keys_ref, 0, far_swapped, short_side)
        place_if(keys_ref, 1, last, long_side & end)
        place_if(keys_ref, 1, last_swapped, short_side & end)
        place_if(keys_ref, 1, near_swapped, long_side & middle)
        place_if(keys_ref, 1, near, short_side & middle)
    else:
        for step in range(count):
            keys_ref[:, step * rows : (step + 1) * rows] = blocks[step][...]
    stacked = ROWS_AT_ONCE // rows
    bias = jnp.concatenate([bias_ref[:, bias_ref.shape[1] - keys :]] * stacked, axis=0)
    for group in range(folded_ref.shape[0] // ROWS_AT_ONCE):
        lines = slice(group * ROWS_AT_ONCE, (group + 1) * ROWS_AT_ONCE)
        scores = jnp.dot(folded_ref[lines, :], keys_ref[...], preferred_element_type=jnp.float32)
        scores = scores + bias
        old_peak = peak_ref[lines, :1]
        peak = jnp.maximum(old_peak, jnp.max(scores, axis=1, keepdims=True))
        factor = jnp.exp2((old_peak - peak) * jnp.float32(EXPONENT))
        weights = jnp.exp2((scores - peak) * jnp.float32(EXPONENT))
        total = total_ref[lines, :1] * factor + jnp.sum(weights, axis=1, keepdims=True)
        mixed = lax.dot_general(
            weights.astype(jnp.bfloat16), keys_ref[:LATENT, :], NT, preferred_element_type=jnp.float32
        )
        mixed = ((sums_ref[lines, :] * factor + mixed) / total).astype(jnp.bfloat16)
        for inner in range(stacked):
            head = group * stacked + inner
            columns = slice(head * HEAD_DIM, (head + 1) * HEAD_DIM)
            value = jnp.dot(
                mixed[inner * rows : (inner + 1) * rows, :],
                values_ref[:, columns],
                preferred_element_type=jnp.float32,
            )
            attended_ref[:, columns] = value.astype(jnp.bfloat16)

    for slot in range(PARTS):
        if slot == PARTS - 1:
            last_copy.wait()
            weight = last_part[...]
        else:
            weight = part_refs[slot][...]
        outs[slot][...] = jnp.dot(
            attended_ref[...], weight, preferred_element_type=jnp.float32
        ).astype(outs[slot].dtype)


def finish(folded, bias, values, state, parts, w_out, blocks, out_types):
    lines = folded.shape[0]
    rows = bias.shape[0]
    width = w_out.shape[1] // PARTS
    keys = bias.shape[1] - rows * (2 if is_paired() else 1)
    flops = 2 * lines * (keys * (2 * LATENT + ROPE) + LATENT * HEAD_DIM)
    flops += 2 * rows * w_out.size
    return pl.pallas_call(
        functools.partial(finish_kernel, is_paired(), len(blocks)),
        out_shape=[jax.ShapeDtypeStruct((rows, width), kind) for kind in out_types],
        in_specs=[VMEM] * 9 + [HBM] + [VMEM] * len(blocks),
        out_specs=[VMEM] * PARTS,
        scratch_shapes=[
            pltpu.VMEM((LATENT + ROPE, keys), jnp.bfloat16),
            pltpu.VMEM((rows, w_out.shape[0]), jnp.bfloat16),
            pltpu.VMEM((w_out.shape[0], width), jnp.bfloat16),
            pltpu.SemaphoreType.DMA((1,)),
        ],
        compiler_params=pltpu.CompilerParams(vmem_limit_bytes=VMEM_BYTES),
        cost_estimate=pl.CostEstimate(
            flops=flops, bytes_accessed=w_out.size // 2, transcendentals=lines * keys
        ),
        name="finish",
    )(folded, bias, values, *state, *parts, in_hbm(w_out), *blocks)


def along_ring(ctx, head):
    if head & 1 == 0:
        return (ctx + 1, head) if ctx < 3 else (ctx, head ^ 1)
    return (ctx - 1, head) if ctx > 0 else (ctx, head ^ 1)


def other_core(ctx, head):
    return ctx, head ^ 1


def other_chip(ctx, head):
    return ctx, head ^ 2


def shards(queries, latent, w_keys, w_values, w_out, block_order, valid_lengths):
    ctx_count = lax.axis_size("ctx")
    block = latent.T
    prepared = prepare(block_order, valid_lengths, queries, w_keys, w_values, w_out)

    if not is_paired():
        blocks = []
        for step in range(1, ctx_count):
            blocks.append(routed(block, lambda ctx, head: ((ctx + step) % ctx_count, head)))
        folded, bias, values, part_0 = prepared
        *state, part_1, part_2 = begin(folded, bias, w_out, [block])
        parts = [part_0, part_1, part_2]
        kinds = [jnp.bfloat16] * PARTS
        shares = finish(folded, bias, values, state, parts, w_out, blocks, kinds)
        whole = jnp.concatenate(shares, axis=1)
        return lax.psum_scatter(whole, "head", scatter_dimension=1, tiled=True)

    near = routed(block, along_ring)
    near, prepared = lax.optimization_barrier((near, prepared))
    folded, bias, values, part_0 = prepared
    far = routed(near, along_ring)
    near_swapped = routed(near, other_core)
    begun = begin(folded, bias, w_out, [block, near, near_swapped])
    far, begun = lax.optimization_barrier((far, begun))
    *state, part_1, part_2 = begun
    last = routed(far, along_ring)
    far_swapped = routed(far, other_core)
    last_swapped = routed(last, other_core)
    across, beside, far_part, own = finish(
        folded,
        bias,
        values,
        state,
        [part_0, part_1, part_2],
        w_out,
        [near, near_swapped, far, far_swapped, last, last_swapped],
        [jnp.bfloat16, jnp.bfloat16, jnp.float32, jnp.float32],
    )
    far_part = (far_part + routed(across, other_core).astype(jnp.float32)).astype(jnp.bfloat16)
    far_part, beside = lax.optimization_barrier((far_part, beside))
    far_part = routed(far_part, other_chip).astype(jnp.float32)
    beside = routed(beside, other_core).astype(jnp.float32)
    return (own + beside + far_part).astype(jnp.bfloat16)


def solution(mesh):
    in_specs = (
        P(("groups", "ctx"), "head"),
        P(("groups", "ctx"), None),
        P(None, "head"),
        P(None, "head"),
        P("head", None),
        P("groups"),
        P("groups"),
    )
    out_specs = P(("groups", "ctx"), "head")
    return jax.shard_map(shards, mesh=mesh, in_specs=in_specs, out_specs=out_specs, check_vma=False)
```

time: 28.7 us -> 32.6 us (1.14)
  waiting for transfers between devices: 9.4 us -> 12.9 us
  Pallas kernels: 8.04 us -> 8.91 us
  starting transfers between devices: 10.2 us -> 9.8 us
    ppermute x7 -> x9, waiting for transfers between devices: 9.4 us -> 12.9 us  [routed(): return lax.ppermute(value, ('ctx', 'head'), pairs)]
    pallas_call x1 -> x2, Pallas kernels: 4.05 us -> 6.59 us  [the longest x1 4.46 us: finish(): pl.pallas_call(functools.partial(finish_kernel, is_paired(), len(blocks))...]
    pallas_call x1, Pallas kernels: 3.99 us -> 2.32 us  [prepare(): pl.pallas_call(functools.partial(prepare_kernel, rows), out_shape=[jax.Sh...]
    ppermute x7 -> x9, starting transfers between devices: 10.2 us -> 9.8 us  [routed(): return lax.ppermute(value, ('ctx', 'head'), pairs)]
  transfers between devices with their start and end apart: 7 -> 9, of which waited for: 5 -> 6; matrix products, arithmetic and copies ran while one was open for 0% -> 0% of each run, Pallas kernels for 14% -> 14%
where the time goes in v4:
time: 32.6 us; the launch traced here: 32.5 us
  waiting for transfers between devices  12.9 us (40%)
  starting transfers between devices  9.8 us (30%)
  Pallas kernels  8.91 us (27%)
  other arithmetic  0.81 us (2%)
    ppermute x9, waiting for transfers between devices, routed(): return lax.ppermute(value, ('ctx', 'head'), pairs)  12.9 us
    ppermute x9, starting transfers between devices, routed(): return lax.ppermute(value, ('ctx', 'head'), pairs)  9.8 us
    pallas_call x1, Pallas kernels, finish(): pl.pallas_call(functools.partial(finish_kernel, is_paired(), len(blocks))...  4.46 us
    pallas_call x1, Pallas kernels, prepare(): pl.pallas_call(functools.partial(prepare_kernel, rows), out_shape=[jax.Sh...  2.32 us
    pallas_call x1, Pallas kernels, begin(): pl.pallas_call(functools.partial(begin_kernel, is_paired()), out_shape=[j...  2.13 us
    convert_element_type x1, other arithmetic, shards(): return (own + beside + far_part).astype(jnp.bfloat16)  0.76 us
  transfers between devices with their start and end apart: 9, of which 6 were waited for; matrix products, arithmetic and copies ran while one was open for 0% of the time, Pallas kernels for 14%

profile of v4, /device:TPU:0, one launch (start us, length us, event | category | flops | bytes accessed | tf_op | source)
XLA Modules:
  0.0 32.5 jit_solution(8984871609844307621)
XLA Ops:
  0.0 0.0 copy-start
  0.0 3.0 %collective-permute-start = (bf16[576,128]{1,0:T(8,128)(2,1)}, bf16[576,128]{1,0:T(8,128)(2,1)S(1)}, u32[]{:S(2)}, u32[]{:S(2)}) collective-permute-start(bf16[576,128]{1,0:T(8,128)(2,1)} %bitcast.1), channel_id=1, source_target_pairs={{0,4},{1,0},{2,6},{3,2},{4,8},{5,1},{6,10},{7,3},{8,12},{9,5},{10,... | collective-permute-start | bytes 442376 | tf_op jit(solution)/shard_map/ppermute | solution.py:30
  3.0 2.3 %prepare.1 = (bf16[1024,576]{1,0:T(8,128)(2,1)S(1)}, f32[128,512]{1,0:T(8,128)S(1)}, bf16[512,1024]{1,0:T(8,128)(2,1)S(1)}, bf16[1024,896]{1,0:T(8,128)(2,1)S(1)}) custom-call(s32[8]{0:T(128)} %order_hbm.1, s32[8]{0:T(128)} %lens_hbm.1, bf16[128,1536]{1,0:T(8,128)(2,1)} %queries_ref.1, bf16[512,1024]{1,0:T(8,128)(2,1)} %w_keys_ref.1, ...), custom_call_target="tpu_custom_call" | custom-call | flops 134217728 | bytes 4325376 | tf_op jit(solution)/shard_map/prepare/pallas_call | solution.py:133
  5.4 0.7 %collective-permute-done.rest_1_.refs_10_ = bf16[576,128]{1,0:T(8,128)(2,1)S(1)} collective-permute-done((bf16[576,128]{1,0:T(8,128)(2,1)}, bf16[576,128]{1,0:T(8,128)(2,1)S(1)}, u32[]{:S(2)}, u32[]{:S(2)}) %collective-permute-start) | collective-permute-done | bytes 147488 | tf_op jit(solution)/shard_map/ppermute | solution.py:30
  6.0 0.0 collective-permute-start.2
  6.0 2.4 %collective-permute-start.1 = (bf16[576,128]{1,0:T(8,128)(2,1)S(1)}, bf16[576,128]{1,0:T(8,128)(2,1)S(1)}, u32[]{:S(2)}, u32[]{:S(2)}) collective-permute-start(bf16[576,128]{1,0:T(8,128)(2,1)S(1)} %collective-permute-done.rest_1_.refs_10_), channel_id=1, source_target_pairs={{0,4},{1,0},{2,6},{3,2},{4,8},{5,1},{6,10},{7,3},{8,12},{9,5},{10,... | collective-permute-start | bytes 442376 | tf_op jit(solution)/shard_map/ppermute | solution.py:30
  8.4 0.0 collective-permute-done.2.rest_2_.refs_11_
  8.4 0.0 copy-done
  8.4 2.1 %begin.1 = (f32[1024,128]{1,0:T(8,128)S(1)}, f32[1024,128]{1,0:T(8,128)S(1)}, f32[1024,512]{1,0:T(8,128)S(1)}, bf16[1024,896]{1,0:T(8,128)(2,1)S(1)}, bf16[1024,896]{1,0:T(8,128)(2,1)S(1)}) custom-call(bf16[1024,576]{1,0:T(8,128)(2,1)S(1)} %get-tuple-element.35.folded_ref.refs_0_, f32[128,512]{1,0:T(8,128)S(1)} %get-tuple-element.36.bias_ref.refs_1_, ...), custom_call_target="tpu_custom_call" | custom-call | flops 570425344 | bytes 3670016 | tf_op jit(solution)/shard_map/begin/pallas_call | solution.py:218
  10.5 0.5 %collective-permute-done.1.refs_12_ = bf16[576,128]{1,0:T(8,128)(2,1)S(1)} collective-permute-done((bf16[576,128]{1,0:T(8,128)(2,1)S(1)}, bf16[576,128]{1,0:T(8,128)(2,1)S(1)}, u32[]{:S(2)}, u32[]{:S(2)}) %collective-permute-start.1) | collective-permute-done | bytes 147488 | tf_op jit(solution)/shard_map/ppermute | solution.py:30
  11.1 2.5 %collective-permute-start.4 = (bf16[576,128]{1,0:T(8,128)(2,1)S(1)}, bf16[576,128]{1,0:T(8,128)(2,1)S(1)}, u32[]{:S(2)}, u32[]{:S(2)}) collective-permute-start(bf16[576,128]{1,0:T(8,128)(2,1)S(1)} %collective-permute-done.1.refs_12_), channel_id=1, source_target_pairs={{0,4},{1,0},{2,6},{3,2},{4,8},{5,1},{6,10},{7,3},{8,12},{9,5},{10,... | collective-permute-start | bytes 442376 | tf_op jit(solution)/shard_map/ppermute | solution.py:30
  13.5 0.0 collective-permute-start.3
  13.5 2.7 %collective-permute-done.4.refs_14_ = bf16[576,128]{1,0:T(8,128)(2,1)S(1)} collective-permute-done((bf16[576,128]{1,0:T(8,128)(2,1)S(1)}, bf16[576,128]{1,0:T(8,128)(2,1)S(1)}, u32[]{:S(2)}, u32[]{:S(2)}) %collective-permute-start.4) | collective-permute-done | bytes 147488 | tf_op jit(solution)/shard_map/ppermute | solution.py:30
  16.2 0.0 collective-permute-start.5
  16.2 0.0 collective-permute-done.3.refs_13_
  16.2 1.4 %collective-permute-done.5.refs_15_ = bf16[576,128]{1,0:T(8,128)(2,1)S(1)} collective-permute-done((bf16[576,128]{1,0:T(8,128)(2,1)S(1)}, bf16[576,128]{1,0:T(8,128)(2,1)S(1)}, u32[]{:S(2)}, u32[]{:S(2)}) %collective-permute-start.5) | collective-permute-done | bytes 147488 | tf_op jit(solution)/shard_map/ppermute | solution.py:30
  17.6 4.5 %finish.1 = (bf16[128,896]{1,0:T(8,128)(2,1)S(1)}, bf16[128,896]{1,0:T(8,128)(2,1)S(1)}, f32[128,896]{1,0:T(8,128)S(1)}, f32[128,896]{1,0:T(8,128)S(1)}) custom-call(bf16[1024,576]{1,0:T(8,128)(2,1)S(1)} %get-tuple-element.35.folded_ref.refs_0_, f32[128,512]{1,0:T(8,128)S(1)} %get-tuple-element.36.bias_ref.refs_1_, ...), custom_call_target="tpu_custom_call" | custom-call | flops 1644167168 | bytes 1835008 | tf_op jit(solution)/shard_map/finish/pallas_call | solution.py:307
  22.0 0.2 collective-permute-start.6
  22.2 1.3 %collective-permute-done.6 = bf16[128,896]{1,0:T(8,128)(2,1)S(1)} collective-permute-done((bf16[128,896]{1,0:T(8,128)(2,1)S(1)}, bf16[128,896]{1,0:T(8,128)(2,1)S(1)}, u32[]{:S(2)}, u32[]{:S(2)}) %collective-permute-start.6) | collective-permute-done | bytes 229408 | tf_op jit(solution)/shard_map/ppermute | solution.py:30
  23.6 0.1 add_convert_fusion.1
  23.7 0.2 collective-permute-start.7
  23.9 1.5 %collective-permute-start.8 = (bf16[128,896]{1,0:T(8,128)(2,1)S(1)}, bf16[128,896]{1,0:T(8,128)(2,1)S(1)}, u32[]{:S(2)}, u32[]{:S(2)}) collective-permute-start(bf16[128,896]{1,0:T(8,128)(2,1)S(1)} %add_convert_fusion.1), channel_id=1, source_target_pairs={{0,2},{1,3},{2,0},{3,1},{4,6},{5,7},{6,4},{7,5},{8,10},{9,11},{10,... | collective-permute-start | bytes 688136 | tf_op jit(solution)/shard_map/ppermute | solution.py:30
  25.4 0.0 collective-permute-done.7
  25.4 6.3 %collective-permute-done.8 = bf16[128,896]{1,0:T(8,128)(2,1)S(1)} collective-permute-done((bf16[128,896]{1,0:T(8,128)(2,1)S(1)}, bf16[128,896]{1,0:T(8,128)(2,1)S(1)}, u32[]{:S(2)}, u32[]{:S(2)}) %collective-permute-start.8) | collective-permute-done | bytes 229408 | tf_op jit(solution)/shard_map/ppermute | solution.py:30
  31.7 0.8 %add_convert_fusion = bf16[128,896]{1,0:T(8,128)(2,1)} fusion(bf16[128,896]{1,0:T(8,128)(2,1)S(1)} %collective-permute-done.8, f32[128,896]{1,0:T(8,128)S(1)} %get-tuple-element.51, bf16[128,896]{1,0:T(8,128)(2,1)S(1)} %collective-permute-done.7), kind=kLoop, calls=%fused_computation | loop fusion | flops 573440 | bytes 1146880 | tf_op jit(solution)/shard_map/convert_element_type | solution.py:382
Async XLA Ops:
  0.0 8.4 %copy-start = (bf16[128,576]{0,1:T(8,128)(2,1)S(1)}, bf16[128,576]{0,1:T(8,128)(2,1)}, u32[]{:S(2)}) copy-start(bf16[128,576]{0,1:T(8,128)(2,1)} %param.8) | copy-start | bytes 442372
  0.0 6.0 %collective-permute-start = (bf16[576,128]{1,0:T(8,128)(2,1)}, bf16[576,128]{1,0:T(8,128)(2,1)S(1)}, u32[]{:S(2)}, u32[]{:S(2)}) collective-permute-start(bf16[576,128]{1,0:T(8,128)(2,1)} %bitcast.1), channel_id=1, source_target_pairs={{0,4},{1,0},{2,6},{3,2},{4,8},{5,1},{6,10},{7,3},{8,12},{9,5},{10,... | collective-permute-start | bytes 442376 | tf_op jit(solution)/shard_map/ppermute | solution.py:30
  6.0 2.4 %collective-permute-start.2 = (bf16[576,128]{1,0:T(8,128)(2,1)S(1)}, bf16[576,128]{1,0:T(8,128)(2,1)S(1)}, u32[]{:S(2)}, u32[]{:S(2)}) collective-permute-start(bf16[576,128]{1,0:T(8,128)(2,1)S(1)} %collective-permute-done.rest_1_.refs_10_), channel_id=1, source_target_pairs={{0,1},{1,0},{2,3},{3,2},{4,5},{5,4},{6,7},{7,6},{8,9},{9,8},{10,11... | collective-permute-start | bytes 442376 | tf_op jit(solution)/shard_map/ppermute | solution.py:30
  6.0 5.0 %collective-permute-start.1 = (bf16[576,128]{1,0:T(8,128)(2,1)S(1)}, bf16[576,128]{1,0:T(8,128)(2,1)S(1)}, u32[]{:S(2)}, u32[]{:S(2)}) collective-permute-start(bf16[576,128]{1,0:T(8,128)(2,1)S(1)} %collective-permute-done.rest_1_.refs_10_), channel_id=1, source_target_pairs={{0,4},{1,0},{2,6},{3,2},{4,8},{5,1},{6,10},{7,3},{8,12},{9,5},{10,... | collective-permute-start | bytes 442376 | tf_op jit(solution)/shard_map/ppermute | solution.py:30
  11.1 5.1 %collective-permute-start.4 = (bf16[576,128]{1,0:T(8,128)(2,1)S(1)}, bf16[576,128]{1,0:T(8,128)(2,1)S(1)}, u32[]{:S(2)}, u32[]{:S(2)}) collective-permute-start(bf16[576,128]{1,0:T(8,128)(2,1)S(1)} %collective-permute-done.1.refs_12_), channel_id=1, source_target_pairs={{0,4},{1,0},{2,6},{3,2},{4,8},{5,1},{6,10},{7,3},{8,12},{9,5},{10,... | collective-permute-start | bytes 442376 | tf_op jit(solution)/shard_map/ppermute | solution.py:30
  13.5 2.7 %collective-permute-start.3 = (bf16[576,128]{1,0:T(8,128)(2,1)S(1)}, bf16[576,128]{1,0:T(8,128)(2,1)S(1)}, u32[]{:S(2)}, u32[]{:S(2)}) collective-permute-start(bf16[576,128]{1,0:T(8,128)(2,1)S(1)} %collective-permute-done.1.refs_12_), channel_id=1, source_target_pairs={{0,1},{1,0},{2,3},{3,2},{4,5},{5,4},{6,7},{7,6},{8,9},{9,8},{10,11... | collective-permute-start | bytes 442376 | tf_op jit(solution)/shard_map/ppermute | solution.py:30
  16.2 1.4 %collective-permute-start.5 = (bf16[576,128]{1,0:T(8,128)(2,1)S(1)}, bf16[576,128]{1,0:T(8,128)(2,1)S(1)}, u32[]{:S(2)}, u32[]{:S(2)}) collective-permute-start(bf16[576,128]{1,0:T(8,128)(2,1)S(1)} %collective-permute-done.4.refs_14_), channel_id=1, source_target_pairs={{0,1},{1,0},{2,3},{3,2},{4,5},{5,4},{6,7},{7,6},{8,9},{9,8},{10,11... | collective-permute-start | bytes 442376 | tf_op jit(solution)/shard_map/ppermute | solution.py:30
  22.0 1.6 %collective-permute-start.6 = (bf16[128,896]{1,0:T(8,128)(2,1)S(1)}, bf16[128,896]{1,0:T(8,128)(2,1)S(1)}, u32[]{:S(2)}, u32[]{:S(2)}) collective-permute-start(bf16[128,896]{1,0:T(8,128)(2,1)S(1)} %get-tuple-element.53), channel_id=1, source_target_pairs={{0,1},{1,0},{2,3},{3,2},{4,5},{5,4},{6,7},{7,6},{8,9},{9,8},{10,11... | collective-permute-start | bytes 688136 | tf_op jit(solution)/shard_map/ppermute | solution.py:30
  23.7 1.7 %collective-permute-start.7 = (bf16[128,896]{1,0:T(8,128)(2,1)S(1)}, bf16[128,896]{1,0:T(8,128)(2,1)S(1)}, u32[]{:S(2)}, u32[]{:S(2)}) collective-permute-start(bf16[128,896]{1,0:T(8,128)(2,1)S(1)} %get-tuple-element.55), channel_id=1, source_target_pairs={{0,1},{1,0},{2,3},{3,2},{4,5},{5,4},{6,7},{7,6},{8,9},{9,8},{10,11... | collective-permute-start | bytes 688136 | tf_op jit(solution)/shard_map/ppermute | solution.py:30
  23.9 7.9 %collective-permute-start.8 = (bf16[128,896]{1,0:T(8,128)(2,1)S(1)}, bf16[128,896]{1,0:T(8,128)(2,1)S(1)}, u32[]{:S(2)}, u32[]{:S(2)}) collective-permute-start(bf16[128,896]{1,0:T(8,128)(2,1)S(1)} %add_convert_fusion.1), channel_id=1, source_target_pairs={{0,2},{1,3},{2,0},{3,1},{4,6},{5,7},{6,4},{7,5},{8,10},{9,11},{10,... | collective-permute-start | bytes 688136 | tf_op jit(solution)/shard_map/ppermute | solution.py:30

commit v5 on v3

v5 whole, which is shorter than its diff:
```python
import functools

import jax
import jax.numpy as jnp
from jax import lax
from jax.experimental import pallas as pl
from jax.experimental.pallas import tpu as pltpu
from jax.sharding import PartitionSpec as P

LATENT = 512
ROPE = 64
HEAD_DIM = 128
QUERY = HEAD_DIM + ROPE
PARTS = 4
ROWS_AT_ONCE = 256
NT = (((1,), (1,)), ((), ()))
VMEM_BYTES = 32 * 1024 * 1024
HIDDEN = -1e30


def routed(value, route):
    ctx_count = lax.axis_size("ctx")
    head_count = lax.axis_size("head")
    pairs = []
    for ctx in range(ctx_count):
        for head in range(head_count):
            target = route(ctx, head)
            if target is not None:
                pairs.append((ctx * head_count + head, target[0] * head_count + target[1]))
    return lax.ppermute(value, ("ctx", "head"), pairs)


def is_paired():
    return lax.axis_size("ctx") == 4 and lax.axis_size("head") == 4


def key_sources():
    count = lax.axis_size("ctx")
    ctx = lax.axis_index("ctx")
    if is_paired():
        step = 1 + 2 * (lax.axis_index("head") & 1)
        return [ctx, (ctx - step) & 3, (ctx + step) & 3, ctx ^ 2]
    return [ctx] + [lax.rem(ctx + (count - step), count) for step in range(1, count)]


def part_order():
    if is_paired():
        head = lax.axis_index("head")
        return [head ^ 3, head ^ 2, head ^ 1, head]
    return list(range(PARTS))


VMEM = pl.BlockSpec(memory_space=pltpu.VMEM)
HBM = pl.BlockSpec(memory_space=pltpu.HBM)
PARAMS = pltpu.CompilerParams(vmem_limit_bytes=VMEM_BYTES)
EXPONENT = QUERY**-0.5 * 1.4426950408889634


def prepare_kernel(half, *refs):
    order_hbm, lens_hbm, queries_ref, w_keys_ref, w_values_ref, w_out_ref = refs[:6]
    folded_ref, bias_ref, values_ref = refs[6:9]
    part_refs = refs[9 : 9 + PARTS]
    order_ref, lens_ref, query_buffer, key_buffer, sems = refs[9 + PARTS :]
    width = w_out_ref.shape[1] // PARTS
    heads = w_keys_ref.shape[1] // HEAD_DIM
    rows = 2 * half
    scalars = [
        pltpu.make_async_copy(order_hbm, order_ref, sems.at[0]),
        pltpu.make_async_copy(lens_hbm, lens_ref, sems.at[1]),
    ]
    first = [
        pltpu.make_async_copy(queries_ref, query_buffer, sems.at[2]),
        pltpu.make_async_copy(w_keys_ref, key_buffer, sems.at[3]),
    ]
    later = [pltpu.make_async_copy(w_values_ref, values_ref, sems.at[4])]
    for slot, part in enumerate(part_order()):
        start = pl.multiple_of(part * width, 128)
        source = w_out_ref.at[:, pl.ds(start, width)]
        later.append(pltpu.make_async_copy(source, part_refs[slot], sems.at[5 + slot]))
    for copy in scalars + first + later:
        copy.start()

    for copy in scalars:
        copy.wait()
    ctx = lax.axis_index("ctx")
    row = lax.broadcasted_iota(jnp.int32, (rows, rows), 0)
    lane = lax.broadcasted_iota(jnp.int32, (rows, rows), 1)
    query_pos = jnp.where(row < half, order_ref[2 * ctx], order_ref[2 * ctx + 1]) * half + row % half
    offset = lane % half
    for step, source in enumerate(key_sources()):
        key_place = jnp.where(lane < half, order_ref[2 * source], order_ref[2 * source + 1])
        length = jnp.where(lane < half, lens_ref[2 * source], lens_ref[2 * source + 1])
        visible = (key_place * half + offset <= query_pos) & (offset < length)
        bias_ref[:, step * rows : (step + 1) * rows] = jnp.where(visible, 0.0, HIDDEN)

    for copy in first:
        copy.wait()
    for head in range(heads):
        nope = query_buffer[:, head * QUERY : head * QUERY + HEAD_DIM]
        rope = query_buffer[:, head * QUERY + HEAD_DIM : (head + 1) * QUERY]
        weight = key_buffer[:, head * HEAD_DIM : (head + 1) * HEAD_DIM]
        product = lax.dot_general(nope, weight, NT, preferred_element_type=jnp.float32)
        product = product.astype(jnp.bfloat16)
        for side in range(2):
            target = slice((side * heads + head) * half, (side * heads + head + 1) * half)
            origin = slice(side * half, (side + 1) * half)
            folded_ref[target, :LATENT] = product[origin, :]
            folded_ref[target, LATENT:] = rope[origin, :]
    for copy in later:
        copy.wait()


def prepare(*operands):
    order, lens, queries, w_keys, w_values, w_out = operands
    rows = queries.shape[0]
    count = lax.axis_size("ctx")
    heads = w_keys.shape[1] // HEAD_DIM
    part = jax.ShapeDtypeStruct((w_out.shape[0], w_out.shape[1] // PARTS), jnp.bfloat16)
    return pl.pallas_call(
        functools.partial(prepare_kernel, rows // 2),
        out_shape=[
            jax.ShapeDtypeStruct((heads * rows, LATENT + ROPE), jnp.bfloat16),
            jax.ShapeDtypeStruct((rows, count * rows), jnp.float32),
            jax.ShapeDtypeStruct(w_values.shape, jnp.bfloat16),
        ]
        + [part] * PARTS,
        in_specs=[HBM] * 6,
        out_specs=[VMEM] * (3 + PARTS),
        scratch_shapes=[
            pltpu.SMEM(order.shape, jnp.int32),
            pltpu.SMEM(lens.shape, jnp.int32),
            pltpu.VMEM(queries.shape, jnp.bfloat16),
            pltpu.VMEM(w_keys.shape, jnp.bfloat16),
            pltpu.SemaphoreType.DMA((5 + PARTS,)),
        ],
        compiler_params=PARAMS,
        cost_estimate=pl.CostEstimate(
            flops=2 * rows * heads * HEAD_DIM * LATENT,
            bytes_accessed=2 * (queries.size + w_keys.size + w_values.size + w_out.size),
            transcendentals=0,
        ),
        name="prepare",
    )(*[pltpu.with_memory_space_constraint(item, pltpu.HBM) for item in operands])


def attend_rows(side, folded_ref, bias_ref, values_ref, keys_ref, attended_ref):
    half = bias_ref.shape[0] // 2
    heads = values_ref.shape[1] // HEAD_DIM
    stacked = ROWS_AT_ONCE // half
    bias = jnp.concatenate([bias_ref[side * half : (side + 1) * half, :]] * stacked, axis=0)
    for group in range(heads // stacked):
        start = side * heads * half + group * ROWS_AT_ONCE
        scores = jnp.dot(
            folded_ref[start : start + ROWS_AT_ONCE, :],
            keys_ref[...],
            preferred_element_type=jnp.float32,
        )
        scores = scores + bias
        peak = jnp.max(scores, axis=1, keepdims=True)
        weights = jnp.exp2((scores - peak) * jnp.float32(EXPONENT))
        total = jnp.sum(weights, axis=1, keepdims=True)
        mixed = lax.dot_general(
            weights.astype(jnp.bfloat16), keys_ref[:LATENT, :], NT, preferred_element_type=jnp.float32
        )
        mixed = (mixed / total).astype(jnp.bfloat16)
        for inner in range(stacked):
            head = group * stacked + inner
            columns = slice(head * HEAD_DIM, (head + 1) * HEAD_DIM)
            value = jnp.dot(
                mixed[inner * half : (inner + 1) * half, :],
                values_ref[:, columns],
                preferred_element_type=jnp.float32,
            )
            attended_ref[:, columns] = value.astype(jnp.bfloat16)


def project(attended_ref, part_ref, share_ref):
    share = jnp.dot(attended_ref[...], part_ref[...], preferred_element_type=jnp.float32)
    share_ref[...] = share.astype(share_ref.dtype)


def place_if(keys_ref, slot, block_ref, condition):
    rows = block_ref.shape[1]

    @pl.when(condition)
    def _():
        keys_ref[:, slot * rows : (slot + 1) * rows] = block_ref[...]


def first_half_kernel(count, paired, folded_ref, bias_ref, values_ref, part_ref, *rest):
    blocks, (keys_ref, attended_ref, share_ref) = rest[:count], rest[count:]
    rows = blocks[0].shape[1]
    certain = count - 2 if paired else count
    for slot in range(certain):
        keys_ref[:, slot * rows : (slot + 1) * rows] = blocks[slot][...]
    if paired:
        direct = (lax.axis_index("ctx") ^ lax.axis_index("head")) & 1 == 0
        place_if(keys_ref, certain, blocks[certain], direct)
        place_if(keys_ref, certain, blocks[certain + 1], jnp.logical_not(direct))
    attend_rows(0, folded_ref, bias_ref, values_ref, keys_ref, attended_ref)
    project(attended_ref, part_ref, share_ref)


def second_half_kernel(folded_ref, bias_ref, values_ref, part_ref, keys_ref, attended_ref, share_ref):
    attend_rows(1, folded_ref, bias_ref, values_ref, keys_ref, attended_ref)
    project(attended_ref, part_ref, share_ref)


def attend_half(folded, bias, values, part, blocks, kind, keys=None):
    rows, key_count = bias.shape
    half = rows // 2
    heads = values.shape[1] // HEAD_DIM
    flops = 2 * heads * half * (key_count * (2 * LATENT + ROPE) + LATENT * HEAD_DIM)
    outs = [
        jax.ShapeDtypeStruct((half, values.shape[1]), jnp.bfloat16),
        jax.ShapeDtypeStruct((half, part.shape[1]), kind),
    ]
    if keys is None:
        kernel = functools.partial(first_half_kernel, len(blocks), is_paired())
        outs = [jax.ShapeDtypeStruct((LATENT + ROPE, key_count), jnp.bfloat16)] + outs
        extra = blocks
    else:
        kernel = second_half_kernel
        extra = [keys]
    return pl.pallas_call(
        kernel,
        out_shape=outs,
        in_specs=[VMEM] * (4 + len(extra)),
        out_specs=[VMEM] * len(outs),
        compiler_params=PARAMS,
        cost_estimate=pl.CostEstimate(
            flops=flops + 2 * half * part.size,
            bytes_accessed=folded.size + 2 * (values.size + part.size),
            transcendentals=heads * half * key_count,
        ),
        name="first_half" if keys is None else "second_half",
    )(folded, bias, values, part, *extra)


def project_kernel(attended_ref, *refs):
    count = len(refs) // 2
    for part_ref, share_ref in zip(refs[:count], refs[count:]):
        project(attended_ref, part_ref, share_ref)


def project_parts(attended, parts, kinds):
    half = attended.shape[0]
    shares = [
        jax.ShapeDtypeStruct((half, part.shape[1]), kind) for part, kind in zip(parts, kinds)
    ]
    size = sum(part.size for part in parts)
    return pl.pallas_call(
        project_kernel,
        out_shape=shares,
        in_specs=[VMEM] * (1 + len(parts)),
        out_specs=[VMEM] * len(parts),
        compiler_params=PARAMS,
        cost_estimate=pl.CostEstimate(
            flops=2 * half * size, bytes_accessed=2 * size, transcendentals=0
        ),
        name="project_parts",
    )(attended, *parts)


def next_to(ctx, head):
    return (ctx + 1 + 2 * (head & 1)) & 3, head


def two_away(ctx, head):
    return (ctx ^ 2 if (ctx ^ head) & 1 == 0 else ctx), head


def other_core(ctx, head):
    return ctx, head ^ 1


def other_chip(ctx, head):
    return ctx, head ^ 2


def shards(queries, latent, w_keys, w_values, w_out, block_order, valid_lengths):
    ctx_count = lax.axis_size("ctx")
    block = latent.T
    prepared = prepare(block_order, valid_lengths, queries, w_keys, w_values, w_out)
    narrow, wide = jnp.bfloat16, jnp.float32

    if not is_paired():
        blocks = [block]
        for step in range(1, ctx_count):
            blocks.append(routed(block, lambda ctx, head: ((ctx + step) % ctx_count, head)))
        folded, bias, values, *parts = prepared
        keys, first, share = attend_half(folded, bias, values, parts[0], blocks, narrow)
        shares = [share] + list(project_parts(first, parts[1:], [narrow] * 3))
        upper = jnp.concatenate(shares, axis=1)
        second, share = attend_half(folded, bias, values, parts[0], None, narrow, keys)
        shares = [share] + list(project_parts(second, parts[1:], [narrow] * 3))
        lower = jnp.concatenate(shares, axis=1)
        whole = jnp.concatenate([upper, lower], axis=0)
        return lax.psum_scatter(whole, "head", scatter_dimension=1, tiled=True)

    near = routed(block, next_to)
    far = routed(block, two_away)
    near, prepared = lax.optimization_barrier((near, prepared))
    near_swapped = routed(near, other_core)
    far, _ = lax.optimization_barrier((far, near))
    far_swapped = routed(far, other_core)
    folded, bias, values, *parts = prepared

    def send_on(attended, across):
        received = routed(across, other_core)
        far_part, beside, own = project_parts(attended, parts[1:], [wide, narrow, wide])
        far_part = (far_part + received.astype(wide)).astype(narrow)
        far_part, beside = lax.optimization_barrier((far_part, beside))
        return far_part, beside, own

    blocks = [block, near, near_swapped, far, far_swapped]
    keys, attended, across = attend_half(folded, bias, values, parts[0], blocks, narrow)
    far_part, beside, own = send_on(attended, across)
    keys, far_part = lax.optimization_barrier((keys, far_part))
    upper = (routed(far_part, other_chip), routed(beside, other_core), own)
    attended, across = attend_half(folded, bias, values, parts[0], None, narrow, keys)
    far_part, beside, own = send_on(attended, across)
    lower = (routed(far_part, other_chip), routed(beside, other_core), own)
    halves = [
        (own + beside.astype(wide) + far_part.astype(wide)).astype(narrow)
        for far_part, beside, own in (upper, lower)
    ]
    return jnp.concatenate(halves, axis=0)


def solution(mesh):
    in_specs = (
        P(("groups", "ctx"), "head"),
        P(("groups", "ctx"), None),
        P(None, "head"),
        P(None, "head"),
        P("head", None),
        P("groups"),
        P("groups"),
    )
    out_specs = P(("groups", "ctx"), "head")
    return jax.shard_map(shards, mesh=mesh, in_specs=in_specs, out_specs=out_specs, check_vma=False)
```

time: 28.7 us -> 28.9 us (level)
  waiting for transfers between devices: 9.4 us -> 6.52 us
  Pallas kernels: 8.04 us -> 9.99 us
  starting transfers between devices: 10.2 us -> 11.3 us
    ppermute x7 -> x10, waiting for transfers between devices: 9.4 us -> 6.52 us  [routed(): return lax.ppermute(value, ('ctx', 'head'), pairs)]
    pallas_call x2 -> x5, Pallas kernels: 8.04 us -> 9.99 us  [the longest x1 3.99 us: prepare(): pl.pallas_call(functools.partial(prepare_kernel, rows // 2), out_shape=[j...]
    ppermute x7 -> x10, starting transfers between devices: 10.2 us -> 11.3 us  [routed(): return lax.ppermute(value, ('ctx', 'head'), pairs)]
    concatenate x0 -> x1, other arithmetic: none -> 0.71 us  [shards(): return jnp.concatenate(halves, axis=0)]
    convert_element_type x2 -> x4, other arithmetic: 0.81 us -> 0.13 us  [the longest x2 0.08 us: shards(): (own + beside.astype(wide) + far_part.astype(wide)).astype(narrow)]
  transfers between devices with their start and end apart: 7 -> 10, of which waited for: 5 -> 5; matrix products, arithmetic and copies ran while one was open for 0% -> 0% of each run, Pallas kernels for 14% -> 21%
where the time goes in v5:
time: 28.9 us; the launch traced here: 28.8 us
  starting transfers between devices  11.3 us (39%)
  Pallas kernels  9.99 us (35%)
  waiting for transfers between devices  6.52 us (23%)
  other arithmetic  0.83 us (3%)
    ppermute x10, starting transfers between devices, routed(): return lax.ppermute(value, ('ctx', 'head'), pairs)  11.3 us
    ppermute x10, waiting for transfers between devices, routed(): return lax.ppermute(value, ('ctx', 'head'), pairs)  6.52 us
    pallas_call x1, Pallas kernels, prepare(): pl.pallas_call(functools.partial(prepare_kernel, rows // 2), out_shape=[j...  3.99 us
    pallas_call x2, Pallas kernels, attend_half(): pl.pallas_call(kernel, out_shape=outs, in_specs=[VMEM] * (4 + len(extra))...  3.93 us
    pallas_call x2, Pallas kernels, project_parts(): pl.pallas_call(project_kernel, out_shape=shares, in_specs=[VMEM] * (1 + l...  2.07 us
    concatenate x1, other arithmetic, shards(): return jnp.concatenate(halves, axis=0)  0.71 us
  transfers between devices with their start and end apart: 10, of which 5 were waited for; matrix products, arithmetic and copies ran while one was open for 0% of the time, Pallas kernels for 21%

profile of v5, /device:TPU:0, one launch (start us, length us, event | category | flops | bytes accessed | tf_op | source)
XLA Modules:
  0.0 28.8 jit_solution(2601706743341834838)
XLA Ops:
  0.0 0.0 copy-start
  0.0 3.0 %collective-permute-start = (bf16[576,128]{1,0:T(8,128)(2,1)}, bf16[576,128]{1,0:T(8,128)(2,1)S(1)}, u32[]{:S(2)}, u32[]{:S(2)}) collective-permute-start(bf16[576,128]{1,0:T(8,128)(2,1)} %bitcast.1), channel_id=1, source_target_pairs={{0,4},{1,13},{2,6},{3,15},{4,8},{5,1},{6,10},{7,3},{8,12},{9,5},{1... | collective-permute-start | bytes 442376 | tf_op jit(solution)/shard_map/ppermute | solution.py:30
  3.0 4.5 %collective-permute-start.2 = (bf16[576,128]{1,0:T(8,128)(2,1)}, bf16[576,128]{1,0:T(8,128)(2,1)S(1)}, u32[]{:S(2)}, u32[]{:S(2)}) collective-permute-start(bf16[576,128]{1,0:T(8,128)(2,1)} %bitcast.2), channel_id=1, source_target_pairs={{0,8},{1,1},{2,10},{3,3},{4,4},{5,13},{6,6},{7,15},{8,0},{9,9},{10... | collective-permute-start | bytes 442376 | tf_op jit(solution)/shard_map/ppermute | solution.py:30
  7.5 4.0 %prepare.1 = (bf16[1024,576]{1,0:T(8,128)(2,1)S(1)}, f32[128,512]{1,0:T(8,128)S(1)}, bf16[512,1024]{1,0:T(8,128)(2,1)S(1)}, bf16[1024,896]{1,0:T(8,128)(2,1)S(1)...) custom-call(s32[8]{0:T(128)} %refs_0_.1, s32[8]{0:T(128)} %refs_1_.1, ...), custom_call_target="tpu_custom_call" | custom-call | flops 134217728 | bytes 9830400 | tf_op jit(solution)/shard_map/prepare/pallas_call | solution.py:119
  11.5 0.0 collective-permute-done.rest_1_
  11.5 0.9 %collective-permute-done.2.rest_3_ = bf16[576,128]{1,0:T(8,128)(2,1)S(1)} collective-permute-done((bf16[576,128]{1,0:T(8,128)(2,1)}, bf16[576,128]{1,0:T(8,128)(2,1)S(1)}, u32[]{:S(2)}, u32[]{:S(2)}) %collective-permute-start.2) | collective-permute-done | bytes 147488 | tf_op jit(solution)/shard_map/ppermute | solution.py:30
  12.4 0.0 collective-permute-start.3
  12.4 0.5 %collective-permute-start.1 = (bf16[576,128]{1,0:T(8,128)(2,1)S(1)}, bf16[576,128]{1,0:T(8,128)(2,1)S(1)}, u32[]{:S(2)}, u32[]{:S(2)}) collective-permute-start(bf16[576,128]{1,0:T(8,128)(2,1)S(1)} %collective-permute-done.rest_1_), channel_id=1, source_target_pairs={{0,1},{1,0},{2,3},{3,2},{4,5},{5,4},{6,7},{7,6},{8,9},{9,8},{10,11... | collective-permute-start | bytes 442376 | tf_op jit(solution)/shard_map/ppermute | solution.py:30
  12.9 0.9 %collective-permute-done.3.rest_4_ = bf16[576,128]{1,0:T(8,128)(2,1)S(1)} collective-permute-done((bf16[576,128]{1,0:T(8,128)(2,1)S(1)}, bf16[576,128]{1,0:T(8,128)(2,1)S(1)}, u32[]{:S(2)}, u32[]{:S(2)}) %collective-permute-start.3) | collective-permute-done | bytes 147488 | tf_op jit(solution)/shard_map/ppermute | solution.py:30
  13.8 0.2 collective-permute-done.1.rest_2_
  14.0 0.0 copy-done
  14.0 2.0 %first_half.1 = (bf16[576,512]{1,0:T(8,128)(2,1)S(1)}, bf16[64,1024]{1,0:T(8,128)(2,1)S(1)}, bf16[64,896]{1,0:T(8,128)(2,1)S(1)}) custom-call(bf16[1024,576]{1,0:T(8,128)(2,1)S(1)} %get-tuple-element.45.folded_ref, f32[128,512]{1,0:T(8,128)S(1)} %get-tuple-element.46.bias_ref, bf16[512,1024]{1,0:T(8,128)(2,1)S(1)} %get-tuple-element.47.values_ref, ...), custom_call_target="tpu_custom_call" | custom-call | flops 754974720 | bytes 3473408 | tf_op jit(solution)/shard_map/first_half/pallas_call | solution.py:225
  16.1 0.4 %collective-permute-start.4 = (bf16[64,896]{1,0:T(8,128)(2,1)S(1)}, bf16[64,896]{1,0:T(8,128)(2,1)S(1)}, u32[]{:S(2)}, u32[]{:S(2)}) collective-permute-start(bf16[64,896]{1,0:T(8,128)(2,1)S(1)} %get-tuple-element.57), channel_id=1, source_target_pairs={{0,1},{1,0},{2,3},{3,2},{4,5},{5,4},{6,7},{7,6},{8,9},{9,8},{10,11... | collective-permute-start | bytes 344072 | tf_op jit(solution)/shard_map/ppermute | solution.py:30
  16.4 1.0 %project_parts.2 = (f32[64,896]{1,0:T(8,128)S(1)}, bf16[64,896]{1,0:T(8,128)(2,1)S(1)}, f32[64,896]{1,0:T(8,128)S(1)}) custom-call(bf16[64,1024]{1,0:T(8,128)(2,1)S(1)} %get-tuple-element.51.attended_ref, bf16[1024,896]{1,0:T(8,128)(2,1)S(1)} %get-tuple-element.52.refs_0_, bf16[1024,896]{1,0:T(8,128)(2,1)S(1)} %get-tuple-element.53.refs_1_, ...), custom_call_target="tpu_custom_call" | custom-call | flops 352321536 | bytes 5505024 | tf_op jit(solution)/shard_map/project_parts/pallas_call | solution.py:252
  17.5 0.0 collective-permute-done.4
  17.5 1.9 %second_half.1 = (bf16[64,1024]{1,0:T(8,128)(2,1)S(1)}, bf16[64,896]{1,0:T(8,128)(2,1)S(1)}) custom-call(bf16[1024,576]{1,0:T(8,128)(2,1)S(1)} %get-tuple-element.45.folded_ref, f32[128,512]{1,0:T(8,128)S(1)} %get-tuple-element.46.bias_ref, bf16[512,1024]{1,0:T(8,128)(2,1)S(1)} %get-tuple-element.47.values_ref, ...), custom_call_target="tpu_custom_call" | custom-call | flops 754974720 | bytes 3473408 | tf_op jit(solution)/shard_map/second_half/pallas_call | solution.py:225
  19.4 0.3 %collective-permute-start.7 = (bf16[64,896]{1,0:T(8,128)(2,1)S(1)}, bf16[64,896]{1,0:T(8,128)(2,1)S(1)}, u32[]{:S(2)}, u32[]{:S(2)}) collective-permute-start(bf16[64,896]{1,0:T(8,128)(2,1)S(1)} %get-tuple-element.67), channel_id=1, source_target_pairs={{0,1},{1,0},{2,3},{3,2},{4,5},{5,4},{6,7},{7,6},{8,9},{9,8},{10,11... | collective-permute-start | bytes 344072 | tf_op jit(solution)/shard_map/ppermute | solution.py:30
  19.8 1.5 %collective-permute-start.6 = (bf16[64,896]{1,0:T(8,128)(2,1)S(1)}, bf16[64,896]{1,0:T(8,128)(2,1)S(1)}, u32[]{:S(2)}, u32[]{:S(2)}) collective-permute-start(bf16[64,896]{1,0:T(8,128)(2,1)S(1)} %add_convert_fusion.3), channel_id=1, source_target_pairs={{0,2},{1,3},{2,0},{3,1},{4,6},{5,7},{6,4},{7,5},{8,10},{9,11},{10,... | collective-permute-start | bytes 344072 | tf_op jit(solution)/shard_map/ppermute | solution.py:30
  21.2 0.0 collective-permute-start.5
  21.2 1.0 %project_parts.3 = (f32[64,896]{1,0:T(8,128)S(1)}, bf16[64,896]{1,0:T(8,128)(2,1)S(1)}, f32[64,896]{1,0:T(8,128)S(1)}) custom-call(bf16[64,1024]{1,0:T(8,128)(2,1)S(1)} %get-tuple-element.64.attended_ref, bf16[1024,896]{1,0:T(8,128)(2,1)S(1)} %get-tuple-element.52.refs_0_, bf16[1024,896]{1,0:T(8,128)(2,1)S(1)} %get-tuple-element.53.refs_1_, ...), custom_call_target="tpu_custom_call" | custom-call | flops 352321536 | bytes 5505024 | tf_op jit(solution)/shard_map/project_parts/pallas_call | solution.py:252
  22.3 0.0 collective-permute-done.7
  22.3 0.6 %collective-permute-start.8 = (bf16[64,896]{1,0:T(8,128)(2,1)S(1)}, bf16[64,896]{1,0:T(8,128)(2,1)S(1)}, u32[]{:S(2)}, u32[]{:S(2)}) collective-permute-start(bf16[64,896]{1,0:T(8,128)(2,1)S(1)} %get-tuple-element.69), channel_id=1, source_target_pairs={{0,1},{1,0},{2,3},{3,2},{4,5},{5,4},{6,7},{7,6},{8,9},{9,8},{10,11... | collective-permute-start | bytes 344072 | tf_op jit(solution)/shard_map/ppermute | solution.py:30
  22.9 0.5 %collective-permute-start.9 = (bf16[64,896]{1,0:T(8,128)(2,1)S(1)}, bf16[64,896]{1,0:T(8,128)(2,1)S(1)}, u32[]{:S(2)}, u32[]{:S(2)}) collective-permute-start(bf16[64,896]{1,0:T(8,128)(2,1)S(1)} %add_convert_fusion.1), channel_id=1, source_target_pairs={{0,2},{1,3},{2,0},{3,1},{4,6},{5,7},{6,4},{7,5},{8,10},{9,11},{10,... | collective-permute-start | bytes 344072 | tf_op jit(solution)/shard_map/ppermute | solution.py:30
  23.4 1.6 %collective-permute-done.6 = bf16[64,896]{1,0:T(8,128)(2,1)S(1)} collective-permute-done((bf16[64,896]{1,0:T(8,128)(2,1)S(1)}, bf16[64,896]{1,0:T(8,128)(2,1)S(1)}, u32[]{:S(2)}, u32[]{:S(2)}) %collective-permute-start.6) | collective-permute-done | bytes 114720 | tf_op jit(solution)/shard_map/ppermute | solution.py:30
  25.0 0.0 collective-permute-done.5
  25.1 0.0 collective-permute-done.8
  25.1 2.9 %collective-permute-done.9 = bf16[64,896]{1,0:T(8,128)(2,1)S(1)} collective-permute-done((bf16[64,896]{1,0:T(8,128)(2,1)S(1)}, bf16[64,896]{1,0:T(8,128)(2,1)S(1)}, u32[]{:S(2)}, u32[]{:S(2)}) %collective-permute-start.9) | collective-permute-done | bytes 114720 | tf_op jit(solution)/shard_map/ppermute | solution.py:30
  28.1 0.7 %pad_maximum_fusion = bf16[128,896]{1,0:T(8,128)(2,1)} fusion(bf16[64,896]{1,0:T(8,128)(2,1)S(1)} %add_convert_fusion, bf16[64,896]{1,0:T(8,128)(2,1)S(1)} %add_convert_fusion.2), kind=kLoop, calls=%fused_computation | loop fusion | flops 458752 | bytes 458752 | tf_op jit(solution)/shard_map/concatenate | solution.py:328
  (4 shorter events, 0.1 us)
Async XLA Ops:
  0.0 14.0 %copy-start = (bf16[128,576]{0,1:T(8,128)(2,1)S(1)}, bf16[128,576]{0,1:T(8,128)(2,1)}, u32[]{:S(2)}) copy-start(bf16[128,576]{0,1:T(8,128)(2,1)} %param.8) | copy-start | bytes 442372
  0.0 11.5 %collective-permute-start = (bf16[576,128]{1,0:T(8,128)(2,1)}, bf16[576,128]{1,0:T(8,128)(2,1)S(1)}, u32[]{:S(2)}, u32[]{:S(2)}) collective-permute-start(bf16[576,128]{1,0:T(8,128)(2,1)} %bitcast.1), channel_id=1, source_target_pairs={{0,4},{1,13},{2,6},{3,15},{4,8},{5,1},{6,10},{7,3},{8,12},{9,5},{1... | collective-permute-start | bytes 442376 | tf_op jit(solution)/shard_map/ppermute | solution.py:30
  3.0 9.4 %collective-permute-start.2 = (bf16[576,128]{1,0:T(8,128)(2,1)}, bf16[576,128]{1,0:T(8,128)(2,1)S(1)}, u32[]{:S(2)}, u32[]{:S(2)}) collective-permute-start(bf16[576,128]{1,0:T(8,128)(2,1)} %bitcast.2), channel_id=1, source_target_pairs={{0,8},{1,1},{2,10},{3,3},{4,4},{5,13},{6,6},{7,15},{8,0},{9,9},{10... | collective-permute-start | bytes 442376 | tf_op jit(solution)/shard_map/ppermute | solution.py:30
  12.4 1.4 %collective-permute-start.3 = (bf16[576,128]{1,0:T(8,128)(2,1)S(1)}, bf16[576,128]{1,0:T(8,128)(2,1)S(1)}, u32[]{:S(2)}, u32[]{:S(2)}) collective-permute-start(bf16[576,128]{1,0:T(8,128)(2,1)S(1)} %collective-permute-done.2.rest_3_), channel_id=1, source_target_pairs={{0,1},{1,0},{2,3},{3,2},{4,5},{5,4},{6,7},{7,6},{8,9},{9,8},{10,11... | collective-permute-start | bytes 442376 | tf_op jit(solution)/shard_map/ppermute | solution.py:30
  12.4 1.6 %collective-permute-start.1 = (bf16[576,128]{1,0:T(8,128)(2,1)S(1)}, bf16[576,128]{1,0:T(8,128)(2,1)S(1)}, u32[]{:S(2)}, u32[]{:S(2)}) collective-permute-start(bf16[576,128]{1,0:T(8,128)(2,1)S(1)} %collective-permute-done.rest_1_), channel_id=1, source_target_pairs={{0,1},{1,0},{2,3},{3,2},{4,5},{5,4},{6,7},{7,6},{8,9},{9,8},{10,11... | collective-permute-start | bytes 442376 | tf_op jit(solution)/shard_map/ppermute | solution.py:30
  16.1 1.4 %collective-permute-start.4 = (bf16[64,896]{1,0:T(8,128)(2,1)S(1)}, bf16[64,896]{1,0:T(8,128)(2,1)S(1)}, u32[]{:S(2)}, u32[]{:S(2)}) collective-permute-start(bf16[64,896]{1,0:T(8,128)(2,1)S(1)} %get-tuple-element.57), channel_id=1, source_target_pairs={{0,1},{1,0},{2,3},{3,2},{4,5},{5,4},{6,7},{7,6},{8,9},{9,8},{10,11... | collective-permute-start | bytes 344072 | tf_op jit(solution)/shard_map/ppermute | solution.py:30
  19.4 2.9 %collective-permute-start.7 = (bf16[64,896]{1,0:T(8,128)(2,1)S(1)}, bf16[64,896]{1,0:T(8,128)(2,1)S(1)}, u32[]{:S(2)}, u32[]{:S(2)}) collective-permute-start(bf16[64,896]{1,0:T(8,128)(2,1)S(1)} %get-tuple-element.67), channel_id=1, source_target_pairs={{0,1},{1,0},{2,3},{3,2},{4,5},{5,4},{6,7},{7,6},{8,9},{9,8},{10,11... | collective-permute-start | bytes 344072 | tf_op jit(solution)/shard_map/ppermute | solution.py:30
  19.8 5.3 %collective-permute-start.6 = (bf16[64,896]{1,0:T(8,128)(2,1)S(1)}, bf16[64,896]{1,0:T(8,128)(2,1)S(1)}, u32[]{:S(2)}, u32[]{:S(2)}) collective-permute-start(bf16[64,896]{1,0:T(8,128)(2,1)S(1)} %add_convert_fusion.3), channel_id=1, source_target_pairs={{0,2},{1,3},{2,0},{3,1},{4,6},{5,7},{6,4},{7,5},{8,10},{9,11},{10,... | collective-permute-start | bytes 344072 | tf_op jit(solution)/shard_map/ppermute | solution.py:30
  21.2 3.8 %collective-permute-start.5 = (bf16[64,896]{1,0:T(8,128)(2,1)S(1)}, bf16[64,896]{1,0:T(8,128)(2,1)S(1)}, u32[]{:S(2)}, u32[]{:S(2)}) collective-permute-start(bf16[64,896]{1,0:T(8,128)(2,1)S(1)} %get-tuple-element.59), channel_id=1, source_target_pairs={{0,1},{1,0},{2,3},{3,2},{4,5},{5,4},{6,7},{7,6},{8,9},{9,8},{10,11... | collective-permute-start | bytes 344072 | tf_op jit(solution)/shard_map/ppermute | solution.py:30
  22.3 2.8 %collective-permute-start.8 = (bf16[64,896]{1,0:T(8,128)(2,1)S(1)}, bf16[64,896]{1,0:T(8,128)(2,1)S(1)}, u32[]{:S(2)}, u32[]{:S(2)}) collective-permute-start(bf16[64,896]{1,0:T(8,128)(2,1)S(1)} %get-tuple-element.69), channel_id=1, source_target_pairs={{0,1},{1,0},{2,3},{3,2},{4,5},{5,4},{6,7},{7,6},{8,9},{9,8},{10,11... | collective-permute-start | bytes 344072 | tf_op jit(solution)/shard_map/ppermute | solution.py:30
  22.9 5.1 %collective-permute-start.9 = (bf16[64,896]{1,0:T(8,128)(2,1)S(1)}, bf16[64,896]{1,0:T(8,128)(2,1)S(1)}, u32[]{:S(2)}, u32[]{:S(2)}) collective-permute-start(bf16[64,896]{1,0:T(8,128)(2,1)S(1)} %add_convert_fusion.1), channel_id=1, source_target_pairs={{0,2},{1,3},{2,0},{3,1},{4,6},{5,7},{6,4},{7,5},{8,10},{9,11},{10,... | collective-permute-start | bytes 344072 | tf_op jit(solution)/shard_map/ppermute | solution.py:30

commit v6 on v5

v6 whole, which is shorter than its diff:
```python
import functools

import jax
import jax.numpy as jnp
from jax import lax
from jax.experimental import pallas as pl
from jax.experimental.pallas import tpu as pltpu
from jax.sharding import PartitionSpec as P

LATENT = 512
ROPE = 64
HEAD_DIM = 128
QUERY = HEAD_DIM + ROPE
PARTS = 4
ROWS_AT_ONCE = 256
NT = (((1,), (1,)), ((), ()))
VMEM_BYTES = 32 * 1024 * 1024
HIDDEN = -1e30


def routed(value, route):
    ctx_count = lax.axis_size("ctx")
    head_count = lax.axis_size("head")
    pairs = []
    for ctx in range(ctx_count):
        for head in range(head_count):
            target = route(ctx, head)
            if target is not None:
                pairs.append((ctx * head_count + head, target[0] * head_count + target[1]))
    return lax.ppermute(value, ("ctx", "head"), pairs)


def is_paired():
    return lax.axis_size("ctx") == 4 and lax.axis_size("head") == 4


def key_sources():
    count = lax.axis_size("ctx")
    ctx = lax.axis_index("ctx")
    if is_paired():
        step = 1 + 2 * (lax.axis_index("head") & 1)
        return [ctx, (ctx - step) & 3, (ctx + step) & 3, ctx ^ 2]
    return [ctx] + [lax.rem(ctx + (count - step), count) for step in range(1, count)]


def part_order():
    if is_paired():
        head = lax.axis_index("head")
        return [head ^ 3, head ^ 2, head ^ 1, head]
    return list(range(PARTS))


VMEM = pl.BlockSpec(memory_space=pltpu.VMEM)
HBM = pl.BlockSpec(memory_space=pltpu.HBM)
FIRST_PIECE = 512
PARAMS = pltpu.CompilerParams(vmem_limit_bytes=VMEM_BYTES)
SHORT = pl.CostEstimate(flops=1024, bytes_accessed=1024, transcendentals=0)
EXPONENT = QUERY**-0.5 * 1.4426950408889634


def prepare_kernel(half, *refs):
    order_hbm, lens_hbm, queries_ref, w_keys_ref, w_values_ref, w_out_ref = refs[:6]
    folded_ref, bias_ref, values_ref = refs[6:9]
    part_refs = refs[9 : 9 + PARTS]
    order_ref, lens_ref, query_buffer, key_buffer, sems = refs[9 + PARTS :]
    width = w_out_ref.shape[1] // PARTS
    heads = w_keys_ref.shape[1] // HEAD_DIM
    rows = 2 * half
    scalars = [
        pltpu.make_async_copy(order_hbm, order_ref, sems.at[0]),
        pltpu.make_async_copy(lens_hbm, lens_ref, sems.at[1]),
    ]
    first = [
        pltpu.make_async_copy(queries_ref, query_buffer, sems.at[2]),
        pltpu.make_async_copy(w_keys_ref, key_buffer, sems.at[3]),
    ]
    later = [pltpu.make_async_copy(w_values_ref, values_ref, sems.at[4])]
    for slot, part in enumerate(part_order()):
        start = pl.multiple_of(part * width, 128)
        source = w_out_ref.at[:, pl.ds(start, width)]
        later.append(pltpu.make_async_copy(source, part_refs[slot], sems.at[5 + slot]))
    for copy in scalars + first + later:
        copy.start()

    for copy in scalars:
        copy.wait()
    ctx = lax.axis_index("ctx")
    row = lax.broadcasted_iota(jnp.int32, (rows, rows), 0)
    lane = lax.broadcasted_iota(jnp.int32, (rows, rows), 1)
    query_pos = jnp.where(row < half, order_ref[2 * ctx], order_ref[2 * ctx + 1]) * half + row % half
    offset = lane % half
    for step, source in enumerate(key_sources()):
        key_place = jnp.where(lane < half, order_ref[2 * source], order_ref[2 * source + 1])
        length = jnp.where(lane < half, lens_ref[2 * source], lens_ref[2 * source + 1])
        visible = (key_place * half + offset <= query_pos) & (offset < length)
        bias_ref[:, step * rows : (step + 1) * rows] = jnp.where(visible, 0.0, HIDDEN)

    for copy in first:
        copy.wait()
    for head in range(heads):
        nope = query_buffer[:, head * QUERY : head * QUERY + HEAD_DIM]
        rope = query_buffer[:, head * QUERY + HEAD_DIM : (head + 1) * QUERY]
        weight = key_buffer[:, head * HEAD_DIM : (head + 1) * HEAD_DIM]
        product = lax.dot_general(nope, weight, NT, preferred_element_type=jnp.float32)
        here = slice(head * rows, (head + 1) * rows)
        folded_ref[here, :LATENT] = product.astype(jnp.bfloat16)
        folded_ref[here, LATENT:] = rope
    for copy in later:
        copy.wait()


def prepare(*operands):
    order, lens, queries, w_keys, w_values, w_out = operands
    rows = queries.shape[0]
    count = lax.axis_size("ctx")
    heads = w_keys.shape[1] // HEAD_DIM
    part = jax.ShapeDtypeStruct((w_out.shape[0], w_out.shape[1] // PARTS), jnp.bfloat16)
    return pl.pallas_call(
        functools.partial(prepare_kernel, rows // 2),
        out_shape=[
            jax.ShapeDtypeStruct((heads * rows, LATENT + ROPE), jnp.bfloat16),
            jax.ShapeDtypeStruct((rows, count * rows), jnp.float32),
            jax.ShapeDtypeStruct(w_values.shape, jnp.bfloat16),
        ]
        + [part] * PARTS,
        in_specs=[HBM] * 6,
        out_specs=[VMEM] * (3 + PARTS),
        scratch_shapes=[
            pltpu.SMEM(order.shape, jnp.int32),
            pltpu.SMEM(lens.shape, jnp.int32),
            pltpu.VMEM(queries.shape, jnp.bfloat16),
            pltpu.VMEM(w_keys.shape, jnp.bfloat16),
            pltpu.SemaphoreType.DMA((5 + PARTS,)),
        ],
        compiler_params=PARAMS,
        cost_estimate=pl.CostEstimate(
            flops=2 * rows * heads * HEAD_DIM * LATENT,
            bytes_accessed=2 * (queries.size + w_keys.size + w_values.size + w_out.size),
            transcendentals=0,
        ),
        name="prepare",
    )(*[pltpu.with_memory_space_constraint(item, pltpu.HBM) for item in operands])


def place_if(keys_ref, slot, block_ref, condition):
    rows = block_ref.shape[1]

    @pl.when(condition)
    def _():
        keys_ref[:, slot * rows : (slot + 1) * rows] = block_ref[...]


def project(attended_ref, part_ref, share_refs):
    start = 0
    for share_ref in share_refs:
        stop = start + share_ref.shape[1]
        share = jnp.dot(
            attended_ref[...], part_ref[:, start:stop], preferred_element_type=jnp.float32
        )
        share_ref[...] = share.astype(share_ref.dtype)
        start = stop


def attend_kernel(count, paired, folded_ref, bias_ref, values_ref, part_ref, *rest):
    blocks, (attended_ref, *shares, keys_ref) = rest[:count], rest[count:]
    rows = bias_ref.shape[0]
    heads = values_ref.shape[1] // HEAD_DIM
    certain = count - 2 if paired else count
    for slot in range(certain):
        keys_ref[:, slot * rows : (slot + 1) * rows] = blocks[slot][...]
    if paired:
        direct = (lax.axis_index("ctx") ^ lax.axis_index("head")) & 1 == 0
        place_if(keys_ref, certain, blocks[certain], direct)
        place_if(keys_ref, certain, blocks[certain + 1], jnp.logical_not(direct))
    stacked = ROWS_AT_ONCE // rows
    bias = jnp.concatenate([bias_ref[...]] * stacked, axis=0)
    for group in range(heads // stacked):
        lines = slice(group * ROWS_AT_ONCE, (group + 1) * ROWS_AT_ONCE)
        scores = jnp.dot(folded_ref[lines, :], keys_ref[...], preferred_element_type=jnp.float32)
        scores = scores + bias
        peak = jnp.max(scores, axis=1, keepdims=True)
        weights = jnp.exp2((scores - peak) * jnp.float32(EXPONENT))
        inverse = 1.0 / jnp.sum(weights, axis=1, keepdims=True)
        mixed = lax.dot_general(
            weights.astype(jnp.bfloat16), keys_ref[:LATENT, :], NT, preferred_element_type=jnp.float32
        ).astype(jnp.bfloat16)
        for inner in range(stacked):
            head = group * stacked + inner
            columns = slice(head * HEAD_DIM, (head + 1) * HEAD_DIM)
            lines = slice(inner * rows, (inner + 1) * rows)
            value = jnp.dot(
                mixed[lines, :], values_ref[:, columns], preferred_element_type=jnp.float32
            )
            attended_ref[:, columns] = (value * inverse[lines, :]).astype(jnp.bfloat16)
    project(attended_ref, part_ref, shares)


def share_shapes(rows, widths, kind):
    return [jax.ShapeDtypeStruct((rows, width), kind) for width in widths]


def attend(folded, bias, values, part, blocks, widths):
    rows, keys = bias.shape
    heads = values.shape[1] // HEAD_DIM
    flops = 2 * heads * rows * (keys * (2 * LATENT + ROPE) + LATENT * HEAD_DIM)
    return pl.pallas_call(
        functools.partial(attend_kernel, len(blocks), is_paired()),
        out_shape=share_shapes(rows, [values.shape[1]] + widths, jnp.bfloat16),
        in_specs=[VMEM] * (4 + len(blocks)),
        out_specs=[VMEM] * (1 + len(widths)),
        scratch_shapes=[pltpu.VMEM((LATENT + ROPE, keys), jnp.bfloat16)],
        compiler_params=PARAMS,
        cost_estimate=pl.CostEstimate(
            flops=flops + 2 * rows * part.size,
            bytes_accessed=2 * (folded.size + values.size + part.size),
            transcendentals=heads * rows * keys,
        ),
        name="attend",
    )(folded, bias, values, part, *blocks)


def project_kernel(pieces, attended_ref, *refs):
    parts, shares = refs[: len(pieces)], list(refs[len(pieces) :])
    for part_ref, count in zip(parts, pieces):
        project(attended_ref, part_ref, shares[:count])
        shares = shares[count:]


def project_parts(attended, parts, outs):
    flat = [out for group in outs for out in group]
    return pl.pallas_call(
        functools.partial(project_kernel, [len(group) for group in outs]),
        out_shape=flat,
        in_specs=[VMEM] * (1 + len(parts)),
        out_specs=[VMEM] * len(flat),
        compiler_params=PARAMS,
        cost_estimate=SHORT,
        name="project_parts",
    )(attended, *parts)


def next_to(ctx, head):
    return (ctx + 1 + 2 * (head & 1)) & 3, head


def two_away(ctx, head):
    return (ctx ^ 2 if (ctx ^ head) & 1 == 0 else ctx), head


def other_core(ctx, head):
    return ctx, head ^ 1


def other_chip(ctx, head):
    return ctx, head ^ 2


def shards(queries, latent, w_keys, w_values, w_out, block_order, valid_lengths):
    ctx_count = lax.axis_size("ctx")
    rows = queries.shape[0]
    width = w_out.shape[1] // PARTS
    block = latent.T
    prepared = prepare(block_order, valid_lengths, queries, w_keys, w_values, w_out)
    narrow, wide = jnp.bfloat16, jnp.float32

    if not is_paired():
        blocks = [block]
        for step in range(1, ctx_count):
            blocks.append(routed(block, lambda ctx, head: ((ctx + step) % ctx_count, head)))
        folded, bias, values, *parts = prepared
        attended, share = attend(folded, bias, values, parts[0], blocks, [width])
        outs = [share_shapes(rows, [width], narrow)] * (PARTS - 1)
        shares = [share] + list(project_parts(attended, parts[1:], outs))
        whole = jnp.concatenate(shares, axis=1)
        return lax.psum_scatter(whole, "head", scatter_dimension=1, tiled=True)

    widths = [FIRST_PIECE, width - FIRST_PIECE]
    near = routed(block, next_to)
    far = routed(block, two_away)
    near, prepared = lax.optimization_barrier((near, prepared))
    near_swapped = routed(near, other_core)
    far, near_swapped = lax.optimization_barrier((far, near_swapped))
    far_swapped = routed(far, other_core)
    folded, bias, values, *parts = prepared
    blocks = [block, near, near_swapped, far, far_swapped]

    attended, *across = attend(folded, bias, values, parts[0], blocks, widths)
    received = [routed(piece, other_core) for piece in across]
    sums = project_parts(attended, parts[1:2], [share_shapes(rows, widths, wide)])
    sums = [(mine + other.astype(wide)).astype(narrow) for mine, other in zip(sums, received)]
    first = routed(sums[0], other_chip)
    attended, sums[1] = lax.optimization_barrier((attended, sums[1]))
    second = routed(sums[1], other_chip)
    outs = [share_shapes(rows, [width], narrow), share_shapes(rows, [width], wide)]
    beside, own = project_parts(attended, parts[2:], outs)
    beside, first = lax.optimization_barrier((beside, first))
    beside = routed(beside, other_core)
    other = jnp.concatenate([first, second], axis=1)
    return (own + beside.astype(wide) + other.astype(wide)).astype(narrow)


def solution(mesh):
    in_specs = (
        P(("groups", "ctx"), "head"),
        P(("groups", "ctx"), None),
        P(None, "head"),
        P(None, "head"),
        P("head", None),
        P("groups"),
        P("groups"),
    )
    out_specs = P(("groups", "ctx"), "head")
    return jax.shard_map(shards, mesh=mesh, in_specs=in_specs, out_specs=out_specs, check_vma=False)
```

time: 28.9 us -> 30.7 us (1.062)
  waiting for transfers between devices: 6.52 us -> 10 us
  Pallas kernels: 9.99 us -> 8.34 us
    ppermute x10 -> x9, waiting for transfers between devices: 6.52 us -> 10 us  [routed(): return lax.ppermute(value, ('ctx', 'head'), pairs)]
    pallas_call x4 -> x3, Pallas kernels: 6 us -> 4.35 us  [the longest x1 3.19 us: attend(): pl.pallas_call(functools.partial(attend_kernel, len(blocks), is_paired())...]
    concatenate x1 -> x0, other arithmetic: 0.71 us -> none  [shards(): return jnp.concatenate(halves, axis=0)]
    convert_element_type x4 -> x3, other arithmetic: 0.13 us -> 0.82 us  [the longest x1 0.77 us: shards(): return (own + beside.astype(wide) + other.astype(wide)).astype(narrow)]
    ppermute x10 -> x9, starting transfers between devices: 11.3 us -> 11.3 us  [routed(): return lax.ppermute(value, ('ctx', 'head'), pairs)]
  transfers between devices with their start and end apart: 10 -> 9, of which waited for: 5 -> 6; matrix products, arithmetic and copies ran while one was open for 0% -> 0% of each run, Pallas kernels for 21% -> 17%
where the time goes in v6:
time: 30.7 us; the launch traced here: 30.6 us
  starting transfers between devices  11.3 us (37%)
  waiting for transfers between devices  10 us (33%)
  Pallas kernels  8.34 us (27%)
  other arithmetic  0.82 us (3%)
    ppermute x9, starting transfers between devices, routed(): return lax.ppermute(value, ('ctx', 'head'), pairs)  11.3 us
    ppermute x9, waiting for transfers between devices, routed(): return lax.ppermute(value, ('ctx', 'head'), pairs)  10 us
    pallas_call x1, Pallas kernels, prepare(): pl.pallas_call(functools.partial(prepare_kernel, rows // 2), out_shape=[j...  3.99 us
    pallas_call x1, Pallas kernels, attend(): pl.pallas_call(functools.partial(attend_kernel, len(blocks), is_paired())...  3.19 us
    pallas_call x2, Pallas kernels, project_parts(): pl.pallas_call(functools.partial(project_kernel, [len(group) for group in...  1.16 us
    convert_element_type x1, other arithmetic, shards(): return (own + beside.astype(wide) + other.astype(wide)).astype(narrow)  0.77 us
  transfers between devices with their start and end apart: 9, of which 6 were waited for; matrix products, arithmetic and copies ran while one was open for 0% of the time, Pallas kernels for 17%

profile of v6, /device:TPU:0, one launch (start us, length us, event | category | flops | bytes accessed | tf_op | source)
XLA Modules:
  0.0 30.6 jit_solution(12966153441359350252)
XLA Ops:
  0.0 0.0 copy-start
  0.0 3.0 %collective-permute-start = (bf16[576,128]{1,0:T(8,128)(2,1)}, bf16[576,128]{1,0:T(8,128)(2,1)S(1)}, u32[]{:S(2)}, u32[]{:S(2)}) collective-permute-start(bf16[576,128]{1,0:T(8,128)(2,1)} %bitcast.1), channel_id=1, source_target_pairs={{0,4},{1,13},{2,6},{3,15},{4,8},{5,1},{6,10},{7,3},{8,12},{9,5},{1... | collective-permute-start | bytes 442376 | tf_op jit(solution)/shard_map/ppermute | solution.py:30
  3.0 4.5 %collective-permute-start.1 = (bf16[576,128]{1,0:T(8,128)(2,1)}, bf16[576,128]{1,0:T(8,128)(2,1)S(1)}, u32[]{:S(2)}, u32[]{:S(2)}) collective-permute-start(bf16[576,128]{1,0:T(8,128)(2,1)} %bitcast.2), channel_id=1, source_target_pairs={{0,8},{1,1},{2,10},{3,3},{4,4},{5,13},{6,6},{7,15},{8,0},{9,9},{10... | collective-permute-start | bytes 442376 | tf_op jit(solution)/shard_map/ppermute | solution.py:30
  7.5 4.0 %prepare.1 = (bf16[1024,576]{1,0:T(8,128)(2,1)S(1)}, f32[128,512]{1,0:T(8,128)S(1)}, bf16[512,1024]{1,0:T(8,128)(2,1)S(1)}, bf16[1024,896]{1,0:T(8,128)(2,1)S(1)...) custom-call(s32[8]{0:T(128)} %refs_0_.1, s32[8]{0:T(128)} %refs_1_.1, ...), custom_call_target="tpu_custom_call" | custom-call | flops 134217728 | bytes 9830400 | tf_op jit(solution)/shard_map/prepare/pallas_call | solution.py:118
  11.5 0.0 collective-permute-done.rest_1_
  11.5 0.1 collective-permute-start.2
  11.6 0.8 %collective-permute-done.1.rest_3_ = bf16[576,128]{1,0:T(8,128)(2,1)S(1)} collective-permute-done((bf16[576,128]{1,0:T(8,128)(2,1)}, bf16[576,128]{1,0:T(8,128)(2,1)S(1)}, u32[]{:S(2)}, u32[]{:S(2)}) %collective-permute-start.1) | collective-permute-done | bytes 147488 | tf_op jit(solution)/shard_map/ppermute | solution.py:30
  12.4 0.5 %collective-permute-done.2.rest_2_ = bf16[576,128]{1,0:T(8,128)(2,1)S(1)} collective-permute-done((bf16[576,128]{1,0:T(8,128)(2,1)S(1)}, bf16[576,128]{1,0:T(8,128)(2,1)S(1)}, u32[]{:S(2)}, u32[]{:S(2)}) %collective-permute-start.2) | collective-permute-done | bytes 147488 | tf_op jit(solution)/shard_map/ppermute | solution.py:30
  13.0 0.1 collective-permute-start.3
  13.1 1.2 %collective-permute-done.3.rest_4_ = bf16[576,128]{1,0:T(8,128)(2,1)S(1)} collective-permute-done((bf16[576,128]{1,0:T(8,128)(2,1)S(1)}, bf16[576,128]{1,0:T(8,128)(2,1)S(1)}, u32[]{:S(2)}, u32[]{:S(2)}) %collective-permute-start.3) | collective-permute-done | bytes 147488 | tf_op jit(solution)/shard_map/ppermute | solution.py:30
  14.3 0.0 copy-done
  14.3 3.2 %attend.1 = (bf16[128,1024]{1,0:T(8,128)(2,1)S(1)}, bf16[128,512]{1,0:T(8,128)(2,1)S(1)}, bf16[128,384]{1,0:T(8,128)(2,1)S(1)}) custom-call(bf16[1024,576]{1,0:T(8,128)(2,1)S(1)} %get-tuple-element.40.folded_ref, f32[128,512]{1,0:T(8,128)S(1)} %get-tuple-element.41.bias_ref, bf16[512,1024]{1,0:T(8,128)(2,1)S(1)} %get-tuple-element.42.values_ref, ...), custom_call_target="tpu_custom_call" | custom-call | flops 1509949440 | bytes 4063232 | tf_op jit(solution)/shard_map/attend/pallas_call | solution.py:206
  17.5 0.2 collective-permute-start.5
  17.7 0.4 %collective-permute-start.4 = (bf16[128,384]{1,0:T(8,128)(2,1)S(1)}, bf16[128,384]{1,0:T(8,128)(2,1)S(1)}, u32[]{:S(2)}, u32[]{:S(2)}) collective-permute-start(bf16[128,384]{1,0:T(8,128)(2,1)S(1)} %get-tuple-element.50), channel_id=1, source_target_pairs={{0,1},{1,0},{2,3},{3,2},{4,5},{5,4},{6,7},{7,6},{8,9},{9,8},{10,11... | collective-permute-start | bytes 294920 | tf_op jit(solution)/shard_map/ppermute | solution.py:30
  18.1 0.4 %project_parts.2 = (f32[128,512]{1,0:T(8,128)S(1)}, f32[128,384]{1,0:T(8,128)S(1)}) custom-call(bf16[128,1024]{1,0:T(8,128)(2,1)S(1)} %get-tuple-element.51.attended_ref, bf16[1024,896]{1,0:T(8,128)(2,1)S(1)} %get-tuple-element.48.refs_0_), custom_call_target="tpu_custom_call" | custom-call | flops 1024 | bytes 1024 | tf_op jit(solution)/shard_map/project_parts/pallas_call | solution.py:231
  18.6 0.4 %collective-permute-done.5 = bf16[128,512]{1,0:T(8,128)(2,1)S(1)} collective-permute-done((bf16[128,512]{1,0:T(8,128)(2,1)S(1)}, bf16[128,512]{1,0:T(8,128)(2,1)S(1)}, u32[]{:S(2)}, u32[]{:S(2)}) %collective-permute-start.5) | collective-permute-done | bytes 131104 | tf_op jit(solution)/shard_map/ppermute | solution.py:30
  19.0 1.6 %collective-permute-start.6 = (bf16[128,512]{1,0:T(8,128)(2,1)S(1)}, bf16[128,512]{1,0:T(8,128)(2,1)S(1)}, u32[]{:S(2)}, u32[]{:S(2)}) collective-permute-start(bf16[128,512]{1,0:T(8,128)(2,1)S(1)} %add_convert_fusion.1), channel_id=1, source_target_pairs={{0,2},{1,3},{2,0},{3,1},{4,6},{5,7},{6,4},{7,5},{8,10},{9,11},{10,... | collective-permute-start | bytes 393224 | tf_op jit(solution)/shard_map/ppermute | solution.py:30
  20.5 0.0 collective-permute-done.4
  20.6 0.7 %project_parts.3 = (bf16[128,896]{1,0:T(8,128)(2,1)S(1)}, f32[128,896]{1,0:T(8,128)S(1)}) custom-call(bf16[128,1024]{1,0:T(8,128)(2,1)S(1)} %get-tuple-element.51.attended_ref, bf16[1024,896]{1,0:T(8,128)(2,1)S(1)} %get-tuple-element.52.refs_0_, bf16[1024,896]{1,0:T(8,128)(2,1)S(1)} %get-tuple-element.53.refs_1_), custom_call_target="tpu_custom_call" | custom-call | flops 1024 | bytes 1024 | tf_op jit(solution)/shard_map/project_parts/pallas_call | solution.py:231
  21.3 3.3 %collective-permute-done.6 = bf16[128,512]{1,0:T(8,128)(2,1)S(1)} collective-permute-done((bf16[128,512]{1,0:T(8,128)(2,1)S(1)}, bf16[128,512]{1,0:T(8,128)(2,1)S(1)}, u32[]{:S(2)}, u32[]{:S(2)}) %collective-permute-start.6) | collective-permute-done | bytes 131104 | tf_op jit(solution)/shard_map/ppermute | solution.py:30
  24.6 0.0 collective-permute-start.7
  24.6 1.5 %collective-permute-start.8 = (bf16[128,384]{1,0:T(8,128)(2,1)S(1)}, bf16[128,384]{1,0:T(8,128)(2,1)S(1)}, u32[]{:S(2)}, u32[]{:S(2)}) collective-permute-start(bf16[128,384]{1,0:T(8,128)(2,1)S(1)} %add_convert_fusion.2), channel_id=1, source_target_pairs={{0,2},{1,3},{2,0},{3,1},{4,6},{5,7},{6,4},{7,5},{8,10},{9,11},{10,... | collective-permute-start | bytes 294920 | tf_op jit(solution)/shard_map/ppermute | solution.py:30
  26.1 3.7 %collective-permute-done.8 = bf16[128,384]{1,0:T(8,128)(2,1)S(1)} collective-permute-done((bf16[128,384]{1,0:T(8,128)(2,1)S(1)}, bf16[128,384]{1,0:T(8,128)(2,1)S(1)}, u32[]{:S(2)}, u32[]{:S(2)}) %collective-permute-start.8) | collective-permute-done | bytes 98336 | tf_op jit(solution)/shard_map/ppermute | solution.py:30
  29.8 0.0 collective-permute-done.7
  29.8 0.8 %add_convert_fusion = bf16[128,896]{1,0:T(8,128)(2,1)} fusion(f32[128,896]{1,0:T(8,128)S(1)} %get-tuple-element.54, bf16[128,896]{1,0:T(8,128)(2,1)S(1)} %collective-permute-done.7, bf16[128,384]{1,0:T(8,128)(2,1)S(1)} %collective-permute-done.8, bf16[128,512]{1,0:T(8,128)(2,1)S(1)} %collective-permute-done.6), kind=kLoop, calls=%fused_computation | loop fusion | flops 917504 | bytes 1146880 | tf_op jit(solution)/shard_map/convert_element_type | solution.py:299
  (2 shorter events, 0.0 us)
Async XLA Ops:
  0.0 14.3 %copy-start = (bf16[128,576]{0,1:T(8,128)(2,1)S(1)}, bf16[128,576]{0,1:T(8,128)(2,1)}, u32[]{:S(2)}) copy-start(bf16[128,576]{0,1:T(8,128)(2,1)} %param.8) | copy-start | bytes 442372
  0.0 11.5 %collective-permute-start = (bf16[576,128]{1,0:T(8,128)(2,1)}, bf16[576,128]{1,0:T(8,128)(2,1)S(1)}, u32[]{:S(2)}, u32[]{:S(2)}) collective-permute-start(bf16[576,128]{1,0:T(8,128)(2,1)} %bitcast.1), channel_id=1, source_target_pairs={{0,4},{1,13},{2,6},{3,15},{4,8},{5,1},{6,10},{7,3},{8,12},{9,5},{1... | collective-permute-start | bytes 442376 | tf_op jit(solution)/shard_map/ppermute | solution.py:30
  3.0 9.4 %collective-permute-start.1 = (bf16[576,128]{1,0:T(8,128)(2,1)}, bf16[576,128]{1,0:T(8,128)(2,1)S(1)}, u32[]{:S(2)}, u32[]{:S(2)}) collective-permute-start(bf16[576,128]{1,0:T(8,128)(2,1)} %bitcast.2), channel_id=1, source_target_pairs={{0,8},{1,1},{2,10},{3,3},{4,4},{5,13},{6,6},{7,15},{8,0},{9,9},{10... | collective-permute-start | bytes 442376 | tf_op jit(solution)/shard_map/ppermute | solution.py:30
  11.5 1.4 %collective-permute-start.2 = (bf16[576,128]{1,0:T(8,128)(2,1)S(1)}, bf16[576,128]{1,0:T(8,128)(2,1)S(1)}, u32[]{:S(2)}, u32[]{:S(2)}) collective-permute-start(bf16[576,128]{1,0:T(8,128)(2,1)S(1)} %collective-permute-done.rest_1_), channel_id=1, source_target_pairs={{0,1},{1,0},{2,3},{3,2},{4,5},{5,4},{6,7},{7,6},{8,9},{9,8},{10,11... | collective-permute-start | bytes 442376 | tf_op jit(solution)/shard_map/ppermute | solution.py:30
  13.0 1.4 %collective-permute-start.3 = (bf16[576,128]{1,0:T(8,128)(2,1)S(1)}, bf16[576,128]{1,0:T(8,128)(2,1)S(1)}, u32[]{:S(2)}, u32[]{:S(2)}) collective-permute-start(bf16[576,128]{1,0:T(8,128)(2,1)S(1)} %collective-permute-done.1.rest_3_), channel_id=1, source_target_pairs={{0,1},{1,0},{2,3},{3,2},{4,5},{5,4},{6,7},{7,6},{8,9},{9,8},{10,11... | collective-permute-start | bytes 442376 | tf_op jit(solution)/shard_map/ppermute | solution.py:30
  17.5 1.4 %collective-permute-start.5 = (bf16[128,512]{1,0:T(8,128)(2,1)S(1)}, bf16[128,512]{1,0:T(8,128)(2,1)S(1)}, u32[]{:S(2)}, u32[]{:S(2)}) collective-permute-start(bf16[128,512]{1,0:T(8,128)(2,1)S(1)} %get-tuple-element.57), channel_id=1, source_target_pairs={{0,1},{1,0},{2,3},{3,2},{4,5},{5,4},{6,7},{7,6},{8,9},{9,8},{10,11... | collective-permute-start | bytes 393224 | tf_op jit(solution)/shard_map/ppermute | solution.py:30
  17.7 2.8 %collective-permute-start.4 = (bf16[128,384]{1,0:T(8,128)(2,1)S(1)}, bf16[128,384]{1,0:T(8,128)(2,1)S(1)}, u32[]{:S(2)}, u32[]{:S(2)}) collective-permute-start(bf16[128,384]{1,0:T(8,128)(2,1)S(1)} %get-tuple-element.50), channel_id=1, source_target_pairs={{0,1},{1,0},{2,3},{3,2},{4,5},{5,4},{6,7},{7,6},{8,9},{9,8},{10,11... | collective-permute-start | bytes 294920 | tf_op jit(solution)/shard_map/ppermute | solution.py:30
  19.0 5.6 %collective-permute-start.6 = (bf16[128,512]{1,0:T(8,128)(2,1)S(1)}, bf16[128,512]{1,0:T(8,128)(2,1)S(1)}, u32[]{:S(2)}, u32[]{:S(2)}) collective-permute-start(bf16[128,512]{1,0:T(8,128)(2,1)S(1)} %add_convert_fusion.1), channel_id=1, source_target_pairs={{0,2},{1,3},{2,0},{3,1},{4,6},{5,7},{6,4},{7,5},{8,10},{9,11},{10,... | collective-permute-start | bytes 393224 | tf_op jit(solution)/shard_map/ppermute | solution.py:30
  24.6 5.2 %collective-permute-start.7 = (bf16[128,896]{1,0:T(8,128)(2,1)S(1)}, bf16[128,896]{1,0:T(8,128)(2,1)S(1)}, u32[]{:S(2)}, u32[]{:S(2)}) collective-permute-start(bf16[128,896]{1,0:T(8,128)(2,1)S(1)} %get-tuple-element.58), channel_id=1, source_target_pairs={{0,1},{1,0},{2,3},{3,2},{4,5},{5,4},{6,7},{7,6},{8,9},{9,8},{10,11... | collective-permute-start | bytes 688136 | tf_op jit(solution)/shard_map/ppermute | solution.py:30
  24.6 5.2 %collective-permute-start.8 = (bf16[128,384]{1,0:T(8,128)(2,1)S(1)}, bf16[128,384]{1,0:T(8,128)(2,1)S(1)}, u32[]{:S(2)}, u32[]{:S(2)}) collective-permute-start(bf16[128,384]{1,0:T(8,128)(2,1)S(1)} %add_convert_fusion.2), channel_id=1, source_target_pairs={{0,2},{1,3},{2,0},{3,1},{4,6},{5,7},{6,4},{7,5},{8,10},{9,11},{10,... | collective-permute-start | bytes 294920 | tf_op jit(solution)/shard_map/ppermute | solution.py:30

commit v7 on v6

--- a/solution.py
+++ b/solution.py
@@ -52,7 +52,6 @@
 
 VMEM = pl.BlockSpec(memory_space=pltpu.VMEM)
 HBM = pl.BlockSpec(memory_space=pltpu.HBM)
-FIRST_PIECE = 512
 PARAMS = pltpu.CompilerParams(vmem_limit_bytes=VMEM_BYTES)
 SHORT = pl.CostEstimate(flops=1024, bytes_accessed=1024, transcendentals=0)
 EXPONENT = QUERY**-0.5 * 1.4426950408889634
@@ -162,7 +161,7 @@
 
 
 def attend_kernel(count, paired, folded_ref, bias_ref, values_ref, part_ref, *rest):
-    blocks, (attended_ref, *shares, keys_ref) = rest[:count], rest[count:]
+    blocks, (attended_ref, *shares, keys_ref, latents_ref) = rest[:count], rest[count:]
     rows = bias_ref.shape[0]
     heads = values_ref.shape[1] // HEAD_DIM
     certain = count - 2 if paired else count
@@ -172,6 +171,9 @@
         direct = (lax.axis_index("ctx") ^ lax.axis_index("head")) & 1 == 0
         place_if(keys_ref, certain, blocks[certain], direct)
         place_if(keys_ref, certain, blocks[certain + 1], jnp.logical_not(direct))
+    for slot in range(keys_ref.shape[1] // rows):
+        here = slice(slot * rows, (slot + 1) * rows)
+        latents_ref[here, :] = keys_ref[:LATENT, here].T
     stacked = ROWS_AT_ONCE // rows
     bias = jnp.concatenate([bias_ref[...]] * stacked, axis=0)
     for group in range(heads // stacked):
@@ -181,8 +183,8 @@
         peak = jnp.max(scores, axis=1, keepdims=True)
         weights = jnp.exp2((scores - peak) * jnp.float32(EXPONENT))
         inverse = 1.0 / jnp.sum(weights, axis=1, keepdims=True)
-        mixed = lax.dot_general(
-            weights.astype(jnp.bfloat16), keys_ref[:LATENT, :], NT, preferred_element_type=jnp.float32
+        mixed = jnp.dot(
+            weights.astype(jnp.bfloat16), latents_ref[...], preferred_element_type=jnp.float32
         ).astype(jnp.bfloat16)
         for inner in range(stacked):
             head = group * stacked + inner
@@ -208,7 +210,10 @@
         out_shape=share_shapes(rows, [values.shape[1]] + widths, jnp.bfloat16),
         in_specs=[VMEM] * (4 + len(blocks)),
         out_specs=[VMEM] * (1 + len(widths)),
-        scratch_shapes=[pltpu.VMEM((LATENT + ROPE, keys), jnp.bfloat16)],
+        scratch_shapes=[
+            pltpu.VMEM((LATENT + ROPE, keys), jnp.bfloat16),
+            pltpu.VMEM((keys, LATENT), jnp.bfloat16),
+        ],
         compiler_params=PARAMS,
         cost_estimate=pl.CostEstimate(
             flops=flops + 2 * rows * part.size,
@@ -274,7 +279,6 @@
         whole = jnp.concatenate(shares, axis=1)
         return lax.psum_scatter(whole, "head", scatter_dimension=1, tiled=True)
 
-    widths = [FIRST_PIECE, width - FIRST_PIECE]
     near = routed(block, next_to)
     far = routed(block, two_away)
     near, prepared = lax.optimization_barrier((near, prepared))
@@ -284,19 +288,15 @@
     folded, bias, values, *parts = prepared
     blocks = [block, near, near_swapped, far, far_swapped]
 
-    attended, *across = attend(folded, bias, values, parts[0], blocks, widths)
-    received = [routed(piece, other_core) for piece in across]
-    sums = project_parts(attended, parts[1:2], [share_shapes(rows, widths, wide)])
-    sums = [(mine + other.astype(wide)).astype(narrow) for mine, other in zip(sums, received)]
-    first = routed(sums[0], other_chip)
-    attended, sums[1] = lax.optimization_barrier((attended, sums[1]))
-    second = routed(sums[1], other_chip)
-    outs = [share_shapes(rows, [width], narrow), share_shapes(rows, [width], wide)]
-    beside, own = project_parts(attended, parts[2:], outs)
-    beside, first = lax.optimization_barrier((beside, first))
-    beside = routed(beside, other_core)
-    other = jnp.concatenate([first, second], axis=1)
-    return (own + beside.astype(wide) + other.astype(wide)).astype(narrow)
+    attended, across = attend(folded, bias, values, parts[0], blocks, [width])
+    received = routed(across, other_core)
+    outs = [share_shapes(rows, [width], kind) for kind in (wide, narrow, wide)]
+    far_part, beside, own = project_parts(attended, parts[1:], outs)
+    far_part = (far_part + received.astype(wide)).astype(narrow)
+    far_part, beside = lax.optimization_barrier((far_part, beside))
+    far_part = routed(far_part, other_chip).astype(wide)
+    beside = routed(beside, other_core).astype(wide)
+    return (own + beside + far_part).astype(narrow)
 
 
 def solution(mesh):

time: 30.7 us -> 28.2 us (0.919)
  starting transfers between devices: 11.3 us -> 9.69 us
  waiting for transfers between devices: 10 us -> 9.26 us
    ppermute x9 -> x7, starting transfers between devices: 11.3 us -> 9.69 us  [routed(): return lax.ppermute(value, ('ctx', 'head'), pairs)]
    ppermute x9 -> x7, waiting for transfers between devices: 10 us -> 9.26 us  [routed(): return lax.ppermute(value, ('ctx', 'head'), pairs)]
    pallas_call x2 -> x1, Pallas kernels: 1.16 us -> 0.99 us  [project_parts(): pl.pallas_call(functools.partial(project_kernel, [len(group) for group in...]
    convert_element_type x3 -> x2, other arithmetic: 0.82 us -> 0.82 us  [the longest x1 0.77 us: shards(): return (own + beside + far_part).astype(narrow)]
  transfers between devices with their start and end apart: 9 -> 7, of which waited for: 6 -> 5; matrix products, arithmetic and copies ran while one was open for 0% -> 0% of each run, Pallas kernels for 17% -> 18%
where the time goes in v7:
time: 28.2 us; the launch traced here: 28.1 us
  starting transfers between devices  9.69 us (34%)
  waiting for transfers between devices  9.26 us (33%)
  Pallas kernels  8.23 us (29%)
  other arithmetic  0.82 us (3%)
    ppermute x7, starting transfers between devices, routed(): return lax.ppermute(value, ('ctx', 'head'), pairs)  9.69 us
    ppermute x7, waiting for transfers between devices, routed(): return lax.ppermute(value, ('ctx', 'head'), pairs)  9.26 us
    pallas_call x1, Pallas kernels, prepare(): pl.pallas_call(functools.partial(prepare_kernel, rows // 2), out_shape=[j...  3.99 us
    pallas_call x1, Pallas kernels, attend(): pl.pallas_call(functools.partial(attend_kernel, len(blocks), is_paired())...  3.26 us
    pallas_call x1, Pallas kernels, project_parts(): pl.pallas_call(functools.partial(project_kernel, [len(group) for group in...  0.99 us
    convert_element_type x1, other arithmetic, shards(): return (own + beside + far_part).astype(narrow)  0.77 us
  transfers between devices with their start and end apart: 7, of which 5 were waited for; matrix products, arithmetic and copies ran while one was open for 0% of the time, Pallas kernels for 18%

profile of v7, /device:TPU:0, one launch (start us, length us, event | category | flops | bytes accessed | tf_op | source)
XLA Modules:
  0.0 28.1 jit_solution(1778684616267935338)
XLA Ops:
  0.0 0.0 copy-start
  0.0 3.0 %collective-permute-start = (bf16[576,128]{1,0:T(8,128)(2,1)}, bf16[576,128]{1,0:T(8,128)(2,1)S(1)}, u32[]{:S(2)}, u32[]{:S(2)}) collective-permute-start(bf16[576,128]{1,0:T(8,128)(2,1)} %bitcast.1), channel_id=1, source_target_pairs={{0,4},{1,13},{2,6},{3,15},{4,8},{5,1},{6,10},{7,3},{8,12},{9,5},{1... | collective-permute-start | bytes 442376 | tf_op jit(solution)/shard_map/ppermute | solution.py:30
  3.0 4.5 %collective-permute-start.1 = (bf16[576,128]{1,0:T(8,128)(2,1)}, bf16[576,128]{1,0:T(8,128)(2,1)S(1)}, u32[]{:S(2)}, u32[]{:S(2)}) collective-permute-start(bf16[576,128]{1,0:T(8,128)(2,1)} %bitcast.2), channel_id=1, source_target_pairs={{0,8},{1,1},{2,10},{3,3},{4,4},{5,13},{6,6},{7,15},{8,0},{9,9},{10... | collective-permute-start | bytes 442376 | tf_op jit(solution)/shard_map/ppermute | solution.py:30
  7.5 4.0 %prepare.1 = (bf16[1024,576]{1,0:T(8,128)(2,1)S(1)}, f32[128,512]{1,0:T(8,128)S(1)}, bf16[512,1024]{1,0:T(8,128)(2,1)S(1)}, bf16[1024,896]{1,0:T(8,128)(2,1)S(1)...) custom-call(s32[8]{0:T(128)} %refs_0_.1, s32[8]{0:T(128)} %refs_1_.1, ...), custom_call_target="tpu_custom_call" | custom-call | flops 134217728 | bytes 9830400 | tf_op jit(solution)/shard_map/prepare/pallas_call | solution.py:117
  11.5 0.0 collective-permute-done.rest_1_
  11.5 0.1 collective-permute-start.2
  11.6 0.8 %collective-permute-done.1.rest_3_ = bf16[576,128]{1,0:T(8,128)(2,1)S(1)} collective-permute-done((bf16[576,128]{1,0:T(8,128)(2,1)}, bf16[576,128]{1,0:T(8,128)(2,1)S(1)}, u32[]{:S(2)}, u32[]{:S(2)}) %collective-permute-start.1) | collective-permute-done | bytes 147488 | tf_op jit(solution)/shard_map/ppermute | solution.py:30
  12.4 0.5 %collective-permute-done.2.rest_2_ = bf16[576,128]{1,0:T(8,128)(2,1)S(1)} collective-permute-done((bf16[576,128]{1,0:T(8,128)(2,1)S(1)}, bf16[576,128]{1,0:T(8,128)(2,1)S(1)}, u32[]{:S(2)}, u32[]{:S(2)}) %collective-permute-start.2) | collective-permute-done | bytes 147488 | tf_op jit(solution)/shard_map/ppermute | solution.py:30
  13.0 0.1 collective-permute-start.3
  13.1 1.2 %collective-permute-done.3.rest_4_ = bf16[576,128]{1,0:T(8,128)(2,1)S(1)} collective-permute-done((bf16[576,128]{1,0:T(8,128)(2,1)S(1)}, bf16[576,128]{1,0:T(8,128)(2,1)S(1)}, u32[]{:S(2)}, u32[]{:S(2)}) %collective-permute-start.3) | collective-permute-done | bytes 147488 | tf_op jit(solution)/shard_map/ppermute | solution.py:30
  14.3 0.0 copy-done
  14.3 3.3 %attend.1 = (bf16[128,1024]{1,0:T(8,128)(2,1)S(1)}, bf16[128,896]{1,0:T(8,128)(2,1)S(1)}) custom-call(bf16[1024,576]{1,0:T(8,128)(2,1)S(1)} %get-tuple-element.36.folded_ref, f32[128,512]{1,0:T(8,128)S(1)} %get-tuple-element.37.bias_ref, bf16[512,1024]{1,0:T(8,128)(2,1)S(1)} %get-tuple-element.38.values_ref, ...), custom_call_target="tpu_custom_call" | custom-call | flops 1509949440 | bytes 4063232 | tf_op jit(solution)/shard_map/attend/pallas_call | solution.py:208
  17.6 0.2 collective-permute-start.4
  17.8 1.0 %project_parts.1 = (f32[128,896]{1,0:T(8,128)S(1)}, bf16[128,896]{1,0:T(8,128)(2,1)S(1)}, f32[128,896]{1,0:T(8,128)S(1)}) custom-call(bf16[128,1024]{1,0:T(8,128)(2,1)S(1)} %get-tuple-element.43.attended_ref, bf16[1024,896]{1,0:T(8,128)(2,1)S(1)} %get-tuple-element.44.refs_0_, bf16[1024,896]{1,0:T(8,128)(2,1)S(1)} %get-tuple-element.45.refs_1_, ...), custom_call_target="tpu_custom_call" | custom-call | flops 1024 | bytes 1024 | tf_op jit(solution)/shard_map/project_parts/pallas_call | solution.py:236
  18.8 0.3 %collective-permute-done.4 = bf16[128,896]{1,0:T(8,128)(2,1)S(1)} collective-permute-done((bf16[128,896]{1,0:T(8,128)(2,1)S(1)}, bf16[128,896]{1,0:T(8,128)(2,1)S(1)}, u32[]{:S(2)}, u32[]{:S(2)}) %collective-permute-start.4) | collective-permute-done | bytes 229408 | tf_op jit(solution)/shard_map/ppermute | solution.py:30
  19.2 0.2 collective-permute-start.5
  19.4 1.5 %collective-permute-start.6 = (bf16[128,896]{1,0:T(8,128)(2,1)S(1)}, bf16[128,896]{1,0:T(8,128)(2,1)S(1)}, u32[]{:S(2)}, u32[]{:S(2)}) collective-permute-start(bf16[128,896]{1,0:T(8,128)(2,1)S(1)} %add_convert_fusion.1), channel_id=1, source_target_pairs={{0,2},{1,3},{2,0},{3,1},{4,6},{5,7},{6,4},{7,5},{8,10},{9,11},{10,... | collective-permute-start | bytes 688136 | tf_op jit(solution)/shard_map/ppermute | solution.py:30
  20.9 0.0 collective-permute-done.5
  20.9 6.3 %collective-permute-done.6 = bf16[128,896]{1,0:T(8,128)(2,1)S(1)} collective-permute-done((bf16[128,896]{1,0:T(8,128)(2,1)S(1)}, bf16[128,896]{1,0:T(8,128)(2,1)S(1)}, u32[]{:S(2)}, u32[]{:S(2)}) %collective-permute-start.6) | collective-permute-done | bytes 229408 | tf_op jit(solution)/shard_map/ppermute | solution.py:30
  27.3 0.8 %add_convert_fusion = bf16[128,896]{1,0:T(8,128)(2,1)} fusion(bf16[128,896]{1,0:T(8,128)(2,1)S(1)} %collective-permute-done.6, f32[128,896]{1,0:T(8,128)S(1)} %get-tuple-element.47, bf16[128,896]{1,0:T(8,128)(2,1)S(1)} %collective-permute-done.5), kind=kLoop, calls=%fused_computation | loop fusion | flops 573440 | bytes 1146880 | tf_op jit(solution)/shard_map/convert_element_type | solution.py:299
  (1 shorter events, 0.0 us)
Async XLA Ops:
  0.0 14.3 %copy-start = (bf16[128,576]{0,1:T(8,128)(2,1)S(1)}, bf16[128,576]{0,1:T(8,128)(2,1)}, u32[]{:S(2)}) copy-start(bf16[128,576]{0,1:T(8,128)(2,1)} %param.8) | copy-start | bytes 442372
  0.0 11.5 %collective-permute-start = (bf16[576,128]{1,0:T(8,128)(2,1)}, bf16[576,128]{1,0:T(8,128)(2,1)S(1)}, u32[]{:S(2)}, u32[]{:S(2)}) collective-permute-start(bf16[576,128]{1,0:T(8,128)(2,1)} %bitcast.1), channel_id=1, source_target_pairs={{0,4},{1,13},{2,6},{3,15},{4,8},{5,1},{6,10},{7,3},{8,12},{9,5},{1... | collective-permute-start | bytes 442376 | tf_op jit(solution)/shard_map/ppermute | solution.py:30
  3.0 9.4 %collective-permute-start.1 = (bf16[576,128]{1,0:T(8,128)(2,1)}, bf16[576,128]{1,0:T(8,128)(2,1)S(1)}, u32[]{:S(2)}, u32[]{:S(2)}) collective-permute-start(bf16[576,128]{1,0:T(8,128)(2,1)} %bitcast.2), channel_id=1, source_target_pairs={{0,8},{1,1},{2,10},{3,3},{4,4},{5,13},{6,6},{7,15},{8,0},{9,9},{10... | collective-permute-start | bytes 442376 | tf_op jit(solution)/shard_map/ppermute | solution.py:30
  11.5 1.4 %collective-permute-start.2 = (bf16[576,128]{1,0:T(8,128)(2,1)S(1)}, bf16[576,128]{1,0:T(8,128)(2,1)S(1)}, u32[]{:S(2)}, u32[]{:S(2)}) collective-permute-start(bf16[576,128]{1,0:T(8,128)(2,1)S(1)} %collective-permute-done.rest_1_), channel_id=1, source_target_pairs={{0,1},{1,0},{2,3},{3,2},{4,5},{5,4},{6,7},{7,6},{8,9},{9,8},{10,11... | collective-permute-start | bytes 442376 | tf_op jit(solution)/shard_map/ppermute | solution.py:30
  13.0 1.4 %collective-permute-start.3 = (bf16[576,128]{1,0:T(8,128)(2,1)S(1)}, bf16[576,128]{1,0:T(8,128)(2,1)S(1)}, u32[]{:S(2)}, u32[]{:S(2)}) collective-permute-start(bf16[576,128]{1,0:T(8,128)(2,1)S(1)} %collective-permute-done.1.rest_3_), channel_id=1, source_target_pairs={{0,1},{1,0},{2,3},{3,2},{4,5},{5,4},{6,7},{7,6},{8,9},{9,8},{10,11... | collective-permute-start | bytes 442376 | tf_op jit(solution)/shard_map/ppermute | solution.py:30
  17.6 1.6 %collective-permute-start.4 = (bf16[128,896]{1,0:T(8,128)(2,1)S(1)}, bf16[128,896]{1,0:T(8,128)(2,1)S(1)}, u32[]{:S(2)}, u32[]{:S(2)}) collective-permute-start(bf16[128,896]{1,0:T(8,128)(2,1)S(1)} %get-tuple-element.49), channel_id=1, source_target_pairs={{0,1},{1,0},{2,3},{3,2},{4,5},{5,4},{6,7},{7,6},{8,9},{9,8},{10,11... | collective-permute-start | bytes 688136 | tf_op jit(solution)/shard_map/ppermute | solution.py:30
  19.2 1.7 %collective-permute-start.5 = (bf16[128,896]{1,0:T(8,128)(2,1)S(1)}, bf16[128,896]{1,0:T(8,128)(2,1)S(1)}, u32[]{:S(2)}, u32[]{:S(2)}) collective-permute-start(bf16[128,896]{1,0:T(8,128)(2,1)S(1)} %get-tuple-element.51), channel_id=1, source_target_pairs={{0,1},{1,0},{2,3},{3,2},{4,5},{5,4},{6,7},{7,6},{8,9},{9,8},{10,11... | collective-permute-start | bytes 688136 | tf_op jit(solution)/shard_map/ppermute | solution.py:30
  19.4 7.9 %collective-permute-start.6 = (bf16[128,896]{1,0:T(8,128)(2,1)S(1)}, bf16[128,896]{1,0:T(8,128)(2,1)S(1)}, u32[]{:S(2)}, u32[]{:S(2)}) collective-permute-start(bf16[128,896]{1,0:T(8,128)(2,1)S(1)} %add_convert_fusion.1), channel_id=1, source_target_pairs={{0,2},{1,3},{2,0},{3,1},{4,6},{5,7},{6,4},{7,5},{8,10},{9,11},{10,... | collective-permute-start | bytes 688136 | tf_op jit(solution)/shard_map/ppermute | solution.py:30

commit v8 on v7

--- a/solution.py
+++ b/solution.py
@@ -12,8 +12,7 @@
 HEAD_DIM = 128
 QUERY = HEAD_DIM + ROPE
 PARTS = 4
-ROWS_AT_ONCE = 256
-NT = (((1,), (1,)), ((), ()))
+COLUMNS_AT_ONCE = 256
 VMEM_BYTES = 32 * 1024 * 1024
 HIDDEN = -1e30
 
@@ -61,7 +60,7 @@
     order_hbm, lens_hbm, queries_ref, w_keys_ref, w_values_ref, w_out_ref = refs[:6]
     folded_ref, bias_ref, values_ref = refs[6:9]
     part_refs = refs[9 : 9 + PARTS]
-    order_ref, lens_ref, query_buffer, key_buffer, sems = refs[9 + PARTS :]
+    order_ref, lens_ref, query_buffer, key_buffer, value_buffer, turned_ref, sems = refs[9 + PARTS :]
     width = w_out_ref.shape[1] // PARTS
     heads = w_keys_ref.shape[1] // HEAD_DIM
     rows = 2 * half
@@ -73,37 +72,41 @@
         pltpu.make_async_copy(queries_ref, query_buffer, sems.at[2]),
         pltpu.make_async_copy(w_keys_ref, key_buffer, sems.at[3]),
     ]
-    later = [pltpu.make_async_copy(w_values_ref, values_ref, sems.at[4])]
+    values_copy = pltpu.make_async_copy(w_values_ref, value_buffer, sems.at[4])
+    later = []
     for slot, part in enumerate(part_order()):
         start = pl.multiple_of(part * width, 128)
         source = w_out_ref.at[:, pl.ds(start, width)]
         later.append(pltpu.make_async_copy(source, part_refs[slot], sems.at[5 + slot]))
-    for copy in scalars + first + later:
+    for copy in scalars + first + [values_copy] + later:
         copy.start()
 
     for copy in scalars:
         copy.wait()
     ctx = lax.axis_index("ctx")
-    row = lax.broadcasted_iota(jnp.int32, (rows, rows), 0)
     lane = lax.broadcasted_iota(jnp.int32, (rows, rows), 1)
-    query_pos = jnp.where(row < half, order_ref[2 * ctx], order_ref[2 * ctx + 1]) * half + row % half
-    offset = lane % half
+    key = lax.broadcasted_iota(jnp.int32, (rows, rows), 0)
+    query_pos = jnp.where(lane < half, order_ref[2 * ctx], order_ref[2 * ctx + 1]) * half
+    query_pos = query_pos + lane % half
+    offset = key % half
     for step, source in enumerate(key_sources()):
-        key_place = jnp.where(lane < half, order_ref[2 * source], order_ref[2 * source + 1])
-        length = jnp.where(lane < half, lens_ref[2 * source], lens_ref[2 * source + 1])
+        key_place = jnp.where(key < half, order_ref[2 * source], order_ref[2 * source + 1])
+        length = jnp.where(key < half, lens_ref[2 * source], lens_ref[2 * source + 1])
         visible = (key_place * half + offset <= query_pos) & (offset < length)
-        bias_ref[:, step * rows : (step + 1) * rows] = jnp.where(visible, 0.0, HIDDEN)
+        bias_ref[step * rows : (step + 1) * rows, :] = jnp.where(visible, 0.0, HIDDEN)
 
     for copy in first:
         copy.wait()
+    turned_ref[...] = query_buffer[...].T
     for head in range(heads):
-        nope = query_buffer[:, head * QUERY : head * QUERY + HEAD_DIM]
-        rope = query_buffer[:, head * QUERY + HEAD_DIM : (head + 1) * QUERY]
+        nope = turned_ref[head * QUERY : head * QUERY + HEAD_DIM, :]
         weight = key_buffer[:, head * HEAD_DIM : (head + 1) * HEAD_DIM]
-        product = lax.dot_general(nope, weight, NT, preferred_element_type=jnp.float32)
+        product = jnp.dot(weight, nope, preferred_element_type=jnp.float32)
         here = slice(head * rows, (head + 1) * rows)
-        folded_ref[here, :LATENT] = product.astype(jnp.bfloat16)
-        folded_ref[here, LATENT:] = rope
+        folded_ref[:LATENT, here] = product.astype(jnp.bfloat16)
+        folded_ref[LATENT:, here] = turned_ref[head * QUERY + HEAD_DIM : (head + 1) * QUERY, :]
+    values_copy.wait()
+    values_ref[...] = value_buffer[...].T
     for copy in later:
         copy.wait()
 
@@ -117,9 +120,9 @@
     return pl.pallas_call(
         functools.partial(prepare_kernel, rows // 2),
         out_shape=[
-            jax.ShapeDtypeStruct((heads * rows, LATENT + ROPE), jnp.bfloat16),
-            jax.ShapeDtypeStruct((rows, count * rows), jnp.float32),
-            jax.ShapeDtypeStruct(w_values.shape, jnp.bfloat16),
+            jax.ShapeDtypeStruct((LATENT + ROPE, heads * rows), jnp.bfloat16),
+            jax.ShapeDtypeStruct((count * rows, rows), jnp.float32),
+            jax.ShapeDtypeStruct(w_values.shape[::-1], jnp.bfloat16),
         ]
         + [part] * PARTS,
         in_specs=[HBM] * 6,
@@ -129,6 +132,8 @@
             pltpu.SMEM(lens.shape, jnp.int32),
             pltpu.VMEM(queries.shape, jnp.bfloat16),
             pltpu.VMEM(w_keys.shape, jnp.bfloat16),
+            pltpu.VMEM(w_values.shape, jnp.bfloat16),
+            pltpu.VMEM(queries.shape[::-1], jnp.bfloat16),
             pltpu.SemaphoreType.DMA((5 + PARTS,)),
         ],
         compiler_params=PARAMS,
@@ -161,39 +166,40 @@
 
 
 def attend_kernel(count, paired, folded_ref, bias_ref, values_ref, part_ref, *rest):
-    blocks, (attended_ref, *shares, keys_ref, latents_ref) = rest[:count], rest[count:]
-    rows = bias_ref.shape[0]
-    heads = values_ref.shape[1] // HEAD_DIM
+    blocks, rest = rest[:count], rest[count:]
+    attended_ref, *shares, turned_ref, keys_ref, heads_ref = rest
+    rows = bias_ref.shape[1]
     certain = count - 2 if paired else count
     for slot in range(certain):
-        keys_ref[:, slot * rows : (slot + 1) * rows] = blocks[slot][...]
+        turned_ref[:, slot * rows : (slot + 1) * rows] = blocks[slot][...]
     if paired:
         direct = (lax.axis_index("ctx") ^ lax.axis_index("head")) & 1 == 0
-        place_if(keys_ref, certain, blocks[certain], direct)
-        place_if(keys_ref, certain, blocks[certain + 1], jnp.logical_not(direct))
-    for slot in range(keys_ref.shape[1] // rows):
+        place_if(turned_ref, certain, blocks[certain], direct)
+        place_if(turned_ref, certain, blocks[certain + 1], jnp.logical_not(direct))
+    for slot in range(keys_ref.shape[0] // rows):
         here = slice(slot * rows, (slot + 1) * rows)
-        latents_ref[here, :] = keys_ref[:LATENT, here].T
-    stacked = ROWS_AT_ONCE // rows
-    bias = jnp.concatenate([bias_ref[...]] * stacked, axis=0)
-    for group in range(heads // stacked):
-        lines = slice(group * ROWS_AT_ONCE, (group + 1) * ROWS_AT_ONCE)
-        scores = jnp.dot(folded_ref[lines, :], keys_ref[...], preferred_element_type=jnp.float32)
+        keys_ref[here, :] = turned_ref[:, here].T
+    stacked = COLUMNS_AT_ONCE // rows
+    bias = jnp.concatenate([bias_ref[...]] * stacked, axis=1)
+    for group in range(folded_ref.shape[1] // COLUMNS_AT_ONCE):
+        columns = slice(group * COLUMNS_AT_ONCE, (group + 1) * COLUMNS_AT_ONCE)
+        scores = jnp.dot(keys_ref[...], folded_ref[:, columns], preferred_element_type=jnp.float32)
         scores = scores + bias
-        peak = jnp.max(scores, axis=1, keepdims=True)
+        peak = jnp.max(scores, axis=0, keepdims=True)
         weights = jnp.exp2((scores - peak) * jnp.float32(EXPONENT))
-        inverse = 1.0 / jnp.sum(weights, axis=1, keepdims=True)
+        inverse = 1.0 / jnp.sum(weights, axis=0, keepdims=True)
         mixed = jnp.dot(
-            weights.astype(jnp.bfloat16), latents_ref[...], preferred_element_type=jnp.float32
+            turned_ref[:LATENT, :], weights.astype(jnp.bfloat16), preferred_element_type=jnp.float32
         ).astype(jnp.bfloat16)
         for inner in range(stacked):
             head = group * stacked + inner
-            columns = slice(head * HEAD_DIM, (head + 1) * HEAD_DIM)
-            lines = slice(inner * rows, (inner + 1) * rows)
+            lines = slice(head * HEAD_DIM, (head + 1) * HEAD_DIM)
+            columns = slice(inner * rows, (inner + 1) * rows)
             value = jnp.dot(
-                mixed[lines, :], values_ref[:, columns], preferred_element_type=jnp.float32
+                values_ref[lines, :], mixed[:, columns], preferred_element_type=jnp.float32
             )
-            attended_ref[:, columns] = (value * inverse[lines, :]).astype(jnp.bfloat16)
+            heads_ref[lines, :] = (value * inverse[:, columns]).astype(jnp.bfloat16)
+    attended_ref[...] = heads_ref[...].T
     project(attended_ref, part_ref, shares)
 
 
@@ -202,17 +208,18 @@
 
 
 def attend(folded, bias, values, part, blocks, widths):
-    rows, keys = bias.shape
-    heads = values.shape[1] // HEAD_DIM
+    keys, rows = bias.shape
+    heads = values.shape[0] // HEAD_DIM
     flops = 2 * heads * rows * (keys * (2 * LATENT + ROPE) + LATENT * HEAD_DIM)
     return pl.pallas_call(
         functools.partial(attend_kernel, len(blocks), is_paired()),
-        out_shape=share_shapes(rows, [values.shape[1]] + widths, jnp.bfloat16),
+        out_shape=share_shapes(rows, [values.shape[0]] + widths, jnp.bfloat16),
         in_specs=[VMEM] * (4 + len(blocks)),
         out_specs=[VMEM] * (1 + len(widths)),
         scratch_shapes=[
             pltpu.VMEM((LATENT + ROPE, keys), jnp.bfloat16),
-            pltpu.VMEM((keys, LATENT), jnp.bfloat16),
+            pltpu.VMEM((keys, LATENT + ROPE), jnp.bfloat16),
+            pltpu.VMEM((values.shape[0], rows), jnp.bfloat16),
         ],
         compiler_params=PARAMS,
         cost_estimate=pl.CostEstimate(
@@ -293,7 +300,6 @@
     outs = [share_shapes(rows, [width], kind) for kind in (wide, narrow, wide)]
     far_part, beside, own = project_parts(attended, parts[1:], outs)
     far_part = (far_part + received.astype(wide)).astype(narrow)
-    far_part, beside = lax.optimization_barrier((far_part, beside))
     far_part = routed(far_part, other_chip).astype(wide)
     beside = routed(beside, other_core).astype(wide)
     return (own + beside + far_part).astype(narrow)

time: 28.2 us -> 28.2 us (level)
  waiting for transfers between devices: 9.26 us -> 8.76 us
    ppermute x7, waiting for transfers between devices: 9.26 us -> 8.76 us  [routed(): return lax.ppermute(value, ('ctx', 'head'), pairs)]
  transfers between devices with their start and end apart: 7 -> 7, of which waited for: 5 -> 4; matrix products, arithmetic and copies ran while one was open for 0% -> 0% of each run, Pallas kernels for 18% -> 18%
where the time goes in v8:
time: 28.2 us; the launch traced here: 28 us
  starting transfers between devices  9.92 us (35%)
  waiting for transfers between devices  8.76 us (31%)
  Pallas kernels  8.45 us (30%)
  other arithmetic  0.81 us (3%)
    ppermute x7, starting transfers between devices, routed(): return lax.ppermute(value, ('ctx', 'head'), pairs)  9.92 us
    ppermute x7, waiting for transfers between devices, routed(): return lax.ppermute(value, ('ctx', 'head'), pairs)  8.76 us
    pallas_call x1, Pallas kernels, prepare(): pl.pallas_call(functools.partial(prepare_kernel, rows // 2), out_shape=[j...  3.99 us
    pallas_call x1, Pallas kernels, attend(): pl.pallas_call(functools.partial(attend_kernel, len(blocks), is_paired())...  3.47 us
    pallas_call x1, Pallas kernels, project_parts(): pl.pallas_call(functools.partial(project_kernel, [len(group) for group in...  0.99 us
    convert_element_type x1, other arithmetic, shards(): return (own + beside + far_part).astype(narrow)  0.77 us
  transfers between devices with their start and end apart: 7, of which 4 were waited for; matrix products, arithmetic and copies ran while one was open for 0% of the time, Pallas kernels for 18%

profile of v8, /device:TPU:0, one launch (start us, length us, event | category | flops | bytes accessed | tf_op | source)
XLA Modules:
  0.0 28.0 jit_solution(15295110788181108081)
XLA Ops:
  0.0 0.0 copy-start
  0.0 3.0 %collective-permute-start = (bf16[576,128]{1,0:T(8,128)(2,1)}, bf16[576,128]{1,0:T(8,128)(2,1)S(1)}, u32[]{:S(2)}, u32[]{:S(2)}) collective-permute-start(bf16[576,128]{1,0:T(8,128)(2,1)} %bitcast.1), channel_id=1, source_target_pairs={{0,4},{1,13},{2,6},{3,15},{4,8},{5,1},{6,10},{7,3},{8,12},{9,5},{1... | collective-permute-start | bytes 442376 | tf_op jit(solution)/shard_map/ppermute | solution.py:29
  3.0 4.5 %collective-permute-start.1 = (bf16[576,128]{1,0:T(8,128)(2,1)}, bf16[576,128]{1,0:T(8,128)(2,1)S(1)}, u32[]{:S(2)}, u32[]{:S(2)}) collective-permute-start(bf16[576,128]{1,0:T(8,128)(2,1)} %bitcast.2), channel_id=1, source_target_pairs={{0,8},{1,1},{2,10},{3,3},{4,4},{5,13},{6,6},{7,15},{8,0},{9,9},{10... | collective-permute-start | bytes 442376 | tf_op jit(solution)/shard_map/ppermute | solution.py:29
  7.5 4.0 %prepare.1 = (bf16[576,1024]{1,0:T(8,128)(2,1)S(1)}, f32[512,128]{1,0:T(8,128)S(1)}, bf16[1024,512]{1,0:T(8,128)(2,1)S(1)}, bf16[1024,896]{1,0:T(8,128)(2,1)S(1)...) custom-call(s32[8]{0:T(128)} %refs_0_.1, s32[8]{0:T(128)} %refs_1_.1, ...), custom_call_target="tpu_custom_call" | custom-call | flops 134217728 | bytes 9830400 | tf_op jit(solution)/shard_map/prepare/pallas_call | solution.py:120
  11.5 0.0 collective-permute-done.rest_1_
  11.5 0.1 collective-permute-start.2
  11.6 0.8 %collective-permute-done.1.rest_3_ = bf16[576,128]{1,0:T(8,128)(2,1)S(1)} collective-permute-done((bf16[576,128]{1,0:T(8,128)(2,1)}, bf16[576,128]{1,0:T(8,128)(2,1)S(1)}, u32[]{:S(2)}, u32[]{:S(2)}) %collective-permute-start.1) | collective-permute-done | bytes 147488 | tf_op jit(solution)/shard_map/ppermute | solution.py:29
  12.4 0.5 %collective-permute-done.2.rest_2_ = bf16[576,128]{1,0:T(8,128)(2,1)S(1)} collective-permute-done((bf16[576,128]{1,0:T(8,128)(2,1)S(1)}, bf16[576,128]{1,0:T(8,128)(2,1)S(1)}, u32[]{:S(2)}, u32[]{:S(2)}) %collective-permute-start.2) | collective-permute-done | bytes 147488 | tf_op jit(solution)/shard_map/ppermute | solution.py:29
  13.0 0.1 collective-permute-start.3
  13.1 1.2 %collective-permute-done.3.rest_4_ = bf16[576,128]{1,0:T(8,128)(2,1)S(1)} collective-permute-done((bf16[576,128]{1,0:T(8,128)(2,1)S(1)}, bf16[576,128]{1,0:T(8,128)(2,1)S(1)}, u32[]{:S(2)}, u32[]{:S(2)}) %collective-permute-start.3) | collective-permute-done | bytes 147488 | tf_op jit(solution)/shard_map/ppermute | solution.py:29
  14.3 0.0 copy-done
  14.3 3.5 %attend.1 = (bf16[128,1024]{1,0:T(8,128)(2,1)S(1)}, bf16[128,896]{1,0:T(8,128)(2,1)S(1)}) custom-call(bf16[576,1024]{1,0:T(8,128)(2,1)S(1)} %get-tuple-element.34.folded_ref, f32[512,128]{1,0:T(8,128)S(1)} %get-tuple-element.35.bias_ref, bf16[1024,512]{1,0:T(8,128)(2,1)S(1)} %get-tuple-element.36.values_ref, ...), custom_call_target="tpu_custom_call" | custom-call | flops 1509949440 | bytes 4063232 | tf_op jit(solution)/shard_map/attend/pallas_call | solution.py:214
  17.8 0.2 collective-permute-start.5
  18.0 1.0 %project_parts.1 = (f32[128,896]{1,0:T(8,128)S(1)}, bf16[128,896]{1,0:T(8,128)(2,1)S(1)}, f32[128,896]{1,0:T(8,128)S(1)}) custom-call(bf16[128,1024]{1,0:T(8,128)(2,1)S(1)} %get-tuple-element.41.attended_ref, bf16[1024,896]{1,0:T(8,128)(2,1)S(1)} %get-tuple-element.42.refs_0_, bf16[1024,896]{1,0:T(8,128)(2,1)S(1)} %get-tuple-element.43.refs_1_, ...), custom_call_target="tpu_custom_call" | custom-call | flops 1024 | bytes 1024 | tf_op jit(solution)/shard_map/project_parts/pallas_call | solution.py:243
  19.0 0.4 %collective-permute-start.4 = (bf16[128,896]{1,0:T(8,128)(2,1)S(1)}, bf16[128,896]{1,0:T(8,128)(2,1)S(1)}, u32[]{:S(2)}, u32[]{:S(2)}) collective-permute-start(bf16[128,896]{1,0:T(8,128)(2,1)S(1)} %get-tuple-element.46), channel_id=1, source_target_pairs={{0,1},{1,0},{2,3},{3,2},{4,5},{5,4},{6,7},{7,6},{8,9},{9,8},{10,11... | collective-permute-start | bytes 688136 | tf_op jit(solution)/shard_map/ppermute | solution.py:29
  19.5 0.0 collective-permute-done.5
  19.5 1.6 %collective-permute-start.6 = (bf16[128,896]{1,0:T(8,128)(2,1)S(1)}, bf16[128,896]{1,0:T(8,128)(2,1)S(1)}, u32[]{:S(2)}, u32[]{:S(2)}) collective-permute-start(bf16[128,896]{1,0:T(8,128)(2,1)S(1)} %add_convert_fusion.1), channel_id=1, source_target_pairs={{0,2},{1,3},{2,0},{3,1},{4,6},{5,7},{6,4},{7,5},{8,10},{9,11},{10,... | collective-permute-start | bytes 688136 | tf_op jit(solution)/shard_map/ppermute | solution.py:29
  21.1 0.0 collective-permute-done.4
  21.1 6.2 %collective-permute-done.6 = bf16[128,896]{1,0:T(8,128)(2,1)S(1)} collective-permute-done((bf16[128,896]{1,0:T(8,128)(2,1)S(1)}, bf16[128,896]{1,0:T(8,128)(2,1)S(1)}, u32[]{:S(2)}, u32[]{:S(2)}) %collective-permute-start.6) | collective-permute-done | bytes 229408 | tf_op jit(solution)/shard_map/ppermute | solution.py:29
  27.2 0.8 %add_convert_fusion = bf16[128,896]{1,0:T(8,128)(2,1)} fusion(bf16[128,896]{1,0:T(8,128)(2,1)S(1)} %collective-permute-done.6, f32[128,896]{1,0:T(8,128)S(1)} %get-tuple-element.45, bf16[128,896]{1,0:T(8,128)(2,1)S(1)} %collective-permute-done.4), kind=kLoop, calls=%fused_computation | loop fusion | flops 573440 | bytes 1146880 | tf_op jit(solution)/shard_map/convert_element_type | solution.py:305
  (1 shorter events, 0.0 us)
Async XLA Ops:
  0.0 14.3 %copy-start = (bf16[128,576]{0,1:T(8,128)(2,1)S(1)}, bf16[128,576]{0,1:T(8,128)(2,1)}, u32[]{:S(2)}) copy-start(bf16[128,576]{0,1:T(8,128)(2,1)} %param.8) | copy-start | bytes 442372
  0.0 11.5 %collective-permute-start = (bf16[576,128]{1,0:T(8,128)(2,1)}, bf16[576,128]{1,0:T(8,128)(2,1)S(1)}, u32[]{:S(2)}, u32[]{:S(2)}) collective-permute-start(bf16[576,128]{1,0:T(8,128)(2,1)} %bitcast.1), channel_id=1, source_target_pairs={{0,4},{1,13},{2,6},{3,15},{4,8},{5,1},{6,10},{7,3},{8,12},{9,5},{1... | collective-permute-start | bytes 442376 | tf_op jit(solution)/shard_map/ppermute | solution.py:29
  3.0 9.4 %collective-permute-start.1 = (bf16[576,128]{1,0:T(8,128)(2,1)}, bf16[576,128]{1,0:T(8,128)(2,1)S(1)}, u32[]{:S(2)}, u32[]{:S(2)}) collective-permute-start(bf16[576,128]{1,0:T(8,128)(2,1)} %bitcast.2), channel_id=1, source_target_pairs={{0,8},{1,1},{2,10},{3,3},{4,4},{5,13},{6,6},{7,15},{8,0},{9,9},{10... | collective-permute-start | bytes 442376 | tf_op jit(solution)/shard_map/ppermute | solution.py:29
  11.5 1.4 %collective-permute-start.2 = (bf16[576,128]{1,0:T(8,128)(2,1)S(1)}, bf16[576,128]{1,0:T(8,128)(2,1)S(1)}, u32[]{:S(2)}, u32[]{:S(2)}) collective-permute-start(bf16[576,128]{1,0:T(8,128)(2,1)S(1)} %collective-permute-done.rest_1_), channel_id=1, source_target_pairs={{0,1},{1,0},{2,3},{3,2},{4,5},{5,4},{6,7},{7,6},{8,9},{9,8},{10,11... | collective-permute-start | bytes 442376 | tf_op jit(solution)/shard_map/ppermute | solution.py:29
  13.0 1.4 %collective-permute-start.3 = (bf16[576,128]{1,0:T(8,128)(2,1)S(1)}, bf16[576,128]{1,0:T(8,128)(2,1)S(1)}, u32[]{:S(2)}, u32[]{:S(2)}) collective-permute-start(bf16[576,128]{1,0:T(8,128)(2,1)S(1)} %collective-permute-done.1.rest_3_), channel_id=1, source_target_pairs={{0,1},{1,0},{2,3},{3,2},{4,5},{5,4},{6,7},{7,6},{8,9},{9,8},{10,11... | collective-permute-start | bytes 442376 | tf_op jit(solution)/shard_map/ppermute | solution.py:29
  17.8 1.6 %collective-permute-start.5 = (bf16[128,896]{1,0:T(8,128)(2,1)S(1)}, bf16[128,896]{1,0:T(8,128)(2,1)S(1)}, u32[]{:S(2)}, u32[]{:S(2)}) collective-permute-start(bf16[128,896]{1,0:T(8,128)(2,1)S(1)} %get-tuple-element.48), channel_id=1, source_target_pairs={{0,1},{1,0},{2,3},{3,2},{4,5},{5,4},{6,7},{7,6},{8,9},{9,8},{10,11... | collective-permute-start | bytes 688136 | tf_op jit(solution)/shard_map/ppermute | solution.py:29
  19.0 2.0 %collective-permute-start.4 = (bf16[128,896]{1,0:T(8,128)(2,1)S(1)}, bf16[128,896]{1,0:T(8,128)(2,1)S(1)}, u32[]{:S(2)}, u32[]{:S(2)}) collective-permute-start(bf16[128,896]{1,0:T(8,128)(2,1)S(1)} %get-tuple-element.46), channel_id=1, source_target_pairs={{0,1},{1,0},{2,3},{3,2},{4,5},{5,4},{6,7},{7,6},{8,9},{9,8},{10,11... | collective-permute-start | bytes 688136 | tf_op jit(solution)/shard_map/ppermute | solution.py:29
  19.5 7.7 %collective-permute-start.6 = (bf16[128,896]{1,0:T(8,128)(2,1)S(1)}, bf16[128,896]{1,0:T(8,128)(2,1)S(1)}, u32[]{:S(2)}, u32[]{:S(2)}) collective-permute-start(bf16[128,896]{1,0:T(8,128)(2,1)S(1)} %add_convert_fusion.1), channel_id=1, source_target_pairs={{0,2},{1,3},{2,0},{3,1},{4,6},{5,7},{6,4},{7,5},{8,10},{9,11},{10,... | collective-permute-start | bytes 688136 | tf_op jit(solution)/shard_map/ppermute | solution.py:29

commit v9 on v7

v9 whole, which is shorter than its diff:
```python
import functools

import jax
import jax.numpy as jnp
from jax import lax
from jax.experimental import pallas as pl
from jax.experimental.pallas import tpu as pltpu
from jax.sharding import PartitionSpec as P

LATENT = 512
ROPE = 64
HEAD_DIM = 128
QUERY = HEAD_DIM + ROPE
PARTS = 4
PADDED = 256
NT = (((1,), (1,)), ((), ()))
VMEM_BYTES = 32 * 1024 * 1024
HIDDEN = -1e30


def routed(value, route):
    ctx_count = lax.axis_size("ctx")
    head_count = lax.axis_size("head")
    pairs = []
    for ctx in range(ctx_count):
        for head in range(head_count):
            target = route(ctx, head)
            if target is not None:
                pairs.append((ctx * head_count + head, target[0] * head_count + target[1]))
    return lax.ppermute(value, ("ctx", "head"), pairs)


def is_paired():
    return lax.axis_size("ctx") == 4 and lax.axis_size("head") == 4


def key_sources():
    count = lax.axis_size("ctx")
    ctx = lax.axis_index("ctx")
    if is_paired():
        step = 1 + 2 * (lax.axis_index("head") & 1)
        return [ctx, (ctx - step) & 3, (ctx + step) & 3, ctx ^ 2]
    return [ctx] + [lax.rem(ctx + (count - step), count) for step in range(1, count)]


def part_order():
    if is_paired():
        head = lax.axis_index("head")
        return [head ^ 3, head ^ 2, head ^ 1, head]
    return list(range(PARTS))


VMEM = pl.BlockSpec(memory_space=pltpu.VMEM)
HBM = pl.BlockSpec(memory_space=pltpu.HBM)
PARAMS = pltpu.CompilerParams(vmem_limit_bytes=VMEM_BYTES)
SHORT = pl.CostEstimate(flops=1024, bytes_accessed=1024, transcendentals=0)
EXPONENT = QUERY**-0.5 * 1.4426950408889634


def expand(turned, w_keys_ref, w_values_ref, keys_ref, values_ref):
    rows = turned.shape[1]
    latents = turned.T
    compressed = latents[:, :LATENT]
    rope = jnp.concatenate(
        [latents[:, LATENT:], jnp.zeros((rows, PADDED - QUERY), jnp.bfloat16)], axis=1
    )
    nope = jnp.dot(compressed, w_keys_ref[...], preferred_element_type=jnp.float32)
    nope = nope.astype(jnp.bfloat16)
    for head in range(w_keys_ref.shape[1] // HEAD_DIM):
        middle = head * PADDED + HEAD_DIM
        keys_ref[:, head * PADDED : middle] = nope[:, head * HEAD_DIM : (head + 1) * HEAD_DIM]
        keys_ref[:, middle : (head + 1) * PADDED] = rope
    values = jnp.dot(compressed, w_values_ref[...], preferred_element_type=jnp.float32)
    values_ref[...] = values.astype(jnp.bfloat16)


def prepare_kernel(half, *refs):
    order_hbm, lens_hbm, queries_ref, block_ref, w_keys_ref, w_values_ref, w_out_ref = refs[:7]
    padded_ref, bias_ref, keys_ref, values_ref, key_weight, value_weight = refs[7:13]
    part_refs = refs[13 : 13 + PARTS]
    order_ref, lens_ref, query_buffer, block_buffer, sems = refs[13 + PARTS :]
    width = w_out_ref.shape[1] // PARTS
    heads = w_keys_ref.shape[1] // HEAD_DIM
    rows = 2 * half
    scalars = [
        pltpu.make_async_copy(order_hbm, order_ref, sems.at[0]),
        pltpu.make_async_copy(lens_hbm, lens_ref, sems.at[1]),
    ]
    query_copy = pltpu.make_async_copy(queries_ref, query_buffer, sems.at[2])
    first = [
        pltpu.make_async_copy(block_ref, block_buffer, sems.at[3]),
        pltpu.make_async_copy(w_keys_ref, key_weight, sems.at[4]),
        pltpu.make_async_copy(w_values_ref, value_weight, sems.at[5]),
    ]
    later = []
    for slot, part in enumerate(part_order()):
        start = pl.multiple_of(part * width, 128)
        source = w_out_ref.at[:, pl.ds(start, width)]
        later.append(pltpu.make_async_copy(source, part_refs[slot], sems.at[6 + slot]))
    for copy in scalars + [query_copy] + first + later:
        copy.start()

    for copy in scalars:
        copy.wait()
    ctx = lax.axis_index("ctx")
    row = lax.broadcasted_iota(jnp.int32, (rows, rows), 0)
    lane = lax.broadcasted_iota(jnp.int32, (rows, rows), 1)
    query_pos = jnp.where(row < half, order_ref[2 * ctx], order_ref[2 * ctx + 1]) * half + row % half
    offset = lane % half
    for step, source in enumerate(key_sources()):
        key_place = jnp.where(lane < half, order_ref[2 * source], order_ref[2 * source + 1])
        length = jnp.where(lane < half, lens_ref[2 * source], lens_ref[2 * source + 1])
        visible = (key_place * half + offset <= query_pos) & (offset < length)
        bias_ref[:, step * rows : (step + 1) * rows] = jnp.where(visible, 0.0, HIDDEN)

    query_copy.wait()
    nothing = jnp.zeros((rows, PADDED - QUERY), jnp.bfloat16)
    for head in range(heads):
        query = query_buffer[:, head * QUERY : (head + 1) * QUERY]
        padded_ref[:, head * PADDED : (head + 1) * PADDED] = jnp.concatenate(
            [query, nothing], axis=1
        )
    for copy in first:
        copy.wait()
    expand(block_buffer[...], key_weight, value_weight, keys_ref, values_ref)
    for copy in later:
        copy.wait()


def narrow_shape(*shape):
    return jax.ShapeDtypeStruct(shape, jnp.bfloat16)


def prepare(*operands):
    order, lens, queries, block, w_keys, w_values, w_out = operands
    rows = queries.shape[0]
    count = lax.axis_size("ctx")
    heads = w_keys.shape[1] // HEAD_DIM
    return pl.pallas_call(
        functools.partial(prepare_kernel, rows // 2),
        out_shape=[
            narrow_shape(rows, heads * PADDED),
            jax.ShapeDtypeStruct((rows, count * rows), jnp.float32),
            narrow_shape(rows, heads * PADDED),
            narrow_shape(rows, heads * HEAD_DIM),
            narrow_shape(*w_keys.shape),
            narrow_shape(*w_values.shape),
        ]
        + [narrow_shape(w_out.shape[0], w_out.shape[1] // PARTS)] * PARTS,
        in_specs=[HBM] * 7,
        out_specs=[VMEM] * (6 + PARTS),
        scratch_shapes=[
            pltpu.SMEM(order.shape, jnp.int32),
            pltpu.SMEM(lens.shape, jnp.int32),
            pltpu.VMEM(queries.shape, jnp.bfloat16),
            pltpu.VMEM(block.shape, jnp.bfloat16),
            pltpu.SemaphoreType.DMA((6 + PARTS,)),
        ],
        compiler_params=PARAMS,
        cost_estimate=pl.CostEstimate(
            flops=4 * rows * heads * HEAD_DIM * LATENT,
            bytes_accessed=2 * (queries.size + w_keys.size + w_values.size + w_out.size),
            transcendentals=0,
        ),
        name="prepare",
    )(*[pltpu.with_memory_space_constraint(item, pltpu.HBM) for item in operands])


def expand_kernel(block_ref, w_keys_ref, w_values_ref, keys_ref, values_ref):
    expand(block_ref[...], w_keys_ref, w_values_ref, keys_ref, values_ref)


def expand_block(block, w_keys, w_values):
    rows = block.shape[1]
    heads = w_keys.shape[1] // HEAD_DIM
    return pl.pallas_call(
        expand_kernel,
        out_shape=[narrow_shape(rows, heads * PADDED), narrow_shape(rows, heads * HEAD_DIM)],
        in_specs=[VMEM] * 3,
        out_specs=[VMEM] * 2,
        compiler_params=PARAMS,
        cost_estimate=pl.CostEstimate(
            flops=4 * rows * w_keys.size, bytes_accessed=2 * w_keys.size, transcendentals=0
        ),
        name="expand_block",
    )(block, w_keys, w_values)


def project(attended_ref, part_ref, share_refs):
    start = 0
    for share_ref in share_refs:
        stop = start + share_ref.shape[1]
        share = jnp.dot(
            attended_ref[...], part_ref[:, start:stop], preferred_element_type=jnp.float32
        )
        share_ref[...] = share.astype(share_ref.dtype)
        start = stop


def take_if(target_ref, block_ref, condition):
    @pl.when(condition)
    def _():
        target_ref[...] = block_ref[...]


def attend_kernel(count, padded_ref, bias_ref, key_weight, value_weight, part_ref, *refs):
    direct_ref, swapped_ref = refs[:2]
    keys, values = list(refs[2 : 2 + count]), list(refs[2 + count : 2 + 2 * count])
    attended_ref, *shares, turned_ref, last_keys, last_values = refs[2 + 2 * count :]
    rows = bias_ref.shape[0]
    heads = value_weight.shape[1] // HEAD_DIM
    direct = (lax.axis_index("ctx") ^ lax.axis_index("head")) & 1 == 0
    take_if(turned_ref, direct_ref, direct)
    take_if(turned_ref, swapped_ref, jnp.logical_not(direct))
    expand(turned_ref[...], key_weight, value_weight, last_keys, last_values)
    keys.append(last_keys)
    values.append(last_values)
    for head in range(heads):
        wide = slice(head * PADDED, (head + 1) * PADDED)
        columns = slice(head * HEAD_DIM, (head + 1) * HEAD_DIM)
        query = padded_ref[:, wide]
        pieces = []
        for start in range(0, count + 1, 2):
            pair = jnp.concatenate([ref[:, wide] for ref in keys[start : start + 2]], axis=0)
            pieces.append(lax.dot_general(query, pair, NT, preferred_element_type=jnp.float32))
        scores = jnp.concatenate(pieces, axis=1) + bias_ref[...]
        peak = jnp.max(scores, axis=1, keepdims=True)
        weights = jnp.exp2((scores - peak) * jnp.float32(EXPONENT))
        inverse = 1.0 / jnp.sum(weights, axis=1, keepdims=True)
        value = jnp.dot(
            weights.astype(jnp.bfloat16),
            jnp.concatenate([ref[:, columns] for ref in values], axis=0),
            preferred_element_type=jnp.float32,
        )
        attended_ref[:, columns] = (value * inverse).astype(jnp.bfloat16)
    project(attended_ref, part_ref, shares)


def share_shapes(rows, widths, kind):
    return [jax.ShapeDtypeStruct((rows, width), kind) for width in widths]


def attend(padded, bias, weights, part, last, keys, values, widths):
    rows, key_count = bias.shape
    heads = values[0].shape[1] // HEAD_DIM
    flops = 4 * heads * rows * key_count * PADDED + 4 * rows * weights[0].size
    return pl.pallas_call(
        functools.partial(attend_kernel, len(keys)),
        out_shape=share_shapes(rows, [heads * HEAD_DIM] + widths, jnp.bfloat16),
        in_specs=[VMEM] * (7 + 2 * len(keys)),
        out_specs=[VMEM] * (1 + len(widths)),
        scratch_shapes=[
            pltpu.VMEM(last[0].shape, jnp.bfloat16),
            pltpu.VMEM(keys[0].shape, jnp.bfloat16),
            pltpu.VMEM(values[0].shape, jnp.bfloat16),
        ],
        compiler_params=PARAMS,
        cost_estimate=pl.CostEstimate(
            flops=flops + 2 * rows * part.size,
            bytes_accessed=2 * (weights[0].size + weights[1].size + part.size),
            transcendentals=heads * rows * key_count,
        ),
        name="attend",
    )(padded, bias, *weights, part, *last, *keys, *values)


def project_kernel(pieces, attended_ref, *refs):
    parts, shares = refs[: len(pieces)], list(refs[len(pieces) :])
    for part_ref, count in zip(parts, pieces):
        project(attended_ref, part_ref, shares[:count])
        shares = shares[count:]


def project_parts(attended, parts, outs):
    flat = [out for group in outs for out in group]
    return pl.pallas_call(
        functools.partial(project_kernel, [len(group) for group in outs]),
        out_shape=flat,
        in_specs=[VMEM] * (1 + len(parts)),
        out_specs=[VMEM] * len(flat),
        compiler_params=PARAMS,
        cost_estimate=SHORT,
        name="project_parts",
    )(attended, *parts)


def next_to(ctx, head):
    return (ctx + 1 + 2 * (head & 1)) & 3, head


def two_away(ctx, head):
    return (ctx ^ 2 if (ctx ^ head) & 1 == 0 else ctx), head


def other_core(ctx, head):
    return ctx, head ^ 1


def other_chip(ctx, head):
    return ctx, head ^ 2


def shards(queries, latent, w_keys, w_values, w_out, block_order, valid_lengths):
    ctx_count = lax.axis_size("ctx")
    rows = queries.shape[0]
    width = w_out.shape[1] // PARTS
    block = latent.T
    prepared = prepare(block_order, valid_lengths, queries, block, w_keys, w_values, w_out)
    narrow, wide = jnp.bfloat16, jnp.float32

    if not is_paired():
        blocks = []
        for step in range(1, ctx_count):
            blocks.append(routed(block, lambda ctx, head: ((ctx + step) % ctx_count, head)))
        padded, bias, own_keys, own_values, *weights = prepared
        weights, parts = weights[:2], weights[2:]
        expanded = [(own_keys, own_values)]
        expanded += [expand_block(piece, *weights) for piece in blocks[:-1]]
        keys, values = zip(*expanded)
        last = [blocks[-1], blocks[-1]]
        attended, share = attend(padded, bias, weights, parts[0], last, keys, values, [width])
        outs = [share_shapes(rows, [width], narrow)] * (PARTS - 1)
        shares = [share] + list(project_parts(attended, parts[1:], outs))
        whole = jnp.concatenate(shares, axis=1)
        return lax.psum_scatter(whole, "head", scatter_dimension=1, tiled=True)

    near = routed(block, next_to)
    far = routed(block, two_away)
    near, prepared = lax.optimization_barrier((near, prepared))
    padded, bias, own_keys, own_values, *weights = prepared
    weights, parts = weights[:2], weights[2:]
    near_swapped = routed(near, other_core)
    far, near_swapped = lax.optimization_barrier((far, near_swapped))
    far_swapped = routed(far, other_core)
    expanded = [(own_keys, own_values)]
    expanded += [expand_block(piece, *weights) for piece in (near, near_swapped)]
    keys, values = zip(*expanded)
    last = [far, far_swapped]

    attended, across = attend(padded, bias, weights, parts[0], last, keys, values, [width])
    received = routed(across, other_core)
    outs = [share_shapes(rows, [width], kind) for kind in (wide, narrow, wide)]
    far_part, beside, own = project_parts(attended, parts[1:], outs)
    far_part = (far_part + received.astype(wide)).astype(narrow)
    far_part = routed(far_part, other_chip).astype(wide)
    beside = routed(beside, other_core).astype(wide)
    return (own + beside + far_part).astype(narrow)


def solution(mesh):
    in_specs = (
        P(("groups", "ctx"), "head"),
        P(("groups", "ctx"), None),
        P(None, "head"),
        P(None, "head"),
        P("head", None),
        P("groups"),
        P("groups"),
    )
    out_specs = P(("groups", "ctx"), "head")
    return jax.shard_map(shards, mesh=mesh, in_specs=in_specs, out_specs=out_specs, check_vma=False)
```

time: 28.2 us -> 28 us (level)
  waiting for transfers between devices: 9.26 us -> 7.81 us
  Pallas kernels: 8.23 us -> 9.25 us
    ppermute x7, waiting for transfers between devices: 9.26 us -> 7.81 us  [routed(): return lax.ppermute(value, ('ctx', 'head'), pairs)]
    pallas_call x2 -> x4, Pallas kernels: 7.24 us -> 8.27 us  [the longest x1 4.08 us: prepare(): pl.pallas_call(functools.partial(prepare_kernel, rows // 2), out_shape=[n...]
  transfers between devices with their start and end apart: 7 -> 7, of which waited for: 5 -> 4; matrix products, arithmetic and copies ran while one was open for 0% -> 0% of each run, Pallas kernels for 18% -> 22%
where the time goes in v9:
time: 28 us; the launch traced here: 27.8 us
  starting transfers between devices  9.91 us (35%)
  Pallas kernels  9.25 us (33%)
  waiting for transfers between devices  7.81 us (28%)
  other arithmetic  0.8 us (3%)
    ppermute x7, starting transfers between devices, routed(): return lax.ppermute(value, ('ctx', 'head'), pairs)  9.91 us
    ppermute x7, waiting for transfers between devices, routed(): return lax.ppermute(value, ('ctx', 'head'), pairs)  7.81 us
    pallas_call x1, Pallas kernels, prepare(): pl.pallas_call(functools.partial(prepare_kernel, rows // 2), out_shape=[n...  4.08 us
    pallas_call x1, Pallas kernels, attend(): pl.pallas_call(functools.partial(attend_kernel, len(keys)), out_shape=sha...  3.26 us
    pallas_call x1, Pallas kernels, project_parts(): pl.pallas_call(functools.partial(project_kernel, [len(group) for group in...  0.99 us
    pallas_call x2, Pallas kernels, expand_block(): pl.pallas_call(expand_kernel, out_shape=[narrow_shape(rows, heads * PADDE...  0.93 us
    convert_element_type x1, other arithmetic, shards(): return (own + beside + far_part).astype(narrow)  0.76 us
  transfers between devices with their start and end apart: 7, of which 4 were waited for; matrix products, arithmetic and copies ran while one was open for 0% of the time, Pallas kernels for 22%

profile of v9, /device:TPU:0, one launch (start us, length us, event | category | flops | bytes accessed | tf_op | source)
XLA Modules:
  0.0 27.8 jit_solution(15586724640932937697)
XLA Ops:
  0.0 3.0 %collective-permute-start = (bf16[576,128]{1,0:T(8,128)(2,1)}, bf16[576,128]{1,0:T(8,128)(2,1)S(1)}, u32[]{:S(2)}, u32[]{:S(2)}) collective-permute-start(bf16[576,128]{1,0:T(8,128)(2,1)} %bitcast.1), channel_id=1, source_target_pairs={{0,4},{1,13},{2,6},{3,15},{4,8},{5,1},{6,10},{7,3},{8,12},{9,5},{1... | collective-permute-start | bytes 442376 | tf_op jit(solution)/shard_map/ppermute | solution.py:30
  3.0 4.5 %collective-permute-start.1 = (bf16[576,128]{1,0:T(8,128)(2,1)}, bf16[576,128]{1,0:T(8,128)(2,1)S(1)}, u32[]{:S(2)}, u32[]{:S(2)}) collective-permute-start(bf16[576,128]{1,0:T(8,128)(2,1)} %bitcast.2), channel_id=1, source_target_pairs={{0,8},{1,1},{2,10},{3,3},{4,4},{5,13},{6,6},{7,15},{8,0},{9,9},{10... | collective-permute-start | bytes 442376 | tf_op jit(solution)/shard_map/ppermute | solution.py:30
  7.5 4.1 %prepare.1 = (bf16[128,2048]{1,0:T(8,128)(2,1)S(1)}, f32[128,512]{1,0:T(8,128)S(1)}, bf16[128,2048]{1,0:T(8,128)(2,1)S(1)}, bf16[128,1024]{1,0:T(8,128)(2,1)S(1)...) custom-call(s32[8]{0:T(128)} %refs_0_.1, ...), custom_call_target="tpu_custom_call" | custom-call | flops 268435456 | bytes 9830400 | tf_op jit(solution)/shard_map/prepare/pallas_call | solution.py:139
  11.6 0.0 collective-permute-done.block_ref
  11.6 0.1 collective-permute-start.2
  11.7 0.7 %collective-permute-done.1.refs_0_ = bf16[576,128]{1,0:T(8,128)(2,1)S(1)} collective-permute-done((bf16[576,128]{1,0:T(8,128)(2,1)}, bf16[576,128]{1,0:T(8,128)(2,1)S(1)}, u32[]{:S(2)}, u32[]{:S(2)}) %collective-permute-start.1) | collective-permute-done | bytes 147488 | tf_op jit(solution)/shard_map/ppermute | solution.py:30
  12.4 0.6 %collective-permute-done.2.block_ref = bf16[576,128]{1,0:T(8,128)(2,1)S(1)} collective-permute-done((bf16[576,128]{1,0:T(8,128)(2,1)S(1)}, bf16[576,128]{1,0:T(8,128)(2,1)S(1)}, u32[]{:S(2)}, u32[]{:S(2)}) %collective-permute-start.2) | collective-permute-done | bytes 147488 | tf_op jit(solution)/shard_map/ppermute | solution.py:30
  13.0 0.1 collective-permute-start.3
  13.2 0.5 %expand_block.2 = (bf16[128,2048]{1,0:T(8,128)(2,1)S(1)}, bf16[128,1024]{1,0:T(8,128)(2,1)S(1)}) custom-call(bf16[576,128]{1,0:T(8,128)(2,1)S(1)} %collective-permute-done.block_ref, bf16[512,1024]{1,0:T(8,128)(2,1)S(1)} %get-tuple-element.49.w_keys_ref.key_weight, bf16[512,1024]{1,0:T(8,128)(2,1)S(1)} %get-tuple-element.50.w_values_ref.value_weight), custom_call_target="tpu_custom_call" | custom-call | flops 268435456 | bytes 1048576 | tf_op jit(solution)/shard_map/expand_block/pallas_call | solution.py:176
  13.7 0.5 %expand_block.3 = (bf16[128,2048]{1,0:T(8,128)(2,1)S(1)}, bf16[128,1024]{1,0:T(8,128)(2,1)S(1)}) custom-call(bf16[576,128]{1,0:T(8,128)(2,1)S(1)} %collective-permute-done.2.block_ref, bf16[512,1024]{1,0:T(8,128)(2,1)S(1)} %get-tuple-element.49.w_keys_ref.key_weight, bf16[512,1024]{1,0:T(8,128)(2,1)S(1)} %get-tuple-element.50.w_values_ref.value_weight), custom_call_target="tpu_custom_call" | custom-call | flops 268435456 | bytes 1048576 | tf_op jit(solution)/shard_map/expand_block/pallas_call | solution.py:176
  14.1 0.3 %collective-permute-done.3.refs_1_ = bf16[576,128]{1,0:T(8,128)(2,1)S(1)} collective-permute-done((bf16[576,128]{1,0:T(8,128)(2,1)S(1)}, bf16[576,128]{1,0:T(8,128)(2,1)S(1)}, u32[]{:S(2)}, u32[]{:S(2)}) %collective-permute-start.3) | collective-permute-done | bytes 147488 | tf_op jit(solution)/shard_map/ppermute | solution.py:30
  14.4 3.3 %attend.1 = (bf16[128,1024]{1,0:T(8,128)(2,1)S(1)}, bf16[128,896]{1,0:T(8,128)(2,1)S(1)}) custom-call(bf16[128,2048]{1,0:T(8,128)(2,1)S(1)} %get-tuple-element.47.padded_ref, f32[128,512]{1,0:T(8,128)S(1)} %get-tuple-element.48.bias_ref, bf16[512,1024]{1,0:T(8,128)(2,1)S(1)} %get-tuple-element.49.w_keys_ref.key_weight, ...), custom_call_target="tpu_custom_call" | custom-call | flops 1040187392 | bytes 3932160 | tf_op jit(solution)/shard_map/attend/pallas_call | solution.py:247
  17.7 0.2 collective-permute-start.5
  17.9 1.0 %project_parts.1 = (f32[128,896]{1,0:T(8,128)S(1)}, bf16[128,896]{1,0:T(8,128)(2,1)S(1)}, f32[128,896]{1,0:T(8,128)S(1)}) custom-call(bf16[128,1024]{1,0:T(8,128)(2,1)S(1)} %get-tuple-element.61.attended_ref, bf16[1024,896]{1,0:T(8,128)(2,1)S(1)} %get-tuple-element.62.refs_0_, bf16[1024,896]{1,0:T(8,128)(2,1)S(1)} %get-tuple-element.63.refs_1_, ...), custom_call_target="tpu_custom_call" | custom-call | flops 1024 | bytes 1024 | tf_op jit(solution)/shard_map/project_parts/pallas_call | solution.py:276
  18.9 0.4 %collective-permute-start.4 = (bf16[128,896]{1,0:T(8,128)(2,1)S(1)}, bf16[128,896]{1,0:T(8,128)(2,1)S(1)}, u32[]{:S(2)}, u32[]{:S(2)}) collective-permute-start(bf16[128,896]{1,0:T(8,128)(2,1)S(1)} %get-tuple-element.66), channel_id=1, source_target_pairs={{0,1},{1,0},{2,3},{3,2},{4,5},{5,4},{6,7},{7,6},{8,9},{9,8},{10,11... | collective-permute-start | bytes 688136 | tf_op jit(solution)/shard_map/ppermute | solution.py:30
  19.3 0.0 collective-permute-done.5
  19.4 1.5 %collective-permute-start.6 = (bf16[128,896]{1,0:T(8,128)(2,1)S(1)}, bf16[128,896]{1,0:T(8,128)(2,1)S(1)}, u32[]{:S(2)}, u32[]{:S(2)}) collective-permute-start(bf16[128,896]{1,0:T(8,128)(2,1)S(1)} %add_convert_fusion.1), channel_id=1, source_target_pairs={{0,2},{1,3},{2,0},{3,1},{4,6},{5,7},{6,4},{7,5},{8,10},{9,11},{10,... | collective-permute-start | bytes 688136 | tf_op jit(solution)/shard_map/ppermute | solution.py:30
  20.9 0.0 collective-permute-done.4
  20.9 6.2 %collective-permute-done.6 = bf16[128,896]{1,0:T(8,128)(2,1)S(1)} collective-permute-done((bf16[128,896]{1,0:T(8,128)(2,1)S(1)}, bf16[128,896]{1,0:T(8,128)(2,1)S(1)}, u32[]{:S(2)}, u32[]{:S(2)}) %collective-permute-start.6) | collective-permute-done | bytes 229408 | tf_op jit(solution)/shard_map/ppermute | solution.py:30
  27.1 0.8 %add_convert_fusion = bf16[128,896]{1,0:T(8,128)(2,1)} fusion(bf16[128,896]{1,0:T(8,128)(2,1)S(1)} %collective-permute-done.6, f32[128,896]{1,0:T(8,128)S(1)} %get-tuple-element.65, bf16[128,896]{1,0:T(8,128)(2,1)S(1)} %collective-permute-done.4), kind=kLoop, calls=%fused_computation | loop fusion | flops 573440 | bytes 1146880 | tf_op jit(solution)/shard_map/convert_element_type | solution.py:347
  (1 shorter events, 0.0 us)
Async XLA Ops:
  0.0 11.6 %collective-permute-start = (bf16[576,128]{1,0:T(8,128)(2,1)}, bf16[576,128]{1,0:T(8,128)(2,1)S(1)}, u32[]{:S(2)}, u32[]{:S(2)}) collective-permute-start(bf16[576,128]{1,0:T(8,128)(2,1)} %bitcast.1), channel_id=1, source_target_pairs={{0,4},{1,13},{2,6},{3,15},{4,8},{5,1},{6,10},{7,3},{8,12},{9,5},{1... | collective-permute-start | bytes 442376 | tf_op jit(solution)/shard_map/ppermute | solution.py:30
  3.0 9.4 %collective-permute-start.1 = (bf16[576,128]{1,0:T(8,128)(2,1)}, bf16[576,128]{1,0:T(8,128)(2,1)S(1)}, u32[]{:S(2)}, u32[]{:S(2)}) collective-permute-start(bf16[576,128]{1,0:T(8,128)(2,1)} %bitcast.2), channel_id=1, source_target_pairs={{0,8},{1,1},{2,10},{3,3},{4,4},{5,13},{6,6},{7,15},{8,0},{9,9},{10... | collective-permute-start | bytes 442376 | tf_op jit(solution)/shard_map/ppermute | solution.py:30
  11.6 1.4 %collective-permute-start.2 = (bf16[576,128]{1,0:T(8,128)(2,1)S(1)}, bf16[576,128]{1,0:T(8,128)(2,1)S(1)}, u32[]{:S(2)}, u32[]{:S(2)}) collective-permute-start(bf16[576,128]{1,0:T(8,128)(2,1)S(1)} %collective-permute-done.block_ref), channel_id=1, source_target_pairs={{0,1},{1,0},{2,3},{3,2},{4,5},{5,4},{6,7},{7,6},{8,9},{9,8},{10,11... | collective-permute-start | bytes 442376 | tf_op jit(solution)/shard_map/ppermute | solution.py:30
  13.0 1.4 %collective-permute-start.3 = (bf16[576,128]{1,0:T(8,128)(2,1)S(1)}, bf16[576,128]{1,0:T(8,128)(2,1)S(1)}, u32[]{:S(2)}, u32[]{:S(2)}) collective-permute-start(bf16[576,128]{1,0:T(8,128)(2,1)S(1)} %collective-permute-done.1.refs_0_), channel_id=1, source_target_pairs={{0,1},{1,0},{2,3},{3,2},{4,5},{5,4},{6,7},{7,6},{8,9},{9,8},{10,11... | collective-permute-start | bytes 442376 | tf_op jit(solution)/shard_map/ppermute | solution.py:30
  17.7 1.6 %collective-permute-start.5 = (bf16[128,896]{1,0:T(8,128)(2,1)S(1)}, bf16[128,896]{1,0:T(8,128)(2,1)S(1)}, u32[]{:S(2)}, u32[]{:S(2)}) collective-permute-start(bf16[128,896]{1,0:T(8,128)(2,1)S(1)} %get-tuple-element.68), channel_id=1, source_target_pairs={{0,1},{1,0},{2,3},{3,2},{4,5},{5,4},{6,7},{7,6},{8,9},{9,8},{10,11... | collective-permute-start | bytes 688136 | tf_op jit(solution)/shard_map/ppermute | solution.py:30
  18.9 2.0 %collective-permute-start.4 = (bf16[128,896]{1,0:T(8,128)(2,1)S(1)}, bf16[128,896]{1,0:T(8,128)(2,1)S(1)}, u32[]{:S(2)}, u32[]{:S(2)}) collective-permute-start(bf16[128,896]{1,0:T(8,128)(2,1)S(1)} %get-tuple-element.66), channel_id=1, source_target_pairs={{0,1},{1,0},{2,3},{3,2},{4,5},{5,4},{6,7},{7,6},{8,9},{9,8},{10,11... | collective-permute-start | bytes 688136 | tf_op jit(solution)/shard_map/ppermute | solution.py:30
  19.4 7.7 %collective-permute-start.6 = (bf16[128,896]{1,0:T(8,128)(2,1)S(1)}, bf16[128,896]{1,0:T(8,128)(2,1)S(1)}, u32[]{:S(2)}, u32[]{:S(2)}) collective-permute-start(bf16[128,896]{1,0:T(8,128)(2,1)S(1)} %add_convert_fusion.1), channel_id=1, source_target_pairs={{0,2},{1,3},{2,0},{3,1},{4,6},{5,7},{6,4},{7,5},{8,10},{9,11},{10,... | collective-permute-start | bytes 688136 | tf_op jit(solution)/shard_map/ppermute | solution.py:30

commit v10 on v9

--- a/solution.py
+++ b/solution.py
@@ -75,11 +75,9 @@
 
 
 def prepare_kernel(half, *refs):
-    order_hbm, lens_hbm, queries_ref, block_ref, w_keys_ref, w_values_ref, w_out_ref = refs[:7]
-    padded_ref, bias_ref, keys_ref, values_ref, key_weight, value_weight = refs[7:13]
-    part_refs = refs[13 : 13 + PARTS]
-    order_ref, lens_ref, query_buffer, block_buffer, sems = refs[13 + PARTS :]
-    width = w_out_ref.shape[1] // PARTS
+    order_hbm, lens_hbm, queries_ref, block_ref, w_keys_ref, w_values_ref = refs[:6]
+    padded_ref, bias_ref, keys_ref, values_ref, key_weight, value_weight = refs[6:12]
+    order_ref, lens_ref, query_buffer, block_buffer, sems = refs[12:]
     heads = w_keys_ref.shape[1] // HEAD_DIM
     rows = 2 * half
     scalars = [
@@ -92,12 +90,7 @@
         pltpu.make_async_copy(w_keys_ref, key_weight, sems.at[4]),
         pltpu.make_async_copy(w_values_ref, value_weight, sems.at[5]),
     ]
-    later = []
-    for slot, part in enumerate(part_order()):
-        start = pl.multiple_of(part * width, 128)
-        source = w_out_ref.at[:, pl.ds(start, width)]
-        later.append(pltpu.make_async_copy(source, part_refs[slot], sems.at[6 + slot]))
-    for copy in scalars + [query_copy] + first + later:
+    for copy in scalars + [query_copy] + first:
         copy.start()
 
     for copy in scalars:
@@ -123,8 +116,6 @@
     for copy in first:
         copy.wait()
     expand(block_buffer[...], key_weight, value_weight, keys_ref, values_ref)
-    for copy in later:
-        copy.wait()
 
 
 def narrow_shape(*shape):
@@ -132,7 +123,7 @@
 
 
 def prepare(*operands):
-    order, lens, queries, block, w_keys, w_values, w_out = operands
+    order, lens, queries, block, w_keys, w_values = operands
     rows = queries.shape[0]
     count = lax.axis_size("ctx")
     heads = w_keys.shape[1] // HEAD_DIM
@@ -145,21 +136,20 @@
             narrow_shape(rows, heads * HEAD_DIM),
             narrow_shape(*w_keys.shape),
             narrow_shape(*w_values.shape),
-        ]
-        + [narrow_shape(w_out.shape[0], w_out.shape[1] // PARTS)] * PARTS,
-        in_specs=[HBM] * 7,
-        out_specs=[VMEM] * (6 + PARTS),
+        ],
+        in_specs=[HBM] * 6,
+        out_specs=[VMEM] * 6,
         scratch_shapes=[
             pltpu.SMEM(order.shape, jnp.int32),
             pltpu.SMEM(lens.shape, jnp.int32),
             pltpu.VMEM(queries.shape, jnp.bfloat16),
             pltpu.VMEM(block.shape, jnp.bfloat16),
-            pltpu.SemaphoreType.DMA((6 + PARTS,)),
+            pltpu.SemaphoreType.DMA((6,)),
         ],
         compiler_params=PARAMS,
         cost_estimate=pl.CostEstimate(
             flops=4 * rows * heads * HEAD_DIM * LATENT,
-            bytes_accessed=2 * (queries.size + w_keys.size + w_values.size + w_out.size),
+            bytes_accessed=2 * (queries.size + w_keys.size + w_values.size),
             transcendentals=0,
         ),
         name="prepare",
@@ -203,65 +193,104 @@
         target_ref[...] = block_ref[...]
 
 
-def attend_kernel(count, padded_ref, bias_ref, key_weight, value_weight, part_ref, *refs):
+def attend_kernel(count, padded_ref, bias_ref, key_weight, value_weight, w_out_ref, *refs):
     direct_ref, swapped_ref = refs[:2]
     keys, values = list(refs[2 : 2 + count]), list(refs[2 + count : 2 + 2 * count])
-    attended_ref, *shares, turned_ref, last_keys, last_values = refs[2 + 2 * count :]
+    attended_ref, share_ref, *parts = refs[2 + 2 * count : 3 + 2 * count + PARTS]
+    first_part, turned_ref, last_keys, last_values, scores_ref, weights_ref, sems = refs[
+        3 + 2 * count + PARTS :
+    ]
     rows = bias_ref.shape[0]
     heads = value_weight.shape[1] // HEAD_DIM
+    copies = []
+    for slot, part in enumerate(part_order()):
+        target = parts[slot - 1] if slot else first_part
+        start = pl.multiple_of(part * target.shape[1], 128)
+        source = w_out_ref.at[:, pl.ds(start, target.shape[1])]
+        copies.append(pltpu.make_async_copy(source, target, sems.at[slot]))
+        copies[-1].start()
     direct = (lax.axis_index("ctx") ^ lax.axis_index("head")) & 1 == 0
     take_if(turned_ref, direct_ref, direct)
     take_if(turned_ref, swapped_ref, jnp.logical_not(direct))
-    expand(turned_ref[...], key_weight, value_weight, last_keys, last_values)
     keys.append(last_keys)
     values.append(last_values)
+
+    def lines(head):
+        return slice(head * rows, (head + 1) * rows)
+
+    for start in range(0, count + 1, 2):
+        if start + 2 > count:
+            expand(turned_ref[...], key_weight, value_weight, last_keys, last_values)
+        chosen = keys[start : start + 2]
+        stretch = slice(start * rows, (start + len(chosen)) * rows)
+        for head in range(heads):
+            wide = slice(head * PADDED, (head + 1) * PADDED)
+            pair = jnp.concatenate([ref[:, wide] for ref in chosen], axis=0)
+            product = lax.dot_general(
+                padded_ref[:, wide], pair, NT, preferred_element_type=jnp.float32
+            )
+            scores_ref[lines(head), stretch] = product + bias_ref[:, stretch]
+    peaks = [jnp.max(scores_ref[lines(head), :], axis=1, keepdims=True) for head in range(heads)]
+    inverses = []
     for head in range(heads):
-        wide = slice(head * PADDED, (head + 1) * PADDED)
+        weights = jnp.exp2((scores_ref[lines(head), :] - peaks[head]) * jnp.float32(EXPONENT))
+        weights_ref[lines(head), :] = weights.astype(jnp.bfloat16)
+        inverses.append(1.0 / jnp.sum(weights, axis=1, keepdims=True))
+    for head in range(heads):
         columns = slice(head * HEAD_DIM, (head + 1) * HEAD_DIM)
-        query = padded_ref[:, wide]
-        pieces = []
-        for start in range(0, count + 1, 2):
-            pair = jnp.concatenate([ref[:, wide] for ref in keys[start : start + 2]], axis=0)
-            pieces.append(lax.dot_general(query, pair, NT, preferred_element_type=jnp.float32))
-        scores = jnp.concatenate(pieces, axis=1) + bias_ref[...]
-        peak = jnp.max(scores, axis=1, keepdims=True)
-        weights = jnp.exp2((scores - peak) * jnp.float32(EXPONENT))
-        inverse = 1.0 / jnp.sum(weights, axis=1, keepdims=True)
         value = jnp.dot(
-            weights.astype(jnp.bfloat16),
+            weights_ref[lines(head), :],
             jnp.concatenate([ref[:, columns] for ref in values], axis=0),
             preferred_element_type=jnp.float32,
         )
-        attended_ref[:, columns] = (value * inverse).astype(jnp.bfloat16)
-    project(attended_ref, part_ref, shares)
+        attended_ref[:, columns] = (value * inverses[head]).astype(jnp.bfloat16)
+    copies[0].wait()
+    project(attended_ref, first_part, [share_ref])
+    for copy in copies[1:]:
+        copy.wait()
 
 
 def share_shapes(rows, widths, kind):
     return [jax.ShapeDtypeStruct((rows, width), kind) for width in widths]
 
 
-def attend(padded, bias, weights, part, last, keys, values, widths):
+def attend(padded, bias, weights, w_out, last, keys, values):
     rows, key_count = bias.shape
     heads = values[0].shape[1] // HEAD_DIM
+    width = w_out.shape[1] // PARTS
+    part = narrow_shape(w_out.shape[0], width)
     flops = 4 * heads * rows * key_count * PADDED + 4 * rows * weights[0].size
     return pl.pallas_call(
         functools.partial(attend_kernel, len(keys)),
-        out_shape=share_shapes(rows, [heads * HEAD_DIM] + widths, jnp.bfloat16),
-        in_specs=[VMEM] * (7 + 2 * len(keys)),
-        out_specs=[VMEM] * (1 + len(widths)),
+        out_shape=[narrow_shape(rows, heads * HEAD_DIM), narrow_shape(rows, width)]
+        + [part] * (PARTS - 1),
+        in_specs=[VMEM] * 4 + [HBM] + [VMEM] * (2 + 2 * len(keys)),
+        out_specs=[VMEM] * (1 + PARTS),
         scratch_shapes=[
+            pltpu.VMEM(part.shape, jnp.bfloat16),
             pltpu.VMEM(last[0].shape, jnp.bfloat16),
             pltpu.VMEM(keys[0].shape, jnp.bfloat16),
             pltpu.VMEM(values[0].shape, jnp.bfloat16),
+            pltpu.VMEM((heads * rows, key_count), jnp.float32),
+            pltpu.VMEM((heads * rows, key_count), jnp.bfloat16),
+            pltpu.SemaphoreType.DMA((PARTS,)),
         ],
         compiler_params=PARAMS,
         cost_estimate=pl.CostEstimate(
-            flops=flops + 2 * rows * part.size,
-            bytes_accessed=2 * (weights[0].size + weights[1].size + part.size),
+            flops=flops + 2 * rows * w_out.size // PARTS,
+            bytes_accessed=2 * w_out.size,
             transcendentals=heads * rows * key_count,
         ),
         name="attend",
-    )(padded, bias, *weights, part, *last, *keys, *values)
+    )(
+        padded,
+        bias,
+        *weights,
+        pltpu.with_memory_space_constraint(w_out, pltpu.HBM),
+        *last,
+        *keys,
+        *values,
+    )
 
 
 def project_kernel(pieces, attended_ref, *refs):
@@ -305,7 +334,7 @@
     rows = queries.shape[0]
     width = w_out.shape[1] // PARTS
     block = latent.T
-    prepared = prepare(block_order, valid_lengths, queries, block, w_keys, w_values, w_out)
+    prepared = prepare(block_order, valid_lengths, queries, block, w_keys, w_values)
     narrow, wide = jnp.bfloat16, jnp.float32
 
     if not is_paired():
@@ -313,14 +342,13 @@
         for step in range(1, ctx_count):
             blocks.append(routed(block, lambda ctx, head: ((ctx + step) % ctx_count, head)))
         padded, bias, own_keys, own_values, *weights = prepared
-        weights, parts = weights[:2], weights[2:]
         expanded = [(own_keys, own_values)]
         expanded += [expand_block(piece, *weights) for piece in blocks[:-1]]
         keys, values = zip(*expanded)
         last = [blocks[-1], blocks[-1]]
-        attended, share = attend(padded, bias, weights, parts[0], last, keys, values, [width])
+        attended, share, *parts = attend(padded, bias, weights, w_out, last, keys, values)
         outs = [share_shapes(rows, [width], narrow)] * (PARTS - 1)
-        shares = [share] + list(project_parts(attended, parts[1:], outs))
+        shares = [share] + list(project_parts(attended, parts, outs))
         whole = jnp.concatenate(shares, axis=1)
         return lax.psum_scatter(whole, "head", scatter_dimension=1, tiled=True)
 
@@ -328,19 +356,19 @@
     far = routed(block, two_away)
     near, prepared = lax.optimization_barrier((near, prepared))
     padded, bias, own_keys, own_values, *weights = prepared
-    weights, parts = weights[:2], weights[2:]
     near_swapped = routed(near, other_core)
-    far, near_swapped = lax.optimization_barrier((far, near_swapped))
+    near_keys, near_values = expand_block(near, *weights)
+    far, near_keys = lax.optimization_barrier((far, near_keys))
     far_swapped = routed(far, other_core)
-    expanded = [(own_keys, own_values)]
-    expanded += [expand_block(piece, *weights) for piece in (near, near_swapped)]
-    keys, values = zip(*expanded)
+    other_keys, other_values = expand_block(near_swapped, *weights)
+    keys = [own_keys, near_keys, other_keys]
+    values = [own_values, near_values, other_values]
     last = [far, far_swapped]
 
-    attended, across = attend(padded, bias, weights, parts[0], last, keys, values, [width])
+    attended, across, *parts = attend(padded, bias, weights, w_out, last, keys, values)
     received = routed(across, other_core)
     outs = [share_shapes(rows, [width], kind) for kind in (wide, narrow, wide)]
-    far_part, beside, own = project_parts(attended, parts[1:], outs)
+    far_part, beside, own = project_parts(attended, parts, outs)
     far_part = (far_part + received.astype(wide)).astype(narrow)
     far_part = routed(far_part, other_chip).astype(wide)
     beside = routed(beside, other_core).astype(wide)

time: 28 us -> 27.4 us (0.979)
  Pallas kernels: 9.25 us -> 7.4 us
  waiting for transfers between devices: 7.81 us -> 9.22 us
    pallas_call x1, Pallas kernels: 4.08 us -> 2.26 us  [prepare(): pl.pallas_call(functools.partial(prepare_kernel, rows // 2), out_shape=[n...]
    ppermute x7, waiting for transfers between devices: 7.81 us -> 9.22 us  [routed(): return lax.ppermute(value, ('ctx', 'head'), pairs)]
  transfers between devices with their start and end apart: 7 -> 7, of which waited for: 4 -> 4; matrix products, arithmetic and copies ran while one was open for 0% -> 0% of each run, Pallas kernels for 22% -> 15%
where the time goes in v10:
time: 27.4 us; the launch traced here: 27.2 us
  starting transfers between devices  9.71 us (35%)
  waiting for transfers between devices  9.22 us (34%)
  Pallas kernels  7.4 us (27%)
  other arithmetic  0.8 us (3%)
    ppermute x7, starting transfers between devices, routed(): return lax.ppermute(value, ('ctx', 'head'), pairs)  9.71 us
    ppermute x7, waiting for transfers between devices, routed(): return lax.ppermute(value, ('ctx', 'head'), pairs)  9.22 us
    pallas_call x1, Pallas kernels, attend(): pl.pallas_call(functools.partial(attend_kernel, len(keys)), out_shape=[na...  3.21 us
    pallas_call x1, Pallas kernels, prepare(): pl.pallas_call(functools.partial(prepare_kernel, rows // 2), out_shape=[n...  2.26 us
    pallas_call x1, Pallas kernels, project_parts(): pl.pallas_call(functools.partial(project_kernel, [len(group) for group in...  0.99 us
    pallas_call x2, Pallas kernels, expand_block(): pl.pallas_call(expand_kernel, out_shape=[narrow_shape(rows, heads * PADDE...  0.93 us
    convert_element_type x1, other arithmetic, shards(): return (own + beside + far_part).astype(narrow)  0.76 us
  transfers between devices with their start and end apart: 7, of which 4 were waited for; matrix products, arithmetic and copies ran while one was open for 0% of the time, Pallas kernels for 15%

profile of v10, /device:TPU:0, one launch (start us, length us, event | category | flops | bytes accessed | tf_op | source)
XLA Modules:
  0.0 27.2 jit_solution(5752614261727935085)
XLA Ops:
  0.0 3.0 %collective-permute-start = (bf16[576,128]{1,0:T(8,128)(2,1)}, bf16[576,128]{1,0:T(8,128)(2,1)S(1)}, u32[]{:S(2)}, u32[]{:S(2)}) collective-permute-start(bf16[576,128]{1,0:T(8,128)(2,1)} %bitcast.1), channel_id=1, source_target_pairs={{0,4},{1,13},{2,6},{3,15},{4,8},{5,1},{6,10},{7,3},{8,12},{9,5},{1... | collective-permute-start | bytes 442376 | tf_op jit(solution)/shard_map/ppermute | solution.py:30
  3.0 4.5 %collective-permute-start.1 = (bf16[576,128]{1,0:T(8,128)(2,1)}, bf16[576,128]{1,0:T(8,128)(2,1)S(1)}, u32[]{:S(2)}, u32[]{:S(2)}) collective-permute-start(bf16[576,128]{1,0:T(8,128)(2,1)} %bitcast.2), channel_id=1, source_target_pairs={{0,8},{1,1},{2,10},{3,3},{4,4},{5,13},{6,6},{7,15},{8,0},{9,9},{10... | collective-permute-start | bytes 442376 | tf_op jit(solution)/shard_map/ppermute | solution.py:30
  7.5 2.3 %prepare.1 = (bf16[128,2048]{1,0:T(8,128)(2,1)S(1)}, f32[128,512]{1,0:T(8,128)S(1)}, bf16[128,2048]{1,0:T(8,128)(2,1)S(1)}, bf16[128,1024]{1,0:T(8,128)(2,1)S(1)...) custom-call(s32[8]{0:T(128)} %refs_0_.1, s32[8]{0:T(128)} %refs_1_.1, bf16[128,1536]{1,0:T(8,128)(2,1)} %refs_2_.1, ...), custom_call_target="tpu_custom_call" | custom-call | flops 268435456 | bytes 2490368 | tf_op jit(solution)/shard_map/prepare/pallas_call | solution.py:130
  9.8 0.2 collective-permute-done.block_ref
  9.9 0.0 collective-permute-start.3
  9.9 0.5 %expand_block.2 = (bf16[128,2048]{1,0:T(8,128)(2,1)S(1)}, bf16[128,1024]{1,0:T(8,128)(2,1)S(1)}) custom-call(bf16[576,128]{1,0:T(8,128)(2,1)S(1)} %collective-permute-done.block_ref, bf16[512,1024]{1,0:T(8,128)(2,1)S(1)} %get-tuple-element.40.w_keys_ref.key_weight, bf16[512,1024]{1,0:T(8,128)(2,1)S(1)} %get-tuple-element.41.w_values_ref.value_weight), custom_call_target="tpu_custom_call" | custom-call | flops 268435456 | bytes 1048576 | tf_op jit(solution)/shard_map/expand_block/pallas_call | solution.py:166
  10.4 2.0 %collective-permute-done.1.refs_0_ = bf16[576,128]{1,0:T(8,128)(2,1)S(1)} collective-permute-done((bf16[576,128]{1,0:T(8,128)(2,1)}, bf16[576,128]{1,0:T(8,128)(2,1)S(1)}, u32[]{:S(2)}, u32[]{:S(2)}) %collective-permute-start.1) | collective-permute-done | bytes 147488 | tf_op jit(solution)/shard_map/ppermute | solution.py:30
  12.4 0.0 collective-permute-start.2
  12.4 0.0 collective-permute-done.3.block_ref
  12.4 0.5 %expand_block.3 = (bf16[128,2048]{1,0:T(8,128)(2,1)S(1)}, bf16[128,1024]{1,0:T(8,128)(2,1)S(1)}) custom-call(bf16[576,128]{1,0:T(8,128)(2,1)S(1)} %collective-permute-done.3.block_ref, bf16[512,1024]{1,0:T(8,128)(2,1)S(1)} %get-tuple-element.40.w_keys_ref.key_weight, bf16[512,1024]{1,0:T(8,128)(2,1)S(1)} %get-tuple-element.41.w_values_ref.value_weight), custom_call_target="tpu_custom_call" | custom-call | flops 268435456 | bytes 1048576 | tf_op jit(solution)/shard_map/expand_block/pallas_call | solution.py:166
  12.9 0.9 %collective-permute-done.2.refs_1_ = bf16[576,128]{1,0:T(8,128)(2,1)S(1)} collective-permute-done((bf16[576,128]{1,0:T(8,128)(2,1)S(1)}, bf16[576,128]{1,0:T(8,128)(2,1)S(1)}, u32[]{:S(2)}, u32[]{:S(2)}) %collective-permute-start.2) | collective-permute-done | bytes 147488 | tf_op jit(solution)/shard_map/ppermute | solution.py:30
  13.8 3.2 %attend.1 = (bf16[128,1024]{1,0:T(8,128)(2,1)S(1)}, bf16[128,896]{1,0:T(8,128)(2,1)S(1)}, bf16[1024,896]{1,0:T(8,128)(2,1)S(1)}, bf16[1024,896]{1,0:T(8,128)(2,1)S(1)}, bf16[1024,896]{1,0:T(8,128)(2,1)S(1)}) custom-call(bf16[128,2048]{1,0:T(8,128)(2,1)S(1)} %get-tuple-element.38.padded_ref, f32[128,512]{1,0:T(8,128)S(1)} %get-tuple-element.39.bias_ref, ...), custom_call_target="tpu_custom_call" | custom-call | flops 1040187392 | bytes 7340032 | tf_op jit(solution)/shard_map/attend/pallas_call | solution.py:263
  17.0 0.2 collective-permute-start.5
  17.2 1.0 %project_parts.1 = (f32[128,896]{1,0:T(8,128)S(1)}, bf16[128,896]{1,0:T(8,128)(2,1)S(1)}, f32[128,896]{1,0:T(8,128)S(1)}) custom-call(bf16[128,1024]{1,0:T(8,128)(2,1)S(1)} %get-tuple-element.51.attended_ref, bf16[1024,896]{1,0:T(8,128)(2,1)S(1)} %get-tuple-element.52.refs_0_, bf16[1024,896]{1,0:T(8,128)(2,1)S(1)} %get-tuple-element.53.refs_1_, ...), custom_call_target="tpu_custom_call" | custom-call | flops 1024 | bytes 1024 | tf_op jit(solution)/shard_map/project_parts/pallas_call | solution.py:305
  18.2 0.4 %collective-permute-start.4 = (bf16[128,896]{1,0:T(8,128)(2,1)S(1)}, bf16[128,896]{1,0:T(8,128)(2,1)S(1)}, u32[]{:S(2)}, u32[]{:S(2)}) collective-permute-start(bf16[128,896]{1,0:T(8,128)(2,1)S(1)} %get-tuple-element.56), channel_id=1, source_target_pairs={{0,1},{1,0},{2,3},{3,2},{4,5},{5,4},{6,7},{7,6},{8,9},{9,8},{10,11... | collective-permute-start | bytes 688136 | tf_op jit(solution)/shard_map/ppermute | solution.py:30
  18.7 0.0 collective-permute-done.5
  18.7 1.6 %collective-permute-start.6 = (bf16[128,896]{1,0:T(8,128)(2,1)S(1)}, bf16[128,896]{1,0:T(8,128)(2,1)S(1)}, u32[]{:S(2)}, u32[]{:S(2)}) collective-permute-start(bf16[128,896]{1,0:T(8,128)(2,1)S(1)} %add_convert_fusion.1), channel_id=1, source_target_pairs={{0,2},{1,3},{2,0},{3,1},{4,6},{5,7},{6,4},{7,5},{8,10},{9,11},{10,... | collective-permute-start | bytes 688136 | tf_op jit(solution)/shard_map/ppermute | solution.py:30
  20.3 0.0 collective-permute-done.4
  20.3 6.2 %collective-permute-done.6 = bf16[128,896]{1,0:T(8,128)(2,1)S(1)} collective-permute-done((bf16[128,896]{1,0:T(8,128)(2,1)S(1)}, bf16[128,896]{1,0:T(8,128)(2,1)S(1)}, u32[]{:S(2)}, u32[]{:S(2)}) %collective-permute-start.6) | collective-permute-done | bytes 229408 | tf_op jit(solution)/shard_map/ppermute | solution.py:30
  26.4 0.8 %add_convert_fusion = bf16[128,896]{1,0:T(8,128)(2,1)} fusion(bf16[128,896]{1,0:T(8,128)(2,1)S(1)} %collective-permute-done.6, f32[128,896]{1,0:T(8,128)S(1)} %get-tuple-element.55, bf16[128,896]{1,0:T(8,128)(2,1)S(1)} %collective-permute-done.4), kind=kLoop, calls=%fused_computation | loop fusion | flops 573440 | bytes 1146880 | tf_op jit(solution)/shard_map/convert_element_type | solution.py:375
  (1 shorter events, 0.0 us)
Async XLA Ops:
  0.0 9.9 %collective-permute-start = (bf16[576,128]{1,0:T(8,128)(2,1)}, bf16[576,128]{1,0:T(8,128)(2,1)S(1)}, u32[]{:S(2)}, u32[]{:S(2)}) collective-permute-start(bf16[576,128]{1,0:T(8,128)(2,1)} %bitcast.1), channel_id=1, source_target_pairs={{0,4},{1,13},{2,6},{3,15},{4,8},{5,1},{6,10},{7,3},{8,12},{9,5},{1... | collective-permute-start | bytes 442376 | tf_op jit(solution)/shard_map/ppermute | solution.py:30
  3.0 9.4 %collective-permute-start.1 = (bf16[576,128]{1,0:T(8,128)(2,1)}, bf16[576,128]{1,0:T(8,128)(2,1)S(1)}, u32[]{:S(2)}, u32[]{:S(2)}) collective-permute-start(bf16[576,128]{1,0:T(8,128)(2,1)} %bitcast.2), channel_id=1, source_target_pairs={{0,8},{1,1},{2,10},{3,3},{4,4},{5,13},{6,6},{7,15},{8,0},{9,9},{10... | collective-permute-start | bytes 442376 | tf_op jit(solution)/shard_map/ppermute | solution.py:30
  9.9 2.5 %collective-permute-start.3 = (bf16[576,128]{1,0:T(8,128)(2,1)S(1)}, bf16[576,128]{1,0:T(8,128)(2,1)S(1)}, u32[]{:S(2)}, u32[]{:S(2)}) collective-permute-start(bf16[576,128]{1,0:T(8,128)(2,1)S(1)} %collective-permute-done.block_ref), channel_id=1, source_target_pairs={{0,1},{1,0},{2,3},{3,2},{4,5},{5,4},{6,7},{7,6},{8,9},{9,8},{10,11... | collective-permute-start | bytes 442376 | tf_op jit(solution)/shard_map/ppermute | solution.py:30
  12.4 1.4 %collective-permute-start.2 = (bf16[576,128]{1,0:T(8,128)(2,1)S(1)}, bf16[576,128]{1,0:T(8,128)(2,1)S(1)}, u32[]{:S(2)}, u32[]{:S(2)}) collective-permute-start(bf16[576,128]{1,0:T(8,128)(2,1)S(1)} %collective-permute-done.1.refs_0_), channel_id=1, source_target_pairs={{0,1},{1,0},{2,3},{3,2},{4,5},{5,4},{6,7},{7,6},{8,9},{9,8},{10,11... | collective-permute-start | bytes 442376 | tf_op jit(solution)/shard_map/ppermute | solution.py:30
  17.0 1.6 %collective-permute-start.5 = (bf16[128,896]{1,0:T(8,128)(2,1)S(1)}, bf16[128,896]{1,0:T(8,128)(2,1)S(1)}, u32[]{:S(2)}, u32[]{:S(2)}) collective-permute-start(bf16[128,896]{1,0:T(8,128)(2,1)S(1)} %get-tuple-element.58), channel_id=1, source_target_pairs={{0,1},{1,0},{2,3},{3,2},{4,5},{5,4},{6,7},{7,6},{8,9},{9,8},{10,11... | collective-permute-start | bytes 688136 | tf_op jit(solution)/shard_map/ppermute | solution.py:30
  18.2 2.0 %collective-permute-start.4 = (bf16[128,896]{1,0:T(8,128)(2,1)S(1)}, bf16[128,896]{1,0:T(8,128)(2,1)S(1)}, u32[]{:S(2)}, u32[]{:S(2)}) collective-permute-start(bf16[128,896]{1,0:T(8,128)(2,1)S(1)} %get-tuple-element.56), channel_id=1, source_target_pairs={{0,1},{1,0},{2,3},{3,2},{4,5},{5,4},{6,7},{7,6},{8,9},{9,8},{10,11... | collective-permute-start | bytes 688136 | tf_op jit(solution)/shard_map/ppermute | solution.py:30
  18.7 7.7 %collective-permute-start.6 = (bf16[128,896]{1,0:T(8,128)(2,1)S(1)}, bf16[128,896]{1,0:T(8,128)(2,1)S(1)}, u32[]{:S(2)}, u32[]{:S(2)}) collective-permute-start(bf16[128,896]{1,0:T(8,128)(2,1)S(1)} %add_convert_fusion.1), channel_id=1, source_target_pairs={{0,2},{1,3},{2,0},{3,1},{4,6},{5,7},{6,4},{7,5},{8,10},{9,11},{10,... | collective-permute-start | bytes 688136 | tf_op jit(solution)/shard_map/ppermute | solution.py:30

commit v11 on v10

--- a/solution.py
+++ b/solution.py
@@ -13,7 +13,6 @@
 QUERY = HEAD_DIM + ROPE
 PARTS = 4
 PADDED = 256
-NT = (((1,), (1,)), ((), ()))
 VMEM_BYTES = 32 * 1024 * 1024
 HIDDEN = -1e30
 
@@ -57,27 +56,26 @@
 EXPONENT = QUERY**-0.5 * 1.4426950408889634
 
 
-def expand(turned, w_keys_ref, w_values_ref, keys_ref, values_ref):
+def expand(turned, key_weight, value_weight, keys_ref, values_ref):
     rows = turned.shape[1]
-    latents = turned.T
-    compressed = latents[:, :LATENT]
-    rope = jnp.concatenate(
-        [latents[:, LATENT:], jnp.zeros((rows, PADDED - QUERY), jnp.bfloat16)], axis=1
-    )
-    nope = jnp.dot(compressed, w_keys_ref[...], preferred_element_type=jnp.float32)
+    compressed = turned[:LATENT, :]
+    rope = turned[LATENT:, :]
+    nothing = jnp.zeros((PADDED - QUERY, rows), jnp.bfloat16)
+    nope = jnp.dot(key_weight[...], compressed, preferred_element_type=jnp.float32)
     nope = nope.astype(jnp.bfloat16)
-    for head in range(w_keys_ref.shape[1] // HEAD_DIM):
-        middle = head * PADDED + HEAD_DIM
-        keys_ref[:, head * PADDED : middle] = nope[:, head * HEAD_DIM : (head + 1) * HEAD_DIM]
-        keys_ref[:, middle : (head + 1) * PADDED] = rope
-    values = jnp.dot(compressed, w_values_ref[...], preferred_element_type=jnp.float32)
+    for head in range(key_weight.shape[0] // HEAD_DIM):
+        start = head * PADDED
+        keys_ref[start : start + HEAD_DIM, :] = nope[head * HEAD_DIM : (head + 1) * HEAD_DIM, :]
+        keys_ref[start + HEAD_DIM : start + QUERY, :] = rope
+        keys_ref[start + QUERY : start + PADDED, :] = nothing
+    values = jnp.dot(compressed.T, value_weight[...], preferred_element_type=jnp.float32)
     values_ref[...] = values.astype(jnp.bfloat16)
 
 
 def prepare_kernel(half, *refs):
     order_hbm, lens_hbm, queries_ref, block_ref, w_keys_ref, w_values_ref = refs[:6]
     padded_ref, bias_ref, keys_ref, values_ref, key_weight, value_weight = refs[6:12]
-    order_ref, lens_ref, query_buffer, block_buffer, sems = refs[12:]
+    order_ref, lens_ref, query_buffer, block_buffer, weight_buffer, sems = refs[12:]
     heads = w_keys_ref.shape[1] // HEAD_DIM
     rows = 2 * half
     scalars = [
@@ -87,7 +85,7 @@
     query_copy = pltpu.make_async_copy(queries_ref, query_buffer, sems.at[2])
     first = [
         pltpu.make_async_copy(block_ref, block_buffer, sems.at[3]),
-        pltpu.make_async_copy(w_keys_ref, key_weight, sems.at[4]),
+        pltpu.make_async_copy(w_keys_ref, weight_buffer, sems.at[4]),
         pltpu.make_async_copy(w_values_ref, value_weight, sems.at[5]),
     ]
     for copy in scalars + [query_copy] + first:
@@ -115,6 +113,7 @@
         )
     for copy in first:
         copy.wait()
+    key_weight[...] = weight_buffer[...].T
     expand(block_buffer[...], key_weight, value_weight, keys_ref, values_ref)
 
 
@@ -132,9 +131,9 @@
         out_shape=[
             narrow_shape(rows, heads * PADDED),
             jax.ShapeDtypeStruct((rows, count * rows), jnp.float32),
-            narrow_shape(rows, heads * PADDED),
+            narrow_shape(heads * PADDED, rows),
             narrow_shape(rows, heads * HEAD_DIM),
-            narrow_shape(*w_keys.shape),
+            narrow_shape(*w_keys.shape[::-1]),
             narrow_shape(*w_values.shape),
         ],
         in_specs=[HBM] * 6,
@@ -144,6 +143,7 @@
             pltpu.SMEM(lens.shape, jnp.int32),
             pltpu.VMEM(queries.shape, jnp.bfloat16),
             pltpu.VMEM(block.shape, jnp.bfloat16),
+            pltpu.VMEM(w_keys.shape, jnp.bfloat16),
             pltpu.SemaphoreType.DMA((6,)),
         ],
         compiler_params=PARAMS,
@@ -156,24 +156,26 @@
     )(*[pltpu.with_memory_space_constraint(item, pltpu.HBM) for item in operands])
 
 
-def expand_kernel(block_ref, w_keys_ref, w_values_ref, keys_ref, values_ref):
-    expand(block_ref[...], w_keys_ref, w_values_ref, keys_ref, values_ref)
-
-
-def expand_block(block, w_keys, w_values):
+def expand_kernel(block_ref, key_weight, value_weight, keys_ref, values_ref):
+    expand(block_ref[...], key_weight, value_weight, keys_ref, values_ref)
+
+
+def expand_block(block, key_weight, value_weight):
     rows = block.shape[1]
-    heads = w_keys.shape[1] // HEAD_DIM
+    heads = value_weight.shape[1] // HEAD_DIM
     return pl.pallas_call(
         expand_kernel,
-        out_shape=[narrow_shape(rows, heads * PADDED), narrow_shape(rows, heads * HEAD_DIM)],
+        out_shape=[narrow_shape(heads * PADDED, rows), narrow_shape(rows, heads * HEAD_DIM)],
         in_specs=[VMEM] * 3,
         out_specs=[VMEM] * 2,
         compiler_params=PARAMS,
         cost_estimate=pl.CostEstimate(
-            flops=4 * rows * w_keys.size, bytes_accessed=2 * w_keys.size, transcendentals=0
+            flops=4 * rows * value_weight.size,
+            bytes_accessed=2 * value_weight.size,
+            transcendentals=0,
         ),
         name="expand_block",
-    )(block, w_keys, w_values)
+    )(block, key_weight, value_weight)
 
 
 def project(attended_ref, part_ref, share_refs):
@@ -225,10 +227,8 @@
         stretch = slice(start * rows, (start + len(chosen)) * rows)
         for head in range(heads):
             wide = slice(head * PADDED, (head + 1) * PADDED)
-            pair = jnp.concatenate([ref[:, wide] for ref in chosen], axis=0)
-            product = lax.dot_general(
-                padded_ref[:, wide], pair, NT, preferred_element_type=jnp.float32
-            )
+            pair = jnp.concatenate([ref[wide, :] for ref in chosen], axis=1)
+            product = jnp.dot(padded_ref[:, wide], pair, preferred_element_type=jnp.float32)
             scores_ref[lines(head), stretch] = product + bias_ref[:, stretch]
     peaks = [jnp.max(scores_ref[lines(head), :], axis=1, keepdims=True) for head in range(heads)]
     inverses = []

time: 27.4 us -> 27.4 us (level)
  waiting for transfers between devices: 9.22 us -> 8.68 us
  Pallas kernels: 7.4 us -> 7.85 us
    ppermute x7, waiting for transfers between devices: 9.22 us -> 8.68 us  [routed(): return lax.ppermute(value, ('ctx', 'head'), pairs)]
    pallas_call x2, Pallas kernels: 0.93 us -> 1.23 us  [expand_block(): pl.pallas_call(expand_kernel, out_shape=[narrow_shape(heads * PADDED, row...]
  transfers between devices with their start and end apart: 7 -> 7, of which waited for: 4 -> 3; matrix products, arithmetic and copies ran while one was open for 0% -> 0% of each run, Pallas kernels for 15% -> 17%
where the time goes in v11:
time: 27.4 us; the launch traced here: 27.2 us
  starting transfers between devices  9.78 us (36%)
  waiting for transfers between devices  8.68 us (32%)
  Pallas kernels  7.85 us (29%)
  other arithmetic  0.8 us (3%)
    ppermute x7, starting transfers between devices, routed(): return lax.ppermute(value, ('ctx', 'head'), pairs)  9.78 us
    ppermute x7, waiting for transfers between devices, routed(): return lax.ppermute(value, ('ctx', 'head'), pairs)  8.68 us
    pallas_call x1, Pallas kernels, attend(): pl.pallas_call(functools.partial(attend_kernel, len(keys)), out_shape=[na...  3.21 us
    pallas_call x1, Pallas kernels, prepare(): pl.pallas_call(functools.partial(prepare_kernel, rows // 2), out_shape=[n...  2.42 us
    pallas_call x2, Pallas kernels, expand_block(): pl.pallas_call(expand_kernel, out_shape=[narrow_shape(heads * PADDED, row...  1.23 us
    pallas_call x1, Pallas kernels, project_parts(): pl.pallas_call(functools.partial(project_kernel, [len(group) for group in...  0.99 us
    convert_element_type x1, other arithmetic, shards(): return (own + beside + far_part).astype(narrow)  0.76 us
  transfers between devices with their start and end apart: 7, of which 3 were waited for; matrix products, arithmetic and copies ran while one was open for 0% of the time, Pallas kernels for 17%

profile of v11, /device:TPU:0, one launch (start us, length us, event | category | flops | bytes accessed | tf_op | source)
XLA Modules:
  0.0 27.2 jit_solution(5364878137162155039)
XLA Ops:
  0.0 3.0 %collective-permute-start = (bf16[576,128]{1,0:T(8,128)(2,1)}, bf16[576,128]{1,0:T(8,128)(2,1)S(1)}, u32[]{:S(2)}, u32[]{:S(2)}) collective-permute-start(bf16[576,128]{1,0:T(8,128)(2,1)} %bitcast.1), channel_id=1, source_target_pairs={{0,4},{1,13},{2,6},{3,15},{4,8},{5,1},{6,10},{7,3},{8,12},{9,5},{1... | collective-permute-start | bytes 442376 | tf_op jit(solution)/shard_map/ppermute | solution.py:29
  3.0 4.5 %collective-permute-start.1 = (bf16[576,128]{1,0:T(8,128)(2,1)}, bf16[576,128]{1,0:T(8,128)(2,1)S(1)}, u32[]{:S(2)}, u32[]{:S(2)}) collective-permute-start(bf16[576,128]{1,0:T(8,128)(2,1)} %bitcast.2), channel_id=1, source_target_pairs={{0,8},{1,1},{2,10},{3,3},{4,4},{5,13},{6,6},{7,15},{8,0},{9,9},{10... | collective-permute-start | bytes 442376 | tf_op jit(solution)/shard_map/ppermute | solution.py:29
  7.5 2.4 %prepare.1 = (bf16[128,2048]{1,0:T(8,128)(2,1)S(1)}, f32[128,512]{1,0:T(8,128)S(1)}, bf16[2048,128]{1,0:T(8,128)(2,1)S(1)}, bf16[128,1024]{1,0:T(8,128)(2,1)S(1)...) custom-call(s32[8]{0:T(128)} %refs_0_.1, s32[8]{0:T(128)} %refs_1_.1, bf16[128,1536]{1,0:T(8,128)(2,1)} %refs_2_.1, ...), custom_call_target="tpu_custom_call" | custom-call | flops 268435456 | bytes 2490368 | tf_op jit(solution)/shard_map/prepare/pallas_call | solution.py:129
  9.9 0.0 collective-permute-done.block_ref
  10.0 0.1 collective-permute-start.3
  10.0 0.6 %expand_block.2 = (bf16[2048,128]{1,0:T(8,128)(2,1)S(1)}, bf16[128,1024]{1,0:T(8,128)(2,1)S(1)}) custom-call(bf16[576,128]{1,0:T(8,128)(2,1)S(1)} %collective-permute-done.block_ref, bf16[1024,512]{1,0:T(8,128)(2,1)S(1)} %get-tuple-element.40.key_weight, bf16[512,1024]{1,0:T(8,128)(2,1)S(1)} %get-tuple-element.41.value_weight), custom_call_target="tpu_custom_call" | custom-call | flops 268435456 | bytes 1048576 | tf_op jit(solution)/shard_map/expand_block/pallas_call | solution.py:166
  10.7 1.8 %collective-permute-done.1.refs_0_ = bf16[576,128]{1,0:T(8,128)(2,1)S(1)} collective-permute-done((bf16[576,128]{1,0:T(8,128)(2,1)}, bf16[576,128]{1,0:T(8,128)(2,1)S(1)}, u32[]{:S(2)}, u32[]{:S(2)}) %collective-permute-start.1) | collective-permute-done | bytes 147488 | tf_op jit(solution)/shard_map/ppermute | solution.py:29
  12.4 0.0 collective-permute-start.2
  12.4 0.0 collective-permute-done.3.block_ref
  12.4 0.6 %expand_block.3 = (bf16[2048,128]{1,0:T(8,128)(2,1)S(1)}, bf16[128,1024]{1,0:T(8,128)(2,1)S(1)}) custom-call(bf16[576,128]{1,0:T(8,128)(2,1)S(1)} %collective-permute-done.3.block_ref, bf16[1024,512]{1,0:T(8,128)(2,1)S(1)} %get-tuple-element.40.key_weight, bf16[512,1024]{1,0:T(8,128)(2,1)S(1)} %get-tuple-element.41.value_weight), custom_call_target="tpu_custom_call" | custom-call | flops 268435456 | bytes 1048576 | tf_op jit(solution)/shard_map/expand_block/pallas_call | solution.py:166
  13.1 0.7 %collective-permute-done.2.refs_1_ = bf16[576,128]{1,0:T(8,128)(2,1)S(1)} collective-permute-done((bf16[576,128]{1,0:T(8,128)(2,1)S(1)}, bf16[576,128]{1,0:T(8,128)(2,1)S(1)}, u32[]{:S(2)}, u32[]{:S(2)}) %collective-permute-start.2) | collective-permute-done | bytes 147488 | tf_op jit(solution)/shard_map/ppermute | solution.py:29
  13.8 3.2 %attend.1 = (bf16[128,1024]{1,0:T(8,128)(2,1)S(1)}, bf16[128,896]{1,0:T(8,128)(2,1)S(1)}, bf16[1024,896]{1,0:T(8,128)(2,1)S(1)}, bf16[1024,896]{1,0:T(8,128)(2,1)S(1)}, bf16[1024,896]{1,0:T(8,128)(2,1)S(1)}) custom-call(bf16[128,2048]{1,0:T(8,128)(2,1)S(1)} %get-tuple-element.38.padded_ref, f32[128,512]{1,0:T(8,128)S(1)} %get-tuple-element.39.bias_ref, ...), custom_call_target="tpu_custom_call" | custom-call | flops 1040187392 | bytes 7340032 | tf_op jit(solution)/shard_map/attend/pallas_call | solution.py:263
  17.0 0.2 collective-permute-start.5
  17.2 1.0 %project_parts.1 = (f32[128,896]{1,0:T(8,128)S(1)}, bf16[128,896]{1,0:T(8,128)(2,1)S(1)}, f32[128,896]{1,0:T(8,128)S(1)}) custom-call(bf16[128,1024]{1,0:T(8,128)(2,1)S(1)} %get-tuple-element.51.attended_ref, bf16[1024,896]{1,0:T(8,128)(2,1)S(1)} %get-tuple-element.52.refs_0_, bf16[1024,896]{1,0:T(8,128)(2,1)S(1)} %get-tuple-element.53.refs_1_, ...), custom_call_target="tpu_custom_call" | custom-call | flops 1024 | bytes 1024 | tf_op jit(solution)/shard_map/project_parts/pallas_call | solution.py:305
  18.2 0.4 %collective-permute-start.4 = (bf16[128,896]{1,0:T(8,128)(2,1)S(1)}, bf16[128,896]{1,0:T(8,128)(2,1)S(1)}, u32[]{:S(2)}, u32[]{:S(2)}) collective-permute-start(bf16[128,896]{1,0:T(8,128)(2,1)S(1)} %get-tuple-element.56), channel_id=1, source_target_pairs={{0,1},{1,0},{2,3},{3,2},{4,5},{5,4},{6,7},{7,6},{8,9},{9,8},{10,11... | collective-permute-start | bytes 688136 | tf_op jit(solution)/shard_map/ppermute | solution.py:29
  18.7 0.0 collective-permute-done.5
  18.7 1.6 %collective-permute-start.6 = (bf16[128,896]{1,0:T(8,128)(2,1)S(1)}, bf16[128,896]{1,0:T(8,128)(2,1)S(1)}, u32[]{:S(2)}, u32[]{:S(2)}) collective-permute-start(bf16[128,896]{1,0:T(8,128)(2,1)S(1)} %add_convert_fusion.1), channel_id=1, source_target_pairs={{0,2},{1,3},{2,0},{3,1},{4,6},{5,7},{6,4},{7,5},{8,10},{9,11},{10,... | collective-permute-start | bytes 688136 | tf_op jit(solution)/shard_map/ppermute | solution.py:29
  20.3 0.0 collective-permute-done.4
  20.3 6.2 %collective-permute-done.6 = bf16[128,896]{1,0:T(8,128)(2,1)S(1)} collective-permute-done((bf16[128,896]{1,0:T(8,128)(2,1)S(1)}, bf16[128,896]{1,0:T(8,128)(2,1)S(1)}, u32[]{:S(2)}, u32[]{:S(2)}) %collective-permute-start.6) | collective-permute-done | bytes 229408 | tf_op jit(solution)/shard_map/ppermute | solution.py:29
  26.4 0.8 %add_convert_fusion = bf16[128,896]{1,0:T(8,128)(2,1)} fusion(bf16[128,896]{1,0:T(8,128)(2,1)S(1)} %collective-permute-done.6, f32[128,896]{1,0:T(8,128)S(1)} %get-tuple-element.55, bf16[128,896]{1,0:T(8,128)(2,1)S(1)} %collective-permute-done.4), kind=kLoop, calls=%fused_computation | loop fusion | flops 573440 | bytes 1146880 | tf_op jit(solution)/shard_map/convert_element_type | solution.py:375
  (1 shorter events, 0.0 us)
Async XLA Ops:
  0.0 10.0 %collective-permute-start = (bf16[576,128]{1,0:T(8,128)(2,1)}, bf16[576,128]{1,0:T(8,128)(2,1)S(1)}, u32[]{:S(2)}, u32[]{:S(2)}) collective-permute-start(bf16[576,128]{1,0:T(8,128)(2,1)} %bitcast.1), channel_id=1, source_target_pairs={{0,4},{1,13},{2,6},{3,15},{4,8},{5,1},{6,10},{7,3},{8,12},{9,5},{1... | collective-permute-start | bytes 442376 | tf_op jit(solution)/shard_map/ppermute | solution.py:29
  3.0 9.4 %collective-permute-start.1 = (bf16[576,128]{1,0:T(8,128)(2,1)}, bf16[576,128]{1,0:T(8,128)(2,1)S(1)}, u32[]{:S(2)}, u32[]{:S(2)}) collective-permute-start(bf16[576,128]{1,0:T(8,128)(2,1)} %bitcast.2), channel_id=1, source_target_pairs={{0,8},{1,1},{2,10},{3,3},{4,4},{5,13},{6,6},{7,15},{8,0},{9,9},{10... | collective-permute-start | bytes 442376 | tf_op jit(solution)/shard_map/ppermute | solution.py:29
  10.0 2.5 %collective-permute-start.3 = (bf16[576,128]{1,0:T(8,128)(2,1)S(1)}, bf16[576,128]{1,0:T(8,128)(2,1)S(1)}, u32[]{:S(2)}, u32[]{:S(2)}) collective-permute-start(bf16[576,128]{1,0:T(8,128)(2,1)S(1)} %collective-permute-done.block_ref), channel_id=1, source_target_pairs={{0,1},{1,0},{2,3},{3,2},{4,5},{5,4},{6,7},{7,6},{8,9},{9,8},{10,11... | collective-permute-start | bytes 442376 | tf_op jit(solution)/shard_map/ppermute | solution.py:29
  12.4 1.4 %collective-permute-start.2 = (bf16[576,128]{1,0:T(8,128)(2,1)S(1)}, bf16[576,128]{1,0:T(8,128)(2,1)S(1)}, u32[]{:S(2)}, u32[]{:S(2)}) collective-permute-start(bf16[576,128]{1,0:T(8,128)(2,1)S(1)} %collective-permute-done.1.refs_0_), channel_id=1, source_target_pairs={{0,1},{1,0},{2,3},{3,2},{4,5},{5,4},{6,7},{7,6},{8,9},{9,8},{10,11... | collective-permute-start | bytes 442376 | tf_op jit(solution)/shard_map/ppermute | solution.py:29
  17.0 1.6 %collective-permute-start.5 = (bf16[128,896]{1,0:T(8,128)(2,1)S(1)}, bf16[128,896]{1,0:T(8,128)(2,1)S(1)}, u32[]{:S(2)}, u32[]{:S(2)}) collective-permute-start(bf16[128,896]{1,0:T(8,128)(2,1)S(1)} %get-tuple-element.58), channel_id=1, source_target_pairs={{0,1},{1,0},{2,3},{3,2},{4,5},{5,4},{6,7},{7,6},{8,9},{9,8},{10,11... | collective-permute-start | bytes 688136 | tf_op jit(solution)/shard_map/ppermute | solution.py:29
  18.2 2.0 %collective-permute-start.4 = (bf16[128,896]{1,0:T(8,128)(2,1)S(1)}, bf16[128,896]{1,0:T(8,128)(2,1)S(1)}, u32[]{:S(2)}, u32[]{:S(2)}) collective-permute-start(bf16[128,896]{1,0:T(8,128)(2,1)S(1)} %get-tuple-element.56), channel_id=1, source_target_pairs={{0,1},{1,0},{2,3},{3,2},{4,5},{5,4},{6,7},{7,6},{8,9},{9,8},{10,11... | collective-permute-start | bytes 688136 | tf_op jit(solution)/shard_map/ppermute | solution.py:29
  18.7 7.7 %collective-permute-start.6 = (bf16[128,896]{1,0:T(8,128)(2,1)S(1)}, bf16[128,896]{1,0:T(8,128)(2,1)S(1)}, u32[]{:S(2)}, u32[]{:S(2)}) collective-permute-start(bf16[128,896]{1,0:T(8,128)(2,1)S(1)} %add_convert_fusion.1), channel_id=1, source_target_pairs={{0,2},{1,3},{2,0},{3,1},{4,6},{5,7},{6,4},{7,5},{8,10},{9,11},{10,... | collective-permute-start | bytes 688136 | tf_op jit(solution)/shard_map/ppermute | solution.py:29

commit v12 on v11

--- a/solution.py
+++ b/solution.py
@@ -49,6 +49,13 @@
     return list(range(PARTS))
 
 
+def part_copy(w_out_ref, slot, target, sem):
+    width = target.shape[1]
+    start = pl.multiple_of(part_order()[slot] * width, 128)
+    return pltpu.make_async_copy(w_out_ref.at[:, pl.ds(start, width)], target, sem)
+
+
+EARLY = 2
 VMEM = pl.BlockSpec(memory_space=pltpu.VMEM)
 HBM = pl.BlockSpec(memory_space=pltpu.HBM)
 PARAMS = pltpu.CompilerParams(vmem_limit_bytes=VMEM_BYTES)
@@ -73,9 +80,9 @@
 
 
 def prepare_kernel(half, *refs):
-    order_hbm, lens_hbm, queries_ref, block_ref, w_keys_ref, w_values_ref = refs[:6]
-    padded_ref, bias_ref, keys_ref, values_ref, key_weight, value_weight = refs[6:12]
-    order_ref, lens_ref, query_buffer, block_buffer, weight_buffer, sems = refs[12:]
+    order_hbm, lens_hbm, queries_ref, block_ref, w_keys_ref, w_values_ref, w_out_ref = refs[:7]
+    padded_ref, bias_ref, keys_ref, values_ref, key_weight, value_weight, *parts = refs[7 : 13 + EARLY]
+    order_ref, lens_ref, query_buffer, block_buffer, weight_buffer, sems = refs[13 + EARLY :]
     heads = w_keys_ref.shape[1] // HEAD_DIM
     rows = 2 * half
     scalars = [
@@ -88,7 +95,10 @@
         pltpu.make_async_copy(w_keys_ref, weight_buffer, sems.at[4]),
         pltpu.make_async_copy(w_values_ref, value_weight, sems.at[5]),
     ]
-    for copy in scalars + [query_copy] + first:
+    later = [
+        part_copy(w_out_ref, slot, part, sems.at[6 + slot]) for slot, part in enumerate(parts)
+    ]
+    for copy in scalars + [query_copy] + first + later:
         copy.start()
 
     for copy in scalars:
@@ -115,6 +125,8 @@
         copy.wait()
     key_weight[...] = weight_buffer[...].T
     expand(block_buffer[...], key_weight, value_weight, keys_ref, values_ref)
+    for copy in later:
+        copy.wait()
 
 
 def narrow_shape(*shape):
@@ -122,7 +134,7 @@
 
 
 def prepare(*operands):
-    order, lens, queries, block, w_keys, w_values = operands
+    order, lens, queries, block, w_keys, w_values, w_out = operands
     rows = queries.shape[0]
     count = lax.axis_size("ctx")
     heads = w_keys.shape[1] // HEAD_DIM
@@ -135,21 +147,22 @@
             narrow_shape(rows, heads * HEAD_DIM),
             narrow_shape(*w_keys.shape[::-1]),
             narrow_shape(*w_values.shape),
-        ],
-        in_specs=[HBM] * 6,
-        out_specs=[VMEM] * 6,
+        ]
+        + [narrow_shape(w_out.shape[0], w_out.shape[1] // PARTS)] * EARLY,
+        in_specs=[HBM] * 7,
+        out_specs=[VMEM] * (6 + EARLY),
         scratch_shapes=[
             pltpu.SMEM(order.shape, jnp.int32),
             pltpu.SMEM(lens.shape, jnp.int32),
             pltpu.VMEM(queries.shape, jnp.bfloat16),
             pltpu.VMEM(block.shape, jnp.bfloat16),
             pltpu.VMEM(w_keys.shape, jnp.bfloat16),
-            pltpu.SemaphoreType.DMA((6,)),
+            pltpu.SemaphoreType.DMA((6 + EARLY,)),
         ],
         compiler_params=PARAMS,
         cost_estimate=pl.CostEstimate(
             flops=4 * rows * heads * HEAD_DIM * LATENT,
-            bytes_accessed=2 * (queries.size + w_keys.size + w_values.size),
+            bytes_accessed=2 * (queries.size + w_keys.size + w_values.size) + w_out.size,
             transcendentals=0,
         ),
         name="prepare",
@@ -195,22 +208,21 @@
         target_ref[...] = block_ref[...]
 
 
-def attend_kernel(count, padded_ref, bias_ref, key_weight, value_weight, w_out_ref, *refs):
+def attend_kernel(count, padded_ref, bias_ref, key_weight, value_weight, part_ref, w_out_ref, *refs):
     direct_ref, swapped_ref = refs[:2]
     keys, values = list(refs[2 : 2 + count]), list(refs[2 + count : 2 + 2 * count])
-    attended_ref, share_ref, *parts = refs[2 + 2 * count : 3 + 2 * count + PARTS]
-    first_part, turned_ref, last_keys, last_values, scores_ref, weights_ref, sems = refs[
-        3 + 2 * count + PARTS :
+    attended_ref, share_ref, *parts = refs[2 + 2 * count : 4 + 2 * count + PARTS - EARLY]
+    turned_ref, last_keys, last_values, scores_ref, weights_ref, sems = refs[
+        4 + 2 * count + PARTS - EARLY :
     ]
     rows = bias_ref.shape[0]
     heads = value_weight.shape[1] // HEAD_DIM
-    copies = []
-    for slot, part in enumerate(part_order()):
-        target = parts[slot - 1] if slot else first_part
-        start = pl.multiple_of(part * target.shape[1], 128)
-        source = w_out_ref.at[:, pl.ds(start, target.shape[1])]
-        copies.append(pltpu.make_async_copy(source, target, sems.at[slot]))
-        copies[-1].start()
+    copies = [
+        part_copy(w_out_ref, EARLY + index, part, sems.at[index])
+        for index, part in enumerate(parts)
+    ]
+    for copy in copies:
+        copy.start()
     direct = (lax.axis_index("ctx") ^ lax.axis_index("head")) & 1 == 0
     take_if(turned_ref, direct_ref, direct)
     take_if(turned_ref, swapped_ref, jnp.logical_not(direct))
@@ -244,9 +256,8 @@
             preferred_element_type=jnp.float32,
         )
         attended_ref[:, columns] = (value * inverses[head]).astype(jnp.bfloat16)
-    copies[0].wait()
-    project(attended_ref, first_part, [share_ref])
-    for copy in copies[1:]:
+    project(attended_ref, part_ref, [share_ref])
+    for copy in copies:
         copy.wait()
 
 
@@ -254,26 +265,23 @@
     return [jax.ShapeDtypeStruct((rows, width), kind) for width in widths]
 
 
-def attend(padded, bias, weights, w_out, last, keys, values):
+def attend(padded, bias, weights, part, w_out, last, keys, values):
     rows, key_count = bias.shape
     heads = values[0].shape[1] // HEAD_DIM
-    width = w_out.shape[1] // PARTS
-    part = narrow_shape(w_out.shape[0], width)
     flops = 4 * heads * rows * key_count * PADDED + 4 * rows * weights[0].size
     return pl.pallas_call(
         functools.partial(attend_kernel, len(keys)),
-        out_shape=[narrow_shape(rows, heads * HEAD_DIM), narrow_shape(rows, width)]
-        + [part] * (PARTS - 1),
-        in_specs=[VMEM] * 4 + [HBM] + [VMEM] * (2 + 2 * len(keys)),
-        out_specs=[VMEM] * (1 + PARTS),
+        out_shape=[narrow_shape(rows, heads * HEAD_DIM), narrow_shape(rows, part.shape[1])]
+        + [narrow_shape(*part.shape)] * (PARTS - EARLY),
+        in_specs=[VMEM] * 5 + [HBM] + [VMEM] * (2 + 2 * len(keys)),
+        out_specs=[VMEM] * (2 + PARTS - EARLY),
         scratch_shapes=[
-            pltpu.VMEM(part.shape, jnp.bfloat16),
             pltpu.VMEM(last[0].shape, jnp.bfloat16),
             pltpu.VMEM(keys[0].shape, jnp.bfloat16),
             pltpu.VMEM(values[0].shape, jnp.bfloat16),
             pltpu.VMEM((heads * rows, key_count), jnp.float32),
             pltpu.VMEM((heads * rows, key_count), jnp.bfloat16),
-            pltpu.SemaphoreType.DMA((PARTS,)),
+            pltpu.SemaphoreType.DMA((PARTS - EARLY,)),
         ],
         compiler_params=PARAMS,
         cost_estimate=pl.CostEstimate(
@@ -286,6 +294,7 @@
         padded,
         bias,
         *weights,
+        part,
         pltpu.with_memory_space_constraint(w_out, pltpu.HBM),
         *last,
         *keys,
@@ -334,28 +343,30 @@
     rows = queries.shape[0]
     width = w_out.shape[1] // PARTS
     block = latent.T
-    prepared = prepare(block_order, valid_lengths, queries, block, w_keys, w_values)
+    prepared = prepare(block_order, valid_lengths, queries, block, w_keys, w_values, w_out)
     narrow, wide = jnp.bfloat16, jnp.float32
 
     if not is_paired():
         blocks = []
         for step in range(1, ctx_count):
             blocks.append(routed(block, lambda ctx, head: ((ctx + step) % ctx_count, head)))
-        padded, bias, own_keys, own_values, *weights = prepared
+        padded, bias, own_keys, own_values, *weights, part, second = prepared
         expanded = [(own_keys, own_values)]
         expanded += [expand_block(piece, *weights) for piece in blocks[:-1]]
         keys, values = zip(*expanded)
         last = [blocks[-1], blocks[-1]]
-        attended, share, *parts = attend(padded, bias, weights, w_out, last, keys, values)
+        attended, share, *parts = attend(
+        padded, bias, weights, part, w_out, last, keys, values
+    )
         outs = [share_shapes(rows, [width], narrow)] * (PARTS - 1)
-        shares = [share] + list(project_parts(attended, parts, outs))
+        shares = [share] + list(project_parts(attended, [second] + parts, outs))
         whole = jnp.concatenate(shares, axis=1)
         return lax.psum_scatter(whole, "head", scatter_dimension=1, tiled=True)
 
     near = routed(block, next_to)
     far = routed(block, two_away)
     near, prepared = lax.optimization_barrier((near, prepared))
-    padded, bias, own_keys, own_values, *weights = prepared
+    padded, bias, own_keys, own_values, *weights, part, second = prepared
     near_swapped = routed(near, other_core)
     near_keys, near_values = expand_block(near, *weights)
     far, near_keys = lax.optimization_barrier((far, near_keys))
@@ -365,10 +376,12 @@
     values = [own_values, near_values, other_values]
     last = [far, far_swapped]
 
-    attended, across, *parts = attend(padded, bias, weights, w_out, last, keys, values)
+    attended, across, *parts = attend(
+        padded, bias, weights, part, w_out, last, keys, values
+    )
     received = routed(across, other_core)
     outs = [share_shapes(rows, [width], kind) for kind in (wide, narrow, wide)]
-    far_part, beside, own = project_parts(attended, parts, outs)
+    far_part, beside, own = project_parts(attended, [second] + parts, outs)
     far_part = (far_part + received.astype(wide)).astype(narrow)
     far_part = routed(far_part, other_chip).astype(wide)
     beside = routed(beside, other_core).astype(wide)

time: 27.4 us -> 26.2 us (0.956)
  Pallas kernels: 7.85 us -> 7.28 us
  waiting for transfers between devices: 8.68 us -> 8.12 us
    pallas_call x1, Pallas kernels: 3.21 us -> 2.08 us  [attend(): pl.pallas_call(functools.partial(attend_kernel, len(keys)), out_shape=[na...]
    ppermute x7, waiting for transfers between devices: 8.68 us -> 8.12 us  [routed(): return lax.ppermute(value, ('ctx', 'head'), pairs)]
    pallas_call x1, Pallas kernels: 2.42 us -> 2.98 us  [prepare(): pl.pallas_call(functools.partial(prepare_kernel, rows // 2), out_shape=[n...]
  transfers between devices with their start and end apart: 7 -> 7, of which waited for: 3 -> 3; matrix products, arithmetic and copies ran while one was open for 0% -> 0% of each run, Pallas kernels for 17% -> 20%
where the time goes in v12:
time: 26.2 us; the launch traced here: 26.1 us
  starting transfers between devices  9.78 us (37%)
  waiting for transfers between devices  8.12 us (31%)
  Pallas kernels  7.28 us (28%)
  other arithmetic  0.8 us (3%)
    ppermute x7, starting transfers between devices, routed(): return lax.ppermute(value, ('ctx', 'head'), pairs)  9.78 us
    ppermute x7, waiting for transfers between devices, routed(): return lax.ppermute(value, ('ctx', 'head'), pairs)  8.12 us
    pallas_call x1, Pallas kernels, prepare(): pl.pallas_call(functools.partial(prepare_kernel, rows // 2), out_shape=[n...  2.98 us
    pallas_call x1, Pallas kernels, attend(): pl.pallas_call(functools.partial(attend_kernel, len(keys)), out_shape=[na...  2.08 us
    pallas_call x2, Pallas kernels, expand_block(): pl.pallas_call(expand_kernel, out_shape=[narrow_shape(heads * PADDED, row...  1.23 us
    pallas_call x1, Pallas kernels, project_parts(): pl.pallas_call(functools.partial(project_kernel, [len(group) for group in...  0.98 us
    convert_element_type x1, other arithmetic, shards(): return (own + beside + far_part).astype(narrow)  0.76 us
  transfers between devices with their start and end apart: 7, of which 3 were waited for; matrix products, arithmetic and copies ran while one was open for 0% of the time, Pallas kernels for 20%

profile of v12, /device:TPU:0, one launch (start us, length us, event | category | flops | bytes accessed | tf_op | source)
XLA Modules:
  0.0 26.1 jit_solution(15967557640343535750)
XLA Ops:
  0.0 3.0 %collective-permute-start = (bf16[576,128]{1,0:T(8,128)(2,1)}, bf16[576,128]{1,0:T(8,128)(2,1)S(1)}, u32[]{:S(2)}, u32[]{:S(2)}) collective-permute-start(bf16[576,128]{1,0:T(8,128)(2,1)} %bitcast.1), channel_id=1, source_target_pairs={{0,4},{1,13},{2,6},{3,15},{4,8},{5,1},{6,10},{7,3},{8,12},{9,5},{1... | collective-permute-start | bytes 442376 | tf_op jit(solution)/shard_map/ppermute | solution.py:29
  3.0 4.5 %collective-permute-start.1 = (bf16[576,128]{1,0:T(8,128)(2,1)}, bf16[576,128]{1,0:T(8,128)(2,1)S(1)}, u32[]{:S(2)}, u32[]{:S(2)}) collective-permute-start(bf16[576,128]{1,0:T(8,128)(2,1)} %bitcast.2), channel_id=1, source_target_pairs={{0,8},{1,1},{2,10},{3,3},{4,4},{5,13},{6,6},{7,15},{8,0},{9,9},{10... | collective-permute-start | bytes 442376 | tf_op jit(solution)/shard_map/ppermute | solution.py:29
  7.5 3.0 %prepare.1 = (bf16[128,2048]{1,0:T(8,128)(2,1)S(1)}, f32[128,512]{1,0:T(8,128)S(1)}, bf16[2048,128]{1,0:T(8,128)(2,1)S(1)}, bf16[128,1024]{1,0:T(8,128)(2,1)S(1)...) custom-call(s32[8]{0:T(128)} %refs_0_.1, ...), custom_call_target="tpu_custom_call" | custom-call | flops 268435456 | bytes 6160384 | tf_op jit(solution)/shard_map/prepare/pallas_call | solution.py:141
  10.5 0.0 collective-permute-done.block_ref
  10.5 0.1 collective-permute-start.3
  10.6 0.6 %expand_block.2 = (bf16[2048,128]{1,0:T(8,128)(2,1)S(1)}, bf16[128,1024]{1,0:T(8,128)(2,1)S(1)}) custom-call(bf16[576,128]{1,0:T(8,128)(2,1)S(1)} %collective-permute-done.block_ref, bf16[1024,512]{1,0:T(8,128)(2,1)S(1)} %get-tuple-element.45.key_weight, bf16[512,1024]{1,0:T(8,128)(2,1)S(1)} %get-tuple-element.46.value_weight), custom_call_target="tpu_custom_call" | custom-call | flops 268435456 | bytes 1048576 | tf_op jit(solution)/shard_map/expand_block/pallas_call | solution.py:179
  11.2 1.2 %collective-permute-done.1.refs_0_ = bf16[576,128]{1,0:T(8,128)(2,1)S(1)} collective-permute-done((bf16[576,128]{1,0:T(8,128)(2,1)}, bf16[576,128]{1,0:T(8,128)(2,1)S(1)}, u32[]{:S(2)}, u32[]{:S(2)}) %collective-permute-start.1) | collective-permute-done | bytes 147488 | tf_op jit(solution)/shard_map/ppermute | solution.py:29
  12.4 0.0 collective-permute-start.2
  12.4 0.0 collective-permute-done.3.block_ref
  12.4 0.6 %expand_block.3 = (bf16[2048,128]{1,0:T(8,128)(2,1)S(1)}, bf16[128,1024]{1,0:T(8,128)(2,1)S(1)}) custom-call(bf16[576,128]{1,0:T(8,128)(2,1)S(1)} %collective-permute-done.3.block_ref, bf16[1024,512]{1,0:T(8,128)(2,1)S(1)} %get-tuple-element.45.key_weight, bf16[512,1024]{1,0:T(8,128)(2,1)S(1)} %get-tuple-element.46.value_weight), custom_call_target="tpu_custom_call" | custom-call | flops 268435456 | bytes 1048576 | tf_op jit(solution)/shard_map/expand_block/pallas_call | solution.py:179
  13.1 0.7 %collective-permute-done.2.refs_1_ = bf16[576,128]{1,0:T(8,128)(2,1)S(1)} collective-permute-done((bf16[576,128]{1,0:T(8,128)(2,1)S(1)}, bf16[576,128]{1,0:T(8,128)(2,1)S(1)}, u32[]{:S(2)}, u32[]{:S(2)}) %collective-permute-start.2) | collective-permute-done | bytes 147488 | tf_op jit(solution)/shard_map/ppermute | solution.py:29
  13.8 2.1 %attend.1 = (bf16[128,1024]{1,0:T(8,128)(2,1)S(1)}, bf16[128,896]{1,0:T(8,128)(2,1)S(1)}, bf16[1024,896]{1,0:T(8,128)(2,1)S(1)}, bf16[1024,896]{1,0:T(8,128)(2,1)S(1)}) custom-call(bf16[128,2048]{1,0:T(8,128)(2,1)S(1)} %get-tuple-element.43.padded_ref, f32[128,512]{1,0:T(8,128)S(1)} %get-tuple-element.44.bias_ref, ...), custom_call_target="tpu_custom_call" | custom-call | flops 1040187392 | bytes 7340032 | tf_op jit(solution)/shard_map/attend/pallas_call | solution.py:272
  15.9 0.2 collective-permute-start.5
  16.1 1.0 %project_parts.1 = (f32[128,896]{1,0:T(8,128)S(1)}, bf16[128,896]{1,0:T(8,128)(2,1)S(1)}, f32[128,896]{1,0:T(8,128)S(1)}) custom-call(bf16[128,1024]{1,0:T(8,128)(2,1)S(1)} %get-tuple-element.57.attended_ref, bf16[1024,896]{1,0:T(8,128)(2,1)S(1)} %get-tuple-element.58.refs_0_, bf16[1024,896]{1,0:T(8,128)(2,1)S(1)} %get-tuple-element.59.refs_1_, ...), custom_call_target="tpu_custom_call" | custom-call | flops 1024 | bytes 1024 | tf_op jit(solution)/shard_map/project_parts/pallas_call | solution.py:314
  17.1 0.4 %collective-permute-start.4 = (bf16[128,896]{1,0:T(8,128)(2,1)S(1)}, bf16[128,896]{1,0:T(8,128)(2,1)S(1)}, u32[]{:S(2)}, u32[]{:S(2)}) collective-permute-start(bf16[128,896]{1,0:T(8,128)(2,1)S(1)} %get-tuple-element.62), channel_id=1, source_target_pairs={{0,1},{1,0},{2,3},{3,2},{4,5},{5,4},{6,7},{7,6},{8,9},{9,8},{10,11... | collective-permute-start | bytes 688136 | tf_op jit(solution)/shard_map/ppermute | solution.py:29
  17.5 0.0 collective-permute-done.5
  17.6 1.6 %collective-permute-start.6 = (bf16[128,896]{1,0:T(8,128)(2,1)S(1)}, bf16[128,896]{1,0:T(8,128)(2,1)S(1)}, u32[]{:S(2)}, u32[]{:S(2)}) collective-permute-start(bf16[128,896]{1,0:T(8,128)(2,1)S(1)} %add_convert_fusion.1), channel_id=1, source_target_pairs={{0,2},{1,3},{2,0},{3,1},{4,6},{5,7},{6,4},{7,5},{8,10},{9,11},{10,... | collective-permute-start | bytes 688136 | tf_op jit(solution)/shard_map/ppermute | solution.py:29
  19.1 0.0 collective-permute-done.4
  19.1 6.2 %collective-permute-done.6 = bf16[128,896]{1,0:T(8,128)(2,1)S(1)} collective-permute-done((bf16[128,896]{1,0:T(8,128)(2,1)S(1)}, bf16[128,896]{1,0:T(8,128)(2,1)S(1)}, u32[]{:S(2)}, u32[]{:S(2)}) %collective-permute-start.6) | collective-permute-done | bytes 229408 | tf_op jit(solution)/shard_map/ppermute | solution.py:29
  25.3 0.8 %add_convert_fusion = bf16[128,896]{1,0:T(8,128)(2,1)} fusion(bf16[128,896]{1,0:T(8,128)(2,1)S(1)} %collective-permute-done.6, f32[128,896]{1,0:T(8,128)S(1)} %get-tuple-element.61, bf16[128,896]{1,0:T(8,128)(2,1)S(1)} %collective-permute-done.4), kind=kLoop, calls=%fused_computation | loop fusion | flops 573440 | bytes 1146880 | tf_op jit(solution)/shard_map/convert_element_type | solution.py:388
  (1 shorter events, 0.0 us)
Async XLA Ops:
  0.0 10.5 %collective-permute-start = (bf16[576,128]{1,0:T(8,128)(2,1)}, bf16[576,128]{1,0:T(8,128)(2,1)S(1)}, u32[]{:S(2)}, u32[]{:S(2)}) collective-permute-start(bf16[576,128]{1,0:T(8,128)(2,1)} %bitcast.1), channel_id=1, source_target_pairs={{0,4},{1,13},{2,6},{3,15},{4,8},{5,1},{6,10},{7,3},{8,12},{9,5},{1... | collective-permute-start | bytes 442376 | tf_op jit(solution)/shard_map/ppermute | solution.py:29
  3.0 9.4 %collective-permute-start.1 = (bf16[576,128]{1,0:T(8,128)(2,1)}, bf16[576,128]{1,0:T(8,128)(2,1)S(1)}, u32[]{:S(2)}, u32[]{:S(2)}) collective-permute-start(bf16[576,128]{1,0:T(8,128)(2,1)} %bitcast.2), channel_id=1, source_target_pairs={{0,8},{1,1},{2,10},{3,3},{4,4},{5,13},{6,6},{7,15},{8,0},{9,9},{10... | collective-permute-start | bytes 442376 | tf_op jit(solution)/shard_map/ppermute | solution.py:29
  10.5 1.9 %collective-permute-start.3 = (bf16[576,128]{1,0:T(8,128)(2,1)S(1)}, bf16[576,128]{1,0:T(8,128)(2,1)S(1)}, u32[]{:S(2)}, u32[]{:S(2)}) collective-permute-start(bf16[576,128]{1,0:T(8,128)(2,1)S(1)} %collective-permute-done.block_ref), channel_id=1, source_target_pairs={{0,1},{1,0},{2,3},{3,2},{4,5},{5,4},{6,7},{7,6},{8,9},{9,8},{10,11... | collective-permute-start | bytes 442376 | tf_op jit(solution)/shard_map/ppermute | solution.py:29
  12.4 1.4 %collective-permute-start.2 = (bf16[576,128]{1,0:T(8,128)(2,1)S(1)}, bf16[576,128]{1,0:T(8,128)(2,1)S(1)}, u32[]{:S(2)}, u32[]{:S(2)}) collective-permute-start(bf16[576,128]{1,0:T(8,128)(2,1)S(1)} %collective-permute-done.1.refs_0_), channel_id=1, source_target_pairs={{0,1},{1,0},{2,3},{3,2},{4,5},{5,4},{6,7},{7,6},{8,9},{9,8},{10,11... | collective-permute-start | bytes 442376 | tf_op jit(solution)/shard_map/ppermute | solution.py:29
  15.9 1.6 %collective-permute-start.5 = (bf16[128,896]{1,0:T(8,128)(2,1)S(1)}, bf16[128,896]{1,0:T(8,128)(2,1)S(1)}, u32[]{:S(2)}, u32[]{:S(2)}) collective-permute-start(bf16[128,896]{1,0:T(8,128)(2,1)S(1)} %get-tuple-element.64), channel_id=1, source_target_pairs={{0,1},{1,0},{2,3},{3,2},{4,5},{5,4},{6,7},{7,6},{8,9},{9,8},{10,11... | collective-permute-start | bytes 688136 | tf_op jit(solution)/shard_map/ppermute | solution.py:29
  17.1 2.0 %collective-permute-start.4 = (bf16[128,896]{1,0:T(8,128)(2,1)S(1)}, bf16[128,896]{1,0:T(8,128)(2,1)S(1)}, u32[]{:S(2)}, u32[]{:S(2)}) collective-permute-start(bf16[128,896]{1,0:T(8,128)(2,1)S(1)} %get-tuple-element.62), channel_id=1, source_target_pairs={{0,1},{1,0},{2,3},{3,2},{4,5},{5,4},{6,7},{7,6},{8,9},{9,8},{10,11... | collective-permute-start | bytes 688136 | tf_op jit(solution)/shard_map/ppermute | solution.py:29
  17.6 7.7 %collective-permute-start.6 = (bf16[128,896]{1,0:T(8,128)(2,1)S(1)}, bf16[128,896]{1,0:T(8,128)(2,1)S(1)}, u32[]{:S(2)}, u32[]{:S(2)}) collective-permute-start(bf16[128,896]{1,0:T(8,128)(2,1)S(1)} %add_convert_fusion.1), channel_id=1, source_target_pairs={{0,2},{1,3},{2,0},{3,1},{4,6},{5,7},{6,4},{7,5},{8,10},{9,11},{10,... | collective-permute-start | bytes 688136 | tf_op jit(solution)/shard_map/ppermute | solution.py:29

commit v13 on v12

--- a/solution.py
+++ b/solution.py
@@ -169,6 +169,46 @@
     )(*[pltpu.with_memory_space_constraint(item, pltpu.HBM) for item in operands])
 
 
+def score(padded_ref, bias_ref, first_ref, second_ref, scores_ref, at, into):
+    rows = bias_ref.shape[0]
+    bias = bias_ref[:, at : at + 2 * rows]
+    for head in range(padded_ref.shape[1] // PADDED):
+        wide = slice(head * PADDED, (head + 1) * PADDED)
+        pair = jnp.concatenate([first_ref[wide, :], second_ref[wide, :]], axis=1)
+        product = jnp.dot(padded_ref[:, wide], pair, preferred_element_type=jnp.float32)
+        scores_ref[head * rows : (head + 1) * rows, into : into + 2 * rows] = product + bias
+
+
+def expand_and_score_kernel(
+    block_ref, key_weight, value_weight, padded_ref, bias_ref, first_ref, second_ref, *outs
+):
+    keys_ref, values_ref, scores_ref = outs
+    score(padded_ref, bias_ref, first_ref, second_ref, scores_ref, 0, 0)
+    expand(block_ref[...], key_weight, value_weight, keys_ref, values_ref)
+
+
+def expand_and_score(block, key_weight, value_weight, padded, bias, first, second):
+    rows = block.shape[1]
+    heads = value_weight.shape[1] // HEAD_DIM
+    return pl.pallas_call(
+        expand_and_score_kernel,
+        out_shape=[
+            narrow_shape(heads * PADDED, rows),
+            narrow_shape(rows, heads * HEAD_DIM),
+            jax.ShapeDtypeStruct((heads * rows, 2 * rows), jnp.float32),
+        ],
+        in_specs=[VMEM] * 7,
+        out_specs=[VMEM] * 3,
+        compiler_params=PARAMS,
+        cost_estimate=pl.CostEstimate(
+            flops=4 * rows * value_weight.size + 4 * heads * rows * rows * PADDED,
+            bytes_accessed=2 * value_weight.size,
+            transcendentals=0,
+        ),
+        name="expand_and_score",
+    )(block, key_weight, value_weight, padded, bias, first, second)
+
+
 def expand_kernel(block_ref, key_weight, value_weight, keys_ref, values_ref):
     expand(block_ref[...], key_weight, value_weight, keys_ref, values_ref)
 
@@ -209,12 +249,11 @@
 
 
 def attend_kernel(count, padded_ref, bias_ref, key_weight, value_weight, part_ref, w_out_ref, *refs):
-    direct_ref, swapped_ref = refs[:2]
-    keys, values = list(refs[2 : 2 + count]), list(refs[2 + count : 2 + 2 * count])
-    attended_ref, share_ref, *parts = refs[2 + 2 * count : 4 + 2 * count + PARTS - EARLY]
-    turned_ref, last_keys, last_values, scores_ref, weights_ref, sems = refs[
-        4 + 2 * count + PARTS - EARLY :
-    ]
+    direct_ref, swapped_ref, early_ref = refs[:3]
+    keys, refs = list(refs[3 : 3 + count]), refs[3 + count :]
+    values, refs = list(refs[: count + 2]), refs[count + 2 :]
+    attended_ref, share_ref, *parts = refs[: 2 + PARTS - EARLY]
+    turned_ref, last_keys, last_values, scores_ref, weights_ref, sems = refs[2 + PARTS - EARLY :]
     rows = bias_ref.shape[0]
     heads = value_weight.shape[1] // HEAD_DIM
     copies = [
@@ -235,17 +274,19 @@
     for start in range(0, count + 1, 2):
         if start + 2 > count:
             expand(turned_ref[...], key_weight, value_weight, last_keys, last_values)
-        chosen = keys[start : start + 2]
-        stretch = slice(start * rows, (start + len(chosen)) * rows)
-        for head in range(heads):
-            wide = slice(head * PADDED, (head + 1) * PADDED)
-            pair = jnp.concatenate([ref[wide, :] for ref in chosen], axis=1)
-            product = jnp.dot(padded_ref[:, wide], pair, preferred_element_type=jnp.float32)
-            scores_ref[lines(head), stretch] = product + bias_ref[:, stretch]
-    peaks = [jnp.max(scores_ref[lines(head), :], axis=1, keepdims=True) for head in range(heads)]
+        first_ref, second_ref = keys[start : start + 2]
+        into = start * rows
+        score(padded_ref, bias_ref, first_ref, second_ref, scores_ref, into + 2 * rows, into)
+    peaks = []
+    for head in range(heads):
+        early = jnp.max(early_ref[lines(head), :], axis=1, keepdims=True)
+        peaks.append(
+            jnp.maximum(early, jnp.max(scores_ref[lines(head), :], axis=1, keepdims=True))
+        )
     inverses = []
     for head in range(heads):
-        weights = jnp.exp2((scores_ref[lines(head), :] - peaks[head]) * jnp.float32(EXPONENT))
+        scores = jnp.concatenate([early_ref[lines(head), :], scores_ref[lines(head), :]], axis=1)
+        weights = jnp.exp2((scores - peaks[head]) * jnp.float32(EXPONENT))
         weights_ref[lines(head), :] = weights.astype(jnp.bfloat16)
         inverses.append(1.0 / jnp.sum(weights, axis=1, keepdims=True))
     for head in range(heads):
@@ -265,7 +306,7 @@
     return [jax.ShapeDtypeStruct((rows, width), kind) for width in widths]
 
 
-def attend(padded, bias, weights, part, w_out, last, keys, values):
+def attend(padded, bias, weights, part, w_out, last, early, keys, values):
     rows, key_count = bias.shape
     heads = values[0].shape[1] // HEAD_DIM
     flops = 4 * heads * rows * key_count * PADDED + 4 * rows * weights[0].size
@@ -273,13 +314,13 @@
         functools.partial(attend_kernel, len(keys)),
         out_shape=[narrow_shape(rows, heads * HEAD_DIM), narrow_shape(rows, part.shape[1])]
         + [narrow_shape(*part.shape)] * (PARTS - EARLY),
-        in_specs=[VMEM] * 5 + [HBM] + [VMEM] * (2 + 2 * len(keys)),
+        in_specs=[VMEM] * 5 + [HBM] + [VMEM] * (3 + len(keys) + len(values)),
         out_specs=[VMEM] * (2 + PARTS - EARLY),
         scratch_shapes=[
             pltpu.VMEM(last[0].shape, jnp.bfloat16),
-            pltpu.VMEM(keys[0].shape, jnp.bfloat16),
+            pltpu.VMEM((heads * PADDED, rows), jnp.bfloat16),
             pltpu.VMEM(values[0].shape, jnp.bfloat16),
-            pltpu.VMEM((heads * rows, key_count), jnp.float32),
+            pltpu.VMEM((heads * rows, key_count - 2 * rows), jnp.float32),
             pltpu.VMEM((heads * rows, key_count), jnp.bfloat16),
             pltpu.SemaphoreType.DMA((PARTS - EARLY,)),
         ],
@@ -297,6 +338,7 @@
         part,
         pltpu.with_memory_space_constraint(w_out, pltpu.HBM),
         *last,
+        early,
         *keys,
         *values,
     )
@@ -351,13 +393,17 @@
         for step in range(1, ctx_count):
             blocks.append(routed(block, lambda ctx, head: ((ctx + step) % ctx_count, head)))
         padded, bias, own_keys, own_values, *weights, part, second = prepared
-        expanded = [(own_keys, own_values)]
-        expanded += [expand_block(piece, *weights) for piece in blocks[:-1]]
-        keys, values = zip(*expanded)
+        next_keys, next_values = expand_block(blocks[0], *weights)
+        third_keys, third_values, early = expand_and_score(
+            blocks[1], *weights, padded, bias, own_keys, next_keys
+        )
+        expanded = [expand_block(piece, *weights) for piece in blocks[2:-1]]
+        keys = [third_keys] + [pair[0] for pair in expanded]
+        values = [own_values, next_values, third_values] + [pair[1] for pair in expanded]
         last = [blocks[-1], blocks[-1]]
         attended, share, *parts = attend(
-        padded, bias, weights, part, w_out, last, keys, values
-    )
+            padded, bias, weights, part, w_out, last, early, keys, values
+        )
         outs = [share_shapes(rows, [width], narrow)] * (PARTS - 1)
         shares = [share] + list(project_parts(attended, [second] + parts, outs))
         whole = jnp.concatenate(shares, axis=1)
@@ -371,13 +417,15 @@
     near_keys, near_values = expand_block(near, *weights)
     far, near_keys = lax.optimization_barrier((far, near_keys))
     far_swapped = routed(far, other_core)
-    other_keys, other_values = expand_block(near_swapped, *weights)
-    keys = [own_keys, near_keys, other_keys]
+    other_keys, other_values, early = expand_and_score(
+        near_swapped, *weights, padded, bias, own_keys, near_keys
+    )
+    keys = [other_keys]
     values = [own_values, near_values, other_values]
     last = [far, far_swapped]
 
     attended, across, *parts = attend(
-        padded, bias, weights, part, w_out, last, keys, values
+        padded, bias, weights, part, w_out, last, early, keys, values
     )
     received = routed(across, other_core)
     outs = [share_shapes(rows, [width], kind) for kind in (wide, narrow, wide)]

time: 26.2 us -> 26.2 us (level)
    pallas_call x0 -> x1, Pallas kernels: none -> 0.77 us  [expand_and_score(): pl.pallas_call(expand_and_score_kernel, out_shape=[narrow_shape(heads * P...]
    pallas_call x2 -> x1, Pallas kernels: 1.23 us -> 0.62 us  [expand_block(): pl.pallas_call(expand_kernel, out_shape=[narrow_shape(heads * PADDED, row...]
where the time goes in v13:
time: 26.2 us; the launch traced here: 26.1 us
  starting transfers between devices  9.78 us (37%)
  waiting for transfers between devices  7.97 us (30%)
  Pallas kernels  7.43 us (28%)
  other arithmetic  0.8 us (3%)
    ppermute x7, starting transfers between devices, routed(): return lax.ppermute(value, ('ctx', 'head'), pairs)  9.78 us
    ppermute x7, waiting for transfers between devices, routed(): return lax.ppermute(value, ('ctx', 'head'), pairs)  7.97 us
    pallas_call x1, Pallas kernels, prepare(): pl.pallas_call(functools.partial(prepare_kernel, rows // 2), out_shape=[n...  2.98 us
    pallas_call x1, Pallas kernels, attend(): pl.pallas_call(functools.partial(attend_kernel, len(keys)), out_shape=[na...  2.08 us
    pallas_call x1, Pallas kernels, project_parts(): pl.pallas_call(functools.partial(project_kernel, [len(group) for group in...  0.98 us
    pallas_call x1, Pallas kernels, expand_and_score(): pl.pallas_call(expand_and_score_kernel, out_shape=[narrow_shape(heads * P...  0.77 us
    convert_element_type x1, other arithmetic, shards(): return (own + beside + far_part).astype(narrow)  0.76 us
    pallas_call x1, Pallas kernels, expand_block(): pl.pallas_call(expand_kernel, out_shape=[narrow_shape(heads * PADDED, row...  0.62 us
  transfers between devices with their start and end apart: 7, of which 3 were waited for; matrix products, arithmetic and copies ran while one was open for 0% of the time, Pallas kernels for 20%

profile of v13, /device:TPU:0, one launch (start us, length us, event | category | flops | bytes accessed | tf_op | source)
XLA Modules:
  0.0 26.1 jit_solution(10543641023483016062)
XLA Ops:
  0.0 3.0 %collective-permute-start = (bf16[576,128]{1,0:T(8,128)(2,1)}, bf16[576,128]{1,0:T(8,128)(2,1)S(1)}, u32[]{:S(2)}, u32[]{:S(2)}) collective-permute-start(bf16[576,128]{1,0:T(8,128)(2,1)} %bitcast.1), channel_id=1, source_target_pairs={{0,4},{1,13},{2,6},{3,15},{4,8},{5,1},{6,10},{7,3},{8,12},{9,5},{1... | collective-permute-start | bytes 442376 | tf_op jit(solution)/shard_map/ppermute | solution.py:29
  3.0 4.5 %collective-permute-start.1 = (bf16[576,128]{1,0:T(8,128)(2,1)}, bf16[576,128]{1,0:T(8,128)(2,1)S(1)}, u32[]{:S(2)}, u32[]{:S(2)}) collective-permute-start(bf16[576,128]{1,0:T(8,128)(2,1)} %bitcast.2), channel_id=1, source_target_pairs={{0,8},{1,1},{2,10},{3,3},{4,4},{5,13},{6,6},{7,15},{8,0},{9,9},{10... | collective-permute-start | bytes 442376 | tf_op jit(solution)/shard_map/ppermute | solution.py:29
  7.5 3.0 %prepare.1 = (bf16[128,2048]{1,0:T(8,128)(2,1)S(1)}, f32[128,512]{1,0:T(8,128)S(1)}, bf16[2048,128]{1,0:T(8,128)(2,1)S(1)}, bf16[128,1024]{1,0:T(8,128)(2,1)S(1)...) custom-call(s32[8]{0:T(128)} %refs_0_.1, ...), custom_call_target="tpu_custom_call" | custom-call | flops 268435456 | bytes 6160384 | tf_op jit(solution)/shard_map/prepare/pallas_call | solution.py:141
  10.5 0.0 collective-permute-done.block_ref
  10.5 0.1 collective-permute-start.3
  10.6 0.6 %expand_block.1 = (bf16[2048,128]{1,0:T(8,128)(2,1)S(1)}, bf16[128,1024]{1,0:T(8,128)(2,1)S(1)}) custom-call(bf16[576,128]{1,0:T(8,128)(2,1)S(1)} %collective-permute-done.block_ref, bf16[1024,512]{1,0:T(8,128)(2,1)S(1)} %get-tuple-element.46.key_weight, bf16[512,1024]{1,0:T(8,128)(2,1)S(1)} %get-tuple-element.47.value_weight), custom_call_target="tpu_custom_call" | custom-call | flops 268435456 | bytes 1048576 | tf_op jit(solution)/shard_map/expand_block/pallas_call | solution.py:219
  11.2 1.2 %collective-permute-done.1.refs_0_ = bf16[576,128]{1,0:T(8,128)(2,1)S(1)} collective-permute-done((bf16[576,128]{1,0:T(8,128)(2,1)}, bf16[576,128]{1,0:T(8,128)(2,1)S(1)}, u32[]{:S(2)}, u32[]{:S(2)}) %collective-permute-start.1) | collective-permute-done | bytes 147488 | tf_op jit(solution)/shard_map/ppermute | solution.py:29
  12.4 0.0 collective-permute-start.2
  12.4 0.0 collective-permute-done.3.block_ref
  12.4 0.8 %expand_and_score.1 = (bf16[2048,128]{1,0:T(8,128)(2,1)S(1)}, bf16[128,1024]{1,0:T(8,128)(2,1)S(1)}, f32[1024,256]{1,0:T(8,128)S(1)}) custom-call(bf16[576,128]{1,0:T(8,128)(2,1)S(1)} %collective-permute-done.3.block_ref, bf16[1024,512]{1,0:T(8,128)(2,1)S(1)} %get-tuple-element.46.key_weight, bf16[512,1024]{1,0:T(8,128)(2,1)S(1)} %get-tuple-element.47.value_weight, ...), custom_call_target="tpu_custom_call" | custom-call | flops 402653184 | bytes 1048576 | tf_op jit(solution)/shard_map/expand_and_score/pallas_call | solution.py:193
  13.2 0.6 %collective-permute-done.2.refs_1_ = bf16[576,128]{1,0:T(8,128)(2,1)S(1)} collective-permute-done((bf16[576,128]{1,0:T(8,128)(2,1)S(1)}, bf16[576,128]{1,0:T(8,128)(2,1)S(1)}, u32[]{:S(2)}, u32[]{:S(2)}) %collective-permute-start.2) | collective-permute-done | bytes 147488 | tf_op jit(solution)/shard_map/ppermute | solution.py:29
  13.8 2.1 %attend.1 = (bf16[128,1024]{1,0:T(8,128)(2,1)S(1)}, bf16[128,896]{1,0:T(8,128)(2,1)S(1)}, bf16[1024,896]{1,0:T(8,128)(2,1)S(1)}, bf16[1024,896]{1,0:T(8,128)(2,1)S(1)}) custom-call(bf16[128,2048]{1,0:T(8,128)(2,1)S(1)} %get-tuple-element.44.padded_ref, f32[128,512]{1,0:T(8,128)S(1)} %get-tuple-element.45.bias_ref, ...), custom_call_target="tpu_custom_call" | custom-call | flops 1040187392 | bytes 7340032 | tf_op jit(solution)/shard_map/attend/pallas_call | solution.py:313
  15.9 0.2 collective-permute-start.5
  16.1 1.0 %project_parts.1 = (f32[128,896]{1,0:T(8,128)S(1)}, bf16[128,896]{1,0:T(8,128)(2,1)S(1)}, f32[128,896]{1,0:T(8,128)S(1)}) custom-call(bf16[128,1024]{1,0:T(8,128)(2,1)S(1)} %get-tuple-element.59.attended_ref, bf16[1024,896]{1,0:T(8,128)(2,1)S(1)} %get-tuple-element.60.refs_0_, bf16[1024,896]{1,0:T(8,128)(2,1)S(1)} %get-tuple-element.61.refs_1_, ...), custom_call_target="tpu_custom_call" | custom-call | flops 1024 | bytes 1024 | tf_op jit(solution)/shard_map/project_parts/pallas_call | solution.py:356
  17.1 0.4 %collective-permute-start.4 = (bf16[128,896]{1,0:T(8,128)(2,1)S(1)}, bf16[128,896]{1,0:T(8,128)(2,1)S(1)}, u32[]{:S(2)}, u32[]{:S(2)}) collective-permute-start(bf16[128,896]{1,0:T(8,128)(2,1)S(1)} %get-tuple-element.64), channel_id=1, source_target_pairs={{0,1},{1,0},{2,3},{3,2},{4,5},{5,4},{6,7},{7,6},{8,9},{9,8},{10,11... | collective-permute-start | bytes 688136 | tf_op jit(solution)/shard_map/ppermute | solution.py:29
  17.5 0.0 collective-permute-done.5
  17.6 1.6 %collective-permute-start.6 = (bf16[128,896]{1,0:T(8,128)(2,1)S(1)}, bf16[128,896]{1,0:T(8,128)(2,1)S(1)}, u32[]{:S(2)}, u32[]{:S(2)}) collective-permute-start(bf16[128,896]{1,0:T(8,128)(2,1)S(1)} %add_convert_fusion.1), channel_id=1, source_target_pairs={{0,2},{1,3},{2,0},{3,1},{4,6},{5,7},{6,4},{7,5},{8,10},{9,11},{10,... | collective-permute-start | bytes 688136 | tf_op jit(solution)/shard_map/ppermute | solution.py:29
  19.1 0.0 collective-permute-done.4
  19.1 6.2 %collective-permute-done.6 = bf16[128,896]{1,0:T(8,128)(2,1)S(1)} collective-permute-done((bf16[128,896]{1,0:T(8,128)(2,1)S(1)}, bf16[128,896]{1,0:T(8,128)(2,1)S(1)}, u32[]{:S(2)}, u32[]{:S(2)}) %collective-permute-start.6) | collective-permute-done | bytes 229408 | tf_op jit(solution)/shard_map/ppermute | solution.py:29
  25.3 0.8 %add_convert_fusion = bf16[128,896]{1,0:T(8,128)(2,1)} fusion(bf16[128,896]{1,0:T(8,128)(2,1)S(1)} %collective-permute-done.6, f32[128,896]{1,0:T(8,128)S(1)} %get-tuple-element.63, bf16[128,896]{1,0:T(8,128)(2,1)S(1)} %collective-permute-done.4), kind=kLoop, calls=%fused_computation | loop fusion | flops 573440 | bytes 1146880 | tf_op jit(solution)/shard_map/convert_element_type | solution.py:436
  (1 shorter events, 0.0 us)
Async XLA Ops:
  0.0 10.5 %collective-permute-start = (bf16[576,128]{1,0:T(8,128)(2,1)}, bf16[576,128]{1,0:T(8,128)(2,1)S(1)}, u32[]{:S(2)}, u32[]{:S(2)}) collective-permute-start(bf16[576,128]{1,0:T(8,128)(2,1)} %bitcast.1), channel_id=1, source_target_pairs={{0,4},{1,13},{2,6},{3,15},{4,8},{5,1},{6,10},{7,3},{8,12},{9,5},{1... | collective-permute-start | bytes 442376 | tf_op jit(solution)/shard_map/ppermute | solution.py:29
  3.0 9.4 %collective-permute-start.1 = (bf16[576,128]{1,0:T(8,128)(2,1)}, bf16[576,128]{1,0:T(8,128)(2,1)S(1)}, u32[]{:S(2)}, u32[]{:S(2)}) collective-permute-start(bf16[576,128]{1,0:T(8,128)(2,1)} %bitcast.2), channel_id=1, source_target_pairs={{0,8},{1,1},{2,10},{3,3},{4,4},{5,13},{6,6},{7,15},{8,0},{9,9},{10... | collective-permute-start | bytes 442376 | tf_op jit(solution)/shard_map/ppermute | solution.py:29
  10.5 1.9 %collective-permute-start.3 = (bf16[576,128]{1,0:T(8,128)(2,1)S(1)}, bf16[576,128]{1,0:T(8,128)(2,1)S(1)}, u32[]{:S(2)}, u32[]{:S(2)}) collective-permute-start(bf16[576,128]{1,0:T(8,128)(2,1)S(1)} %collective-permute-done.block_ref), channel_id=1, source_target_pairs={{0,1},{1,0},{2,3},{3,2},{4,5},{5,4},{6,7},{7,6},{8,9},{9,8},{10,11... | collective-permute-start | bytes 442376 | tf_op jit(solution)/shard_map/ppermute | solution.py:29
  12.4 1.4 %collective-permute-start.2 = (bf16[576,128]{1,0:T(8,128)(2,1)S(1)}, bf16[576,128]{1,0:T(8,128)(2,1)S(1)}, u32[]{:S(2)}, u32[]{:S(2)}) collective-permute-start(bf16[576,128]{1,0:T(8,128)(2,1)S(1)} %collective-permute-done.1.refs_0_), channel_id=1, source_target_pairs={{0,1},{1,0},{2,3},{3,2},{4,5},{5,4},{6,7},{7,6},{8,9},{9,8},{10,11... | collective-permute-start | bytes 442376 | tf_op jit(solution)/shard_map/ppermute | solution.py:29
  15.9 1.6 %collective-permute-start.5 = (bf16[128,896]{1,0:T(8,128)(2,1)S(1)}, bf16[128,896]{1,0:T(8,128)(2,1)S(1)}, u32[]{:S(2)}, u32[]{:S(2)}) collective-permute-start(bf16[128,896]{1,0:T(8,128)(2,1)S(1)} %get-tuple-element.66), channel_id=1, source_target_pairs={{0,1},{1,0},{2,3},{3,2},{4,5},{5,4},{6,7},{7,6},{8,9},{9,8},{10,11... | collective-permute-start | bytes 688136 | tf_op jit(solution)/shard_map/ppermute | solution.py:29
  17.1 2.0 %collective-permute-start.4 = (bf16[128,896]{1,0:T(8,128)(2,1)S(1)}, bf16[128,896]{1,0:T(8,128)(2,1)S(1)}, u32[]{:S(2)}, u32[]{:S(2)}) collective-permute-start(bf16[128,896]{1,0:T(8,128)(2,1)S(1)} %get-tuple-element.64), channel_id=1, source_target_pairs={{0,1},{1,0},{2,3},{3,2},{4,5},{5,4},{6,7},{7,6},{8,9},{9,8},{10,11... | collective-permute-start | bytes 688136 | tf_op jit(solution)/shard_map/ppermute | solution.py:29
  17.6 7.7 %collective-permute-start.6 = (bf16[128,896]{1,0:T(8,128)(2,1)S(1)}, bf16[128,896]{1,0:T(8,128)(2,1)S(1)}, u32[]{:S(2)}, u32[]{:S(2)}) collective-permute-start(bf16[128,896]{1,0:T(8,128)(2,1)S(1)} %add_convert_fusion.1), channel_id=1, source_target_pairs={{0,2},{1,3},{2,0},{3,1},{4,6},{5,7},{6,4},{7,5},{8,10},{9,11},{10,... | collective-permute-start | bytes 688136 | tf_op jit(solution)/shard_map/ppermute | solution.py:29

commit v14 on v13

--- a/solution.py
+++ b/solution.py
@@ -55,7 +55,6 @@
     return pltpu.make_async_copy(w_out_ref.at[:, pl.ds(start, width)], target, sem)
 
 
-EARLY = 2
 VMEM = pl.BlockSpec(memory_space=pltpu.VMEM)
 HBM = pl.BlockSpec(memory_space=pltpu.HBM)
 PARAMS = pltpu.CompilerParams(vmem_limit_bytes=VMEM_BYTES)
@@ -81,8 +80,8 @@
 
 def prepare_kernel(half, *refs):
     order_hbm, lens_hbm, queries_ref, block_ref, w_keys_ref, w_values_ref, w_out_ref = refs[:7]
-    padded_ref, bias_ref, keys_ref, values_ref, key_weight, value_weight, *parts = refs[7 : 13 + EARLY]
-    order_ref, lens_ref, query_buffer, block_buffer, weight_buffer, sems = refs[13 + EARLY :]
+    padded_ref, bias_ref, keys_ref, values_ref, key_weight, value_weight, *parts = refs[7 : 13 + PARTS]
+    order_ref, lens_ref, query_buffer, block_buffer, weight_buffer, sems = refs[13 + PARTS :]
     heads = w_keys_ref.shape[1] // HEAD_DIM
     rows = 2 * half
     scalars = [
@@ -148,21 +147,21 @@
             narrow_shape(*w_keys.shape[::-1]),
             narrow_shape(*w_values.shape),
         ]
-        + [narrow_shape(w_out.shape[0], w_out.shape[1] // PARTS)] * EARLY,
+        + [narrow_shape(w_out.shape[0], w_out.shape[1] // PARTS)] * PARTS,
         in_specs=[HBM] * 7,
-        out_specs=[VMEM] * (6 + EARLY),
+        out_specs=[VMEM] * (6 + PARTS),
         scratch_shapes=[
             pltpu.SMEM(order.shape, jnp.int32),
             pltpu.SMEM(lens.shape, jnp.int32),
             pltpu.VMEM(queries.shape, jnp.bfloat16),
             pltpu.VMEM(block.shape, jnp.bfloat16),
             pltpu.VMEM(w_keys.shape, jnp.bfloat16),
-            pltpu.SemaphoreType.DMA((6 + EARLY,)),
+            pltpu.SemaphoreType.DMA((6 + PARTS,)),
         ],
         compiler_params=PARAMS,
         cost_estimate=pl.CostEstimate(
             flops=4 * rows * heads * HEAD_DIM * LATENT,
-            bytes_accessed=2 * (queries.size + w_keys.size + w_values.size) + w_out.size,
+            bytes_accessed=2 * (queries.size + w_keys.size + w_values.size + w_out.size),
             transcendentals=0,
         ),
         name="prepare",
@@ -248,20 +247,13 @@
         target_ref[...] = block_ref[...]
 
 
-def attend_kernel(count, padded_ref, bias_ref, key_weight, value_weight, part_ref, w_out_ref, *refs):
+def attend_kernel(count, padded_ref, bias_ref, key_weight, value_weight, part_ref, *refs):
     direct_ref, swapped_ref, early_ref = refs[:3]
     keys, refs = list(refs[3 : 3 + count]), refs[3 + count :]
     values, refs = list(refs[: count + 2]), refs[count + 2 :]
-    attended_ref, share_ref, *parts = refs[: 2 + PARTS - EARLY]
-    turned_ref, last_keys, last_values, scores_ref, weights_ref, sems = refs[2 + PARTS - EARLY :]
+    attended_ref, share_ref, turned_ref, last_keys, last_values, scores_ref, weights_ref = refs
     rows = bias_ref.shape[0]
     heads = value_weight.shape[1] // HEAD_DIM
-    copies = [
-        part_copy(w_out_ref, EARLY + index, part, sems.at[index])
-        for index, part in enumerate(parts)
-    ]
-    for copy in copies:
-        copy.start()
     direct = (lax.axis_index("ctx") ^ lax.axis_index("head")) & 1 == 0
     take_if(turned_ref, direct_ref, direct)
     take_if(turned_ref, swapped_ref, jnp.logical_not(direct))
@@ -298,36 +290,32 @@
         )
         attended_ref[:, columns] = (value * inverses[head]).astype(jnp.bfloat16)
     project(attended_ref, part_ref, [share_ref])
-    for copy in copies:
-        copy.wait()
 
 
 def share_shapes(rows, widths, kind):
     return [jax.ShapeDtypeStruct((rows, width), kind) for width in widths]
 
 
-def attend(padded, bias, weights, part, w_out, last, early, keys, values):
+def attend(padded, bias, weights, part, last, early, keys, values):
     rows, key_count = bias.shape
     heads = values[0].shape[1] // HEAD_DIM
     flops = 4 * heads * rows * key_count * PADDED + 4 * rows * weights[0].size
     return pl.pallas_call(
         functools.partial(attend_kernel, len(keys)),
-        out_shape=[narrow_shape(rows, heads * HEAD_DIM), narrow_shape(rows, part.shape[1])]
-        + [narrow_shape(*part.shape)] * (PARTS - EARLY),
-        in_specs=[VMEM] * 5 + [HBM] + [VMEM] * (3 + len(keys) + len(values)),
-        out_specs=[VMEM] * (2 + PARTS - EARLY),
+        out_shape=[narrow_shape(rows, heads * HEAD_DIM), narrow_shape(rows, part.shape[1])],
+        in_specs=[VMEM] * (8 + len(keys) + len(values)),
+        out_specs=[VMEM] * 2,
         scratch_shapes=[
             pltpu.VMEM(last[0].shape, jnp.bfloat16),
             pltpu.VMEM((heads * PADDED, rows), jnp.bfloat16),
             pltpu.VMEM(values[0].shape, jnp.bfloat16),
             pltpu.VMEM((heads * rows, key_count - 2 * rows), jnp.float32),
             pltpu.VMEM((heads * rows, key_count), jnp.bfloat16),
-            pltpu.SemaphoreType.DMA((PARTS - EARLY,)),
         ],
         compiler_params=PARAMS,
         cost_estimate=pl.CostEstimate(
-            flops=flops + 2 * rows * w_out.size // PARTS,
-            bytes_accessed=2 * w_out.size,
+            flops=flops + 2 * rows * part.size,
+            bytes_accessed=2 * part.size,
             transcendentals=heads * rows * key_count,
         ),
         name="attend",
@@ -336,7 +324,6 @@
         bias,
         *weights,
         part,
-        pltpu.with_memory_space_constraint(w_out, pltpu.HBM),
         *last,
         early,
         *keys,
@@ -362,6 +349,23 @@
         cost_estimate=SHORT,
         name="project_parts",
     )(attended, *parts)
+
+
+def project_onto_kernel(attended_ref, part_ref, other_ref, sum_ref):
+    own = jnp.dot(attended_ref[...], part_ref[...], preferred_element_type=jnp.float32)
+    sum_ref[...] = own + other_ref[...].astype(jnp.float32)
+
+
+def project_onto(attended, part, other):
+    return pl.pallas_call(
+        project_onto_kernel,
+        out_shape=jax.ShapeDtypeStruct(other.shape, jnp.float32),
+        in_specs=[VMEM] * 3,
+        out_specs=VMEM,
+        compiler_params=PARAMS,
+        cost_estimate=SHORT,
+        name="project_onto",
+    )(attended, part, other)
 
 
 def next_to(ctx, head):
@@ -392,7 +396,8 @@
         blocks = []
         for step in range(1, ctx_count):
             blocks.append(routed(block, lambda ctx, head: ((ctx + step) % ctx_count, head)))
-        padded, bias, own_keys, own_values, *weights, part, second = prepared
+        padded, bias, own_keys, own_values, *weights = prepared
+        weights, parts = weights[:2], weights[2:]
         next_keys, next_values = expand_block(blocks[0], *weights)
         third_keys, third_values, early = expand_and_score(
             blocks[1], *weights, padded, bias, own_keys, next_keys
@@ -401,18 +406,17 @@
         keys = [third_keys] + [pair[0] for pair in expanded]
         values = [own_values, next_values, third_values] + [pair[1] for pair in expanded]
         last = [blocks[-1], blocks[-1]]
-        attended, share, *parts = attend(
-            padded, bias, weights, part, w_out, last, early, keys, values
-        )
+        attended, share = attend(padded, bias, weights, parts[0], last, early, keys, values)
         outs = [share_shapes(rows, [width], narrow)] * (PARTS - 1)
-        shares = [share] + list(project_parts(attended, [second] + parts, outs))
+        shares = [share] + list(project_parts(attended, parts[1:], outs))
         whole = jnp.concatenate(shares, axis=1)
         return lax.psum_scatter(whole, "head", scatter_dimension=1, tiled=True)
 
     near = routed(block, next_to)
     far = routed(block, two_away)
     near, prepared = lax.optimization_barrier((near, prepared))
-    padded, bias, own_keys, own_values, *weights, part, second = prepared
+    padded, bias, own_keys, own_values, *weights = prepared
+    weights, parts = weights[:2], weights[2:]
     near_swapped = routed(near, other_core)
     near_keys, near_values = expand_block(near, *weights)
     far, near_keys = lax.optimization_barrier((far, near_keys))
@@ -424,16 +428,14 @@
     values = [own_values, near_values, other_values]
     last = [far, far_swapped]
 
-    attended, across, *parts = attend(
-        padded, bias, weights, part, w_out, last, early, keys, values
-    )
+    attended, across = attend(padded, bias, weights, parts[0], last, early, keys, values)
     received = routed(across, other_core)
-    outs = [share_shapes(rows, [width], kind) for kind in (wide, narrow, wide)]
-    far_part, beside, own = project_parts(attended, [second] + parts, outs)
+    outs = [share_shapes(rows, [width], kind) for kind in (wide, narrow)]
+    far_part, beside = project_parts(attended, parts[1:3], outs)
     far_part = (far_part + received.astype(wide)).astype(narrow)
     far_part = routed(far_part, other_chip).astype(wide)
-    beside = routed(beside, other_core).astype(wide)
-    return (own + beside + far_part).astype(narrow)
+    beside = routed(beside, other_core)
+    return (project_onto(attended, parts[3], beside) + far_part).astype(narrow)
 
 
 def solution(mesh):

time: 26.2 us -> 26.2 us (level)
  waiting for transfers between devices: 7.97 us -> 6.46 us
  Pallas kernels: 7.43 us -> 8.43 us
  starting transfers between devices: 9.78 us -> 10.2 us
    ppermute x7, waiting for transfers between devices: 7.97 us -> 6.46 us  [routed(): return lax.ppermute(value, ('ctx', 'head'), pairs)]
    pallas_call x1, Pallas kernels: 2.98 us -> 4.08 us  [prepare(): pl.pallas_call(functools.partial(prepare_kernel, rows // 2), out_shape=[n...]
    ppermute x7, starting transfers between devices: 9.78 us -> 10.2 us  [routed(): return lax.ppermute(value, ('ctx', 'head'), pairs)]
    pallas_call x0 -> x1, Pallas kernels: none -> 0.45 us  [project_onto(): pl.pallas_call(project_onto_kernel, out_shape=jax.ShapeDtypeStruct(other....]
    pallas_call x1, Pallas kernels: 0.98 us -> 0.72 us  [project_parts(): pl.pallas_call(functools.partial(project_kernel, [len(group) for group in...]
  transfers between devices with their start and end apart: 7 -> 7, of which waited for: 3 -> 5; matrix products, arithmetic and copies ran while one was open for 0% -> 0% of each run, Pallas kernels for 20% -> 25%
where the time goes in v14:
time: 26.2 us; the launch traced here: 26 us
  starting transfers between devices  10.2 us (39%)
  Pallas kernels  8.43 us (32%)
  waiting for transfers between devices  6.46 us (25%)
  other arithmetic  0.77 us (3%)
    ppermute x7, starting transfers between devices, routed(): return lax.ppermute(value, ('ctx', 'head'), pairs)  10.2 us
    ppermute x7, waiting for transfers between devices, routed(): return lax.ppermute(value, ('ctx', 'head'), pairs)  6.46 us
    pallas_call x1, Pallas kernels, prepare(): pl.pallas_call(functools.partial(prepare_kernel, rows // 2), out_shape=[n...  4.08 us
    pallas_call x1, Pallas kernels, attend(): pl.pallas_call(functools.partial(attend_kernel, len(keys)), out_shape=[na...  1.82 us
    pallas_call x1, Pallas kernels, expand_and_score(): pl.pallas_call(expand_and_score_kernel, out_shape=[narrow_shape(heads * P...  0.76 us
    convert_element_type x1, other arithmetic, shards(): return (project_onto(attended, parts[3], beside) + far_part).astype(narrow)  0.73 us
    pallas_call x1, Pallas kernels, project_parts(): pl.pallas_call(functools.partial(project_kernel, [len(group) for group in...  0.72 us
    pallas_call x1, Pallas kernels, expand_block(): pl.pallas_call(expand_kernel, out_shape=[narrow_shape(heads * PADDED, row...  0.62 us
  transfers between devices with their start and end apart: 7, of which 5 were waited for; matrix products, arithmetic and copies ran while one was open for 0% of the time, Pallas kernels for 25%

profile of v14, /device:TPU:0, one launch (start us, length us, event | category | flops | bytes accessed | tf_op | source)
XLA Modules:
  0.0 26.0 jit_solution(15917867268068651199)
XLA Ops:
  0.0 3.0 %collective-permute-start = (bf16[576,128]{1,0:T(8,128)(2,1)}, bf16[576,128]{1,0:T(8,128)(2,1)S(1)}, u32[]{:S(2)}, u32[]{:S(2)}) collective-permute-start(bf16[576,128]{1,0:T(8,128)(2,1)} %bitcast.1), channel_id=1, source_target_pairs={{0,4},{1,13},{2,6},{3,15},{4,8},{5,1},{6,10},{7,3},{8,12},{9,5},{1... | collective-permute-start | bytes 442376 | tf_op jit(solution)/shard_map/ppermute | solution.py:29
  3.0 4.5 %collective-permute-start.1 = (bf16[576,128]{1,0:T(8,128)(2,1)}, bf16[576,128]{1,0:T(8,128)(2,1)S(1)}, u32[]{:S(2)}, u32[]{:S(2)}) collective-permute-start(bf16[576,128]{1,0:T(8,128)(2,1)} %bitcast.2), channel_id=1, source_target_pairs={{0,8},{1,1},{2,10},{3,3},{4,4},{5,13},{6,6},{7,15},{8,0},{9,9},{10... | collective-permute-start | bytes 442376 | tf_op jit(solution)/shard_map/ppermute | solution.py:29
  7.5 4.1 %prepare.1 = (bf16[128,2048]{1,0:T(8,128)(2,1)S(1)}, f32[128,512]{1,0:T(8,128)S(1)}, bf16[2048,128]{1,0:T(8,128)(2,1)S(1)}, bf16[128,1024]{1,0:T(8,128)(2,1)S(1)...) custom-call(s32[8]{0:T(128)} %refs_0_.1, ...), custom_call_target="tpu_custom_call" | custom-call | flops 268435456 | bytes 9830400 | tf_op jit(solution)/shard_map/prepare/pallas_call | solution.py:140
  11.6 0.0 collective-permute-done.block_ref
  11.6 0.1 collective-permute-start.3
  11.7 0.6 %expand_block.1 = (bf16[2048,128]{1,0:T(8,128)(2,1)S(1)}, bf16[128,1024]{1,0:T(8,128)(2,1)S(1)}) custom-call(bf16[576,128]{1,0:T(8,128)(2,1)S(1)} %collective-permute-done.block_ref, bf16[1024,512]{1,0:T(8,128)(2,1)S(1)} %get-tuple-element.49.key_weight, bf16[512,1024]{1,0:T(8,128)(2,1)S(1)} %get-tuple-element.50.value_weight), custom_call_target="tpu_custom_call" | custom-call | flops 268435456 | bytes 1048576 | tf_op jit(solution)/shard_map/expand_block/pallas_call | solution.py:218
  12.3 0.1 collective-permute-done.1.refs_0_
  12.4 0.5 %collective-permute-start.2 = (bf16[576,128]{1,0:T(8,128)(2,1)S(1)}, bf16[576,128]{1,0:T(8,128)(2,1)S(1)}, u32[]{:S(2)}, u32[]{:S(2)}) collective-permute-start(bf16[576,128]{1,0:T(8,128)(2,1)S(1)} %collective-permute-done.1.refs_0_), channel_id=1, source_target_pairs={{0,1},{1,0},{2,3},{3,2},{4,5},{5,4},{6,7},{7,6},{8,9},{9,8},{10,11... | collective-permute-start | bytes 442376 | tf_op jit(solution)/shard_map/ppermute | solution.py:29
  12.9 0.2 collective-permute-done.3.block_ref
  13.0 0.8 %expand_and_score.1 = (bf16[2048,128]{1,0:T(8,128)(2,1)S(1)}, bf16[128,1024]{1,0:T(8,128)(2,1)S(1)}, f32[1024,256]{1,0:T(8,128)S(1)}) custom-call(bf16[576,128]{1,0:T(8,128)(2,1)S(1)} %collective-permute-done.3.block_ref, bf16[1024,512]{1,0:T(8,128)(2,1)S(1)} %get-tuple-element.49.key_weight, bf16[512,1024]{1,0:T(8,128)(2,1)S(1)} %get-tuple-element.50.value_weight, ...), custom_call_target="tpu_custom_call" | custom-call | flops 402653184 | bytes 1048576 | tf_op jit(solution)/shard_map/expand_and_score/pallas_call | solution.py:192
  13.8 0.1 collective-permute-done.2.refs_1_
  13.9 1.8 %attend.1 = (bf16[128,1024]{1,0:T(8,128)(2,1)S(1)}, bf16[128,896]{1,0:T(8,128)(2,1)S(1)}) custom-call(bf16[128,2048]{1,0:T(8,128)(2,1)S(1)} %get-tuple-element.47.padded_ref, f32[128,512]{1,0:T(8,128)S(1)} %get-tuple-element.48.bias_ref, bf16[1024,512]{1,0:T(8,128)(2,1)S(1)} %get-tuple-element.49.key_weight, ...), custom_call_target="tpu_custom_call" | custom-call | flops 1040187392 | bytes 1835008 | tf_op jit(solution)/shard_map/attend/pallas_call | solution.py:303
  15.7 0.4 %collective-permute-start.5 = (bf16[128,896]{1,0:T(8,128)(2,1)S(1)}, bf16[128,896]{1,0:T(8,128)(2,1)S(1)}, u32[]{:S(2)}, u32[]{:S(2)}) collective-permute-start(bf16[128,896]{1,0:T(8,128)(2,1)S(1)} %get-tuple-element.68), channel_id=1, source_target_pairs={{0,1},{1,0},{2,3},{3,2},{4,5},{5,4},{6,7},{7,6},{8,9},{9,8},{10,11... | collective-permute-start | bytes 688136 | tf_op jit(solution)/shard_map/ppermute | solution.py:29
  16.1 0.7 %project_parts.1 = (f32[128,896]{1,0:T(8,128)S(1)}, bf16[128,896]{1,0:T(8,128)(2,1)S(1)}) custom-call(bf16[128,1024]{1,0:T(8,128)(2,1)S(1)} %get-tuple-element.62.attended_ref, bf16[1024,896]{1,0:T(8,128)(2,1)S(1)} %get-tuple-element.64.refs_0_, bf16[1024,896]{1,0:T(8,128)(2,1)S(1)} %get-tuple-element.65.refs_1_), custom_call_target="tpu_custom_call" | custom-call | flops 1024 | bytes 1024 | tf_op jit(solution)/shard_map/project_parts/pallas_call | solution.py:343
  16.9 0.2 collective-permute-start.4
  17.1 0.2 collective-permute-done.5
  17.3 1.6 %collective-permute-start.6 = (bf16[128,896]{1,0:T(8,128)(2,1)S(1)}, bf16[128,896]{1,0:T(8,128)(2,1)S(1)}, u32[]{:S(2)}, u32[]{:S(2)}) collective-permute-start(bf16[128,896]{1,0:T(8,128)(2,1)S(1)} %add_convert_fusion.1), channel_id=1, source_target_pairs={{0,2},{1,3},{2,0},{3,1},{4,6},{5,7},{6,4},{7,5},{8,10},{9,11},{10,... | collective-permute-start | bytes 688136 | tf_op jit(solution)/shard_map/ppermute | solution.py:29
  18.9 0.0 collective-permute-done.4.other_ref
  18.9 0.4 %project_onto.1 = f32[128,896]{1,0:T(8,128)S(1)} custom-call(bf16[128,1024]{1,0:T(8,128)(2,1)S(1)} %get-tuple-element.62.attended_ref, bf16[1024,896]{1,0:T(8,128)(2,1)S(1)} %get-tuple-element.63.part_ref, bf16[128,896]{1,0:T(8,128)(2,1)S(1)} %collective-permute-done.4.other_ref), custom_call_target="tpu_custom_call" | custom-call | flops 1024 | bytes 1024 | tf_op jit(solution)/shard_map/project_onto/pallas_call | solution.py:360
  19.3 5.9 %collective-permute-done.6 = bf16[128,896]{1,0:T(8,128)(2,1)S(1)} collective-permute-done((bf16[128,896]{1,0:T(8,128)(2,1)S(1)}, bf16[128,896]{1,0:T(8,128)(2,1)S(1)}, u32[]{:S(2)}, u32[]{:S(2)}) %collective-permute-start.6) | collective-permute-done | bytes 229408 | tf_op jit(solution)/shard_map/ppermute | solution.py:29
  25.3 0.7 %add_convert_fusion = bf16[128,896]{1,0:T(8,128)(2,1)} fusion(f32[128,896]{1,0:T(8,128)S(1)} %project_onto.1, bf16[128,896]{1,0:T(8,128)(2,1)S(1)} %collective-permute-done.6), kind=kLoop, calls=%fused_computation | loop fusion | flops 344064 | bytes 917504 | tf_op jit(solution)/shard_map/convert_element_type | solution.py:438
  (1 shorter events, 0.0 us)
Async XLA Ops:
  0.0 11.6 %collective-permute-start = (bf16[576,128]{1,0:T(8,128)(2,1)}, bf16[576,128]{1,0:T(8,128)(2,1)S(1)}, u32[]{:S(2)}, u32[]{:S(2)}) collective-permute-start(bf16[576,128]{1,0:T(8,128)(2,1)} %bitcast.1), channel_id=1, source_target_pairs={{0,4},{1,13},{2,6},{3,15},{4,8},{5,1},{6,10},{7,3},{8,12},{9,5},{1... | collective-permute-start | bytes 442376 | tf_op jit(solution)/shard_map/ppermute | solution.py:29
  3.0 9.4 %collective-permute-start.1 = (bf16[576,128]{1,0:T(8,128)(2,1)}, bf16[576,128]{1,0:T(8,128)(2,1)S(1)}, u32[]{:S(2)}, u32[]{:S(2)}) collective-permute-start(bf16[576,128]{1,0:T(8,128)(2,1)} %bitcast.2), channel_id=1, source_target_pairs={{0,8},{1,1},{2,10},{3,3},{4,4},{5,13},{6,6},{7,15},{8,0},{9,9},{10... | collective-permute-start | bytes 442376 | tf_op jit(solution)/shard_map/ppermute | solution.py:29
  11.6 1.4 %collective-permute-start.3 = (bf16[576,128]{1,0:T(8,128)(2,1)S(1)}, bf16[576,128]{1,0:T(8,128)(2,1)S(1)}, u32[]{:S(2)}, u32[]{:S(2)}) collective-permute-start(bf16[576,128]{1,0:T(8,128)(2,1)S(1)} %collective-permute-done.block_ref), channel_id=1, source_target_pairs={{0,1},{1,0},{2,3},{3,2},{4,5},{5,4},{6,7},{7,6},{8,9},{9,8},{10,11... | collective-permute-start | bytes 442376 | tf_op jit(solution)/shard_map/ppermute | solution.py:29
  12.4 1.5 %collective-permute-start.2 = (bf16[576,128]{1,0:T(8,128)(2,1)S(1)}, bf16[576,128]{1,0:T(8,128)(2,1)S(1)}, u32[]{:S(2)}, u32[]{:S(2)}) collective-permute-start(bf16[576,128]{1,0:T(8,128)(2,1)S(1)} %collective-permute-done.1.refs_0_), channel_id=1, source_target_pairs={{0,1},{1,0},{2,3},{3,2},{4,5},{5,4},{6,7},{7,6},{8,9},{9,8},{10,11... | collective-permute-start | bytes 442376 | tf_op jit(solution)/shard_map/ppermute | solution.py:29
  15.7 1.6 %collective-permute-start.5 = (bf16[128,896]{1,0:T(8,128)(2,1)S(1)}, bf16[128,896]{1,0:T(8,128)(2,1)S(1)}, u32[]{:S(2)}, u32[]{:S(2)}) collective-permute-start(bf16[128,896]{1,0:T(8,128)(2,1)S(1)} %get-tuple-element.68), channel_id=1, source_target_pairs={{0,1},{1,0},{2,3},{3,2},{4,5},{5,4},{6,7},{7,6},{8,9},{9,8},{10,11... | collective-permute-start | bytes 688136 | tf_op jit(solution)/shard_map/ppermute | solution.py:29
  16.9 2.0 %collective-permute-start.4 = (bf16[128,896]{1,0:T(8,128)(2,1)S(1)}, bf16[128,896]{1,0:T(8,128)(2,1)S(1)}, u32[]{:S(2)}, u32[]{:S(2)}) collective-permute-start(bf16[128,896]{1,0:T(8,128)(2,1)S(1)} %get-tuple-element.66), channel_id=1, source_target_pairs={{0,1},{1,0},{2,3},{3,2},{4,5},{5,4},{6,7},{7,6},{8,9},{9,8},{10,11... | collective-permute-start | bytes 688136 | tf_op jit(solution)/shard_map/ppermute | solution.py:29
  17.3 7.9 %collective-permute-start.6 = (bf16[128,896]{1,0:T(8,128)(2,1)S(1)}, bf16[128,896]{1,0:T(8,128)(2,1)S(1)}, u32[]{:S(2)}, u32[]{:S(2)}) collective-permute-start(bf16[128,896]{1,0:T(8,128)(2,1)S(1)} %add_convert_fusion.1), channel_id=1, source_target_pairs={{0,2},{1,3},{2,0},{3,1},{4,6},{5,7},{6,4},{7,5},{8,10},{9,11},{10,... | collective-permute-start | bytes 688136 | tf_op jit(solution)/shard_map/ppermute | solution.py:29

commit v15 on v14

--- a/solution.py
+++ b/solution.py
@@ -13,6 +13,7 @@
 QUERY = HEAD_DIM + ROPE
 PARTS = 4
 PADDED = 256
+FIRST_PIECE = 512
 VMEM_BYTES = 32 * 1024 * 1024
 HIDDEN = -1e30
 
@@ -251,7 +252,7 @@
     direct_ref, swapped_ref, early_ref = refs[:3]
     keys, refs = list(refs[3 : 3 + count]), refs[3 + count :]
     values, refs = list(refs[: count + 2]), refs[count + 2 :]
-    attended_ref, share_ref, turned_ref, last_keys, last_values, scores_ref, weights_ref = refs
+    attended_ref, *shares, turned_ref, last_keys, last_values, scores_ref, weights_ref = refs
     rows = bias_ref.shape[0]
     heads = value_weight.shape[1] // HEAD_DIM
     direct = (lax.axis_index("ctx") ^ lax.axis_index("head")) & 1 == 0
@@ -289,22 +290,22 @@
             preferred_element_type=jnp.float32,
         )
         attended_ref[:, columns] = (value * inverses[head]).astype(jnp.bfloat16)
-    project(attended_ref, part_ref, [share_ref])
+    project(attended_ref, part_ref, shares)
 
 
 def share_shapes(rows, widths, kind):
     return [jax.ShapeDtypeStruct((rows, width), kind) for width in widths]
 
 
-def attend(padded, bias, weights, part, last, early, keys, values):
+def attend(padded, bias, weights, part, last, early, keys, values, widths):
     rows, key_count = bias.shape
     heads = values[0].shape[1] // HEAD_DIM
     flops = 4 * heads * rows * key_count * PADDED + 4 * rows * weights[0].size
     return pl.pallas_call(
         functools.partial(attend_kernel, len(keys)),
-        out_shape=[narrow_shape(rows, heads * HEAD_DIM), narrow_shape(rows, part.shape[1])],
+        out_shape=share_shapes(rows, [heads * HEAD_DIM] + widths, jnp.bfloat16),
         in_specs=[VMEM] * (8 + len(keys) + len(values)),
-        out_specs=[VMEM] * 2,
+        out_specs=[VMEM] * (1 + len(widths)),
         scratch_shapes=[
             pltpu.VMEM(last[0].shape, jnp.bfloat16),
             pltpu.VMEM((heads * PADDED, rows), jnp.bfloat16),
@@ -406,7 +407,9 @@
         keys = [third_keys] + [pair[0] for pair in expanded]
         values = [own_values, next_values, third_values] + [pair[1] for pair in expanded]
         last = [blocks[-1], blocks[-1]]
-        attended, share = attend(padded, bias, weights, parts[0], last, early, keys, values)
+        attended, share = attend(
+            padded, bias, weights, parts[0], last, early, keys, values, [width]
+        )
         outs = [share_shapes(rows, [width], narrow)] * (PARTS - 1)
         shares = [share] + list(project_parts(attended, parts[1:], outs))
         whole = jnp.concatenate(shares, axis=1)
@@ -428,14 +431,17 @@
     values = [own_values, near_values, other_values]
     last = [far, far_swapped]
 
-    attended, across = attend(padded, bias, weights, parts[0], last, early, keys, values)
-    received = routed(across, other_core)
-    outs = [share_shapes(rows, [width], kind) for kind in (wide, narrow)]
-    far_part, beside = project_parts(attended, parts[1:3], outs)
-    far_part = (far_part + received.astype(wide)).astype(narrow)
-    far_part = routed(far_part, other_chip).astype(wide)
+    widths = [FIRST_PIECE, width - FIRST_PIECE]
+    attended, *across = attend(
+        padded, bias, weights, parts[0], last, early, keys, values, widths
+    )
+    received = [routed(piece, other_core) for piece in across]
+    outs = [share_shapes(rows, widths, wide), share_shapes(rows, [width], narrow)]
+    *sums, beside = project_parts(attended, parts[1:3], outs)
+    sums = [(mine + other.astype(wide)).astype(narrow) for mine, other in zip(sums, received)]
+    far_part = jnp.concatenate([routed(piece, other_chip) for piece in sums], axis=1)
     beside = routed(beside, other_core)
-    return (project_onto(attended, parts[3], beside) + far_part).astype(narrow)
+    return (project_onto(attended, parts[3], beside) + far_part.astype(wide)).astype(narrow)
 
 
 def solution(mesh):

time: 26.2 us -> 26.1 us (level)
  starting transfers between devices: 10.2 us -> 11.2 us
  waiting for transfers between devices: 6.46 us -> 5.46 us
    ppermute x7 -> x9, waiting for transfers between devices: 6.46 us -> 5.46 us  [routed(): return lax.ppermute(value, ('ctx', 'head'), pairs)]
    ppermute x7 -> x9, starting transfers between devices: 10.2 us -> 11.2 us  [routed(): return lax.ppermute(value, ('ctx', 'head'), pairs)]
    convert_element_type x2 -> x3, other arithmetic: 0.77 us -> 0.78 us  [the longest x1 0.73 us: shards(): (project_onto(attended, parts[3], beside) + far_part.astype(wide)).astype...]
  transfers between devices with their start and end apart: 7 -> 9, of which waited for: 5 -> 4; matrix products, arithmetic and copies ran while one was open for 0% -> 0% of each run, Pallas kernels for 25% -> 26%
where the time goes in v15:
time: 26.1 us; the launch traced here: 25.9 us
  starting transfers between devices  11.2 us (43%)
  Pallas kernels  8.44 us (32%)
  waiting for transfers between devices  5.46 us (21%)
  other arithmetic  0.78 us (3%)
    ppermute x9, starting transfers between devices, routed(): return lax.ppermute(value, ('ctx', 'head'), pairs)  11.2 us
    ppermute x9, waiting for transfers between devices, routed(): return lax.ppermute(value, ('ctx', 'head'), pairs)  5.46 us
    pallas_call x1, Pallas kernels, prepare(): pl.pallas_call(functools.partial(prepare_kernel, rows // 2), out_shape=[n...  4.08 us
    pallas_call x1, Pallas kernels, attend(): pl.pallas_call(functools.partial(attend_kernel, len(keys)), out_shape=sha...  1.82 us
    pallas_call x1, Pallas kernels, expand_and_score(): pl.pallas_call(expand_and_score_kernel, out_shape=[narrow_shape(heads * P...  0.76 us
    convert_element_type x1, other arithmetic, shards(): (project_onto(attended, parts[3], beside) + far_part.astype(wide)).astype...  0.73 us
    pallas_call x1, Pallas kernels, project_parts(): pl.pallas_call(functools.partial(project_kernel, [len(group) for group in...  0.72 us
    pallas_call x1, Pallas kernels, expand_block(): pl.pallas_call(expand_kernel, out_shape=[narrow_shape(heads * PADDED, row...  0.62 us
  transfers between devices with their start and end apart: 9, of which 4 were waited for; matrix products, arithmetic and copies ran while one was open for 0% of the time, Pallas kernels for 26%

profile of v15, /device:TPU:0, one launch (start us, length us, event | category | flops | bytes accessed | tf_op | source)
XLA Modules:
  0.0 25.9 jit_solution(8429642318769586027)
XLA Ops:
  0.0 3.0 %collective-permute-start = (bf16[576,128]{1,0:T(8,128)(2,1)}, bf16[576,128]{1,0:T(8,128)(2,1)S(1)}, u32[]{:S(2)}, u32[]{:S(2)}) collective-permute-start(bf16[576,128]{1,0:T(8,128)(2,1)} %bitcast.1), channel_id=1, source_target_pairs={{0,4},{1,13},{2,6},{3,15},{4,8},{5,1},{6,10},{7,3},{8,12},{9,5},{1... | collective-permute-start | bytes 442376 | tf_op jit(solution)/shard_map/ppermute | solution.py:30
  3.0 4.5 %collective-permute-start.1 = (bf16[576,128]{1,0:T(8,128)(2,1)}, bf16[576,128]{1,0:T(8,128)(2,1)S(1)}, u32[]{:S(2)}, u32[]{:S(2)}) collective-permute-start(bf16[576,128]{1,0:T(8,128)(2,1)} %bitcast.2), channel_id=1, source_target_pairs={{0,8},{1,1},{2,10},{3,3},{4,4},{5,13},{6,6},{7,15},{8,0},{9,9},{10... | collective-permute-start | bytes 442376 | tf_op jit(solution)/shard_map/ppermute | solution.py:30
  7.5 4.1 %prepare.1 = (bf16[128,2048]{1,0:T(8,128)(2,1)S(1)}, f32[128,512]{1,0:T(8,128)S(1)}, bf16[2048,128]{1,0:T(8,128)(2,1)S(1)}, bf16[128,1024]{1,0:T(8,128)(2,1)S(1)...) custom-call(s32[8]{0:T(128)} %refs_0_.1, ...), custom_call_target="tpu_custom_call" | custom-call | flops 268435456 | bytes 9830400 | tf_op jit(solution)/shard_map/prepare/pallas_call | solution.py:141
  11.6 0.0 collective-permute-done.block_ref
  11.6 0.1 collective-permute-start.3
  11.7 0.6 %expand_block.1 = (bf16[2048,128]{1,0:T(8,128)(2,1)S(1)}, bf16[128,1024]{1,0:T(8,128)(2,1)S(1)}) custom-call(bf16[576,128]{1,0:T(8,128)(2,1)S(1)} %collective-permute-done.block_ref, bf16[1024,512]{1,0:T(8,128)(2,1)S(1)} %get-tuple-element.51.key_weight, bf16[512,1024]{1,0:T(8,128)(2,1)S(1)} %get-tuple-element.52.value_weight), custom_call_target="tpu_custom_call" | custom-call | flops 268435456 | bytes 1048576 | tf_op jit(solution)/shard_map/expand_block/pallas_call | solution.py:219
  12.3 0.1 collective-permute-done.1.refs_0_
  12.4 0.5 %collective-permute-start.2 = (bf16[576,128]{1,0:T(8,128)(2,1)S(1)}, bf16[576,128]{1,0:T(8,128)(2,1)S(1)}, u32[]{:S(2)}, u32[]{:S(2)}) collective-permute-start(bf16[576,128]{1,0:T(8,128)(2,1)S(1)} %collective-permute-done.1.refs_0_), channel_id=1, source_target_pairs={{0,1},{1,0},{2,3},{3,2},{4,5},{5,4},{6,7},{7,6},{8,9},{9,8},{10,11... | collective-permute-start | bytes 442376 | tf_op jit(solution)/shard_map/ppermute | solution.py:30
  12.9 0.2 collective-permute-done.3.block_ref
  13.0 0.8 %expand_and_score.1 = (bf16[2048,128]{1,0:T(8,128)(2,1)S(1)}, bf16[128,1024]{1,0:T(8,128)(2,1)S(1)}, f32[1024,256]{1,0:T(8,128)S(1)}) custom-call(bf16[576,128]{1,0:T(8,128)(2,1)S(1)} %collective-permute-done.3.block_ref, bf16[1024,512]{1,0:T(8,128)(2,1)S(1)} %get-tuple-element.51.key_weight, bf16[512,1024]{1,0:T(8,128)(2,1)S(1)} %get-tuple-element.52.value_weight, ...), custom_call_target="tpu_custom_call" | custom-call | flops 402653184 | bytes 1048576 | tf_op jit(solution)/shard_map/expand_and_score/pallas_call | solution.py:193
  13.8 0.1 collective-permute-done.2.refs_1_
  13.9 1.8 %attend.1 = (bf16[128,1024]{1,0:T(8,128)(2,1)S(1)}, bf16[128,512]{1,0:T(8,128)(2,1)S(1)}, bf16[128,384]{1,0:T(8,128)(2,1)S(1)}) custom-call(bf16[128,2048]{1,0:T(8,128)(2,1)S(1)} %get-tuple-element.49.padded_ref, f32[128,512]{1,0:T(8,128)S(1)} %get-tuple-element.50.bias_ref, bf16[1024,512]{1,0:T(8,128)(2,1)S(1)} %get-tuple-element.51.key_weight, ...), custom_call_target="tpu_custom_call" | custom-call | flops 1040187392 | bytes 1835008 | tf_op jit(solution)/shard_map/attend/pallas_call | solution.py:304
  15.7 0.4 %collective-permute-start.5 = (bf16[128,512]{1,0:T(8,128)(2,1)S(1)}, bf16[128,512]{1,0:T(8,128)(2,1)S(1)}, u32[]{:S(2)}, u32[]{:S(2)}) collective-permute-start(bf16[128,512]{1,0:T(8,128)(2,1)S(1)} %get-tuple-element.70), channel_id=1, source_target_pairs={{0,1},{1,0},{2,3},{3,2},{4,5},{5,4},{6,7},{7,6},{8,9},{9,8},{10,11... | collective-permute-start | bytes 393224 | tf_op jit(solution)/shard_map/ppermute | solution.py:30
  16.1 0.1 collective-permute-start.7
  16.3 0.7 %project_parts.1 = (f32[128,512]{1,0:T(8,128)S(1)}, f32[128,384]{1,0:T(8,128)S(1)}, bf16[128,896]{1,0:T(8,128)(2,1)S(1)}) custom-call(bf16[128,1024]{1,0:T(8,128)(2,1)S(1)} %get-tuple-element.64.attended_ref, bf16[1024,896]{1,0:T(8,128)(2,1)S(1)} %get-tuple-element.66.refs_0_, bf16[1024,896]{1,0:T(8,128)(2,1)S(1)} %get-tuple-element.67.refs_1_), custom_call_target="tpu_custom_call" | custom-call | flops 1024 | bytes 1024 | tf_op jit(solution)/shard_map/project_parts/pallas_call | solution.py:344
  17.0 0.4 %collective-permute-start.4 = (bf16[128,896]{1,0:T(8,128)(2,1)S(1)}, bf16[128,896]{1,0:T(8,128)(2,1)S(1)}, u32[]{:S(2)}, u32[]{:S(2)}) collective-permute-start(bf16[128,896]{1,0:T(8,128)(2,1)S(1)} %get-tuple-element.68), channel_id=1, source_target_pairs={{0,1},{1,0},{2,3},{3,2},{4,5},{5,4},{6,7},{7,6},{8,9},{9,8},{10,11... | collective-permute-start | bytes 688136 | tf_op jit(solution)/shard_map/ppermute | solution.py:30
  17.4 0.0 collective-permute-done.5
  17.5 1.6 %collective-permute-start.6 = (bf16[128,512]{1,0:T(8,128)(2,1)S(1)}, bf16[128,512]{1,0:T(8,128)(2,1)S(1)}, u32[]{:S(2)}, u32[]{:S(2)}) collective-permute-start(bf16[128,512]{1,0:T(8,128)(2,1)S(1)} %add_convert_fusion.1), channel_id=1, source_target_pairs={{0,2},{1,3},{2,0},{3,1},{4,6},{5,7},{6,4},{7,5},{8,10},{9,11},{10,... | collective-permute-start | bytes 393224 | tf_op jit(solution)/shard_map/ppermute | solution.py:30
  19.0 0.0 collective-permute-done.7
  19.1 0.6 %collective-permute-start.8 = (bf16[128,384]{1,0:T(8,128)(2,1)S(1)}, bf16[128,384]{1,0:T(8,128)(2,1)S(1)}, u32[]{:S(2)}, u32[]{:S(2)}) collective-permute-start(bf16[128,384]{1,0:T(8,128)(2,1)S(1)} %add_convert_fusion.2), channel_id=1, source_target_pairs={{0,2},{1,3},{2,0},{3,1},{4,6},{5,7},{6,4},{7,5},{8,10},{9,11},{10,... | collective-permute-start | bytes 294920 | tf_op jit(solution)/shard_map/ppermute | solution.py:30
  19.7 0.0 collective-permute-done.4.other_ref
  19.7 0.4 %project_onto.1 = f32[128,896]{1,0:T(8,128)S(1)} custom-call(bf16[128,1024]{1,0:T(8,128)(2,1)S(1)} %get-tuple-element.64.attended_ref, bf16[1024,896]{1,0:T(8,128)(2,1)S(1)} %get-tuple-element.65.part_ref, bf16[128,896]{1,0:T(8,128)(2,1)S(1)} %collective-permute-done.4.other_ref), custom_call_target="tpu_custom_call" | custom-call | flops 1024 | bytes 1024 | tf_op jit(solution)/shard_map/project_onto/pallas_call | solution.py:361
  20.1 5.1 %collective-permute-done.8 = bf16[128,384]{1,0:T(8,128)(2,1)S(1)} collective-permute-done((bf16[128,384]{1,0:T(8,128)(2,1)S(1)}, bf16[128,384]{1,0:T(8,128)(2,1)S(1)}, u32[]{:S(2)}, u32[]{:S(2)}) %collective-permute-start.8) | collective-permute-done | bytes 98336 | tf_op jit(solution)/shard_map/ppermute | solution.py:30
  25.2 0.0 collective-permute-done.6
  25.2 0.7 %add_convert_fusion = bf16[128,896]{1,0:T(8,128)(2,1)} fusion(f32[128,896]{1,0:T(8,128)S(1)} %project_onto.1, bf16[128,384]{1,0:T(8,128)(2,1)S(1)} %collective-permute-done.8, bf16[128,512]{1,0:T(8,128)(2,1)S(1)} %collective-permute-done.6), kind=kLoop, calls=%fused_computation | loop fusion | flops 688128 | bytes 917504 | tf_op jit(solution)/shard_map/convert_element_type | solution.py:444
  (2 shorter events, 0.0 us)
Async XLA Ops:
  0.0 11.6 %collective-permute-start = (bf16[576,128]{1,0:T(8,128)(2,1)}, bf16[576,128]{1,0:T(8,128)(2,1)S(1)}, u32[]{:S(2)}, u32[]{:S(2)}) collective-permute-start(bf16[576,128]{1,0:T(8,128)(2,1)} %bitcast.1), channel_id=1, source_target_pairs={{0,4},{1,13},{2,6},{3,15},{4,8},{5,1},{6,10},{7,3},{8,12},{9,5},{1... | collective-permute-start | bytes 442376 | tf_op jit(solution)/shard_map/ppermute | solution.py:30
  3.0 9.4 %collective-permute-start.1 = (bf16[576,128]{1,0:T(8,128)(2,1)}, bf16[576,128]{1,0:T(8,128)(2,1)S(1)}, u32[]{:S(2)}, u32[]{:S(2)}) collective-permute-start(bf16[576,128]{1,0:T(8,128)(2,1)} %bitcast.2), channel_id=1, source_target_pairs={{0,8},{1,1},{2,10},{3,3},{4,4},{5,13},{6,6},{7,15},{8,0},{9,9},{10... | collective-permute-start | bytes 442376 | tf_op jit(solution)/shard_map/ppermute | solution.py:30
  11.6 1.4 %collective-permute-start.3 = (bf16[576,128]{1,0:T(8,128)(2,1)S(1)}, bf16[576,128]{1,0:T(8,128)(2,1)S(1)}, u32[]{:S(2)}, u32[]{:S(2)}) collective-permute-start(bf16[576,128]{1,0:T(8,128)(2,1)S(1)} %collective-permute-done.block_ref), channel_id=1, source_target_pairs={{0,1},{1,0},{2,3},{3,2},{4,5},{5,4},{6,7},{7,6},{8,9},{9,8},{10,11... | collective-permute-start | bytes 442376 | tf_op jit(solution)/shard_map/ppermute | solution.py:30
  12.4 1.5 %collective-permute-start.2 = (bf16[576,128]{1,0:T(8,128)(2,1)S(1)}, bf16[576,128]{1,0:T(8,128)(2,1)S(1)}, u32[]{:S(2)}, u32[]{:S(2)}) collective-permute-start(bf16[576,128]{1,0:T(8,128)(2,1)S(1)} %collective-permute-done.1.refs_0_), channel_id=1, source_target_pairs={{0,1},{1,0},{2,3},{3,2},{4,5},{5,4},{6,7},{7,6},{8,9},{9,8},{10,11... | collective-permute-start | bytes 442376 | tf_op jit(solution)/shard_map/ppermute | solution.py:30
  15.7 1.7 %collective-permute-start.5 = (bf16[128,512]{1,0:T(8,128)(2,1)S(1)}, bf16[128,512]{1,0:T(8,128)(2,1)S(1)}, u32[]{:S(2)}, u32[]{:S(2)}) collective-permute-start(bf16[128,512]{1,0:T(8,128)(2,1)S(1)} %get-tuple-element.70), channel_id=1, source_target_pairs={{0,1},{1,0},{2,3},{3,2},{4,5},{5,4},{6,7},{7,6},{8,9},{9,8},{10,11... | collective-permute-start | bytes 393224 | tf_op jit(solution)/shard_map/ppermute | solution.py:30
  16.1 2.9 %collective-permute-start.7 = (bf16[128,384]{1,0:T(8,128)(2,1)S(1)}, bf16[128,384]{1,0:T(8,128)(2,1)S(1)}, u32[]{:S(2)}, u32[]{:S(2)}) collective-permute-start(bf16[128,384]{1,0:T(8,128)(2,1)S(1)} %get-tuple-element.72), channel_id=1, source_target_pairs={{0,1},{1,0},{2,3},{3,2},{4,5},{5,4},{6,7},{7,6},{8,9},{9,8},{10,11... | collective-permute-start | bytes 294920 | tf_op jit(solution)/shard_map/ppermute | solution.py:30
  17.0 2.6 %collective-permute-start.4 = (bf16[128,896]{1,0:T(8,128)(2,1)S(1)}, bf16[128,896]{1,0:T(8,128)(2,1)S(1)}, u32[]{:S(2)}, u32[]{:S(2)}) collective-permute-start(bf16[128,896]{1,0:T(8,128)(2,1)S(1)} %get-tuple-element.68), channel_id=1, source_target_pairs={{0,1},{1,0},{2,3},{3,2},{4,5},{5,4},{6,7},{7,6},{8,9},{9,8},{10,11... | collective-permute-start | bytes 688136 | tf_op jit(solution)/shard_map/ppermute | solution.py:30
  17.5 7.7 %collective-permute-start.6 = (bf16[128,512]{1,0:T(8,128)(2,1)S(1)}, bf16[128,512]{1,0:T(8,128)(2,1)S(1)}, u32[]{:S(2)}, u32[]{:S(2)}) collective-permute-start(bf16[128,512]{1,0:T(8,128)(2,1)S(1)} %add_convert_fusion.1), channel_id=1, source_target_pairs={{0,2},{1,3},{2,0},{3,1},{4,6},{5,7},{6,4},{7,5},{8,10},{9,11},{10,... | collective-permute-start | bytes 393224 | tf_op jit(solution)/shard_map/ppermute | solution.py:30
  19.1 6.1 %collective-permute-start.8 = (bf16[128,384]{1,0:T(8,128)(2,1)S(1)}, bf16[128,384]{1,0:T(8,128)(2,1)S(1)}, u32[]{:S(2)}, u32[]{:S(2)}) collective-permute-start(bf16[128,384]{1,0:T(8,128)(2,1)S(1)} %add_convert_fusion.2), channel_id=1, source_target_pairs={{0,2},{1,3},{2,0},{3,1},{4,6},{5,7},{6,4},{7,5},{8,10},{9,11},{10,... | collective-permute-start | bytes 294920 | tf_op jit(solution)/shard_map/ppermute | solution.py:30

commit v16 on v14

--- a/solution.py
+++ b/solution.py
@@ -62,7 +62,7 @@
 EXPONENT = QUERY**-0.5 * 1.4426950408889634
 
 
-def expand(turned, key_weight, value_weight, keys_ref, values_ref):
+def expand_keys(turned, key_weight, keys_ref):
     rows = turned.shape[1]
     compressed = turned[:LATENT, :]
     rope = turned[LATENT:, :]
@@ -74,8 +74,17 @@
         keys_ref[start : start + HEAD_DIM, :] = nope[head * HEAD_DIM : (head + 1) * HEAD_DIM, :]
         keys_ref[start + HEAD_DIM : start + QUERY, :] = rope
         keys_ref[start + QUERY : start + PADDED, :] = nothing
+
+
+def expand_values(turned, value_weight, values_ref):
+    compressed = turned[:LATENT, :]
     values = jnp.dot(compressed.T, value_weight[...], preferred_element_type=jnp.float32)
     values_ref[...] = values.astype(jnp.bfloat16)
+
+
+def expand(turned, key_weight, value_weight, keys_ref, values_ref):
+    expand_keys(turned, key_weight, keys_ref)
+    expand_values(turned, value_weight, values_ref)
 
 
 def prepare_kernel(half, *refs):
@@ -265,10 +274,11 @@
 
     for start in range(0, count + 1, 2):
         if start + 2 > count:
-            expand(turned_ref[...], key_weight, value_weight, last_keys, last_values)
+            expand_keys(turned_ref[...], key_weight, last_keys)
         first_ref, second_ref = keys[start : start + 2]
         into = start * rows
         score(padded_ref, bias_ref, first_ref, second_ref, scores_ref, into + 2 * rows, into)
+    expand_values(turned_ref[...], value_weight, last_values)
     peaks = []
     for head in range(heads):
         early = jnp.max(early_ref[lines(head), :], axis=1, keepdims=True)

time: 26.2 us -> 26.4 us (level)
  no operation moved by 1% of the time
where the time goes in v16:
time: 26.4 us; the launch traced here: 26.2 us
  starting transfers between devices  10.2 us (39%)
  Pallas kernels  8.62 us (33%)
  waiting for transfers between devices  6.46 us (24%)
  other arithmetic  0.77 us (3%)
    ppermute x7, starting transfers between devices, routed(): return lax.ppermute(value, ('ctx', 'head'), pairs)  10.2 us
    ppermute x7, waiting for transfers between devices, routed(): return lax.ppermute(value, ('ctx', 'head'), pairs)  6.46 us
    pallas_call x1, Pallas kernels, prepare(): pl.pallas_call(functools.partial(prepare_kernel, rows // 2), out_shape=[n...  4.08 us
    pallas_call x1, Pallas kernels, attend(): pl.pallas_call(functools.partial(attend_kernel, len(keys)), out_shape=[na...  2.01 us
    pallas_call x1, Pallas kernels, expand_and_score(): pl.pallas_call(expand_and_score_kernel, out_shape=[narrow_shape(heads * P...  0.76 us
    convert_element_type x1, other arithmetic, shards(): return (project_onto(attended, parts[3], beside) + far_part).astype(narrow)  0.73 us
    pallas_call x1, Pallas kernels, project_parts(): pl.pallas_call(functools.partial(project_kernel, [len(group) for group in...  0.72 us
    pallas_call x1, Pallas kernels, expand_block(): pl.pallas_call(expand_kernel, out_shape=[narrow_shape(heads * PADDED, row...  0.62 us
  transfers between devices with their start and end apart: 7, of which 5 were waited for; matrix products, arithmetic and copies ran while one was open for 0% of the time, Pallas kernels for 25%

profile of v16, /device:TPU:0, one launch (start us, length us, event | category | flops | bytes accessed | tf_op | source)
XLA Modules:
  0.0 26.2 jit_solution(2961583903513077145)
XLA Ops:
  0.0 3.0 %collective-permute-start = (bf16[576,128]{1,0:T(8,128)(2,1)}, bf16[576,128]{1,0:T(8,128)(2,1)S(1)}, u32[]{:S(2)}, u32[]{:S(2)}) collective-permute-start(bf16[576,128]{1,0:T(8,128)(2,1)} %bitcast.1), channel_id=1, source_target_pairs={{0,4},{1,13},{2,6},{3,15},{4,8},{5,1},{6,10},{7,3},{8,12},{9,5},{1... | collective-permute-start | bytes 442376 | tf_op jit(solution)/shard_map/ppermute | solution.py:29
  3.0 4.5 %collective-permute-start.1 = (bf16[576,128]{1,0:T(8,128)(2,1)}, bf16[576,128]{1,0:T(8,128)(2,1)S(1)}, u32[]{:S(2)}, u32[]{:S(2)}) collective-permute-start(bf16[576,128]{1,0:T(8,128)(2,1)} %bitcast.2), channel_id=1, source_target_pairs={{0,8},{1,1},{2,10},{3,3},{4,4},{5,13},{6,6},{7,15},{8,0},{9,9},{10... | collective-permute-start | bytes 442376 | tf_op jit(solution)/shard_map/ppermute | solution.py:29
  7.5 4.1 %prepare.1 = (bf16[128,2048]{1,0:T(8,128)(2,1)S(1)}, f32[128,512]{1,0:T(8,128)S(1)}, bf16[2048,128]{1,0:T(8,128)(2,1)S(1)}, bf16[128,1024]{1,0:T(8,128)(2,1)S(1)...) custom-call(s32[8]{0:T(128)} %refs_0_.1, ...), custom_call_target="tpu_custom_call" | custom-call | flops 268435456 | bytes 9830400 | tf_op jit(solution)/shard_map/prepare/pallas_call | solution.py:149
  11.6 0.0 collective-permute-done.block_ref
  11.6 0.1 collective-permute-start.3
  11.7 0.6 %expand_block.1 = (bf16[2048,128]{1,0:T(8,128)(2,1)S(1)}, bf16[128,1024]{1,0:T(8,128)(2,1)S(1)}) custom-call(bf16[576,128]{1,0:T(8,128)(2,1)S(1)} %collective-permute-done.block_ref, bf16[1024,512]{1,0:T(8,128)(2,1)S(1)} %get-tuple-element.49.key_weight, bf16[512,1024]{1,0:T(8,128)(2,1)S(1)} %get-tuple-element.50.value_weight), custom_call_target="tpu_custom_call" | custom-call | flops 268435456 | bytes 1048576 | tf_op jit(solution)/shard_map/expand_block/pallas_call | solution.py:227
  12.3 0.1 collective-permute-done.1.refs_0_
  12.4 0.5 %collective-permute-start.2 = (bf16[576,128]{1,0:T(8,128)(2,1)S(1)}, bf16[576,128]{1,0:T(8,128)(2,1)S(1)}, u32[]{:S(2)}, u32[]{:S(2)}) collective-permute-start(bf16[576,128]{1,0:T(8,128)(2,1)S(1)} %collective-permute-done.1.refs_0_), channel_id=1, source_target_pairs={{0,1},{1,0},{2,3},{3,2},{4,5},{5,4},{6,7},{7,6},{8,9},{9,8},{10,11... | collective-permute-start | bytes 442376 | tf_op jit(solution)/shard_map/ppermute | solution.py:29
  12.9 0.2 collective-permute-done.3.block_ref
  13.0 0.8 %expand_and_score.1 = (bf16[2048,128]{1,0:T(8,128)(2,1)S(1)}, bf16[128,1024]{1,0:T(8,128)(2,1)S(1)}, f32[1024,256]{1,0:T(8,128)S(1)}) custom-call(bf16[576,128]{1,0:T(8,128)(2,1)S(1)} %collective-permute-done.3.block_ref, bf16[1024,512]{1,0:T(8,128)(2,1)S(1)} %get-tuple-element.49.key_weight, bf16[512,1024]{1,0:T(8,128)(2,1)S(1)} %get-tuple-element.50.value_weight, ...), custom_call_target="tpu_custom_call" | custom-call | flops 402653184 | bytes 1048576 | tf_op jit(solution)/shard_map/expand_and_score/pallas_call | solution.py:201
  13.8 0.1 collective-permute-done.2.refs_1_
  13.9 2.0 %attend.1 = (bf16[128,1024]{1,0:T(8,128)(2,1)S(1)}, bf16[128,896]{1,0:T(8,128)(2,1)S(1)}) custom-call(bf16[128,2048]{1,0:T(8,128)(2,1)S(1)} %get-tuple-element.47.padded_ref, f32[128,512]{1,0:T(8,128)S(1)} %get-tuple-element.48.bias_ref, bf16[1024,512]{1,0:T(8,128)(2,1)S(1)} %get-tuple-element.49.key_weight, ...), custom_call_target="tpu_custom_call" | custom-call | flops 1040187392 | bytes 1835008 | tf_op jit(solution)/shard_map/attend/pallas_call | solution.py:313
  15.9 0.4 %collective-permute-start.5 = (bf16[128,896]{1,0:T(8,128)(2,1)S(1)}, bf16[128,896]{1,0:T(8,128)(2,1)S(1)}, u32[]{:S(2)}, u32[]{:S(2)}) collective-permute-start(bf16[128,896]{1,0:T(8,128)(2,1)S(1)} %get-tuple-element.68), channel_id=1, source_target_pairs={{0,1},{1,0},{2,3},{3,2},{4,5},{5,4},{6,7},{7,6},{8,9},{9,8},{10,11... | collective-permute-start | bytes 688136 | tf_op jit(solution)/shard_map/ppermute | solution.py:29
  16.3 0.7 %project_parts.1 = (f32[128,896]{1,0:T(8,128)S(1)}, bf16[128,896]{1,0:T(8,128)(2,1)S(1)}) custom-call(bf16[128,1024]{1,0:T(8,128)(2,1)S(1)} %get-tuple-element.62.attended_ref, bf16[1024,896]{1,0:T(8,128)(2,1)S(1)} %get-tuple-element.64.refs_0_, bf16[1024,896]{1,0:T(8,128)(2,1)S(1)} %get-tuple-element.65.refs_1_), custom_call_target="tpu_custom_call" | custom-call | flops 1024 | bytes 1024 | tf_op jit(solution)/shard_map/project_parts/pallas_call | solution.py:353
  17.1 0.2 collective-permute-start.4
  17.3 0.2 collective-permute-done.5
  17.5 1.6 %collective-permute-start.6 = (bf16[128,896]{1,0:T(8,128)(2,1)S(1)}, bf16[128,896]{1,0:T(8,128)(2,1)S(1)}, u32[]{:S(2)}, u32[]{:S(2)}) collective-permute-start(bf16[128,896]{1,0:T(8,128)(2,1)S(1)} %add_convert_fusion.1), channel_id=1, source_target_pairs={{0,2},{1,3},{2,0},{3,1},{4,6},{5,7},{6,4},{7,5},{8,10},{9,11},{10,... | collective-permute-start | bytes 688136 | tf_op jit(solution)/shard_map/ppermute | solution.py:29
  19.1 0.0 collective-permute-done.4.other_ref
  19.1 0.4 %project_onto.1 = f32[128,896]{1,0:T(8,128)S(1)} custom-call(bf16[128,1024]{1,0:T(8,128)(2,1)S(1)} %get-tuple-element.62.attended_ref, bf16[1024,896]{1,0:T(8,128)(2,1)S(1)} %get-tuple-element.63.part_ref, bf16[128,896]{1,0:T(8,128)(2,1)S(1)} %collective-permute-done.4.other_ref), custom_call_target="tpu_custom_call" | custom-call | flops 1024 | bytes 1024 | tf_op jit(solution)/shard_map/project_onto/pallas_call | solution.py:370
  19.5 5.9 %collective-permute-done.6 = bf16[128,896]{1,0:T(8,128)(2,1)S(1)} collective-permute-done((bf16[128,896]{1,0:T(8,128)(2,1)S(1)}, bf16[128,896]{1,0:T(8,128)(2,1)S(1)}, u32[]{:S(2)}, u32[]{:S(2)}) %collective-permute-start.6) | collective-permute-done | bytes 229408 | tf_op jit(solution)/shard_map/ppermute | solution.py:29
  25.4 0.7 %add_convert_fusion = bf16[128,896]{1,0:T(8,128)(2,1)} fusion(f32[128,896]{1,0:T(8,128)S(1)} %project_onto.1, bf16[128,896]{1,0:T(8,128)(2,1)S(1)} %collective-permute-done.6), kind=kLoop, calls=%fused_computation | loop fusion | flops 344064 | bytes 917504 | tf_op jit(solution)/shard_map/convert_element_type | solution.py:448
  (1 shorter events, 0.0 us)
Async XLA Ops:
  0.0 11.6 %collective-permute-start = (bf16[576,128]{1,0:T(8,128)(2,1)}, bf16[576,128]{1,0:T(8,128)(2,1)S(1)}, u32[]{:S(2)}, u32[]{:S(2)}) collective-permute-start(bf16[576,128]{1,0:T(8,128)(2,1)} %bitcast.1), channel_id=1, source_target_pairs={{0,4},{1,13},{2,6},{3,15},{4,8},{5,1},{6,10},{7,3},{8,12},{9,5},{1... | collective-permute-start | bytes 442376 | tf_op jit(solution)/shard_map/ppermute | solution.py:29
  3.0 9.4 %collective-permute-start.1 = (bf16[576,128]{1,0:T(8,128)(2,1)}, bf16[576,128]{1,0:T(8,128)(2,1)S(1)}, u32[]{:S(2)}, u32[]{:S(2)}) collective-permute-start(bf16[576,128]{1,0:T(8,128)(2,1)} %bitcast.2), channel_id=1, source_target_pairs={{0,8},{1,1},{2,10},{3,3},{4,4},{5,13},{6,6},{7,15},{8,0},{9,9},{10... | collective-permute-start | bytes 442376 | tf_op jit(solution)/shard_map/ppermute | solution.py:29
  11.6 1.4 %collective-permute-start.3 = (bf16[576,128]{1,0:T(8,128)(2,1)S(1)}, bf16[576,128]{1,0:T(8,128)(2,1)S(1)}, u32[]{:S(2)}, u32[]{:S(2)}) collective-permute-start(bf16[576,128]{1,0:T(8,128)(2,1)S(1)} %collective-permute-done.block_ref), channel_id=1, source_target_pairs={{0,1},{1,0},{2,3},{3,2},{4,5},{5,4},{6,7},{7,6},{8,9},{9,8},{10,11... | collective-permute-start | bytes 442376 | tf_op jit(solution)/shard_map/ppermute | solution.py:29
  12.4 1.5 %collective-permute-start.2 = (bf16[576,128]{1,0:T(8,128)(2,1)S(1)}, bf16[576,128]{1,0:T(8,128)(2,1)S(1)}, u32[]{:S(2)}, u32[]{:S(2)}) collective-permute-start(bf16[576,128]{1,0:T(8,128)(2,1)S(1)} %collective-permute-done.1.refs_0_), channel_id=1, source_target_pairs={{0,1},{1,0},{2,3},{3,2},{4,5},{5,4},{6,7},{7,6},{8,9},{9,8},{10,11... | collective-permute-start | bytes 442376 | tf_op jit(solution)/shard_map/ppermute | solution.py:29
  15.9 1.6 %collective-permute-start.5 = (bf16[128,896]{1,0:T(8,128)(2,1)S(1)}, bf16[128,896]{1,0:T(8,128)(2,1)S(1)}, u32[]{:S(2)}, u32[]{:S(2)}) collective-permute-start(bf16[128,896]{1,0:T(8,128)(2,1)S(1)} %get-tuple-element.68), channel_id=1, source_target_pairs={{0,1},{1,0},{2,3},{3,2},{4,5},{5,4},{6,7},{7,6},{8,9},{9,8},{10,11... | collective-permute-start | bytes 688136 | tf_op jit(solution)/shard_map/ppermute | solution.py:29
  17.1 2.0 %collective-permute-start.4 = (bf16[128,896]{1,0:T(8,128)(2,1)S(1)}, bf16[128,896]{1,0:T(8,128)(2,1)S(1)}, u32[]{:S(2)}, u32[]{:S(2)}) collective-permute-start(bf16[128,896]{1,0:T(8,128)(2,1)S(1)} %get-tuple-element.66), channel_id=1, source_target_pairs={{0,1},{1,0},{2,3},{3,2},{4,5},{5,4},{6,7},{7,6},{8,9},{9,8},{10,11... | collective-permute-start | bytes 688136 | tf_op jit(solution)/shard_map/ppermute | solution.py:29
  17.5 7.9 %collective-permute-start.6 = (bf16[128,896]{1,0:T(8,128)(2,1)S(1)}, bf16[128,896]{1,0:T(8,128)(2,1)S(1)}, u32[]{:S(2)}, u32[]{:S(2)}) collective-permute-start(bf16[128,896]{1,0:T(8,128)(2,1)S(1)} %add_convert_fusion.1), channel_id=1, source_target_pairs={{0,2},{1,3},{2,0},{3,1},{4,6},{5,7},{6,4},{7,5},{8,10},{9,11},{10,... | collective-permute-start | bytes 688136 | tf_op jit(solution)/shard_map/ppermute | solution.py:29
